TPU v7x, 32 devices: a whole 2x2x4 slice. The times are simulated.
32 devices in a mesh: grp: 2 (over x), blk: 16 (over z, y, core).
Axes of the slice: x: 2, y: 2, z: 4, core: 2. Of those that a mesh axis runs over, the one named last changes fastest.
Arguments:
- tokens: bfloat16 [512, 6144], P(('grp', 'blk')), parts along dimension 0, may hold values from -6 to 6
- cotangent: bfloat16 [128, 6144], P(('grp', 'blk')), parts along dimension 0, may hold values from -2.390625 to 2.390625
- gate_weight: bfloat16 [6144, 8192], P(None, 'blk'), may hold values from -0.078125 to 0.078125
- up_weight: bfloat16 [6144, 8192], P(None, 'blk'), may hold values from -0.078125 to 0.078125
- down_weight: bfloat16 [8192, 6144], P('blk'), may hold values from -0.0625 to 0.0625
- logits: float32 [512, 8], P(('grp', 'blk')), parts along dimension 0, may hold values from -24 to 300, as said below
- ref_logits: float32 [512, 8], P(('grp', 'blk')), parts along dimension 0, may hold values from -24 to 300, as said below
- routes: int32 [512, 2], P(('grp', 'blk')), parts along dimension 0, may hold values from 0 to 7, as said below
Outputs:
- grad_gate: bfloat16 [12288, 8192], P('grp', 'blk'), parts along dimension 0
- grad_up: bfloat16 [12288, 8192], P('grp', 'blk'), parts along dimension 0
- grad_down: bfloat16 [16384, 6144], P(('grp', 'blk')), parts along dimension 0
- grad_tokens: bfloat16 [512, 6144], P(('grp', 'blk')), parts along dimension 0
- grad_logits: float32 [512, 8], P(('grp', 'blk')), parts along dimension 0
- entropy: float32 [512], P(('grp', 'blk')), parts along dimension 0
- divergence: float32 [512], P(('grp', 'blk')), parts along dimension 0
There are 2 independent parts, one for each index of `grp`. A program takes and returns all parts, laid end to end along the dimension named above; an argument that names none is the same for every part. Nothing has to cross between parts.
Inputs may be any that keep to these rules, and one draw needn't show every extreme that they name: `routes`: each row names two different experts. In each aligned block of 16 rows (the tokens of one index of blk) between half of 4 and 4 rows name expert 0, and in every draw some block has exactly 4. `logits`: finite values. `ref_logits`: finite values.
All inputs are finite; a program needn't handle non-finite values.
Results may differ from a plain program's by a relative error of at most 0.0056.
Values may be sent and summed in bfloat16 or wider, within the bound.
No kernel may reach another device: no remote copies, remote signals or barrier semaphores. Data moves between devices by JAX's collectives and lax.ppermute only.
A program may use at most 128 MiB of HBM per device.

v0:
```python
import jax
import jax.numpy as jnp
from jax import lax
from jax.sharding import PartitionSpec as P


def contract_rows(left, right):
    return lax.dot_general(
        left, right, (((0,), (0,)), ((), ())), preferred_element_type=jnp.float32
    )


def contract_cols(left, right):
    return lax.dot_general(
        left, right, (((1,), (1,)), ((), ())), preferred_element_type=jnp.float32
    )


def shards(tokens, cotangent, gate_weight, up_weight, down_weight, logits, ref_logits, routes):
    policy_log = jax.nn.log_softmax(logits, axis=1)
    frozen_log = jax.nn.log_softmax(ref_logits, axis=1)
    probs = jnp.exp(policy_log)
    entropy = -jnp.sum(probs * policy_log, axis=1)
    divergence = jnp.sum(probs * (policy_log - frozen_log), axis=1)
    is_window = routes == 0
    routed = jnp.any(is_window, axis=1)
    partner = routes[:, 0] + routes[:, 1]
    columns = jnp.arange(logits.shape[1], dtype=jnp.int32)
    partner_hot = (columns[None, :] == partner[:, None]).astype(jnp.float32)
    partner_logit = jnp.sum(logits * partner_hot, axis=1)
    gate = jnp.where(routed, jax.nn.sigmoid(logits[:, 0] - partner_logit), jnp.float32(0.0))
    gate_low = gate.astype(jnp.bfloat16)
    slot_count = cotangent.shape[0]
    position = jnp.cumsum(routed.astype(jnp.int32)) - 1
    slot_ids = jnp.arange(slot_count, dtype=jnp.int32)
    select = (position[None, :] == slot_ids[:, None]) & routed[None, :]
    select_low = select.astype(jnp.bfloat16)
    select_full = select.astype(jnp.float32)
    x_slots = jnp.dot(select_low, tokens, preferred_element_type=jnp.float32).astype(jnp.bfloat16)
    g_slots = jnp.sum(select_full * gate_low.astype(jnp.float32)[None, :], axis=1).astype(
        jnp.bfloat16
    )
    x_all, y_all, g_all = (
        lax.all_gather(x_slots, "blk", axis=0, tiled=True),
        lax.all_gather(cotangent, "blk", axis=0, tiled=True),
        lax.all_gather(g_slots, "blk", axis=0, tiled=True),
    )
    pre_gate = jnp.dot(x_all, gate_weight, preferred_element_type=jnp.float32)
    pre_up = jnp.dot(x_all, up_weight, preferred_element_type=jnp.float32)
    sig = jax.nn.sigmoid(pre_gate)
    act = pre_gate * sig
    hidden = act * pre_up
    g_col = g_all.astype(jnp.float32)[:, None]
    weighted = (g_col * hidden).astype(jnp.bfloat16)
    back = contract_cols(y_all, down_weight)
    store_products = jnp.sum(hidden * back, axis=1)
    scaled = g_col * back
    store_gate = (scaled * pre_up * sig * (1.0 + pre_gate * (1.0 - sig))).astype(jnp.bfloat16)
    store_up = (scaled * act).astype(jnp.bfloat16)
    acc_gate = contract_rows(x_all, store_gate)
    acc_up = contract_rows(x_all, store_up)
    acc_down = contract_rows(weighted, y_all)
    slot_products = lax.psum_scatter(store_products, "blk", scatter_dimension=0, tiled=True)
    slot_grads = lax.psum_scatter(
        contract_cols(store_gate, gate_weight) + contract_cols(store_up, up_weight),
        "blk",
        scatter_dimension=0,
        tiled=True,
    )
    grad_tokens = lax.dot_general(
        select_full,
        slot_grads,
        (((0,), (0,)), ((), ())),
        precision=lax.Precision.HIGHEST,
        preferred_element_type=jnp.float32,
    ).astype(jnp.bfloat16)
    token_products = jnp.sum(select_full * slot_products[:, None], axis=0)
    slope = gate * (1.0 - gate)
    window_hot = (columns == 0).astype(jnp.float32)
    kl_grad = probs * (policy_log - frozen_log - divergence[:, None])
    grad_logits = kl_grad + (window_hot[None, :] - partner_hot) * (token_products * slope)[:, None]
    return (
        acc_gate.astype(jnp.bfloat16),
        acc_up.astype(jnp.bfloat16),
        acc_down.astype(jnp.bfloat16),
        grad_tokens,
        grad_logits,
        entropy,
        divergence,
    )


def solution(mesh):
    in_specs = (
        P(("grp", "blk"), None),
        P(("grp", "blk"), None),
        P(None, "blk"),
        P(None, "blk"),
        P("blk", None),
        P(("grp", "blk"), None),
        P(("grp", "blk"), None),
        P(("grp", "blk"), None),
    )
    out_specs = (
        P("grp", "blk"),
        P("grp", "blk"),
        P(("grp", "blk"), None),
        P(("grp", "blk"), None),
        P(("grp", "blk"), None),
        P(("grp", "blk")),
        P(("grp", "blk")),
    )
    return jax.shard_map(shards, mesh=mesh, in_specs=in_specs, out_specs=out_specs, check_vma=False)
```

profile of v0, /device:TPU:0, one launch (start us, length us, event | category | flops | bytes accessed | tf_op | source)
XLA Modules:
  0.0 245.3 jit_solution(14294669739316227574)
XLA Ops:
  7.2 0.0 copy-start
  7.2 0.0 all-reduce.5.cloned.1.call-start
  7.2 0.7 compare_reduce_fusion
  8.0 0.8 add_bitcast_fusion
  8.7 0.7 reduce_max.14
  9.4 0.7 reduce_max.13
  10.1 0.7 exponential_reduce_fusion.1
  10.9 0.7 exponential_reduce_fusion
  11.6 0.7 fusion.7
  12.3 0.7 convert_convert_fusion
  13.0 0.1 copy.18
  13.1 0.1 add_reduce_fusion
  13.3 0.2 fusion
  13.4 25.5 %all-gather = bf16[16,4,6144]{2,1,0:T(4,128)(2,1)S(1)} all-gather(bf16[1,4,6144]{2,1,0:T(4,128)(2,1)S(1)} %fusion), channel_id=1, replica_groups=mesh['grp'=2,'blk'=16] {'blk'}, dimensions={0}, use_global_device_ids=true | all-gather | bytes 835584 | tf_op jit(solution)/shard_map/all_gather | solution.py:44
  38.9 0.2 reshape.81
  39.1 0.0 copy-start.1
  39.1 0.0 copy-start.6
  39.1 4.1 %fusion.21 = f32[64,512]{1,0:T(8,128)S(1)} fusion(bf16[64,6144]{1,0:T(8,128)(2,1)S(1)} %reshape.81, bf16[6144,512]{1,0:T(8,128)(2,1)} %param.11), kind=kOutput, calls=%fused_computation.52 | convolution fusion | flops 402653184 | bytes 7208960 | tf_op jit(solution)/shard_map/dot_general | solution.py:48
  43.2 0.4 copy-done.1
  43.7 1.2 fusion.20
  44.9 0.0 copy-start.8
  44.9 0.0 copy-done.6
  44.9 19.6 %all-gather.1 = bf16[16,4,6144]{2,1,0:T(4,128)(2,1)S(1)} all-gather(bf16[1,4,6144]{2,1,0:T(4,128)(2,1)S(1)} %bitcast.58), channel_id=1, replica_groups=mesh['grp'=2,'blk'=16] {'blk'}, dimensions={0}, use_global_device_ids=true | all-gather | bytes 835584 | tf_op jit(solution)/shard_map/all_gather | solution.py:45
  64.5 0.2 reshape.83
  64.7 0.0 copy-start.2
  64.7 0.9 copy-done.2
  65.6 5.6 %multiply_reduce_fusion = (f32[64]{0:T(128)S(1)}, f32[64,512]{1,0:T(8,128)}) fusion(f32[64,512]{1,0:T(8,128)S(1)} %fusion.20, f32[64,512]{1,0:T(8,128)S(1)} %fusion.21, bf16[64,6144]{1,0:T(8,128)(2,1)S(1)} %reshape.83, bf16[512,6144]{1,0:T(8,128)(2,1)} %param.13), kind=kOutput, calls=%fused_computation.7 | convolution fusion | flops 402882496 | bytes 7471360 | tf_op jit(solution)/shard_map/dot_general | solution.py:14
  71.2 0.0 slice-start
  71.2 31.4 %all-reduce.2 = f32[64]{0:T(128)S(1)} all-reduce(f32[64]{0:T(128)S(1)} %get-tuple-element.17), channel_id=3, replica_groups=mesh['grp'=2,'blk'=16] {'blk'}, use_global_device_ids=true, to_apply=%region_9.11.clone | all-reduce | flops 64 | bytes 512
  102.6 0.6 fusion.17
  104.5 0.1 dynamic-slice.4
  104.6 0.1 select_reduce_fusion.1
  104.7 0.2 dynamic-update-slice
  104.9 29.5 %all-reduce = bf16[64]{0:T(256)(128)(2,1)S(1)} all-reduce(bf16[64]{0:T(256)(128)(2,1)S(1)} %dynamic-update-slice), channel_id=1, replica_groups=mesh['grp'=2,'blk'=16] {'blk'}, use_global_device_ids=true, to_apply=%add | all-reduce | flops 64 | bytes 256
  134.5 1.0 multiply_convert_fusion.1
  135.5 0.0 slice-start.1
  135.5 4.9 %fusion.22 = f32[64,6144]{1,0:T(8,128)S(1)} fusion(bf16[64,512]{1,0:T(8,128)(2,1)S(1)} %get-tuple-element.14, bf16[6144,512]{1,0:T(8,128)(2,1)} %param.11), kind=kOutput, calls=%fused_computation.53 | convolution fusion | flops 402653184 | bytes 7929856 | tf_op jit(solution)/shard_map/dot_general | solution.py:14
  140.4 3.2 %convolution_add_fusion = f32[64,6144]{1,0:T(8,128)} fusion(f32[64,6144]{1,0:T(8,128)S(1)} %fusion.22, bf16[64,512]{1,0:T(8,128)(2,1)S(1)} %get-tuple-element.13, bf16[6144,512]{1,0:T(8,128)(2,1)S(1)} %bitcast.57), kind=kOutput, calls=%fused_computation.3 | convolution fusion | flops 403046400 | bytes 9502720 | tf_op jit(solution)/shard_map/dot_general | solution.py:14
  143.6 0.0 all-reduce.5.cloned.1.call-update
  143.6 0.0 copy-start.4
  143.6 0.0 copy-start.5
  143.7 4.5 %convolution_convert_fusion.1 = bf16[6144,512]{1,0:T(8,128)(2,1)} fusion(bf16[64,6144]{1,0:T(8,128)(2,1)S(1)} %reshape.81, bf16[64,512]{1,0:T(8,128)(2,1)S(1)} %get-tuple-element.13), kind=kOutput, calls=%fused_computation.1 | convolution fusion | flops 405798912 | bytes 7143424 | tf_op jit(solution)/shard_map/dot_general | solution.py:8
  148.2 0.5 neg.19
  148.7 0.7 fusion.6
  149.4 4.5 %convolution_convert_fusion.2 = bf16[6144,512]{1,0:T(8,128)(2,1)} fusion(bf16[64,6144]{1,0:T(8,128)(2,1)S(1)} %reshape.81, bf16[64,512]{1,0:T(8,128)(2,1)S(1)} %get-tuple-element.14), kind=kOutput, calls=%fused_computation.2 | convolution fusion | flops 405798912 | bytes 7143424 | tf_op jit(solution)/shard_map/dot_general | solution.py:8
  153.9 4.6 %convolution_convert_fusion = bf16[512,6144]{1,0:T(8,128)(2,1)} fusion(bf16[64,6144]{1,0:T(8,128)(2,1)S(1)} %copy-done.3, f32[64]{0:T(128)S(1)} %convert_element_type.73, f32[64,512]{1,0:T(8,128)S(1)} %fusion.20, f32[64,512]{1,0:T(8,128)S(1)} %fusion.21), kind=kOutput, calls=%fused_computation | convolution fusion | flops 406028288 | bytes 7340288 | tf_op jit(solution)/shard_map/dot_general | solution.py:8
  158.5 77.9 %all-reduce.5.cloned.1.call-done = f32[64,6144]{1,0:T(8,128)} async-done(((f32[64,6144]{1,0:T(8,128)}), f32[64,6144]{1,0:T(8,128)}) %all-reduce.5.cloned.1.call-update) | async-done | bytes 1572880
  236.5 2.0 convolution_convert_fusion.3
  (19 shorter events, 0.1 us)
Async XLA Ops:
  7.2 6.1 %copy-start = (bf16[16,6144]{1,0:T(8,128)(2,1)S(1)}, bf16[16,6144]{1,0:T(8,128)(2,1)}, u32[]{:S(2)}) copy-start(bf16[16,6144]{1,0:T(8,128)(2,1)} %param.9) | copy-start | bytes 589828
  7.2 229.3 %all-reduce.5.cloned.1.call-start = ((), (), s32[]{:S(2)}) async-start(), calls=%async_computation | async-start | bytes 3145728
  12.3 136.4 %copy-start.7 = (f32[16]{0:T(128)}, f32[16]{0:T(128)S(1)}, u32[]{:S(2)}) copy-start(f32[16]{0:T(128)S(1)} %get-tuple-element.9) | copy-start | bytes 196
  39.1 4.6 %copy-start.1 = (bf16[6144,512]{1,0:T(8,128)(2,1)S(1)}, bf16[6144,512]{1,0:T(8,128)(2,1)}, u32[]{:S(2)}) copy-start(bf16[6144,512]{1,0:T(8,128)(2,1)} %param.12) | copy-start | bytes 18874372
  39.1 5.8 %copy-start.6 = (bf16[4,6144]{1,0:T(4,128)(2,1)S(1)}, bf16[4,6144]{1,0:T(4,128)(2,1)}, u32[]{:S(2)}) copy-start(bf16[4,6144]{1,0:T(4,128)(2,1)} %param.10) | copy-start | bytes 147460
  44.9 57.7 %copy-start.8 = (u32[32]{0:T(128)S(1)}, u32[32]{0:T(128)}, u32[]{:S(2)}) copy-start(u32[32]{0:T(128)} %constant.31) | copy-start | bytes 388
  64.7 0.9 copy-start.2
  71.2 69.3 %slice-start = ((s8[6291456]{0:T(1024)(128)(4,1)}), s8[2097152]{0:T(1024)(128)(4,1)S(1)}, s32[]{:S(2)}) async-start(s8[6291456]{0:T(1024)(128)(4,1)} %bitcast.56), calls=%async_computation.1 | async-start | bytes 4194304
  135.5 5.0 %slice-start.1 = ((s8[6291456]{0:T(1024)(128)(4,1)}), s8[4194304]{0:T(1024)(128)(4,1)S(1)}, s32[]{:S(2)}) async-start(s8[6291456]{0:T(1024)(128)(4,1)} %bitcast.56), calls=%async_computation.2 | async-start | bytes 8388608
  143.6 5.1 %copy-start.4 = (f32[16,8]{0,1:T(8,128)S(1)}, f32[16,8]{0,1:T(8,128)}, u32[]{:S(2)}) copy-start(f32[16,8]{0,1:T(8,128)} %param.14) | copy-start | bytes 1540
  143.6 5.1 %copy-start.5 = (f32[16,8]{0,1:T(8,128)S(1)}, f32[16,8]{0,1:T(8,128)}, u32[]{:S(2)}) copy-start(f32[16,8]{0,1:T(8,128)} %param.15) | copy-start | bytes 1540
  148.2 5.7 %copy-start.3 = (bf16[64,6144]{1,0:T(8,128)(2,1)S(1)}, bf16[64,6144]{1,0:T(8,128)(2,1)}, u32[]{:S(2)}) copy-start(bf16[64,6144]{1,0:T(8,128)(2,1)} %copy-done.2) | copy-start | bytes 2359300
Sparse Core Ops, SparseCore 0:
  143.7 92.6 all-reduce.4
where the time goes:
time: 246 us; the launch traced here: 245 us
  blocking collectives  106 us (43%)
  waiting for transfers between devices  78 us (32%)
  matrix products  34.8 us (14%)
  between operations  15.6 us (6%)
  other arithmetic  8.23 us (3%)
  local copies, waits for them, and re-layouts  2.75 us (1%)
    unnamed x2, waiting for transfers between devices  78 us
    unnamed x2, blocking collectives  60.9 us
    all_gather x1, blocking collectives, shards(): lax.all_gather(x_slots, 'blk', axis=0, tiled=True)  25.5 us
    all_gather x1, blocking collectives, shards(): lax.all_gather(cotangent, 'blk', axis=0, tiled=True)  19.6 us
    dot_general x3, matrix products, contract_cols(): lax.dot_general(left, right, (((1,), (1,)), ((), ())), preferred_element_...  13.7 us
    dot_general x3, matrix products, contract_rows(): lax.dot_general(left, right, (((0,), (0,)), ((), ())), preferred_element_...  13.6 us
  transfers between devices with their start and end apart: 1, of which 1 were waited for; matrix products, arithmetic and copies ran while one was open for 6% of the time, Pallas kernels for 0%

commit v1 on v0

v1 whole, which is shorter than its diff:
```python
import jax
import jax.numpy as jnp
from jax import lax
from jax.sharding import PartitionSpec as P


def contract_rows(left, right):
    return lax.dot_general(
        left, right, (((0,), (0,)), ((), ())), preferred_element_type=jnp.float32
    )


def contract_cols(left, right):
    return lax.dot_general(
        left, right, (((1,), (1,)), ((), ())), preferred_element_type=jnp.float32
    )


def make_shards(n):
    nz = n // 4

    def z_shift(d):
        return [(z * 4 + r, ((z + d) % nz) * 4 + r) for z in range(nz) for r in range(4)]

    def flip(bit):
        return [(i, i ^ bit) for i in range(n)]

    def gather(block):
        column = [block] + [lax.ppermute(block, "blk", z_shift(d)) for d in range(1, nz)]
        column = jnp.stack(column)
        plane = jnp.concatenate([column, lax.ppermute(column, "blk", flip(2))])
        whole = jnp.concatenate([plane, lax.ppermute(plane, "blk", flip(1))])
        return whole.reshape(n * block.shape[0], block.shape[1])

    def scatter(part):
        rows = part.shape[0] // n
        part = part.reshape(2, n // 2, rows, part.shape[1])
        got = lax.ppermute(part[1].astype(jnp.bfloat16), "blk", flip(1))
        part = part[0] + got.astype(jnp.float32)
        part = part.reshape(2, nz, rows, part.shape[2])
        got = lax.ppermute(part[1].astype(jnp.bfloat16), "blk", flip(2))
        part = part[0] + got.astype(jnp.float32)
        total = part[0]
        low = part.astype(jnp.bfloat16)
        for d in range(1, nz):
            got = lax.ppermute(low[d], "blk", z_shift(nz - d))
            total = total + got.astype(jnp.float32)
        return total

    def shards(
        tokens, cotangent, gate_weight, up_weight, down_weight, logits, ref_logits, routes
    ):
        policy_log = jax.nn.log_softmax(logits, axis=1)
        frozen_log = jax.nn.log_softmax(ref_logits, axis=1)
        probs = jnp.exp(policy_log)
        entropy = -jnp.sum(probs * policy_log, axis=1)
        divergence = jnp.sum(probs * (policy_log - frozen_log), axis=1)
        is_window = routes == 0
        routed = jnp.any(is_window, axis=1)
        partner = routes[:, 0] + routes[:, 1]
        columns = jnp.arange(logits.shape[1], dtype=jnp.int32)
        partner_hot = (columns[None, :] == partner[:, None]).astype(jnp.float32)
        partner_logit = jnp.sum(logits * partner_hot, axis=1)
        gate = jnp.where(
            routed, jax.nn.sigmoid(logits[:, 0] - partner_logit), jnp.float32(0.0)
        )
        gate_low = gate.astype(jnp.bfloat16)
        slot_count, width = cotangent.shape
        position = jnp.cumsum(routed.astype(jnp.int32)) - 1
        slot_ids = jnp.arange(slot_count, dtype=jnp.int32)
        select = (position[None, :] == slot_ids[:, None]) & routed[None, :]
        select_low = select.astype(jnp.bfloat16)
        select_full = select.astype(jnp.float32)
        x_slots = jnp.dot(select_low, tokens, preferred_element_type=jnp.float32).astype(
            jnp.bfloat16
        )
        g_slots = jnp.sum(select_full * gate_low.astype(jnp.float32)[None, :], axis=1).astype(
            jnp.bfloat16
        )
        y_all = gather(cotangent)
        send = jnp.concatenate(
            [x_slots, jnp.broadcast_to(g_slots[:, None], (slot_count, 128))], axis=1
        )
        xg_all = gather(send)
        x_all = xg_all[:, :width]
        g_col = xg_all[:, width : width + 1].astype(jnp.float32)
        pre_gate = jnp.dot(x_all, gate_weight, preferred_element_type=jnp.float32)
        pre_up = jnp.dot(x_all, up_weight, preferred_element_type=jnp.float32)
        sig = jax.nn.sigmoid(pre_gate)
        act = pre_gate * sig
        hidden = act * pre_up
        weighted = (g_col * hidden).astype(jnp.bfloat16)
        back = contract_cols(y_all, down_weight)
        products = jnp.sum(hidden * back, axis=1)
        scaled = g_col * back
        store_gate = (scaled * pre_up * sig * (1.0 + pre_gate * (1.0 - sig))).astype(
            jnp.bfloat16
        )
        store_up = (scaled * act).astype(jnp.bfloat16)
        row_grad = contract_cols(store_gate, gate_weight) + contract_cols(store_up, up_weight)
        high = lax.reduce_precision(products, 8, 7)
        low = products - high
        lane = jnp.arange(128, dtype=jnp.int32)[None, :]
        extra = jnp.where(lane == 0, high[:, None], jnp.where(lane == 1, low[:, None], 0.0))
        home = scatter(jnp.concatenate([row_grad, extra], axis=1))
        acc_gate = contract_rows(x_all, store_gate)
        acc_up = contract_rows(x_all, store_up)
        acc_down = contract_rows(weighted, y_all)
        slot_grads = home[:, :width].astype(jnp.bfloat16)
        slot_products = home[:, width] + home[:, width + 1]
        grad_tokens = contract_rows(select_low, slot_grads).astype(jnp.bfloat16)
        token_products = jnp.sum(select_full * slot_products[:, None], axis=0)
        slope = gate * (1.0 - gate)
        window_hot = (columns == 0).astype(jnp.float32)
        kl_grad = probs * (policy_log - frozen_log - divergence[:, None])
        grad_logits = (
            kl_grad + (window_hot[None, :] - partner_hot) * (token_products * slope)[:, None]
        )
        return (
            acc_gate.astype(jnp.bfloat16),
            acc_up.astype(jnp.bfloat16),
            acc_down.astype(jnp.bfloat16),
            grad_tokens,
            grad_logits,
            entropy,
            divergence,
        )

    return shards


def solution(mesh):
    in_specs = (
        P(("grp", "blk"), None),
        P(("grp", "blk"), None),
        P(None, "blk"),
        P(None, "blk"),
        P("blk", None),
        P(("grp", "blk"), None),
        P(("grp", "blk"), None),
        P(("grp", "blk"), None),
    )
    out_specs = (
        P("grp", "blk"),
        P("grp", "blk"),
        P(("grp", "blk"), None),
        P(("grp", "blk"), None),
        P(("grp", "blk"), None),
        P(("grp", "blk")),
        P(("grp", "blk")),
    )
    return jax.shard_map(
        make_shards(mesh.shape["blk"]),
        mesh=mesh,
        in_specs=in_specs,
        out_specs=out_specs,
        check_vma=False,
    )
```

time: 246 us -> 78.9 us (0.32)
  blocking collectives: 106 us -> 0 us
  waiting for transfers between devices: 78 us -> 9.12 us
  starting transfers between devices: 0.04 us -> 20.3 us
  between operations: 15.6 us -> 1.17 us
    unnamed x2 -> x0, waiting for transfers between devices: 78 us -> none
    unnamed x2 -> x0, blocking collectives: 60.9 us -> none
    all_gather x2 -> x0, blocking collectives: 45.1 us -> none  [the longest x1 25.5 us: shards(): lax.all_gather(x_slots, 'blk', axis=0, tiled=True)]
    ppermute x0 -> x15, starting transfers between devices: none -> 20.3 us  [the longest x6 12 us: gather(): lax.ppermute(block, 'blk', z_shift(d))]
    ppermute x0 -> x15, waiting for transfers between devices: none -> 9.12 us  [the longest x2 6.53 us: gather(): plane = jnp.concatenate([column, lax.ppermute(column, 'blk', flip(2))])]
    dot_general x3, matrix products: 13.7 us -> 9.09 us  [contract_cols(): lax.dot_general(left, right, (((1,), (1,)), ((), ())), preferred_element_...]
    dot_general x1, matrix products: 1.2 us -> 4.12 us  [shards(): pre_up = jnp.dot(x_all, up_weight, preferred_element_type=jnp.float32)]
    dot_general x3 -> x4, matrix products: 13.6 us -> 15.5 us  [contract_rows(): lax.dot_general(left, right, (((0,), (0,)), ((), ())), preferred_element_...]
  transfers between devices with their start and end apart: 1 -> 15, of which waited for: 1 -> 4; matrix products, arithmetic and copies ran while one was open for 6% -> 32% of each run, Pallas kernels for 0% -> 0%
where the time goes in v1:
time: 78.9 us; the launch traced here: 78.4 us
  matrix products  33 us (42%)
  starting transfers between devices  20.3 us (26%)
  other arithmetic  10.4 us (13%)
  waiting for transfers between devices  9.12 us (12%)
  local copies, waits for them, and re-layouts  4.39 us (6%)
  between operations  1.17 us (1%)
    dot_general x4, matrix products, contract_rows(): lax.dot_general(left, right, (((0,), (0,)), ((), ())), preferred_element_...  15.5 us
    ppermute x6, starting transfers between devices, gather(): lax.ppermute(block, 'blk', z_shift(d))  12 us
    dot_general x3, matrix products, contract_cols(): lax.dot_general(left, right, (((1,), (1,)), ((), ())), preferred_element_...  9.09 us
    ppermute x2, waiting for transfers between devices, gather(): plane = jnp.concatenate([column, lax.ppermute(column, 'blk', flip(2))])  6.53 us
    dot_general x1, matrix products, shards(): pre_gate = jnp.dot(x_all, gate_weight, preferred_element_type=jnp.float32)  4.13 us
    dot_general x1, matrix products, shards(): pre_up = jnp.dot(x_all, up_weight, preferred_element_type=jnp.float32)  4.12 us
    ppermute x3, starting transfers between devices, scatter(): got = lax.ppermute(low[d], 'blk', z_shift(nz - d))  4 us
    ppermute x2, starting transfers between devices, gather(): plane = jnp.concatenate([column, lax.ppermute(column, 'blk', flip(2))])  2.35 us
  transfers between devices with their start and end apart: 15, of which 4 were waited for; matrix products, arithmetic and copies ran while one was open for 32% of the time, Pallas kernels for 0%

profile of v1, /device:TPU:0, one launch (start us, length us, event | category | flops | bytes accessed | tf_op | source)
XLA Modules:
  0.0 78.4 jit_solution(16897341313650672759)
XLA Ops:
  0.6 3.1 %collective-permute-start.5 = (bf16[4,6144]{1,0:T(4,128)(2,1)}, bf16[4,6144]{1,0:T(4,128)(2,1)S(1)}, u32[]{:S(2)}, u32[]{:S(2)}) collective-permute-start(bf16[4,6144]{1,0:T(4,128)(2,1)} %param.10), channel_id=1, source_target_pairs={{0,4},{1,5},{2,6},{3,7},{4,8},{5,9},{6,10},{7,11},{8,12},{9,13},{1... | collective-permute-start | bytes 147464 | tf_op jit(solution)/shard_map/ppermute | solution.py:29
  3.7 2.1 %collective-permute-start.7 = (bf16[4,6144]{1,0:T(4,128)(2,1)}, bf16[4,6144]{1,0:T(4,128)(2,1)S(1)}, u32[]{:S(2)}, u32[]{:S(2)}) collective-permute-start(bf16[4,6144]{1,0:T(4,128)(2,1)} %param.10), channel_id=1, source_target_pairs={{0,12},{1,13},{2,14},{3,15},{4,0},{5,1},{6,2},{7,3},{8,4},{9,5},{1... | collective-permute-start | bytes 147464 | tf_op jit(solution)/shard_map/ppermute | solution.py:29
  5.8 0.9 %collective-permute-start.6 = (bf16[4,6144]{1,0:T(4,128)(2,1)}, bf16[4,6144]{1,0:T(4,128)(2,1)S(1)}, u32[]{:S(2)}, u32[]{:S(2)}) collective-permute-start(bf16[4,6144]{1,0:T(4,128)(2,1)} %param.10), channel_id=1, source_target_pairs={{0,8},{1,9},{2,10},{3,11},{4,12},{5,13},{6,14},{7,15},{8,0},{9,1},... | collective-permute-start | bytes 147464 | tf_op jit(solution)/shard_map/ppermute | solution.py:29
  6.8 0.7 compare_reduce_fusion
  7.5 0.8 add_bitcast_fusion
  8.2 0.7 reduce_max.14
  8.9 0.7 reduce_max.13
  9.6 0.7 exponential_reduce_fusion.1
  10.4 0.7 exponential_reduce_fusion
  11.1 0.7 fusion.15
  11.8 0.7 convert_convert_fusion
  12.9 0.2 convolution_convert_fusion.4
  13.2 2.0 %collective-permute-start.1 = (bf16[4,6272]{1,0:T(4,128)(2,1)S(1)}, bf16[4,6272]{1,0:T(4,128)(2,1)S(1)}, u32[]{:S(2)}, u32[]{:S(2)}) collective-permute-start(bf16[4,6272]{1,0:T(4,128)(2,1)S(1)} %get-tuple-element.34), channel_id=1, source_target_pairs={{0,8},{1,9},{2,10},{3,11},{4,12},{5,13},{6,14},{7,15},{8,0},{9,1},... | collective-permute-start | bytes 150536 | tf_op jit(solution)/shard_map/ppermute | solution.py:29
  15.3 0.8 %constant_dynamic-update-slice_fusion.15 = (bf16[8,4,6144]{2,1,0:T(4,128)(2,1)S(1)}, bf16[16,4,6144]{2,1,0:T(4,128)(2,1)S(1)}) fusion(bf16[4,6144]{1,0:T(4,128)(2,1)} %param.10), kind=kLoop, calls=%fused_computation.53 | loop fusion | bytes 147456
  16.1 0.5 compare_convert_fusion
  16.7 0.5 neg.19
  17.2 3.8 %collective-permute-start.2 = (bf16[4,6272]{1,0:T(4,128)(2,1)S(1)}, bf16[4,6272]{1,0:T(4,128)(2,1)S(1)}, u32[]{:S(2)}, u32[]{:S(2)}) collective-permute-start(bf16[4,6272]{1,0:T(4,128)(2,1)S(1)} %get-tuple-element.34), channel_id=1, source_target_pairs={{0,12},{1,13},{2,14},{3,15},{4,0},{5,1},{6,2},{7,3},{8,4},{9,5},{1... | collective-permute-start | bytes 150536 | tf_op jit(solution)/shard_map/ppermute | solution.py:29
  21.0 1.0 %pad_maximum_fusion.2 = bf16[4,4,6144]{2,1,0:T(4,128)(2,1)S(1)} fusion(bf16[1,4,6144]{2,1,0:T(4,128)(2,1)S(1)} %bitcast.100, bf16[1,4,6144]{2,1,0:T(4,128)(2,1)S(1)} %bitcast.102, bf16[1,4,6144]{2,1,0:T(4,128)(2,1)S(1)} %bitcast.101, bf16[1,4,6144]{2,1,0:T(4,128)(2,1)} %bitcast.99), kind=kLoop, calls=%fused_computation.21 | loop fusion | flops 294912 | bytes 393216 | tf_op jit(solution)/shard_map/stack | solution.py:30
  22.0 1.7 %collective-permute-start.8 = (bf16[4,4,6144]{2,1,0:T(4,128)(2,1)S(1)}, bf16[4,4,6144]{2,1,0:T(4,128)(2,1)S(1)}, u32[]{:S(2)}, u32[]{:S(2)}) collective-permute-start(bf16[4,4,6144]{2,1,0:T(4,128)(2,1)S(1)} %pad_maximum_fusion.2), channel_id=1, source_target_pairs={{0,2},{1,3},{2,0},{3,1},{4,6},{5,7},{6,4},{7,5},{8,10},{9,11},{10,... | collective-permute-start | bytes 589832 | tf_op jit(solution)/shard_map/ppermute | solution.py:31
  23.9 0.2 pad_maximum_fusion.1
  24.1 0.6 collective-permute-start.3
  24.8 4.6 %collective-permute-done.8 = bf16[4,4,6144]{2,1,0:T(4,128)(2,1)S(1)} collective-permute-done((bf16[4,4,6144]{2,1,0:T(4,128)(2,1)S(1)}, bf16[4,4,6144]{2,1,0:T(4,128)(2,1)S(1)}, u32[]{:S(2)}, u32[]{:S(2)}) %collective-permute-start.8) | collective-permute-done | bytes 196640 | tf_op jit(solution)/shard_map/ppermute | solution.py:31
  29.7 1.9 %collective-permute-done.3 = bf16[4,4,6272]{2,1,0:T(4,128)(2,1)S(1)} collective-permute-done((bf16[4,4,6272]{2,1,0:T(4,128)(2,1)S(1)}, bf16[4,4,6272]{2,1,0:T(4,128)(2,1)S(1)}, u32[]{:S(2)}, u32[]{:S(2)}) %collective-permute-start.3) | collective-permute-done | bytes 200736 | tf_op jit(solution)/shard_map/ppermute | solution.py:31
  31.8 0.2 constant_dynamic-update-slice_fusion.16
  32.0 0.2 reshape.112
  32.2 1.4 %collective-permute-done.4 = bf16[8,4,6272]{2,1,0:T(4,128)(2,1)S(1)} collective-permute-done((bf16[8,4,6272]{2,1,0:T(4,128)(2,1)S(1)}, bf16[8,4,6272]{2,1,0:T(4,128)(2,1)S(1)}, u32[]{:S(2)}, u32[]{:S(2)}) %collective-permute-start.4) | collective-permute-done | bytes 401440 | tf_op jit(solution)/shard_map/ppermute | solution.py:32
  33.5 0.2 constant_dynamic-update-slice_fusion.5
  33.7 0.2 reshape.111
  34.0 4.1 %fusion.4 = f32[64,512]{1,0:T(8,128)S(1)} fusion(bf16[6144,512]{1,0:T(8,128)(2,1)} %param.11, bf16[64,6272]{1,0:T(8,128)(2,1)S(1)} %reshape.111), kind=kOutput, calls=%fused_computation.14 | convolution fusion | flops 402653184 | bytes 7208960 | tf_op jit(solution)/shard_map/dot_general | solution.py:87
  38.1 4.1 %fusion.6 = f32[64,512]{1,0:T(8,128)S(1)} fusion(bf16[6144,512]{1,0:T(8,128)(2,1)} %param.12, bf16[64,6272]{1,0:T(8,128)(2,1)S(1)} %reshape.111), kind=kOutput, calls=%fused_computation.16 | convolution fusion | flops 402653184 | bytes 7208960 | tf_op jit(solution)/shard_map/dot_general | solution.py:88
  42.3 5.1 %multiply_reduce_fusion = (f32[64]{0:T(128)S(1)}, bf16[64,512]{1,0:T(8,128)(2,1)S(1)}, bf16[64,512]{1,0:T(8,128)(2,1)S(1)}) fusion(f32[64,512]{1,0:T(8,128)S(1)} %fusion.6, f32[64,512]{1,0:T(8,128)S(1)} %fusion.4, f32[64]{0:T(128)S(1)} %bitcast_convert_fusion.1, bf16[64,6144]{1,0:T(8,128)(2,1)S(1)} %reshape.112, bf16[512,6144]{1,0:T(8,128)(2,1)} %param.13), kind=kOutput, calls=%fused_computation.22 | convolution fusion | flops 403210176 | bytes 7471616 | tf_op jit(solution)/shard_map/dot_general | solution.py:14
  47.5 2.0 %fusion.30 = f32[64,6144]{1,0:T(8,128)S(1)} fusion(bf16[64,512]{1,0:T(8,128)(2,1)S(1)} %get-tuple-element.16, bf16[6144,512]{1,0:T(8,128)(2,1)S(1)} %bitcast.95), kind=kOutput, calls=%fused_computation.104 | convolution fusion | flops 402653184 | bytes 7929856 | tf_op jit(solution)/shard_map/dot_general | solution.py:14
  49.5 2.0 %convolution_add_fusion = f32[64,6144]{1,0:T(8,128)S(1)} fusion(f32[64,6144]{1,0:T(8,128)S(1)} %fusion.30, bf16[64,512]{1,0:T(8,128)(2,1)S(1)} %get-tuple-element.17, bf16[6144,512]{1,0:T(8,128)(2,1)S(1)} %bitcast.93), kind=kOutput, calls=%fused_computation.3 | convolution fusion | flops 403046400 | bytes 9502720 | tf_op jit(solution)/shard_map/dot_general | solution.py:14
  51.6 0.8 %fusion.1 = bf16[32,6272]{1,0:T(8,128)(2,1)} fusion(f32[64,128]{1,0:T(8,128)S(1)} %select_select_fusion, f32[64,6144]{1,0:T(8,128)S(1)} %convolution_add_fusion), kind=kLoop, calls=%fused_computation.10 | loop fusion | flops 802816 | bytes 2007040 | tf_op jit(solution)/shard_map/convert.3
  52.5 0.2 squeeze.26
  52.7 1.1 %convert_element_type.105 = bf16[8,4,6272]{2,1,0:T(4,128)(2,1)S(1)} reshape(bf16[32,6272]{1,0:T(8,128)(2,1)} %fusion.1) | data formatting | bytes 802816 | tf_op jit(solution)/shard_map/convert_element_type | solution.py:38
  53.9 0.2 collective-permute-start.10
  54.1 5.5 %convolution_convert_fusion = bf16[512,6144]{1,0:T(8,128)(2,1)} fusion(bf16[64,6144]{1,0:T(8,128)(2,1)S(1)} %reshape.112, f32[64]{0:T(128)S(1)} %bitcast_convert_fusion.1, f32[64,512]{1,0:T(8,128)} %copy-done.1, f32[64,512]{1,0:T(8,128)S(1)} %fusion.4), kind=kOutput, calls=%fused_computation | convolution fusion | flops 406028288 | bytes 7340288 | tf_op jit(solution)/shard_map/dot_general | solution.py:8
  59.8 1.6 %collective-permute-start.11 = (bf16[4,4,6272]{2,1,0:T(4,128)(2,1)S(1)}, bf16[4,4,6272]{2,1,0:T(4,128)(2,1)S(1)}, u32[]{:S(2)}, u32[]{:S(2)}) collective-permute-start(bf16[4,4,6272]{2,1,0:T(4,128)(2,1)S(1)} %copy.39), channel_id=1, source_target_pairs={{0,2},{1,3},{2,0},{3,1},{4,6},{5,7},{6,4},{7,5},{8,10},{9,11},{10,... | collective-permute-start | bytes 602120 | tf_op jit(solution)/shard_map/ppermute | solution.py:41
  61.4 4.5 %convolution_convert_fusion.1 = bf16[6144,512]{1,0:T(8,128)(2,1)} fusion(bf16[64,512]{1,0:T(8,128)(2,1)S(1)} %copy-done.5, bf16[64,6272]{1,0:T(8,128)(2,1)S(1)} %reshape.111), kind=kOutput, calls=%fused_computation.1 | convolution fusion | flops 405798912 | bytes 7143424 | tf_op jit(solution)/shard_map/dot_general | solution.py:8
  66.0 1.2 %collective-permute-done.11 = bf16[4,4,6272]{2,1,0:T(4,128)(2,1)S(1)} collective-permute-done((bf16[4,4,6272]{2,1,0:T(4,128)(2,1)S(1)}, bf16[4,4,6272]{2,1,0:T(4,128)(2,1)S(1)}, u32[]{:S(2)}, u32[]{:S(2)}) %collective-permute-start.11) | collective-permute-done | bytes 200736 | tf_op jit(solution)/shard_map/ppermute | solution.py:41
  67.3 0.3 fusion.28
  67.8 1.8 %collective-permute-start.14 = (bf16[4,6272]{1,0:T(4,128)(2,1)S(1)}, bf16[4,6272]{1,0:T(4,128)(2,1)S(1)}, u32[]{:S(2)}, u32[]{:S(2)}) collective-permute-start(bf16[4,6272]{1,0:T(4,128)(2,1)S(1)} %bitcast.104), channel_id=1, source_target_pairs={{0,4},{1,5},{2,6},{3,7},{4,8},{5,9},{6,10},{7,11},{8,12},{9,13},{1... | collective-permute-start | bytes 150536 | tf_op jit(solution)/shard_map/ppermute | solution.py:46
  69.6 2.1 %collective-permute-start.12 = (bf16[4,6272]{1,0:T(4,128)(2,1)S(1)}, bf16[4,6272]{1,0:T(4,128)(2,1)S(1)}, u32[]{:S(2)}, u32[]{:S(2)}) collective-permute-start(bf16[4,6272]{1,0:T(4,128)(2,1)S(1)} %bitcast.103), channel_id=1, source_target_pairs={{0,12},{1,13},{2,14},{3,15},{4,0},{5,1},{6,2},{7,3},{8,4},{9,5},{1... | collective-permute-start | bytes 150536 | tf_op jit(solution)/shard_map/ppermute | solution.py:46
  71.7 4.5 %convolution_convert_fusion.2 = bf16[6144,512]{1,0:T(8,128)(2,1)} fusion(bf16[64,512]{1,0:T(8,128)(2,1)S(1)} %copy-done.3, bf16[64,6272]{1,0:T(8,128)(2,1)S(1)} %reshape.111), kind=kOutput, calls=%fused_computation.2 | convolution fusion | flops 405798912 | bytes 7143424 | tf_op jit(solution)/shard_map/dot_general | solution.py:8
  76.4 0.2 fusion.16
  76.6 0.9 %convolution_convert_fusion.3 = bf16[16,6144]{1,0:T(8,128)(2,1)} fusion(pred[4,16]{1,0:T(4,128)(4,1)S(1)} %get-tuple-element.14, f32[4,6272]{1,0:T(4,128)S(1)} %fusion.10), kind=kOutput, calls=%fused_computation.4 | convolution fusion | flops 884736 | bytes 246272 | tf_op jit(solution)/shard_map/dot_general | solution.py:8
  77.7 0.7 fusion.14
  (90 shorter events, 2.4 us)
Async XLA Ops:
  0.6 12.3 %copy-start = (bf16[16,6144]{1,0:T(8,128)(2,1)S(1)}, bf16[16,6144]{1,0:T(8,128)(2,1)}, u32[]{:S(2)}) copy-start(bf16[16,6144]{1,0:T(8,128)(2,1)} %param.9) | copy-start | bytes 589828
  0.6 16.5 %collective-permute-start.5 = (bf16[4,6144]{1,0:T(4,128)(2,1)}, bf16[4,6144]{1,0:T(4,128)(2,1)S(1)}, u32[]{:S(2)}, u32[]{:S(2)}) collective-permute-start(bf16[4,6144]{1,0:T(4,128)(2,1)} %param.10), channel_id=1, source_target_pairs={{0,4},{1,5},{2,6},{3,7},{4,8},{5,9},{6,10},{7,11},{8,12},{9,13},{1... | collective-permute-start | bytes 147464 | tf_op jit(solution)/shard_map/ppermute | solution.py:29
  3.7 17.3 %collective-permute-start.7 = (bf16[4,6144]{1,0:T(4,128)(2,1)}, bf16[4,6144]{1,0:T(4,128)(2,1)S(1)}, u32[]{:S(2)}, u32[]{:S(2)}) collective-permute-start(bf16[4,6144]{1,0:T(4,128)(2,1)} %param.10), channel_id=1, source_target_pairs={{0,12},{1,13},{2,14},{3,15},{4,0},{5,1},{6,2},{7,3},{8,4},{9,5},{1... | collective-permute-start | bytes 147464 | tf_op jit(solution)/shard_map/ppermute | solution.py:29
  5.8 15.2 %collective-permute-start.6 = (bf16[4,6144]{1,0:T(4,128)(2,1)}, bf16[4,6144]{1,0:T(4,128)(2,1)S(1)}, u32[]{:S(2)}, u32[]{:S(2)}) collective-permute-start(bf16[4,6144]{1,0:T(4,128)(2,1)} %param.10), channel_id=1, source_target_pairs={{0,8},{1,9},{2,10},{3,11},{4,12},{5,13},{6,14},{7,15},{8,0},{9,1},... | collective-permute-start | bytes 147464 | tf_op jit(solution)/shard_map/ppermute | solution.py:29
  10.3 2.7 %copy-start.9 = (f32[16]{0:T(128)}, f32[16]{0:T(128)S(1)}, u32[]{:S(2)}) copy-start(f32[16]{0:T(128)S(1)} %log.9) | copy-start | bytes 196
  11.1 1.6 %copy-start.11 = (f32[16]{0:T(128)}, f32[16]{0:T(128)S(1)}, u32[]{:S(2)}) copy-start(f32[16]{0:T(128)S(1)} %log.10) | copy-start | bytes 196
  11.8 65.8 %copy-start.8 = (f32[16]{0:T(128)}, f32[16]{0:T(128)S(1)}, u32[]{:S(2)}) copy-start(f32[16]{0:T(128)S(1)} %get-tuple-element.9) | copy-start | bytes 196
  13.2 10.7 %collective-permute-start.1 = (bf16[4,6272]{1,0:T(4,128)(2,1)S(1)}, bf16[4,6272]{1,0:T(4,128)(2,1)S(1)}, u32[]{:S(2)}, u32[]{:S(2)}) collective-permute-start(bf16[4,6272]{1,0:T(4,128)(2,1)S(1)} %get-tuple-element.34), channel_id=1, source_target_pairs={{0,8},{1,9},{2,10},{3,11},{4,12},{5,13},{6,14},{7,15},{8,0},{9,1},... | collective-permute-start | bytes 150536 | tf_op jit(solution)/shard_map/ppermute | solution.py:29
  15.2 8.6 %collective-permute-start = (bf16[4,6272]{1,0:T(4,128)(2,1)S(1)}, bf16[4,6272]{1,0:T(4,128)(2,1)S(1)}, u32[]{:S(2)}, u32[]{:S(2)}) collective-permute-start(bf16[4,6272]{1,0:T(4,128)(2,1)S(1)} %get-tuple-element.34), channel_id=1, source_target_pairs={{0,4},{1,5},{2,6},{3,7},{4,8},{5,9},{6,10},{7,11},{8,12},{9,13},{1... | collective-permute-start | bytes 150536 | tf_op jit(solution)/shard_map/ppermute | solution.py:29
  17.2 6.7 %collective-permute-start.2 = (bf16[4,6272]{1,0:T(4,128)(2,1)S(1)}, bf16[4,6272]{1,0:T(4,128)(2,1)S(1)}, u32[]{:S(2)}, u32[]{:S(2)}) collective-permute-start(bf16[4,6272]{1,0:T(4,128)(2,1)S(1)} %get-tuple-element.34), channel_id=1, source_target_pairs={{0,12},{1,13},{2,14},{3,15},{4,0},{5,1},{6,2},{7,3},{8,4},{9,5},{1... | collective-permute-start | bytes 150536 | tf_op jit(solution)/shard_map/ppermute | solution.py:29
  22.0 7.5 %collective-permute-start.8 = (bf16[4,4,6144]{2,1,0:T(4,128)(2,1)S(1)}, bf16[4,4,6144]{2,1,0:T(4,128)(2,1)S(1)}, u32[]{:S(2)}, u32[]{:S(2)}) collective-permute-start(bf16[4,4,6144]{2,1,0:T(4,128)(2,1)S(1)} %pad_maximum_fusion.2), channel_id=1, source_target_pairs={{0,2},{1,3},{2,0},{3,1},{4,6},{5,7},{6,4},{7,5},{8,10},{9,11},{10,... | collective-permute-start | bytes 589832 | tf_op jit(solution)/shard_map/ppermute | solution.py:31
  24.1 7.5 %collective-permute-start.3 = (bf16[4,4,6272]{2,1,0:T(4,128)(2,1)S(1)}, bf16[4,4,6272]{2,1,0:T(4,128)(2,1)S(1)}, u32[]{:S(2)}, u32[]{:S(2)}) collective-permute-start(bf16[4,4,6272]{2,1,0:T(4,128)(2,1)S(1)} %pad_maximum_fusion.1), channel_id=1, source_target_pairs={{0,2},{1,3},{2,0},{3,1},{4,6},{5,7},{6,4},{7,5},{8,10},{9,11},{10,... | collective-permute-start | bytes 602120 | tf_op jit(solution)/shard_map/ppermute | solution.py:31
  29.6 2.2 %collective-permute-start.9 = (bf16[8,4,6144]{2,1,0:T(4,128)(2,1)S(1)}, bf16[8,4,6144]{2,1,0:T(4,128)(2,1)S(1)}, u32[]{:S(2)}, u32[]{:S(2)}) collective-permute-start(bf16[8,4,6144]{2,1,0:T(4,128)(2,1)S(1)} %get-tuple-element.23), channel_id=1, source_target_pairs={{0,1},{1,0},{2,3},{3,2},{4,5},{5,4},{6,7},{7,6},{8,9},{9,8},{10,11... | collective-permute-start | bytes 1179656 | tf_op jit(solution)/shard_map/ppermute | solution.py:32
  31.7 1.8 %collective-permute-start.4 = (bf16[8,4,6272]{2,1,0:T(4,128)(2,1)S(1)}, bf16[8,4,6272]{2,1,0:T(4,128)(2,1)S(1)}, u32[]{:S(2)}, u32[]{:S(2)}) collective-permute-start(bf16[8,4,6272]{2,1,0:T(4,128)(2,1)S(1)} %get-tuple-element.21), channel_id=1, source_target_pairs={{0,1},{1,0},{2,3},{3,2},{4,5},{5,4},{6,7},{7,6},{8,9},{9,8},{10,11... | collective-permute-start | bytes 1204232 | tf_op jit(solution)/shard_map/ppermute | solution.py:32
  34.0 13.4 %slice-start.2 = ((s8[6291456]{0:T(1024)(128)(4,1)}), s8[4194304]{0:T(1024)(128)(4,1)S(1)}, s32[]{:S(2)}) async-start(s8[6291456]{0:T(1024)(128)(4,1)} %bitcast.94), calls=%async_computation.2 | async-start | bytes 8388608
  38.1 9.3 %slice-start.3 = ((s8[6291456]{0:T(1024)(128)(4,1)}), s8[2097152]{0:T(1024)(128)(4,1)S(1)}, s32[]{:S(2)}) async-start(s8[6291456]{0:T(1024)(128)(4,1)} %bitcast.94), calls=%async_computation.3 | async-start | bytes 4194304
  42.3 7.2 %copy-start.1 = (f32[64,512]{1,0:T(8,128)}, f32[64,512]{1,0:T(8,128)S(1)}, u32[]{:S(2)}) copy-start(f32[64,512]{1,0:T(8,128)S(1)} %fusion.6) | copy-start | bytes 393220
  42.3 7.2 %slice-start = ((s8[6291456]{0:T(1024)(128)(4,1)}), s8[4194304]{0:T(1024)(128)(4,1)S(1)}, s32[]{:S(2)}) async-start(s8[6291456]{0:T(1024)(128)(4,1)} %bitcast.92), calls=%async_computation | async-start | bytes 8388608
  47.4 2.1 %copy-start.2 = (bf16[64,512]{1,0:T(8,128)(2,1)}, bf16[64,512]{1,0:T(8,128)(2,1)S(1)}, u32[]{:S(2)}) copy-start(bf16[64,512]{1,0:T(8,128)(2,1)S(1)} %get-tuple-element.16) | copy-start | bytes 196612
  47.4 4.1 %copy-start.4 = (bf16[64,512]{1,0:T(8,128)(2,1)}, bf16[64,512]{1,0:T(8,128)(2,1)S(1)}, u32[]{:S(2)}) copy-start(bf16[64,512]{1,0:T(8,128)(2,1)S(1)} %get-tuple-element.17) | copy-start | bytes 196612
  47.5 2.0 %slice-start.1 = ((s8[6291456]{0:T(1024)(128)(4,1)}), s8[2097152]{0:T(1024)(128)(4,1)S(1)}, s32[]{:S(2)}) async-start(s8[6291456]{0:T(1024)(128)(4,1)} %bitcast.92), calls=%async_computation.1 | async-start | bytes 4194304
  53.9 7.6 %copy-start.5 = (bf16[64,512]{1,0:T(8,128)(2,1)S(1)}, bf16[64,512]{1,0:T(8,128)(2,1)}, u32[]{:S(2)}) copy-start(bf16[64,512]{1,0:T(8,128)(2,1)} %copy-done.4) | copy-start | bytes 196612
  53.9 5.7 %collective-permute-start.10 = (bf16[8,4,6272]{2,0,1:T(8,128)(2,1)S(1)}, bf16[8,4,6272]{2,0,1:T(8,128)(2,1)S(1)}, u32[]{:S(2)}, u32[]{:S(2)}) collective-permute-start(bf16[8,4,6272]{2,0,1:T(8,128)(2,1)S(1)} %copy.37), channel_id=1, source_target_pairs={{0,1},{1,0},{2,3},{3,2},{4,5},{5,4},{6,7},{7,6},{8,9},{9,8},{10,11... | collective-permute-start | bytes 1204232 | tf_op jit(solution)/shard_map/ppermute | solution.py:38
  59.8 11.9 %copy-start.3 = (bf16[64,512]{1,0:T(8,128)(2,1)S(1)}, bf16[64,512]{1,0:T(8,128)(2,1)}, u32[]{:S(2)}) copy-start(bf16[64,512]{1,0:T(8,128)(2,1)} %copy-done.2) | copy-start | bytes 196612
  59.8 7.3 %collective-permute-start.11 = (bf16[4,4,6272]{2,1,0:T(4,128)(2,1)S(1)}, bf16[4,4,6272]{2,1,0:T(4,128)(2,1)S(1)}, u32[]{:S(2)}, u32[]{:S(2)}) collective-permute-start(bf16[4,4,6272]{2,1,0:T(4,128)(2,1)S(1)} %copy.39), channel_id=1, source_target_pairs={{0,2},{1,3},{2,0},{3,1},{4,6},{5,7},{6,4},{7,5},{8,10},{9,11},{10,... | collective-permute-start | bytes 602120 | tf_op jit(solution)/shard_map/ppermute | solution.py:41
  67.7 8.6 %collective-permute-start.13 = (bf16[4,6272]{1,0:T(4,128)(2,1)S(1)}, bf16[4,6272]{1,0:T(4,128)(2,1)S(1)}, u32[]{:S(2)}, u32[]{:S(2)}) collective-permute-start(bf16[4,6272]{1,0:T(4,128)(2,1)S(1)} %bitcast.105), channel_id=1, source_target_pairs={{0,8},{1,9},{2,10},{3,11},{4,12},{5,13},{6,14},{7,15},{8,0},{9,1},... | collective-permute-start | bytes 150536 | tf_op jit(solution)/shard_map/ppermute | solution.py:46
  67.8 8.6 %collective-permute-start.14 = (bf16[4,6272]{1,0:T(4,128)(2,1)S(1)}, bf16[4,6272]{1,0:T(4,128)(2,1)S(1)}, u32[]{:S(2)}, u32[]{:S(2)}) collective-permute-start(bf16[4,6272]{1,0:T(4,128)(2,1)S(1)} %bitcast.104), channel_id=1, source_target_pairs={{0,4},{1,5},{2,6},{3,7},{4,8},{5,9},{6,10},{7,11},{8,12},{9,13},{1... | collective-permute-start | bytes 150536 | tf_op jit(solution)/shard_map/ppermute | solution.py:46
  69.6 8.0 %copy-start.6 = (f32[16,8]{0,1:T(8,128)S(1)}, f32[16,8]{0,1:T(8,128)}, u32[]{:S(2)}) copy-start(f32[16,8]{0,1:T(8,128)} %param.14) | copy-start | bytes 1540
  69.6 8.1 %copy-start.7 = (f32[16,8]{0,1:T(8,128)S(1)}, f32[16,8]{0,1:T(8,128)}, u32[]{:S(2)}) copy-start(f32[16,8]{0,1:T(8,128)} %param.15) | copy-start | bytes 1540
  69.6 8.1 %copy-start.10 = (f32[16]{0:T(128)S(1)}, f32[16]{0:T(128)}, u32[]{:S(2)}) copy-start(f32[16]{0:T(128)} %copy-done.9) | copy-start | bytes 196
  69.6 8.1 %copy-start.12 = (f32[16]{0:T(128)S(1)}, f32[16]{0:T(128)}, u32[]{:S(2)}) copy-start(f32[16]{0:T(128)} %copy-done.11) | copy-start | bytes 196
  69.6 8.1 %copy-start.13 = (f32[8]{0:T(128)S(1)}, f32[8]{0:T(128)}, u32[]{:S(2)}) copy-start(f32[8]{0:T(128)} %compare_convert_fusion) | copy-start | bytes 100
  69.6 6.7 %collective-permute-start.12 = (bf16[4,6272]{1,0:T(4,128)(2,1)S(1)}, bf16[4,6272]{1,0:T(4,128)(2,1)S(1)}, u32[]{:S(2)}, u32[]{:S(2)}) collective-permute-start(bf16[4,6272]{1,0:T(4,128)(2,1)S(1)} %bitcast.103), channel_id=1, source_target_pairs={{0,12},{1,13},{2,14},{3,15},{4,0},{5,1},{6,2},{7,3},{8,4},{9,5},{1... | collective-permute-start | bytes 150536 | tf_op jit(solution)/shard_map/ppermute | solution.py:46

commit v2 on v0

v2 whole, which is shorter than its diff:
```python
import jax
import jax.numpy as jnp
from jax import lax
from jax.experimental import pallas as pl
from jax.experimental.pallas import tpu as pltpu
from jax.sharding import PartitionSpec as P

F32 = jnp.float32
BF16 = jnp.bfloat16
LANES = 128
MIB = 1 << 20


def dot(left, right, dims):
    return lax.dot_general(left, right, (dims, ((), ())), preferred_element_type=F32)


def whole(count):
    return [pl.BlockSpec(memory_space=pltpu.VMEM)] * count


def call(kernel, outs, args, flops, moved, limit=8):
    return pl.pallas_call(
        kernel,
        out_shape=[jax.ShapeDtypeStruct(s, t) for s, t in outs],
        in_specs=whole(len(args)),
        out_specs=whole(len(outs)),
        compiler_params=pltpu.CompilerParams(vmem_limit_bytes=limit * MIB),
        cost_estimate=pl.CostEstimate(flops=flops, bytes_accessed=moved, transcendentals=0),
    )(*args)


def lane_pair(rows, first, second):
    lane = lax.broadcasted_iota(jnp.int32, (rows, LANES), 1)
    return jnp.where(lane == 0, first, jnp.where(lane == 1, second, 0.0))


def split_pair(value):
    high = value.astype(BF16).astype(F32)
    return lane_pair(value.shape[0], high, value - high)


def router_kernel(
    tokens, logits, ref_logits, routes, send, entropy, divergence, base, coef, select_out
):
    slots, width = send.shape[0], tokens.shape[1]
    experts, count = logits.shape
    x, r = logits[...], ref_logits[...]
    shifted = x - jnp.max(x, axis=0, keepdims=True)
    policy_log = shifted - jnp.log(jnp.sum(jnp.exp(shifted), axis=0, keepdims=True))
    shifted = r - jnp.max(r, axis=0, keepdims=True)
    frozen_log = shifted - jnp.log(jnp.sum(jnp.exp(shifted), axis=0, keepdims=True))
    probs = jnp.exp(policy_log)
    ratio = policy_log - frozen_log
    div = jnp.sum(probs * ratio, axis=0, keepdims=True)
    entropy[...] = -jnp.sum(probs * policy_log, axis=0, keepdims=True)
    divergence[...] = div
    base[...] = probs * (ratio - div)
    first, second = routes[0:1, :], routes[1:2, :]
    routed = jnp.where((first == 0) | (second == 0), 1.0, 0.0)
    expert = lax.broadcasted_iota(jnp.int32, (experts, count), 0)
    partner_hot = jnp.where(expert == first + second, 1.0, 0.0)
    partner_logit = jnp.sum(x * partner_hot, axis=0, keepdims=True)
    gate = jnp.where(routed > 0.0, jax.nn.sigmoid(x[0:1, :] - partner_logit), 0.0)
    coef[...] = (jnp.where(expert == 0, 1.0, 0.0) - partner_hot) * (gate * (1.0 - gate))
    token = lax.broadcasted_iota(jnp.int32, (1, count), 1)
    position = jnp.full((1, count), -1.0, F32)
    for t in range(count):
        position += jnp.where(token >= t, routed[:, t : t + 1], 0.0)
    slot = lax.broadcasted_iota(jnp.int32, (count, count), 0)
    hit = (slot == position.astype(jnp.int32)) & (routed > 0.0) & (slot < slots)
    select = jnp.where(hit, 1.0, 0.0)
    select_out[...] = select
    x_slots = dot(select.astype(BF16), tokens[...], ((1,), (0,)))
    send[:, :width] = x_slots[:slots].astype(BF16)
    gate_low = gate.astype(BF16).astype(F32)
    g_slots = jnp.sum(select * gate_low, axis=1, keepdims=True)
    send[:, width:] = jnp.broadcast_to(g_slots[:slots], (slots, LANES)).astype(BF16)


def back_kernel(y, down, back):
    back[...] = dot(y[...], down[...], ((1,), (1,)))


def expert_kernel(x, back, gate_w, up_w, send, keep, weighted, d_gate, d_up, acc_gate, acc_up):
    rows, width = x.shape[0], gate_w.shape[0]
    half = rows // 2
    step = 1536

    def fore(i, carry):
        at = pl.ds(pl.multiple_of(i * step, step), step)
        xs = x[:, at]
        acc_gate[...] += dot(xs, gate_w[at, :], ((1,), (0,)))
        acc_up[...] += dot(xs, up_w[at, :], ((1,), (0,)))
        return carry

    acc_gate[...] = jnp.zeros_like(acc_gate)
    acc_up[...] = jnp.zeros_like(acc_up)
    lax.fori_loop(0, width // step, fore, 0)
    pre_gate, pre_up = acc_gate[...], acc_up[...]
    g = x[:, width:][:, 0:1].astype(F32)
    sig = jax.nn.sigmoid(pre_gate)
    act = pre_gate * sig
    hidden = act * pre_up
    weighted[...] = (g * hidden).astype(BF16)
    products = jnp.sum(hidden * back[...], axis=1, keepdims=True)
    scaled = g * back[...]
    d_gate[...] = (scaled * pre_up * sig * (1.0 + pre_gate * (1.0 - sig))).astype(BF16)
    d_up[...] = (scaled * act).astype(BF16)
    keep[:, width:] = lane_pair(half, products[:half], 0.0)
    send[:, width:] = split_pair(products[half:]).astype(BF16)
    wide = 512

    def rear(i, carry):
        at = pl.ds(pl.multiple_of(i * wide, wide), wide)
        part = dot(d_gate[...], gate_w[at, :], ((1,), (1,)))
        part += dot(d_up[...], up_w[at, :], ((1,), (1,)))
        keep[:, at] = part[:half]
        send[:, at] = part[half:].astype(BF16)
        return carry

    lax.fori_loop(0, width // wide, rear, 0)


def fold_kernel(have, got, keep, send):
    half = keep.shape[0]
    width = keep.shape[1] - LANES
    total = have[:, :width] + got[:, :width].astype(F32)
    keep[:, :width] = total[:half]
    send[:, :width] = total[half:].astype(BF16)
    tail = have[:, width:] + got[:, width:].astype(F32)
    value = tail[:, 0:1] + tail[:, 1:2]
    keep[:, width:] = lane_pair(half, value[:half], 0.0)
    send[:, width:] = split_pair(value[half:]).astype(BF16)


def home_kernel(have, got, select, base, coef, grad_tokens, grad_logits):
    slots = have.shape[0]
    width = have.shape[1] - LANES
    count = select.shape[0]
    total = (have[:, :width] + got[:, :width].astype(F32)).astype(BF16)
    padded = jnp.concatenate([total, jnp.zeros((count - slots, width), BF16)], axis=0)
    grad_tokens[...] = dot(select[...].astype(BF16), padded, ((0,), (0,))).astype(BF16)
    tail = have[:, width:] + got[:, width:].astype(F32)
    value = tail[:, 0:1] + tail[:, 1:2]
    token_products = jnp.sum(select[0:slots, :] * value, axis=0, keepdims=True)
    grad_logits[...] = base[...] + coef[...] * token_products


def rows_kernel(left, right, out):
    out[...] = dot(left[...], right[...], ((0,), (0,))).astype(BF16)


def grad_rows(left, right):
    slots, cols = right.shape
    rows = left.shape[1] // 1024 * 1024
    return pl.pallas_call(
        rows_kernel,
        grid=(rows // 1024,),
        out_shape=jax.ShapeDtypeStruct((rows, cols), BF16),
        in_specs=[
            pl.BlockSpec((slots, 1024), lambda i: (0, i)),
            pl.BlockSpec((slots, cols), lambda i: (0, 0)),
        ],
        out_specs=pl.BlockSpec((1024, cols), lambda i: (i, 0)),
        compiler_params=pltpu.CompilerParams(vmem_limit_bytes=16 * MIB),
        cost_estimate=pl.CostEstimate(
            flops=8 * slots * rows * cols, bytes_accessed=2 * rows * cols, transcendentals=0
        ),
    )(left, right)


def grad_cols(left, right):
    slots, rows = left.shape
    cols = right.shape[1]
    return pl.pallas_call(
        rows_kernel,
        grid=(cols // 1024,),
        out_shape=jax.ShapeDtypeStruct((rows, cols), BF16),
        in_specs=[
            pl.BlockSpec((slots, rows), lambda i: (0, 0)),
            pl.BlockSpec((slots, 1024), lambda i: (0, i)),
        ],
        out_specs=pl.BlockSpec((rows, 1024), lambda i: (0, i)),
        compiler_params=pltpu.CompilerParams(vmem_limit_bytes=16 * MIB),
        cost_estimate=pl.CostEstimate(
            flops=8 * slots * rows * cols, bytes_accessed=2 * rows * cols, transcendentals=0
        ),
    )(left, right)


def make_shards(n):
    z_bits = []
    bit = n // 2
    while bit >= 4:
        z_bits.append(bit)
        bit //= 2
    nz = n // 4

    def swap(block, bit):
        return lax.ppermute(block, "blk", [(i, i ^ bit) for i in range(n)])

    def grow(block, bits):
        block = block[None]
        for bit in bits:
            block = jnp.concatenate([block, swap(block, bit)])
        return block

    def shards(
        tokens, cotangent, gate_weight, up_weight, down_weight, logits, ref_logits, routes
    ):
        count, width = tokens.shape
        slots = cotangent.shape[0]
        experts = logits.shape[1]
        hidden = down_weight.shape[0]
        rows = n * slots
        wide = width + LANES
        gate_w = pltpu.with_memory_space_constraint(gate_weight, pltpu.VMEM)
        up_w = pltpu.with_memory_space_constraint(up_weight, pltpu.VMEM)
        down_w = pltpu.with_memory_space_constraint(down_weight, pltpu.VMEM)

        send, entropy, divergence, base, coef, select = call(
            router_kernel,
            [
                ((slots, wide), BF16),
                ((1, count), F32),
                ((1, count), F32),
                ((experts, count), F32),
                ((experts, count), F32),
                ((count, count), F32),
            ],
            [tokens, logits.T, ref_logits.T, routes.T],
            1 << 20,
            1 << 18,
        )

        y_part = grow(cotangent, [2] + z_bits)
        y_part = y_part.reshape(nz, 2, slots, width).transpose(1, 0, 2, 3)
        y_part = y_part.reshape(rows // 2, width)
        y_all = jnp.concatenate([y_part, swap(y_part, 1)])
        x_part = grow(send, z_bits + [2]).reshape(rows // 2, wide)
        x_all = jnp.concatenate([x_part, swap(x_part, 1)])

        work = 2 * rows * width * hidden
        (back,) = call(
            back_kernel, [((rows, hidden), F32)], [y_all, down_w], 4 * work, 2 * width * hidden, 16
        )
        half = rows // 2
        low, keep, weighted, d_gate, d_up = pl.pallas_call(
            expert_kernel,
            out_shape=[
                jax.ShapeDtypeStruct((half, wide), BF16),
                jax.ShapeDtypeStruct((half, wide), F32),
                jax.ShapeDtypeStruct((rows, hidden), BF16),
                jax.ShapeDtypeStruct((rows, hidden), BF16),
                jax.ShapeDtypeStruct((rows, hidden), BF16),
            ],
            in_specs=whole(4),
            out_specs=whole(5),
            scratch_shapes=[pltpu.VMEM((rows, hidden), F32)] * 2,
            compiler_params=pltpu.CompilerParams(vmem_limit_bytes=32 * MIB),
            cost_estimate=pl.CostEstimate(
                flops=16 * work, bytes_accessed=4 * width * hidden, transcendentals=0
            ),
        )(x_all, back, gate_w, up_w)

        for bit in [1, 2] + z_bits[::-1]:
            got = swap(low, bit)
            if bit == z_bits[0]:
                break
            half //= 2
            keep, low = call(
                fold_kernel,
                [((half, wide), F32), ((half, wide), BF16)],
                [keep, got],
                4 * half * wide,
                16 * half * wide,
            )

        grad_down = grad_cols(weighted, y_all)
        grad_gate = grad_rows(x_all, d_gate)
        grad_up = grad_rows(x_all, d_up)

        grad_tokens, grad_logits = call(
            home_kernel,
            [((count, width), BF16), ((experts, count), F32)],
            [keep, got, select, base, coef],
            1 << 20,
            1 << 18,
        )
        return (
            grad_gate,
            grad_up,
            grad_down,
            grad_tokens,
            grad_logits.T,
            entropy.reshape(count),
            divergence.reshape(count),
        )

    return shards


def solution(mesh):
    in_specs = (
        P(("grp", "blk"), None),
        P(("grp", "blk"), None),
        P(None, "blk"),
        P(None, "blk"),
        P("blk", None),
        P(("grp", "blk"), None),
        P(("grp", "blk"), None),
        P(("grp", "blk"), None),
    )
    out_specs = (
        P("grp", "blk"),
        P("grp", "blk"),
        P(("grp", "blk"), None),
        P(("grp", "blk"), None),
        P(("grp", "blk"), None),
        P(("grp", "blk")),
        P(("grp", "blk")),
    )
    return jax.shard_map(
        make_shards(mesh.shape["blk"]),
        mesh=mesh,
        in_specs=in_specs,
        out_specs=out_specs,
        check_vma=False,
    )
```

time: 246 us -> 70.5 us (0.29)
  blocking collectives: 106 us -> 0 us
  waiting for transfers between devices: 78 us -> 12.5 us
  matrix products: 34.8 us -> 0 us
  Pallas kernels: 0 us -> 26.7 us
  starting transfers between devices: 0.04 us -> 14.9 us
  between operations: 15.6 us -> 0.76 us
  local copies, waits for them, and re-layouts: 2.75 us -> 11.8 us
  other arithmetic: 8.23 us -> 3.38 us
    unnamed x2 -> x0, waiting for transfers between devices: 78 us -> none
    unnamed x2 -> x0, blocking collectives: 60.9 us -> none
    all_gather x2 -> x0, blocking collectives: 45.1 us -> none  [the longest x1 25.5 us: shards(): lax.all_gather(x_slots, 'blk', axis=0, tiled=True)]
    dot_general x10 -> x0, matrix products: 34.8 us -> none  [the longest x3 13.7 us: contract_cols(): lax.dot_general(left, right, (((1,), (1,)), ((), ())), preferred_element_...]
    pallas_call x0 -> x10, Pallas kernels: none -> 26.7 us  [the longest x2 9.84 us: grad_rows(): pl.pallas_call(rows_kernel, grid=(rows // 1024,), out_shape=jax.ShapeDtyp...]
    ppermute x0 -> x12, starting transfers between devices: none -> 14.9 us  [swap(): return lax.ppermute(block, 'blk', [(i, i ^ bit) for i in range(n)])]
    ppermute x0 -> x12, waiting for transfers between devices: none -> 12.5 us  [swap(): return lax.ppermute(block, 'blk', [(i, i ^ bit) for i in range(n)])]
    unnamed x28 -> x16, local copies, waits for them, and re-layouts: 2.65 us -> 11.4 us
  transfers between devices with their start and end apart: 1 -> 12, of which waited for: 1 -> 6; matrix products, arithmetic and copies ran while one was open for 6% -> 5% of each run, Pallas kernels for 0% -> 25%
where the time goes in v2:
time: 70.5 us; the launch traced here: 70 us
  Pallas kernels  26.7 us (38%)
  starting transfers between devices  14.9 us (21%)
  waiting for transfers between devices  12.5 us (18%)
  local copies, waits for them, and re-layouts  11.8 us (17%)
  other arithmetic  3.38 us (5%)
  between operations  0.76 us (1%)
    ppermute x12, starting transfers between devices, swap(): return lax.ppermute(block, 'blk', [(i, i ^ bit) for i in range(n)])  14.9 us
    ppermute x12, waiting for transfers between devices, swap(): return lax.ppermute(block, 'blk', [(i, i ^ bit) for i in range(n)])  12.5 us
    unnamed x16, local copies, waits for them, and re-layouts  11.4 us
    pallas_call x2, Pallas kernels, grad_rows(): pl.pallas_call(rows_kernel, grid=(rows // 1024,), out_shape=jax.ShapeDtyp...  9.84 us
    pallas_call x1, Pallas kernels, shards(): pl.pallas_call(expert_kernel, out_shape=[jax.ShapeDtypeStruct((half, wide...  8.02 us
    pallas_call x1, Pallas kernels, grad_cols(): pl.pallas_call(rows_kernel, grid=(cols // 1024,), out_shape=jax.ShapeDtyp...  4.79 us
    pallas_call x6, Pallas kernels, call(): pl.pallas_call(kernel, out_shape=[jax.ShapeDtypeStruct(s, t) for s, t in...  4.1 us
    concatenate x6, other arithmetic, grow(): block = jnp.concatenate([block, swap(block, bit)])  3.38 us
  transfers between devices with their start and end apart: 12, of which 6 were waited for; matrix products, arithmetic and copies ran while one was open for 5% of the time, Pallas kernels for 25%

profile of v2, /device:TPU:0, one launch (start us, length us, event | category | flops | bytes accessed | tf_op | source)
XLA Modules:
  0.0 70.0 jit_solution(15970597383917145779)
XLA Ops:
  0.6 3.0 %collective-permute-start.4 = (bf16[1,4,6144]{2,1,0:T(4,128)(2,1)}, bf16[1,4,6144]{2,1,0:T(4,128)(2,1)S(1)}, u32[]{:S(2)}, u32[]{:S(2)}) collective-permute-start(bf16[1,4,6144]{2,1,0:T(4,128)(2,1)} %bitcast.21), channel_id=1, source_target_pairs={{0,2},{1,3},{2,0},{3,1},{4,6},{5,7},{6,4},{7,5},{8,10},{9,11},{10,... | collective-permute-start | bytes 147464 | tf_op jit(solution)/shard_map/ppermute | solution.py:201
  3.7 0.9 %copy-done.1 = bf16[16,6144]{1,0:T(8,128)(2,1)S(1)} copy-done((bf16[16,6144]{1,0:T(8,128)(2,1)S(1)}, bf16[16,6144]{1,0:T(8,128)(2,1)}, u32[]{:S(2)}) %copy-start.1) | copy-done | bytes 196632
  4.6 0.7 copy-done.2
  5.3 0.7 copy-done.3
  6.0 0.7 copy-done.4
  6.6 0.7 %shard_map.135 = (bf16[4,6272]{1,0:T(4,128)(2,1)S(1)}, f32[1,16]{1,0:T(1,128)}, f32[1,16]{1,0:T(1,128)}, f32[8,16]{1,0:T(8,128)S(1)}, f32[8,16]{1,0:T(8,128)S(1)}, /*index=5*/f32[16,16]{1,0:T(8,128)S(1)}) custom-call(bf16[16,6144]{1,0:T(8,128)(2,1)S(1)} %copy-done.1, f32[8,16]{1,0:T(8,128)S(1)} %bitcast.16, f32[8,16]{1,0:T(8,128)S(1)} %bitcast.17, ...), custom_call_target="tpu_custom_call" | custom-call | flops 1048576 | bytes 262144 | tf_op jit(solution)/shard_map/pallas_call | solution.py:23
  7.4 2.6 %collective-permute-start = (bf16[1,4,6272]{2,1,0:T(4,128)(2,1)S(1)}, bf16[1,4,6272]{2,1,0:T(4,128)(2,1)S(1)}, u32[]{:S(2)}, u32[]{:S(2)}) collective-permute-start(bf16[1,4,6272]{2,1,0:T(4,128)(2,1)S(1)} %bitcast.12), channel_id=1, source_target_pairs={{0,8},{1,9},{2,10},{3,11},{4,12},{5,13},{6,14},{7,15},{8,0},{9,1},... | collective-permute-start | bytes 150536 | tf_op jit(solution)/shard_map/ppermute | solution.py:201
  10.0 0.9 %pad_maximum_fusion.5 = bf16[2,4,6144]{2,1,0:T(4,128)(2,1)S(1)} fusion(bf16[1,4,6144]{2,1,0:T(4,128)(2,1)S(1)} %collective-permute-done.4, bf16[1,4,6144]{2,1,0:T(4,128)(2,1)} %bitcast.22), kind=kLoop, calls=%fused_computation.6 | loop fusion | flops 49152 | bytes 196608 | tf_op jit(solution)/shard_map/concatenate | solution.py:206
  10.8 0.4 collective-permute-start.5
  11.2 1.3 %collective-permute-done = bf16[1,4,6272]{2,1,0:T(4,128)(2,1)S(1)} collective-permute-done((bf16[1,4,6272]{2,1,0:T(4,128)(2,1)S(1)}, bf16[1,4,6272]{2,1,0:T(4,128)(2,1)S(1)}, u32[]{:S(2)}, u32[]{:S(2)}) %collective-permute-start) | collective-permute-done | bytes 50208 | tf_op jit(solution)/shard_map/ppermute | solution.py:201
  12.5 0.1 pad_maximum_fusion.4
  12.6 3.2 %collective-permute-start.1 = (bf16[2,4,6272]{2,1,0:T(4,128)(2,1)S(1)}, bf16[2,4,6272]{2,1,0:T(4,128)(2,1)S(1)}, u32[]{:S(2)}, u32[]{:S(2)}) collective-permute-start(bf16[2,4,6272]{2,1,0:T(4,128)(2,1)S(1)} %pad_maximum_fusion.4), channel_id=1, source_target_pairs={{0,4},{1,5},{2,6},{3,7},{4,0},{5,1},{6,2},{7,3},{8,12},{9,13},{10,... | collective-permute-start | bytes 301064 | tf_op jit(solution)/shard_map/ppermute | solution.py:201
  15.7 2.3 %collective-permute-done.5 = bf16[2,4,6144]{2,1,0:T(4,128)(2,1)S(1)} collective-permute-done((bf16[2,4,6144]{2,1,0:T(4,128)(2,1)S(1)}, bf16[2,4,6144]{2,1,0:T(4,128)(2,1)S(1)}, u32[]{:S(2)}, u32[]{:S(2)}) %collective-permute-start.5) | collective-permute-done | bytes 98336 | tf_op jit(solution)/shard_map/ppermute | solution.py:201
  18.0 0.9 %pad_maximum_fusion.3 = bf16[4,4,6144]{2,1,0:T(4,128)(2,1)S(1)} fusion(bf16[2,4,6144]{2,1,0:T(4,128)(2,1)S(1)} %collective-permute-done.5, bf16[1,4,6144]{2,1,0:T(4,128)(2,1)S(1)} %collective-permute-done.4, bf16[1,4,6144]{2,1,0:T(4,128)(2,1)} %bitcast.23), kind=kLoop, calls=%fused_computation.4 | loop fusion | flops 196608 | bytes 393216 | tf_op jit(solution)/shard_map/concatenate | solution.py:206
  19.0 0.1 collective-permute-start.6
  19.1 0.0 collective-permute-done.1
  19.1 0.1 pad_maximum_fusion.2
  19.2 0.6 collective-permute-start.2
  19.8 4.9 %collective-permute-done.6 = bf16[4,4,6144]{2,1,0:T(4,128)(2,1)S(1)} collective-permute-done((bf16[4,4,6144]{2,1,0:T(4,128)(2,1)S(1)}, bf16[4,4,6144]{2,1,0:T(4,128)(2,1)S(1)}, u32[]{:S(2)}, u32[]{:S(2)}) %collective-permute-start.6) | collective-permute-done | bytes 196640 | tf_op jit(solution)/shard_map/ppermute | solution.py:201
  24.7 1.1 %pad_maximum_fusion.1 = bf16[8,4,6144]{2,1,0:T(4,128)(2,1)S(1)} fusion(bf16[4,4,6144]{2,1,0:T(4,128)(2,1)S(1)} %collective-permute-done.6, bf16[2,4,6144]{2,1,0:T(4,128)(2,1)S(1)} %collective-permute-done.5, bf16[1,4,6144]{2,1,0:T(4,128)(2,1)S(1)} %collective-permute-done.4, bf16[1,4,6144]{2,1,0:T(4,128)(2,1)} %bitcast.24), kind=kLoop, calls=%fused_computation.1 | loop fusion | flops 589824 | bytes 786432 | tf_op jit(solution)/shard_map/concatenate | solution.py:206
  25.8 0.1 copy.17
  25.9 0.1 reshape.31
  26.0 0.1 collective-permute-start.7
  26.1 0.0 collective-permute-done.2
  26.1 0.3 pad_maximum_fusion
  26.4 0.1 reshape.29
  26.5 0.6 collective-permute-start.3
  27.1 0.7 collective-permute-done.7
  27.8 0.0 copy-start
  27.8 2.8 %copy-done = bf16[512,6144]{1,0:T(8,128)(2,1)S(1)} copy-done((bf16[512,6144]{1,0:T(8,128)(2,1)S(1)}, bf16[512,6144]{1,0:T(8,128)(2,1)}, u32[]{:S(2)}) %copy-start) | copy-done | bytes 6291480
  30.6 2.0 %shard_map.136.back = f32[64,512]{1,0:T(8,128)S(1)} custom-call(bf16[64,6144]{1,0:T(8,128)(2,1)S(1)} %constant_dynamic-update-slice_fusion.2.y.right, bf16[512,6144]{1,0:T(8,128)(2,1)S(1)} %copy-done), custom_call_target="tpu_custom_call" | custom-call | flops 1610612736 | bytes 6291456 | tf_op jit(solution)/shard_map/pallas_call | solution.py:23
  32.7 0.0 copy-start.5
  32.7 2.8 %copy-done.5 = bf16[6144,512]{1,0:T(8,128)(2,1)S(1)} copy-done((bf16[6144,512]{1,0:T(8,128)(2,1)S(1)}, bf16[6144,512]{1,0:T(8,128)(2,1)}, u32[]{:S(2)}) %copy-start.5) | copy-done | bytes 6291480
  35.5 2.8 %copy-done.6 = bf16[6144,512]{1,0:T(8,128)(2,1)S(1)} copy-done((bf16[6144,512]{1,0:T(8,128)(2,1)S(1)}, bf16[6144,512]{1,0:T(8,128)(2,1)}, u32[]{:S(2)}) %copy-start.6) | copy-done | bytes 6291480
  38.3 8.0 %shard_map.137 = (bf16[32,6272]{1,0:T(8,128)(2,1)S(1)}, f32[32,6272]{1,0:T(8,128)S(1)}, bf16[64,512]{1,0:T(8,128)(2,1)S(1)}, bf16[64,512]{1,0:T(8,128)(2,1)S(1)}, bf16[64,512]{1,0:T(8,128)(2,1)S(1)}) custom-call(bf16[64,6272]{1,0:T(8,128)(2,1)S(1)} %constant_dynamic-update-slice_fusion.x.left, f32[64,512]{1,0:T(8,128)S(1)} %shard_map.136.back, ...), custom_call_target="tpu_custom_call" | custom-call | flops 6442450944 | bytes 12582912 | tf_op jit(solution)/shard_map/pallas_call | solution.py:249
  46.3 0.2 collective-permute-start.8
  46.5 1.6 %collective-permute-done.8.got = bf16[32,6272]{1,0:T(8,128)(2,1)S(1)} collective-permute-done((bf16[32,6272]{1,0:T(8,128)(2,1)S(1)}, bf16[32,6272]{1,0:T(8,128)(2,1)S(1)}, u32[]{:S(2)}, u32[]{:S(2)}) %collective-permute-start.8) | collective-permute-done | bytes 401440 | tf_op jit(solution)/shard_map/ppermute | solution.py:201
  48.1 0.2 shard_map.141
  48.2 0.6 collective-permute-start.9
  48.8 4.8 %shard_map.140 = bf16[512,6144]{1,0:T(8,128)(2,1)} custom-call(bf16[64,512]{1,0:T(8,128)(2,1)S(1)} %get-tuple-element.29.left, bf16[64,6144]{1,0:T(8,128)(2,1)S(1)} %constant_dynamic-update-slice_fusion.2.y.right), custom_call_target="tpu_custom_call" | custom-call | flops 1610612736 | bytes 6291456 | tf_op jit(solution)/shard_map/pallas_call | solution.py:176
  53.6 1.7 %collective-permute-done.9.got = bf16[16,6272]{1,0:T(8,128)(2,1)S(1)} collective-permute-done((bf16[16,6272]{1,0:T(8,128)(2,1)S(1)}, bf16[16,6272]{1,0:T(8,128)(2,1)S(1)}, u32[]{:S(2)}, u32[]{:S(2)}) %collective-permute-start.9) | collective-permute-done | bytes 200736 | tf_op jit(solution)/shard_map/ppermute | solution.py:201
  55.3 0.1 shard_map.142
  55.5 0.2 collective-permute-start.10
  55.7 4.9 %shard_map.138 = bf16[6144,512]{1,0:T(8,128)(2,1)} custom-call(bf16[64,6272]{1,0:T(8,128)(2,1)S(1)} %constant_dynamic-update-slice_fusion.x.left, bf16[64,512]{1,0:T(8,128)(2,1)S(1)} %get-tuple-element.27.right), custom_call_target="tpu_custom_call" | custom-call | flops 1610612736 | bytes 6291456 | tf_op jit(solution)/shard_map/pallas_call | solution.py:157
  60.6 0.2 shard_map.143
  60.8 3.4 %collective-permute-start.11 = (bf16[4,6272]{1,0:T(4,128)(2,1)S(1)}, bf16[4,6272]{1,0:T(4,128)(2,1)S(1)}, u32[]{:S(2)}, u32[]{:S(2)}) collective-permute-start(bf16[4,6272]{1,0:T(4,128)(2,1)S(1)} %get-tuple-element.37), channel_id=1, source_target_pairs={{0,8},{1,9},{2,10},{3,11},{4,12},{5,13},{6,14},{7,15},{8,0},{9,1},... | collective-permute-start | bytes 150536 | tf_op jit(solution)/shard_map/ppermute | solution.py:201
  64.2 4.9 %shard_map.139 = bf16[6144,512]{1,0:T(8,128)(2,1)} custom-call(bf16[64,6272]{1,0:T(8,128)(2,1)S(1)} %constant_dynamic-update-slice_fusion.x.left, bf16[64,512]{1,0:T(8,128)(2,1)S(1)} %get-tuple-element.28.right), custom_call_target="tpu_custom_call" | custom-call | flops 1610612736 | bytes 6291456 | tf_op jit(solution)/shard_map/pallas_call | solution.py:157
  69.1 0.9 %shard_map.144 = (bf16[16,6144]{1,0:T(8,128)(2,1)}, f32[8,16]{1,0:T(8,128)}) custom-call(f32[4,6272]{1,0:T(4,128)S(1)} %get-tuple-element.36.have, bf16[4,6272]{1,0:T(4,128)(2,1)S(1)} %collective-permute-done.11.got, f32[16,16]{1,0:T(8,128)S(1)} %get-tuple-element.38.select, f32[8,16]{1,0:T(8,128)S(1)} %get-tuple-element.39.base, ...), custom_call_target="tpu_custom_call" | custom-call | flops 1048576 | bytes 262144 | tf_op jit(solution)/shard_map/pallas_call | solution.py:23
  (13 shorter events, 0.1 us)
Async XLA Ops:
  0.6 9.3 %collective-permute-start.4 = (bf16[1,4,6144]{2,1,0:T(4,128)(2,1)}, bf16[1,4,6144]{2,1,0:T(4,128)(2,1)S(1)}, u32[]{:S(2)}, u32[]{:S(2)}) collective-permute-start(bf16[1,4,6144]{2,1,0:T(4,128)(2,1)} %bitcast.21), channel_id=1, source_target_pairs={{0,2},{1,3},{2,0},{3,1},{4,6},{5,7},{6,4},{7,5},{8,10},{9,11},{10,... | collective-permute-start | bytes 147464 | tf_op jit(solution)/shard_map/ppermute | solution.py:201
  3.7 0.9 %copy-start.1 = (bf16[16,6144]{1,0:T(8,128)(2,1)S(1)}, bf16[16,6144]{1,0:T(8,128)(2,1)}, u32[]{:S(2)}) copy-start(bf16[16,6144]{1,0:T(8,128)(2,1)} %tokens.1) | copy-start | bytes 589828
  4.6 0.7 copy-start.2
  5.3 0.7 copy-start.3
  6.0 0.7 copy-start.4
  7.4 5.1 %collective-permute-start = (bf16[1,4,6272]{2,1,0:T(4,128)(2,1)S(1)}, bf16[1,4,6272]{2,1,0:T(4,128)(2,1)S(1)}, u32[]{:S(2)}, u32[]{:S(2)}) collective-permute-start(bf16[1,4,6272]{2,1,0:T(4,128)(2,1)S(1)} %bitcast.12), channel_id=1, source_target_pairs={{0,8},{1,9},{2,10},{3,11},{4,12},{5,13},{6,14},{7,15},{8,0},{9,1},... | collective-permute-start | bytes 150536 | tf_op jit(solution)/shard_map/ppermute | solution.py:201
  10.8 7.2 %collective-permute-start.5 = (bf16[2,4,6144]{2,1,0:T(4,128)(2,1)S(1)}, bf16[2,4,6144]{2,1,0:T(4,128)(2,1)S(1)}, u32[]{:S(2)}, u32[]{:S(2)}) collective-permute-start(bf16[2,4,6144]{2,1,0:T(4,128)(2,1)S(1)} %pad_maximum_fusion.5), channel_id=1, source_target_pairs={{0,8},{1,9},{2,10},{3,11},{4,12},{5,13},{6,14},{7,15},{8,0},{9,1},... | collective-permute-start | bytes 294920 | tf_op jit(solution)/shard_map/ppermute | solution.py:201
  12.6 6.5 %collective-permute-start.1 = (bf16[2,4,6272]{2,1,0:T(4,128)(2,1)S(1)}, bf16[2,4,6272]{2,1,0:T(4,128)(2,1)S(1)}, u32[]{:S(2)}, u32[]{:S(2)}) collective-permute-start(bf16[2,4,6272]{2,1,0:T(4,128)(2,1)S(1)} %pad_maximum_fusion.4), channel_id=1, source_target_pairs={{0,4},{1,5},{2,6},{3,7},{4,0},{5,1},{6,2},{7,3},{8,12},{9,13},{10,... | collective-permute-start | bytes 301064 | tf_op jit(solution)/shard_map/ppermute | solution.py:201
  19.0 5.7 %collective-permute-start.6 = (bf16[4,4,6144]{2,1,0:T(4,128)(2,1)S(1)}, bf16[4,4,6144]{2,1,0:T(4,128)(2,1)S(1)}, u32[]{:S(2)}, u32[]{:S(2)}) collective-permute-start(bf16[4,4,6144]{2,1,0:T(4,128)(2,1)S(1)} %pad_maximum_fusion.3), channel_id=1, source_target_pairs={{0,4},{1,5},{2,6},{3,7},{4,0},{5,1},{6,2},{7,3},{8,12},{9,13},{10,... | collective-permute-start | bytes 589832 | tf_op jit(solution)/shard_map/ppermute | solution.py:201
  19.2 6.9 %collective-permute-start.2 = (bf16[4,4,6272]{2,1,0:T(4,128)(2,1)S(1)}, bf16[4,4,6272]{2,1,0:T(4,128)(2,1)S(1)}, u32[]{:S(2)}, u32[]{:S(2)}) collective-permute-start(bf16[4,4,6272]{2,1,0:T(4,128)(2,1)S(1)} %pad_maximum_fusion.2), channel_id=1, source_target_pairs={{0,2},{1,3},{2,0},{3,1},{4,6},{5,7},{6,4},{7,5},{8,10},{9,11},{10,... | collective-permute-start | bytes 602120 | tf_op jit(solution)/shard_map/ppermute | solution.py:201
  26.0 1.8 %collective-permute-start.7 = (bf16[32,6144]{1,0:T(8,128)(2,1)S(1)}, bf16[32,6144]{1,0:T(8,128)(2,1)S(1)}, u32[]{:S(2)}, u32[]{:S(2)}) collective-permute-start(bf16[32,6144]{1,0:T(8,128)(2,1)S(1)} %reshape.31), channel_id=1, source_target_pairs={{0,1},{1,0},{2,3},{3,2},{4,5},{5,4},{6,7},{7,6},{8,9},{9,8},{10,11... | collective-permute-start | bytes 1179656 | tf_op jit(solution)/shard_map/ppermute | solution.py:201
  26.5 6.1 %collective-permute-start.3 = (bf16[32,6272]{1,0:T(8,128)(2,1)S(1)}, bf16[32,6272]{1,0:T(8,128)(2,1)S(1)}, u32[]{:S(2)}, u32[]{:S(2)}) collective-permute-start(bf16[32,6272]{1,0:T(8,128)(2,1)S(1)} %reshape.29), channel_id=1, source_target_pairs={{0,1},{1,0},{2,3},{3,2},{4,5},{5,4},{6,7},{7,6},{8,9},{9,8},{10,11... | collective-permute-start | bytes 1204232 | tf_op jit(solution)/shard_map/ppermute | solution.py:201
  27.8 2.8 %copy-start = (bf16[512,6144]{1,0:T(8,128)(2,1)S(1)}, bf16[512,6144]{1,0:T(8,128)(2,1)}, u32[]{:S(2)}) copy-start(bf16[512,6144]{1,0:T(8,128)(2,1)} %down.1) | copy-start | bytes 18874372
  32.7 2.8 %copy-start.5 = (bf16[6144,512]{1,0:T(8,128)(2,1)S(1)}, bf16[6144,512]{1,0:T(8,128)(2,1)}, u32[]{:S(2)}) copy-start(bf16[6144,512]{1,0:T(8,128)(2,1)} %gate_w.1) | copy-start | bytes 18874372
  35.5 2.8 %copy-start.6 = (bf16[6144,512]{1,0:T(8,128)(2,1)S(1)}, bf16[6144,512]{1,0:T(8,128)(2,1)}, u32[]{:S(2)}) copy-start(bf16[6144,512]{1,0:T(8,128)(2,1)} %up_w.1) | copy-start | bytes 18874372
  46.3 1.8 %collective-permute-start.8 = (bf16[32,6272]{1,0:T(8,128)(2,1)S(1)}, bf16[32,6272]{1,0:T(8,128)(2,1)S(1)}, u32[]{:S(2)}, u32[]{:S(2)}) collective-permute-start(bf16[32,6272]{1,0:T(8,128)(2,1)S(1)} %get-tuple-element.31), channel_id=1, source_target_pairs={{0,1},{1,0},{2,3},{3,2},{4,5},{5,4},{6,7},{7,6},{8,9},{9,8},{10,11... | collective-permute-start | bytes 1204232 | tf_op jit(solution)/shard_map/ppermute | solution.py:201
  48.2 7.1 %collective-permute-start.9 = (bf16[16,6272]{1,0:T(8,128)(2,1)S(1)}, bf16[16,6272]{1,0:T(8,128)(2,1)S(1)}, u32[]{:S(2)}, u32[]{:S(2)}) collective-permute-start(bf16[16,6272]{1,0:T(8,128)(2,1)S(1)} %get-tuple-element.33), channel_id=1, source_target_pairs={{0,2},{1,3},{2,0},{3,1},{4,6},{5,7},{6,4},{7,5},{8,10},{9,11},{10,... | collective-permute-start | bytes 602120 | tf_op jit(solution)/shard_map/ppermute | solution.py:201
  55.5 5.1 %collective-permute-start.10 = (bf16[8,6272]{1,0:T(8,128)(2,1)S(1)}, bf16[8,6272]{1,0:T(8,128)(2,1)S(1)}, u32[]{:S(2)}, u32[]{:S(2)}) collective-permute-start(bf16[8,6272]{1,0:T(8,128)(2,1)S(1)} %get-tuple-element.35), channel_id=1, source_target_pairs={{0,4},{1,5},{2,6},{3,7},{4,0},{5,1},{6,2},{7,3},{8,12},{9,13},{10,... | collective-permute-start | bytes 301064 | tf_op jit(solution)/shard_map/ppermute | solution.py:201
  60.8 8.3 %collective-permute-start.11 = (bf16[4,6272]{1,0:T(4,128)(2,1)S(1)}, bf16[4,6272]{1,0:T(4,128)(2,1)S(1)}, u32[]{:S(2)}, u32[]{:S(2)}) collective-permute-start(bf16[4,6272]{1,0:T(4,128)(2,1)S(1)} %get-tuple-element.37), channel_id=1, source_target_pairs={{0,8},{1,9},{2,10},{3,11},{4,12},{5,13},{6,14},{7,15},{8,0},{9,1},... | collective-permute-start | bytes 150536 | tf_op jit(solution)/shard_map/ppermute | solution.py:201

commit v3 on v2

--- a/solution.py
+++ b/solution.py
@@ -1,3 +1,5 @@
+import functools
+
 import jax
 import jax.numpy as jnp
 from jax import lax
@@ -41,8 +43,31 @@
 
 
 def router_kernel(
-    tokens, logits, ref_logits, routes, send, entropy, divergence, base, coef, select_out
+    tokens_in,
+    logits_in,
+    ref_in,
+    routes_in,
+    send,
+    entropy,
+    divergence,
+    base,
+    coef,
+    select_out,
+    tokens,
+    logits,
+    ref_logits,
+    routes,
+    sems,
 ):
+    sources = (logits_in, ref_in, routes_in, tokens_in)
+    targets = (logits, ref_logits, routes, tokens)
+    copies = [
+        pltpu.make_async_copy(s, t, sems.at[i]) for i, (s, t) in enumerate(zip(sources, targets))
+    ]
+    for copy in copies:
+        copy.start()
+    for copy in copies[:3]:
+        copy.wait()
     slots, width = send.shape[0], tokens.shape[1]
     experts, count = logits.shape
     x, r = logits[...], ref_logits[...]
@@ -71,32 +96,63 @@
     hit = (slot == position.astype(jnp.int32)) & (routed > 0.0) & (slot < slots)
     select = jnp.where(hit, 1.0, 0.0)
     select_out[...] = select
-    x_slots = dot(select.astype(BF16), tokens[...], ((1,), (0,)))
-    send[:, :width] = x_slots[:slots].astype(BF16)
     gate_low = gate.astype(BF16).astype(F32)
     g_slots = jnp.sum(select * gate_low, axis=1, keepdims=True)
     send[:, width:] = jnp.broadcast_to(g_slots[:slots], (slots, LANES)).astype(BF16)
-
-
-def back_kernel(y, down, back):
-    back[...] = dot(y[...], down[...], ((1,), (1,)))
-
-
-def expert_kernel(x, back, gate_w, up_w, send, keep, weighted, d_gate, d_up, acc_gate, acc_up):
-    rows, width = x.shape[0], gate_w.shape[0]
+    copies[3].wait()
+    x_slots = dot(select.astype(BF16), tokens[...], ((1,), (0,)))
+    send[:, :width] = x_slots[:slots].astype(BF16)
+
+
+def back_kernel(y, down_in, back, down, sems):
+    step = down.shape[2]
+
+    def copy(i):
+        at = pl.ds(pl.multiple_of(i * step, step), step)
+        return pltpu.make_async_copy(down_in.at[:, at], down.at[i], sems.at[i])
+
+    for i in range(down.shape[0]):
+        copy(i).start()
+    back[...] = jnp.zeros_like(back)
+
+    def body(i, carry):
+        copy(i).wait()
+        at = pl.ds(pl.multiple_of(i * step, step), step)
+        back[...] += dot(y[:, at], down[i], ((1,), (1,)))
+        return carry
+
+    lax.fori_loop(0, down.shape[0], body, 0)
+
+
+def expert_kernel(
+    x, back, gate_in, up_in, send, keep, weighted, d_both, gate_w, up_w, acc_gate, acc_up, sems
+):
+    rows, width, hidden_dim = x.shape[0], gate_w.shape[0], gate_w.shape[1]
     half = rows // 2
-    step = 1536
+    chunks = sems.shape[1]
+    step = width // chunks
+
+    def copy(k, i):
+        at = pl.ds(pl.multiple_of(i * step, step), step)
+        source, target = ((gate_in, gate_w), (up_in, up_w))[k]
+        return pltpu.make_async_copy(source.at[at], target.at[at], sems.at[k, i])
+
+    for i in range(chunks):
+        copy(0, i).start()
+        copy(1, i).start()
 
     def fore(i, carry):
         at = pl.ds(pl.multiple_of(i * step, step), step)
         xs = x[:, at]
+        copy(0, i).wait()
         acc_gate[...] += dot(xs, gate_w[at, :], ((1,), (0,)))
+        copy(1, i).wait()
         acc_up[...] += dot(xs, up_w[at, :], ((1,), (0,)))
         return carry
 
     acc_gate[...] = jnp.zeros_like(acc_gate)
     acc_up[...] = jnp.zeros_like(acc_up)
-    lax.fori_loop(0, width // step, fore, 0)
+    lax.fori_loop(0, chunks, fore, 0)
     pre_gate, pre_up = acc_gate[...], acc_up[...]
     g = x[:, width:][:, 0:1].astype(F32)
     sig = jax.nn.sigmoid(pre_gate)
@@ -105,16 +161,18 @@
     weighted[...] = (g * hidden).astype(BF16)
     products = jnp.sum(hidden * back[...], axis=1, keepdims=True)
     scaled = g * back[...]
-    d_gate[...] = (scaled * pre_up * sig * (1.0 + pre_gate * (1.0 - sig))).astype(BF16)
-    d_up[...] = (scaled * act).astype(BF16)
+    d_gate = (scaled * pre_up * sig * (1.0 + pre_gate * (1.0 - sig))).astype(BF16)
+    d_up = (scaled * act).astype(BF16)
+    d_both[:, :hidden_dim] = d_gate
+    d_both[:, hidden_dim:] = d_up
     keep[:, width:] = lane_pair(half, products[:half], 0.0)
     send[:, width:] = split_pair(products[half:]).astype(BF16)
     wide = 512
 
     def rear(i, carry):
         at = pl.ds(pl.multiple_of(i * wide, wide), wide)
-        part = dot(d_gate[...], gate_w[at, :], ((1,), (1,)))
-        part += dot(d_up[...], up_w[at, :], ((1,), (1,)))
+        part = dot(d_both[:, :hidden_dim], gate_w[at, :], ((1,), (1,)))
+        part += dot(d_both[:, hidden_dim:], up_w[at, :], ((1,), (1,)))
         keep[:, at] = part[:half]
         send[:, at] = part[half:].astype(BF16)
         return carry
@@ -147,46 +205,97 @@
     grad_logits[...] = base[...] + coef[...] * token_products
 
 
-def rows_kernel(left, right, out):
-    out[...] = dot(left[...], right[...], ((0,), (0,))).astype(BF16)
-
-
-def grad_rows(left, right):
-    slots, cols = right.shape
-    rows = left.shape[1] // 1024 * 1024
+def down_kernel(weighted, y, out, buf, sems):
+    chunks, _, step = buf.shape
+
+    def copy(i):
+        at = pl.ds(pl.multiple_of(i * step, step), step)
+        return pltpu.make_async_copy(buf.at[i], out.at[:, at], sems.at[i])
+
+    def body(i, carry):
+        at = pl.ds(pl.multiple_of(i * step, step), step)
+        buf[i] = dot(weighted[...], y[:, at], ((0,), (0,))).astype(BF16)
+        copy(i).start()
+        return carry
+
+    def finish(i, carry):
+        copy(i).wait()
+        return carry
+
+    lax.fori_loop(0, chunks, body, 0)
+    lax.fori_loop(0, chunks, finish, 0)
+
+
+def pair_kernel(first_row, x, d_both, *refs):
+    gate_out, up_out, gate_buf, up_buf, sems = refs[-5:]
+    chunks, step, cols = gate_buf.shape
+
+    def copy(k, i):
+        at = pl.ds(pl.multiple_of(first_row + i * step, step), step)
+        source, target = ((gate_buf, gate_out), (up_buf, up_out))[k]
+        return pltpu.make_async_copy(source.at[i], target.at[at], sems.at[k, i])
+
+    def body(i, carry):
+        at = pl.ds(pl.multiple_of(first_row + i * step, step), step)
+        both = dot(x[:, at], d_both[...], ((0,), (0,))).astype(BF16)
+        gate_buf[i] = both[:, :cols]
+        up_buf[i] = both[:, cols:]
+        copy(0, i).start()
+        copy(1, i).start()
+        return carry
+
+    def finish(i, carry):
+        copy(0, i).wait()
+        copy(1, i).wait()
+        return carry
+
+    lax.fori_loop(0, chunks, body, 0)
+    lax.fori_loop(0, chunks, finish, 0)
+
+
+def grad_down_of(weighted, y):
+    hidden, width = weighted.shape[1], y.shape[1]
+    step = 512
     return pl.pallas_call(
-        rows_kernel,
-        grid=(rows // 1024,),
-        out_shape=jax.ShapeDtypeStruct((rows, cols), BF16),
-        in_specs=[
-            pl.BlockSpec((slots, 1024), lambda i: (0, i)),
-            pl.BlockSpec((slots, cols), lambda i: (0, 0)),
+        down_kernel,
+        out_shape=jax.ShapeDtypeStruct((hidden, width), BF16),
+        in_specs=whole(2),
+        out_specs=pl.BlockSpec(memory_space=pl.ANY),
+        scratch_shapes=[
+            pltpu.VMEM((width // step, hidden, step), BF16),
+            pltpu.SemaphoreType.DMA((width // step,)),
         ],
-        out_specs=pl.BlockSpec((1024, cols), lambda i: (i, 0)),
         compiler_params=pltpu.CompilerParams(vmem_limit_bytes=16 * MIB),
         cost_estimate=pl.CostEstimate(
-            flops=8 * slots * rows * cols, bytes_accessed=2 * rows * cols, transcendentals=0
+            flops=8 * weighted.size * width, bytes_accessed=2 * hidden * width, transcendentals=0
         ),
-    )(left, right)
-
-
-def grad_cols(left, right):
-    slots, rows = left.shape
-    cols = right.shape[1]
+    )(weighted, y)
+
+
+def grad_pair_of(x, d_both, width, part, parts, before):
+    cols = d_both.shape[1] // 2
+    step = 256
+    rows = width // parts
+    outs = [jax.ShapeDtypeStruct((width, cols), BF16)] * 2
+    anywhere = pl.BlockSpec(memory_space=pl.ANY)
     return pl.pallas_call(
-        rows_kernel,
-        grid=(cols // 1024,),
-        out_shape=jax.ShapeDtypeStruct((rows, cols), BF16),
-        in_specs=[
-            pl.BlockSpec((slots, rows), lambda i: (0, 0)),
-            pl.BlockSpec((slots, 1024), lambda i: (0, i)),
+        functools.partial(pair_kernel, part * rows),
+        out_shape=outs,
+        in_specs=whole(2) + [anywhere] * len(before),
+        out_specs=[anywhere] * 2,
+        scratch_shapes=[
+            pltpu.VMEM((rows // step, step, cols), BF16),
+            pltpu.VMEM((rows // step, step, cols), BF16),
+            pltpu.SemaphoreType.DMA((2, rows // step)),
         ],
-        out_specs=pl.BlockSpec((rows, 1024), lambda i: (0, i)),
+        input_output_aliases={2 + i: i for i in range(len(before))},
         compiler_params=pltpu.CompilerParams(vmem_limit_bytes=16 * MIB),
         cost_estimate=pl.CostEstimate(
-            flops=8 * slots * rows * cols, bytes_accessed=2 * rows * cols, transcendentals=0
+            flops=8 * x.shape[0] * rows * 2 * cols,
+            bytes_accessed=4 * rows * cols,
+            transcendentals=0,
         ),
-    )(left, right)
+    )(x, d_both, *before)
 
 
 def make_shards(n):
@@ -203,7 +312,7 @@
     def grow(block, bits):
         block = block[None]
         for bit in bits:
-            block = jnp.concatenate([block, swap(block, bit)])
+            block = lax.optimization_barrier(jnp.concatenate([block, swap(block, bit)]))
         return block
 
     def shards(
@@ -215,54 +324,78 @@
         hidden = down_weight.shape[0]
         rows = n * slots
         wide = width + LANES
-        gate_w = pltpu.with_memory_space_constraint(gate_weight, pltpu.VMEM)
-        up_w = pltpu.with_memory_space_constraint(up_weight, pltpu.VMEM)
-        down_w = pltpu.with_memory_space_constraint(down_weight, pltpu.VMEM)
-
-        send, entropy, divergence, base, coef, select = call(
+        anywhere = pl.BlockSpec(memory_space=pl.ANY)
+
+        send, entropy, divergence, base, coef, select = pl.pallas_call(
             router_kernel,
-            [
-                ((slots, wide), BF16),
-                ((1, count), F32),
-                ((1, count), F32),
-                ((experts, count), F32),
-                ((experts, count), F32),
-                ((count, count), F32),
+            out_shape=[
+                jax.ShapeDtypeStruct((slots, wide), BF16),
+                jax.ShapeDtypeStruct((1, count), F32),
+                jax.ShapeDtypeStruct((1, count), F32),
+                jax.ShapeDtypeStruct((experts, count), F32),
+                jax.ShapeDtypeStruct((experts, count), F32),
+                jax.ShapeDtypeStruct((count, count), F32),
             ],
-            [tokens, logits.T, ref_logits.T, routes.T],
-            1 << 20,
-            1 << 18,
-        )
-
-        y_part = grow(cotangent, [2] + z_bits)
-        y_part = y_part.reshape(nz, 2, slots, width).transpose(1, 0, 2, 3)
+            in_specs=[anywhere] * 4,
+            out_specs=whole(6),
+            scratch_shapes=[
+                pltpu.VMEM((count, width), BF16),
+                pltpu.VMEM((experts, count), F32),
+                pltpu.VMEM((experts, count), F32),
+                pltpu.VMEM((2, count), jnp.int32),
+                pltpu.SemaphoreType.DMA((4,)),
+            ],
+            compiler_params=pltpu.CompilerParams(vmem_limit_bytes=8 * MIB),
+            cost_estimate=pl.CostEstimate(
+                flops=1 << 20, bytes_accessed=1 << 18, transcendentals=0
+            ),
+        )(tokens, logits.T, ref_logits.T, routes.T)
+
+        y_part = grow(cotangent, z_bits[:-1] + [2, z_bits[-1]])
+        y_part = y_part.reshape(2, 2, nz // 2, slots, width).transpose(1, 0, 2, 3, 4)
         y_part = y_part.reshape(rows // 2, width)
         y_all = jnp.concatenate([y_part, swap(y_part, 1)])
         x_part = grow(send, z_bits + [2]).reshape(rows // 2, wide)
         x_all = jnp.concatenate([x_part, swap(x_part, 1)])
 
         work = 2 * rows * width * hidden
-        (back,) = call(
-            back_kernel, [((rows, hidden), F32)], [y_all, down_w], 4 * work, 2 * width * hidden, 16
-        )
+        back = pl.pallas_call(
+            back_kernel,
+            out_shape=jax.ShapeDtypeStruct((rows, hidden), F32),
+            in_specs=whole(1) + [anywhere],
+            out_specs=whole(1)[0],
+            scratch_shapes=[
+                pltpu.VMEM((8, hidden, width // 8), BF16),
+                pltpu.SemaphoreType.DMA((8,)),
+            ],
+            compiler_params=pltpu.CompilerParams(vmem_limit_bytes=24 * MIB),
+            cost_estimate=pl.CostEstimate(
+                flops=4 * work, bytes_accessed=2 * width * hidden, transcendentals=0
+            ),
+        )(y_all, down_weight)
         half = rows // 2
-        low, keep, weighted, d_gate, d_up = pl.pallas_call(
+        low, keep, weighted, d_both = pl.pallas_call(
             expert_kernel,
             out_shape=[
                 jax.ShapeDtypeStruct((half, wide), BF16),
                 jax.ShapeDtypeStruct((half, wide), F32),
                 jax.ShapeDtypeStruct((rows, hidden), BF16),
-                jax.ShapeDtypeStruct((rows, hidden), BF16),
-                jax.ShapeDtypeStruct((rows, hidden), BF16),
+                jax.ShapeDtypeStruct((rows, 2 * hidden), BF16),
             ],
-            in_specs=whole(4),
-            out_specs=whole(5),
-            scratch_shapes=[pltpu.VMEM((rows, hidden), F32)] * 2,
+            in_specs=whole(2) + [anywhere] * 2,
+            out_specs=whole(4),
+            scratch_shapes=[
+                pltpu.VMEM((width, hidden), BF16),
+                pltpu.VMEM((width, hidden), BF16),
+                pltpu.VMEM((rows, hidden), F32),
+                pltpu.VMEM((rows, hidden), F32),
+                pltpu.SemaphoreType.DMA((2, 8)),
+            ],
             compiler_params=pltpu.CompilerParams(vmem_limit_bytes=32 * MIB),
             cost_estimate=pl.CostEstimate(
                 flops=16 * work, bytes_accessed=4 * width * hidden, transcendentals=0
             ),
-        )(x_all, back, gate_w, up_w)
+        )(x_all, back, gate_weight, up_weight)
 
         for bit in [1, 2] + z_bits[::-1]:
             got = swap(low, bit)
@@ -277,9 +410,11 @@
                 16 * half * wide,
             )
 
-        grad_down = grad_cols(weighted, y_all)
-        grad_gate = grad_rows(x_all, d_gate)
-        grad_up = grad_rows(x_all, d_up)
+        grad_down = grad_down_of(weighted, y_all)
+        grad_pair = ()
+        for part in range(2):
+            grad_pair = grad_pair_of(x_all, d_both, width, part, 2, grad_pair)
+        grad_gate, grad_up = grad_pair
 
         grad_tokens, grad_logits = call(
             home_kernel,

time: 70.5 us -> 71.7 us (1.017)
  Pallas kernels: 26.7 us -> 31.2 us
  other arithmetic: 3.38 us -> 1.73 us
  waiting for transfers between devices: 12.5 us -> 11.4 us
    pallas_call x3 -> x5, Pallas kernels: 14.6 us -> 19.2 us  [the longest x2 9.6 us: grad_pair_of(): pl.pallas_call(functools.partial(pair_kernel, part * rows), out_shape=out...]
    pallas_call x6 -> x4, Pallas kernels: 4.1 us -> 1.37 us  [call(): pl.pallas_call(kernel, out_shape=[jax.ShapeDtypeStruct(s, t) for s, t in...]
    pallas_call x1, Pallas kernels: 8.02 us -> 10.6 us  [shards(): pl.pallas_call(expert_kernel, out_shape=[jax.ShapeDtypeStruct((half, wide...]
    concatenate x6, other arithmetic: 3.38 us -> 1.73 us  [grow(): block = lax.optimization_barrier(jnp.concatenate([block, swap(block, bit)]))]
    ppermute x12, waiting for transfers between devices: 12.5 us -> 11.4 us  [swap(): return lax.ppermute(block, 'blk', [(i, i ^ bit) for i in range(n)])]
  transfers between devices with their start and end apart: 12 -> 12, of which waited for: 6 -> 6; matrix products, arithmetic and copies ran while one was open for 5% -> 3% of each run, Pallas kernels for 25% -> 27%
where the time goes in v3:
time: 71.7 us; the launch traced here: 71.3 us
  Pallas kernels  31.2 us (44%)
  starting transfers between devices  14.5 us (20%)
  local copies, waits for them, and re-layouts  11.8 us (16%)
  waiting for transfers between devices  11.4 us (16%)
  other arithmetic  1.73 us (2%)
  between operations  0.83 us (1%)
    ppermute x12, starting transfers between devices, swap(): return lax.ppermute(block, 'blk', [(i, i ^ bit) for i in range(n)])  14.5 us
    unnamed x16, local copies, waits for them, and re-layouts  11.4 us
    ppermute x12, waiting for transfers between devices, swap(): return lax.ppermute(block, 'blk', [(i, i ^ bit) for i in range(n)])  11.4 us
    pallas_call x1, Pallas kernels, shards(): pl.pallas_call(expert_kernel, out_shape=[jax.ShapeDtypeStruct((half, wide...  10.6 us
    pallas_call x2, Pallas kernels, grad_pair_of(): pl.pallas_call(functools.partial(pair_kernel, part * rows), out_shape=out...  9.6 us
    pallas_call x1, Pallas kernels, grad_down_of(): pl.pallas_call(down_kernel, out_shape=jax.ShapeDtypeStruct((hidden, width...  4.73 us
    pallas_call x1, Pallas kernels, shards(): pl.pallas_call(back_kernel, out_shape=jax.ShapeDtypeStruct((rows, hidden)...  3.86 us
    concatenate x6, other arithmetic, grow(): block = lax.optimization_barrier(jnp.concatenate([block, swap(block, bit)]))  1.73 us
  transfers between devices with their start and end apart: 12, of which 6 were waited for; matrix products, arithmetic and copies ran while one was open for 3% of the time, Pallas kernels for 27%

profile of v3, /device:TPU:0, one launch (start us, length us, event | category | flops | bytes accessed | tf_op | source)
XLA Modules:
  0.0 71.3 jit_solution(3284206147112868754)
XLA Ops:
  0.6 4.1 %collective-permute-start.4 = (bf16[1,4,6144]{2,1,0:T(4,128)(2,1)}, bf16[1,4,6144]{2,1,0:T(4,128)(2,1)S(1)}, u32[]{:S(2)}, u32[]{:S(2)}) collective-permute-start(bf16[1,4,6144]{2,1,0:T(4,128)(2,1)} %bitcast.19), channel_id=1, source_target_pairs={{0,8},{1,9},{2,10},{3,11},{4,12},{5,13},{6,14},{7,15},{8,0},{9,1},... | collective-permute-start | bytes 147464 | tf_op jit(solution)/shard_map/ppermute | solution.py:310
  4.7 0.9 %copy-done.1 = bf16[16,6144]{1,0:T(8,128)(2,1)S(1)} copy-done((bf16[16,6144]{1,0:T(8,128)(2,1)S(1)}, bf16[16,6144]{1,0:T(8,128)(2,1)}, u32[]{:S(2)}) %copy-start.1) | copy-done | bytes 196632
  5.7 0.7 copy-done.2
  6.4 0.7 copy-done.3
  7.0 0.7 copy-done.4
  7.7 1.0 %shard_map.135 = (bf16[4,6272]{1,0:T(4,128)(2,1)S(1)}, f32[1,16]{1,0:T(1,128)}, f32[1,16]{1,0:T(1,128)}, f32[8,16]{1,0:T(8,128)S(1)}, f32[8,16]{1,0:T(8,128)S(1)}, /*index=5*/f32[16,16]{1,0:T(8,128)S(1)}) custom-call(bf16[16,6144]{1,0:T(8,128)(2,1)S(1)} %copy-done.1, f32[8,16]{1,0:T(8,128)S(1)} %bitcast.14, f32[8,16]{1,0:T(8,128)S(1)} %bitcast.15, ...), custom_call_target="tpu_custom_call" | custom-call | flops 1048576 | bytes 262144 | tf_op jit(solution)/shard_map/pallas_call | solution.py:329
  8.7 0.1 collective-permute-start
  8.8 0.0 collective-permute-done.4
  8.8 0.9 %pad_maximum_fusion.5 = bf16[2,4,6144]{2,1,0:T(4,128)(2,1)S(1)} fusion(bf16[1,4,6144]{2,1,0:T(4,128)(2,1)S(1)} %collective-permute-done.4, bf16[1,4,6144]{2,1,0:T(4,128)(2,1)} %bitcast.20), kind=kLoop, calls=%fused_computation.6 | loop fusion | flops 49152 | bytes 196608 | tf_op jit(solution)/shard_map/concatenate | solution.py:315
  9.7 1.9 %collective-permute-start.5 = (bf16[2,4,6144]{2,1,0:T(4,128)(2,1)S(1)}, bf16[2,4,6144]{2,1,0:T(4,128)(2,1)S(1)}, u32[]{:S(2)}, u32[]{:S(2)}) collective-permute-start(bf16[2,4,6144]{2,1,0:T(4,128)(2,1)S(1)} %pad_maximum_fusion.5), channel_id=1, source_target_pairs={{0,2},{1,3},{2,0},{3,1},{4,6},{5,7},{6,4},{7,5},{8,10},{9,11},{10,... | collective-permute-start | bytes 294920 | tf_op jit(solution)/shard_map/ppermute | solution.py:310
  11.6 2.3 %collective-permute-done = bf16[1,4,6272]{2,1,0:T(4,128)(2,1)S(1)} collective-permute-done((bf16[1,4,6272]{2,1,0:T(4,128)(2,1)S(1)}, bf16[1,4,6272]{2,1,0:T(4,128)(2,1)S(1)}, u32[]{:S(2)}, u32[]{:S(2)}) %collective-permute-start) | collective-permute-done | bytes 50208 | tf_op jit(solution)/shard_map/ppermute | solution.py:310
  13.9 0.1 pad_maximum_fusion.4
  14.0 1.5 %collective-permute-start.1 = (bf16[2,4,6272]{2,1,0:T(4,128)(2,1)S(1)}, bf16[2,4,6272]{2,1,0:T(4,128)(2,1)S(1)}, u32[]{:S(2)}, u32[]{:S(2)}) collective-permute-start(bf16[2,4,6272]{2,1,0:T(4,128)(2,1)S(1)} %pad_maximum_fusion.4), channel_id=1, source_target_pairs={{0,4},{1,5},{2,6},{3,7},{4,0},{5,1},{6,2},{7,3},{8,12},{9,13},{10,... | collective-permute-start | bytes 301064 | tf_op jit(solution)/shard_map/ppermute | solution.py:310
  15.5 0.0 collective-permute-done.5
  15.5 0.1 pad_maximum_fusion.3
  15.6 0.8 %collective-permute-start.6 = (bf16[4,4,6144]{2,1,0:T(4,128)(2,1)S(1)}, bf16[4,4,6144]{2,1,0:T(4,128)(2,1)S(1)}, u32[]{:S(2)}, u32[]{:S(2)}) collective-permute-start(bf16[4,4,6144]{2,1,0:T(4,128)(2,1)S(1)} %pad_maximum_fusion.3), channel_id=1, source_target_pairs={{0,4},{1,5},{2,6},{3,7},{4,0},{5,1},{6,2},{7,3},{8,12},{9,13},{10,... | collective-permute-start | bytes 589832 | tf_op jit(solution)/shard_map/ppermute | solution.py:310
  16.4 3.2 %collective-permute-done.1 = bf16[2,4,6272]{2,1,0:T(4,128)(2,1)S(1)} collective-permute-done((bf16[2,4,6272]{2,1,0:T(4,128)(2,1)S(1)}, bf16[2,4,6272]{2,1,0:T(4,128)(2,1)S(1)}, u32[]{:S(2)}, u32[]{:S(2)}) %collective-permute-start.1) | collective-permute-done | bytes 100384 | tf_op jit(solution)/shard_map/ppermute | solution.py:310
  19.6 0.1 pad_maximum_fusion.2
  19.7 1.6 %collective-permute-start.2 = (bf16[4,4,6272]{2,1,0:T(4,128)(2,1)S(1)}, bf16[4,4,6272]{2,1,0:T(4,128)(2,1)S(1)}, u32[]{:S(2)}, u32[]{:S(2)}) collective-permute-start(bf16[4,4,6272]{2,1,0:T(4,128)(2,1)S(1)} %pad_maximum_fusion.2), channel_id=1, source_target_pairs={{0,2},{1,3},{2,0},{3,1},{4,6},{5,7},{6,4},{7,5},{8,10},{9,11},{10,... | collective-permute-start | bytes 602120 | tf_op jit(solution)/shard_map/ppermute | solution.py:310
  21.3 0.4 collective-permute-done.6
  21.7 0.3 pad_maximum_fusion.1
  22.0 0.1 copy.19
  22.1 0.1 reshape.31
  22.2 0.1 collective-permute-start.7
  22.3 3.2 %collective-permute-done.2 = bf16[4,4,6272]{2,1,0:T(4,128)(2,1)S(1)} collective-permute-done((bf16[4,4,6272]{2,1,0:T(4,128)(2,1)S(1)}, bf16[4,4,6272]{2,1,0:T(4,128)(2,1)S(1)}, u32[]{:S(2)}, u32[]{:S(2)}) %collective-permute-start.2) | collective-permute-done | bytes 200736 | tf_op jit(solution)/shard_map/ppermute | solution.py:310
  25.5 0.3 pad_maximum_fusion
  25.8 0.1 reshape.29
  25.9 0.1 collective-permute-start.3
  26.0 0.0 copy-start
  26.1 2.8 %copy-done = bf16[512,6144]{1,0:T(8,128)(2,1)S(1)} copy-done((bf16[512,6144]{1,0:T(8,128)(2,1)S(1)}, bf16[512,6144]{1,0:T(8,128)(2,1)}, u32[]{:S(2)}) %copy-start) | copy-done | bytes 6291480
  28.8 3.9 %shard_map.136.back = f32[64,512]{1,0:T(8,128)S(1)} custom-call(bf16[64,6144]{1,0:T(8,128)(2,1)S(1)} %constant_dynamic-update-slice_fusion.2.y, bf16[512,6144]{1,0:T(8,128)(2,1)S(1)} %copy-done), custom_call_target="tpu_custom_call" | custom-call | flops 1610612736 | bytes 6291456 | tf_op jit(solution)/shard_map/pallas_call | solution.py:362
  32.7 0.0 copy-start.5
  32.8 2.8 %copy-done.5 = bf16[6144,512]{1,0:T(8,128)(2,1)S(1)} copy-done((bf16[6144,512]{1,0:T(8,128)(2,1)S(1)}, bf16[6144,512]{1,0:T(8,128)(2,1)}, u32[]{:S(2)}) %copy-start.5) | copy-done | bytes 6291480
  35.5 2.8 %copy-done.6 = bf16[6144,512]{1,0:T(8,128)(2,1)S(1)} copy-done((bf16[6144,512]{1,0:T(8,128)(2,1)S(1)}, bf16[6144,512]{1,0:T(8,128)(2,1)}, u32[]{:S(2)}) %copy-start.6) | copy-done | bytes 6291480
  38.3 10.6 %shard_map.137 = (bf16[32,6272]{1,0:T(8,128)(2,1)S(1)}, f32[32,6272]{1,0:T(8,128)S(1)}, bf16[64,512]{1,0:T(8,128)(2,1)S(1)}, bf16[64,1024]{1,0:T(8,128)(2,1)S(1)}) custom-call(bf16[64,6272]{1,0:T(8,128)(2,1)S(1)} %constant_dynamic-update-slice_fusion.x, f32[64,512]{1,0:T(8,128)S(1)} %shard_map.136.back, bf16[6144,512]{1,0:T(8,128)(2,1)S(1)} %copy-done.5, ...), custom_call_target="tpu_custom_call" | custom-call | flops 6442450944 | bytes 12582912 | tf_op jit(solution)/shard_map/pallas_call | solution.py:377
  48.9 0.6 collective-permute-start.8
  49.5 1.4 %collective-permute-done.8.got = bf16[32,6272]{1,0:T(8,128)(2,1)S(1)} collective-permute-done((bf16[32,6272]{1,0:T(8,128)(2,1)S(1)}, bf16[32,6272]{1,0:T(8,128)(2,1)S(1)}, u32[]{:S(2)}, u32[]{:S(2)}) %collective-permute-start.8) | collective-permute-done | bytes 401440 | tf_op jit(solution)/shard_map/ppermute | solution.py:310
  50.9 0.2 shard_map.141
  51.0 1.6 %collective-permute-start.9 = (bf16[16,6272]{1,0:T(8,128)(2,1)S(1)}, bf16[16,6272]{1,0:T(8,128)(2,1)S(1)}, u32[]{:S(2)}, u32[]{:S(2)}) collective-permute-start(bf16[16,6272]{1,0:T(8,128)(2,1)S(1)} %get-tuple-element.39), channel_id=1, source_target_pairs={{0,2},{1,3},{2,0},{3,1},{4,6},{5,7},{6,4},{7,5},{8,10},{9,11},{10,... | collective-permute-start | bytes 602120 | tf_op jit(solution)/shard_map/ppermute | solution.py:310
  52.6 4.8 %shard_map.138 = (bf16[6144,512]{1,0:T(8,128)(2,1)}, bf16[6144,512]{1,0:T(8,128)(2,1)}) custom-call(bf16[64,6272]{1,0:T(8,128)(2,1)S(1)} %constant_dynamic-update-slice_fusion.x, bf16[64,1024]{1,0:T(8,128)(2,1)S(1)} %get-tuple-element.30.d_both), custom_call_target="tpu_custom_call" | custom-call | flops 1610612736 | bytes 6291456 | tf_op jit(solution)/shard_map/pallas_call | solution.py:281
  57.4 0.9 %collective-permute-done.9.got = bf16[16,6272]{1,0:T(8,128)(2,1)S(1)} collective-permute-done((bf16[16,6272]{1,0:T(8,128)(2,1)S(1)}, bf16[16,6272]{1,0:T(8,128)(2,1)S(1)}, u32[]{:S(2)}, u32[]{:S(2)}) %collective-permute-start.9) | collective-permute-done | bytes 200736 | tf_op jit(solution)/shard_map/ppermute | solution.py:310
  58.4 0.1 shard_map.142
  58.5 1.2 %collective-permute-start.10 = (bf16[8,6272]{1,0:T(8,128)(2,1)S(1)}, bf16[8,6272]{1,0:T(8,128)(2,1)S(1)}, u32[]{:S(2)}, u32[]{:S(2)}) collective-permute-start(bf16[8,6272]{1,0:T(8,128)(2,1)S(1)} %get-tuple-element.41), channel_id=1, source_target_pairs={{0,4},{1,5},{2,6},{3,7},{4,0},{5,1},{6,2},{7,3},{8,12},{9,13},{10,... | collective-permute-start | bytes 301064 | tf_op jit(solution)/shard_map/ppermute | solution.py:310
  59.7 4.7 %shard_map.140 = bf16[512,6144]{1,0:T(8,128)(2,1)} custom-call(bf16[64,512]{1,0:T(8,128)(2,1)S(1)} %get-tuple-element.35.weighted, bf16[64,6144]{1,0:T(8,128)(2,1)S(1)} %constant_dynamic-update-slice_fusion.2.y), custom_call_target="tpu_custom_call" | custom-call | flops 1610612736 | bytes 6291456 | tf_op jit(solution)/shard_map/pallas_call | solution.py:259
  64.4 0.2 shard_map.143
  64.6 1.0 %collective-permute-start.11 = (bf16[4,6272]{1,0:T(4,128)(2,1)S(1)}, bf16[4,6272]{1,0:T(4,128)(2,1)S(1)}, u32[]{:S(2)}, u32[]{:S(2)}) collective-permute-start(bf16[4,6272]{1,0:T(4,128)(2,1)S(1)} %get-tuple-element.43), channel_id=1, source_target_pairs={{0,8},{1,9},{2,10},{3,11},{4,12},{5,13},{6,14},{7,15},{8,0},{9,1},... | collective-permute-start | bytes 150536 | tf_op jit(solution)/shard_map/ppermute | solution.py:310
  65.6 4.8 %shard_map.139 = (bf16[6144,512]{1,0:T(8,128)(2,1)}, bf16[6144,512]{1,0:T(8,128)(2,1)}) custom-call(bf16[64,6272]{1,0:T(8,128)(2,1)S(1)} %constant_dynamic-update-slice_fusion.x, bf16[64,1024]{1,0:T(8,128)(2,1)S(1)} %get-tuple-element.30.d_both, bf16[6144,512]{1,0:T(8,128)(2,1)} %get-tuple-element.31.refs_0_, ...), custom_call_target="tpu_custom_call", output_to_operand_aliasing={{0}: (2, {}), {1}: (3, {})} | custom-call | flops 1610612736 | bytes 6291456 | tf_op jit(solution)/shard_map/pallas_call | solution.py:281
  70.4 0.9 %shard_map.144 = (bf16[16,6144]{1,0:T(8,128)(2,1)}, f32[8,16]{1,0:T(8,128)}) custom-call(f32[4,6272]{1,0:T(4,128)S(1)} %get-tuple-element.42.have, bf16[4,6272]{1,0:T(4,128)(2,1)S(1)} %collective-permute-done.11.got, f32[16,16]{1,0:T(8,128)S(1)} %get-tuple-element.44.select, f32[8,16]{1,0:T(8,128)S(1)} %get-tuple-element.45.base, ...), custom_call_target="tpu_custom_call" | custom-call | flops 1048576 | bytes 262144 | tf_op jit(solution)/shard_map/pallas_call | solution.py:25
  (13 shorter events, 0.1 us)
Async XLA Ops:
  0.6 8.2 %collective-permute-start.4 = (bf16[1,4,6144]{2,1,0:T(4,128)(2,1)}, bf16[1,4,6144]{2,1,0:T(4,128)(2,1)S(1)}, u32[]{:S(2)}, u32[]{:S(2)}) collective-permute-start(bf16[1,4,6144]{2,1,0:T(4,128)(2,1)} %bitcast.19), channel_id=1, source_target_pairs={{0,8},{1,9},{2,10},{3,11},{4,12},{5,13},{6,14},{7,15},{8,0},{9,1},... | collective-permute-start | bytes 147464 | tf_op jit(solution)/shard_map/ppermute | solution.py:310
  4.7 0.9 %copy-start.1 = (bf16[16,6144]{1,0:T(8,128)(2,1)S(1)}, bf16[16,6144]{1,0:T(8,128)(2,1)}, u32[]{:S(2)}) copy-start(bf16[16,6144]{1,0:T(8,128)(2,1)} %tokens_in.1) | copy-start | bytes 589828
  5.7 0.7 copy-start.2
  6.3 0.7 copy-start.3
  7.0 0.7 copy-start.4
  8.7 5.2 %collective-permute-start = (bf16[1,4,6272]{2,1,0:T(4,128)(2,1)S(1)}, bf16[1,4,6272]{2,1,0:T(4,128)(2,1)S(1)}, u32[]{:S(2)}, u32[]{:S(2)}) collective-permute-start(bf16[1,4,6272]{2,1,0:T(4,128)(2,1)S(1)} %bitcast.12), channel_id=1, source_target_pairs={{0,8},{1,9},{2,10},{3,11},{4,12},{5,13},{6,14},{7,15},{8,0},{9,1},... | collective-permute-start | bytes 150536 | tf_op jit(solution)/shard_map/ppermute | solution.py:310
  9.7 5.8 %collective-permute-start.5 = (bf16[2,4,6144]{2,1,0:T(4,128)(2,1)S(1)}, bf16[2,4,6144]{2,1,0:T(4,128)(2,1)S(1)}, u32[]{:S(2)}, u32[]{:S(2)}) collective-permute-start(bf16[2,4,6144]{2,1,0:T(4,128)(2,1)S(1)} %pad_maximum_fusion.5), channel_id=1, source_target_pairs={{0,2},{1,3},{2,0},{3,1},{4,6},{5,7},{6,4},{7,5},{8,10},{9,11},{10,... | collective-permute-start | bytes 294920 | tf_op jit(solution)/shard_map/ppermute | solution.py:310
  14.0 5.6 %collective-permute-start.1 = (bf16[2,4,6272]{2,1,0:T(4,128)(2,1)S(1)}, bf16[2,4,6272]{2,1,0:T(4,128)(2,1)S(1)}, u32[]{:S(2)}, u32[]{:S(2)}) collective-permute-start(bf16[2,4,6272]{2,1,0:T(4,128)(2,1)S(1)} %pad_maximum_fusion.4), channel_id=1, source_target_pairs={{0,4},{1,5},{2,6},{3,7},{4,0},{5,1},{6,2},{7,3},{8,12},{9,13},{10,... | collective-permute-start | bytes 301064 | tf_op jit(solution)/shard_map/ppermute | solution.py:310
  15.6 6.1 %collective-permute-start.6 = (bf16[4,4,6144]{2,1,0:T(4,128)(2,1)S(1)}, bf16[4,4,6144]{2,1,0:T(4,128)(2,1)S(1)}, u32[]{:S(2)}, u32[]{:S(2)}) collective-permute-start(bf16[4,4,6144]{2,1,0:T(4,128)(2,1)S(1)} %pad_maximum_fusion.3), channel_id=1, source_target_pairs={{0,4},{1,5},{2,6},{3,7},{4,0},{5,1},{6,2},{7,3},{8,12},{9,13},{10,... | collective-permute-start | bytes 589832 | tf_op jit(solution)/shard_map/ppermute | solution.py:310
  19.7 5.8 %collective-permute-start.2 = (bf16[4,4,6272]{2,1,0:T(4,128)(2,1)S(1)}, bf16[4,4,6272]{2,1,0:T(4,128)(2,1)S(1)}, u32[]{:S(2)}, u32[]{:S(2)}) collective-permute-start(bf16[4,4,6272]{2,1,0:T(4,128)(2,1)S(1)} %pad_maximum_fusion.2), channel_id=1, source_target_pairs={{0,2},{1,3},{2,0},{3,1},{4,6},{5,7},{6,4},{7,5},{8,10},{9,11},{10,... | collective-permute-start | bytes 602120 | tf_op jit(solution)/shard_map/ppermute | solution.py:310
  22.2 3.8 %collective-permute-start.7 = (bf16[32,6144]{1,0:T(8,128)(2,1)S(1)}, bf16[32,6144]{1,0:T(8,128)(2,1)S(1)}, u32[]{:S(2)}, u32[]{:S(2)}) collective-permute-start(bf16[32,6144]{1,0:T(8,128)(2,1)S(1)} %reshape.31), channel_id=1, source_target_pairs={{0,1},{1,0},{2,3},{3,2},{4,5},{5,4},{6,7},{7,6},{8,9},{9,8},{10,11... | collective-permute-start | bytes 1179656 | tf_op jit(solution)/shard_map/ppermute | solution.py:310
  25.9 6.8 %collective-permute-start.3 = (bf16[32,6272]{1,0:T(8,128)(2,1)S(1)}, bf16[32,6272]{1,0:T(8,128)(2,1)S(1)}, u32[]{:S(2)}, u32[]{:S(2)}) collective-permute-start(bf16[32,6272]{1,0:T(8,128)(2,1)S(1)} %reshape.29), channel_id=1, source_target_pairs={{0,1},{1,0},{2,3},{3,2},{4,5},{5,4},{6,7},{7,6},{8,9},{9,8},{10,11... | collective-permute-start | bytes 1204232 | tf_op jit(solution)/shard_map/ppermute | solution.py:310
  26.0 2.8 %copy-start = (bf16[512,6144]{1,0:T(8,128)(2,1)S(1)}, bf16[512,6144]{1,0:T(8,128)(2,1)}, u32[]{:S(2)}) copy-start(bf16[512,6144]{1,0:T(8,128)(2,1)} %down_in.1) | copy-start | bytes 18874372
  32.7 2.8 %copy-start.5 = (bf16[6144,512]{1,0:T(8,128)(2,1)S(1)}, bf16[6144,512]{1,0:T(8,128)(2,1)}, u32[]{:S(2)}) copy-start(bf16[6144,512]{1,0:T(8,128)(2,1)} %gate_in.1) | copy-start | bytes 18874372
  35.5 2.8 %copy-start.6 = (bf16[6144,512]{1,0:T(8,128)(2,1)S(1)}, bf16[6144,512]{1,0:T(8,128)(2,1)}, u32[]{:S(2)}) copy-start(bf16[6144,512]{1,0:T(8,128)(2,1)} %up_in.1) | copy-start | bytes 18874372
  48.9 1.9 %collective-permute-start.8 = (bf16[32,6272]{1,0:T(8,128)(2,1)S(1)}, bf16[32,6272]{1,0:T(8,128)(2,1)S(1)}, u32[]{:S(2)}, u32[]{:S(2)}) collective-permute-start(bf16[32,6272]{1,0:T(8,128)(2,1)S(1)} %get-tuple-element.37), channel_id=1, source_target_pairs={{0,1},{1,0},{2,3},{3,2},{4,5},{5,4},{6,7},{7,6},{8,9},{9,8},{10,11... | collective-permute-start | bytes 1204232 | tf_op jit(solution)/shard_map/ppermute | solution.py:310
  51.0 7.3 %collective-permute-start.9 = (bf16[16,6272]{1,0:T(8,128)(2,1)S(1)}, bf16[16,6272]{1,0:T(8,128)(2,1)S(1)}, u32[]{:S(2)}, u32[]{:S(2)}) collective-permute-start(bf16[16,6272]{1,0:T(8,128)(2,1)S(1)} %get-tuple-element.39), channel_id=1, source_target_pairs={{0,2},{1,3},{2,0},{3,1},{4,6},{5,7},{6,4},{7,5},{8,10},{9,11},{10,... | collective-permute-start | bytes 602120 | tf_op jit(solution)/shard_map/ppermute | solution.py:310
  58.5 5.9 %collective-permute-start.10 = (bf16[8,6272]{1,0:T(8,128)(2,1)S(1)}, bf16[8,6272]{1,0:T(8,128)(2,1)S(1)}, u32[]{:S(2)}, u32[]{:S(2)}) collective-permute-start(bf16[8,6272]{1,0:T(8,128)(2,1)S(1)} %get-tuple-element.41), channel_id=1, source_target_pairs={{0,4},{1,5},{2,6},{3,7},{4,0},{5,1},{6,2},{7,3},{8,12},{9,13},{10,... | collective-permute-start | bytes 301064 | tf_op jit(solution)/shard_map/ppermute | solution.py:310
  64.6 5.8 %collective-permute-start.11 = (bf16[4,6272]{1,0:T(4,128)(2,1)S(1)}, bf16[4,6272]{1,0:T(4,128)(2,1)S(1)}, u32[]{:S(2)}, u32[]{:S(2)}) collective-permute-start(bf16[4,6272]{1,0:T(4,128)(2,1)S(1)} %get-tuple-element.43), channel_id=1, source_target_pairs={{0,8},{1,9},{2,10},{3,11},{4,12},{5,13},{6,14},{7,15},{8,0},{9,1},... | collective-permute-start | bytes 150536 | tf_op jit(solution)/shard_map/ppermute | solution.py:310

commit v4 on v3

--- a/solution.py
+++ b/solution.py
@@ -30,6 +30,10 @@
         compiler_params=pltpu.CompilerParams(vmem_limit_bytes=limit * MIB),
         cost_estimate=pl.CostEstimate(flops=flops, bytes_accessed=moved, transcendentals=0),
     )(*args)
+
+
+def in_hbm(array):
+    return pltpu.with_memory_space_constraint(array, pltpu.HBM)
 
 
 def lane_pair(rows, first, second):
@@ -105,55 +109,43 @@
 
 
 def back_kernel(y, down_in, back, down, sems):
-    step = down.shape[2]
+    chunks, _, step = down.shape
 
     def copy(i):
-        at = pl.ds(pl.multiple_of(i * step, step), step)
-        return pltpu.make_async_copy(down_in.at[:, at], down.at[i], sems.at[i])
-
-    for i in range(down.shape[0]):
+        return pltpu.make_async_copy(down_in.at[:, pl.ds(i * step, step)], down.at[i], sems.at[i])
+
+    for i in range(chunks):
         copy(i).start()
-    back[...] = jnp.zeros_like(back)
-
-    def body(i, carry):
+    for i in range(chunks):
         copy(i).wait()
-        at = pl.ds(pl.multiple_of(i * step, step), step)
-        back[...] += dot(y[:, at], down[i], ((1,), (1,)))
-        return carry
-
-    lax.fori_loop(0, down.shape[0], body, 0)
+        part = dot(y[:, i * step : (i + 1) * step], down[i], ((1,), (1,)))
+        back[...] = part if i == 0 else back[...] + part
 
 
 def expert_kernel(
-    x, back, gate_in, up_in, send, keep, weighted, d_both, gate_w, up_w, acc_gate, acc_up, sems
+    x, back, gate_in, up_in, send, keep, weighted, d_both, both_w, acc, sems
 ):
-    rows, width, hidden_dim = x.shape[0], gate_w.shape[0], gate_w.shape[1]
+    rows, width, hidden_dim = x.shape[0], both_w.shape[0], gate_in.shape[1]
     half = rows // 2
     chunks = sems.shape[1]
     step = width // chunks
 
     def copy(k, i):
-        at = pl.ds(pl.multiple_of(i * step, step), step)
-        source, target = ((gate_in, gate_w), (up_in, up_w))[k]
-        return pltpu.make_async_copy(source.at[at], target.at[at], sems.at[k, i])
+        at = pl.ds(i * step, step)
+        source = (gate_in, up_in)[k]
+        target = both_w.at[at, pl.ds(k * hidden_dim, hidden_dim)]
+        return pltpu.make_async_copy(source.at[at], target, sems.at[k, i])
 
     for i in range(chunks):
         copy(0, i).start()
         copy(1, i).start()
-
-    def fore(i, carry):
-        at = pl.ds(pl.multiple_of(i * step, step), step)
-        xs = x[:, at]
+    for i in range(chunks):
+        at = pl.ds(i * step, step)
         copy(0, i).wait()
-        acc_gate[...] += dot(xs, gate_w[at, :], ((1,), (0,)))
         copy(1, i).wait()
-        acc_up[...] += dot(xs, up_w[at, :], ((1,), (0,)))
-        return carry
-
-    acc_gate[...] = jnp.zeros_like(acc_gate)
-    acc_up[...] = jnp.zeros_like(acc_up)
-    lax.fori_loop(0, chunks, fore, 0)
-    pre_gate, pre_up = acc_gate[...], acc_up[...]
+        part = dot(x[:, at], both_w[at, :], ((1,), (0,)))
+        acc[...] = part if i == 0 else acc[...] + part
+    pre_gate, pre_up = acc[:, :hidden_dim], acc[:, hidden_dim:]
     g = x[:, width:][:, 0:1].astype(F32)
     sig = jax.nn.sigmoid(pre_gate)
     act = pre_gate * sig
@@ -161,23 +153,18 @@
     weighted[...] = (g * hidden).astype(BF16)
     products = jnp.sum(hidden * back[...], axis=1, keepdims=True)
     scaled = g * back[...]
-    d_gate = (scaled * pre_up * sig * (1.0 + pre_gate * (1.0 - sig))).astype(BF16)
-    d_up = (scaled * act).astype(BF16)
-    d_both[:, :hidden_dim] = d_gate
-    d_both[:, hidden_dim:] = d_up
+    d_both[:, :hidden_dim] = (
+        scaled * pre_up * sig * (1.0 + pre_gate * (1.0 - sig))
+    ).astype(BF16)
+    d_both[:, hidden_dim:] = (scaled * act).astype(BF16)
     keep[:, width:] = lane_pair(half, products[:half], 0.0)
     send[:, width:] = split_pair(products[half:]).astype(BF16)
-    wide = 512
-
-    def rear(i, carry):
-        at = pl.ds(pl.multiple_of(i * wide, wide), wide)
-        part = dot(d_both[:, :hidden_dim], gate_w[at, :], ((1,), (1,)))
-        part += dot(d_both[:, hidden_dim:], up_w[at, :], ((1,), (1,)))
+    wide = 1024
+    for i in range(width // wide):
+        at = pl.ds(i * wide, wide)
+        part = dot(d_both[...], both_w[at, :], ((1,), (1,)))
         keep[:, at] = part[:half]
         send[:, at] = part[half:].astype(BF16)
-        return carry
-
-    lax.fori_loop(0, width // wide, rear, 0)
 
 
 def fold_kernel(have, got, keep, send):
@@ -205,7 +192,7 @@
     grad_logits[...] = base[...] + coef[...] * token_products
 
 
-def down_kernel(weighted, y, out, buf, sems):
+def down_kernel(weighted, y, out, buf, turned, sems):
     chunks, _, step = buf.shape
 
     def copy(i):
@@ -214,7 +201,7 @@
 
     def body(i, carry):
         at = pl.ds(pl.multiple_of(i * step, step), step)
-        buf[i] = dot(weighted[...], y[:, at], ((0,), (0,))).astype(BF16)
+        buf[i] = dot(turned[...], y[:, at], ((1,), (0,))).astype(BF16)
         copy(i).start()
         return carry
 
@@ -222,6 +209,7 @@
         copy(i).wait()
         return carry
 
+    turned[...] = weighted[...].astype(F32).T.astype(BF16)
     lax.fori_loop(0, chunks, body, 0)
     lax.fori_loop(0, chunks, finish, 0)
 
@@ -263,6 +251,7 @@
         out_specs=pl.BlockSpec(memory_space=pl.ANY),
         scratch_shapes=[
             pltpu.VMEM((width // step, hidden, step), BF16),
+            pltpu.VMEM((hidden, weighted.shape[0]), BF16),
             pltpu.SemaphoreType.DMA((width // step,)),
         ],
         compiler_params=pltpu.CompilerParams(vmem_limit_bytes=16 * MIB),
@@ -349,7 +338,7 @@
             cost_estimate=pl.CostEstimate(
                 flops=1 << 20, bytes_accessed=1 << 18, transcendentals=0
             ),
-        )(tokens, logits.T, ref_logits.T, routes.T)
+        )(in_hbm(tokens), in_hbm(logits.T), in_hbm(ref_logits.T), in_hbm(routes.T))
 
         y_part = grow(cotangent, z_bits[:-1] + [2, z_bits[-1]])
         y_part = y_part.reshape(2, 2, nz // 2, slots, width).transpose(1, 0, 2, 3, 4)
@@ -365,14 +354,14 @@
             in_specs=whole(1) + [anywhere],
             out_specs=whole(1)[0],
             scratch_shapes=[
-                pltpu.VMEM((8, hidden, width // 8), BF16),
-                pltpu.SemaphoreType.DMA((8,)),
+                pltpu.VMEM((4, hidden, width // 4), BF16),
+                pltpu.SemaphoreType.DMA((4,)),
             ],
             compiler_params=pltpu.CompilerParams(vmem_limit_bytes=24 * MIB),
             cost_estimate=pl.CostEstimate(
                 flops=4 * work, bytes_accessed=2 * width * hidden, transcendentals=0
             ),
-        )(y_all, down_weight)
+        )(y_all, in_hbm(down_weight))
         half = rows // 2
         low, keep, weighted, d_both = pl.pallas_call(
             expert_kernel,
@@ -385,17 +374,15 @@
             in_specs=whole(2) + [anywhere] * 2,
             out_specs=whole(4),
             scratch_shapes=[
-                pltpu.VMEM((width, hidden), BF16),
-                pltpu.VMEM((width, hidden), BF16),
-                pltpu.VMEM((rows, hidden), F32),
-                pltpu.VMEM((rows, hidden), F32),
-                pltpu.SemaphoreType.DMA((2, 8)),
+                pltpu.VMEM((width, 2 * hidden), BF16),
+                pltpu.VMEM((rows, 2 * hidden), F32),
+                pltpu.SemaphoreType.DMA((2, 4)),
             ],
             compiler_params=pltpu.CompilerParams(vmem_limit_bytes=32 * MIB),
             cost_estimate=pl.CostEstimate(
                 flops=16 * work, bytes_accessed=4 * width * hidden, transcendentals=0
             ),
-        )(x_all, back, gate_weight, up_weight)
+        )(x_all, back, in_hbm(gate_weight), in_hbm(up_weight))
 
         for bit in [1, 2] + z_bits[::-1]:
             got = swap(low, bit)

time: 71.7 us -> 60.3 us (0.84)
  local copies, waits for them, and re-layouts: 11.8 us -> 0.44 us
  starting transfers between devices: 14.5 us -> 17.8 us
  waiting for transfers between devices: 11.4 us -> 9.7 us
  Pallas kernels: 31.2 us -> 29.6 us
    unnamed x16 -> x2, local copies, waits for them, and re-layouts: 11.4 us -> 0.06 us
    ppermute x12, starting transfers between devices: 14.5 us -> 17.8 us  [swap(): return lax.ppermute(block, 'blk', [(i, i ^ bit) for i in range(n)])]
    ppermute x12, waiting for transfers between devices: 11.4 us -> 9.7 us  [swap(): return lax.ppermute(block, 'blk', [(i, i ^ bit) for i in range(n)])]
    pallas_call x1, Pallas kernels: 10.6 us -> 9.24 us  [shards(): pl.pallas_call(expert_kernel, out_shape=[jax.ShapeDtypeStruct((half, wide...]
  transfers between devices with their start and end apart: 12 -> 12, of which waited for: 6 -> 8; matrix products, arithmetic and copies ran while one was open for 3% -> 4% of each run, Pallas kernels for 27% -> 32%
where the time goes in v4:
time: 60.3 us; the launch traced here: 60.1 us
  Pallas kernels  29.6 us (49%)
  starting transfers between devices  17.8 us (30%)
  waiting for transfers between devices  9.7 us (16%)
  other arithmetic  1.73 us (3%)
  between operations  0.81 us (1%)
    ppermute x12, starting transfers between devices, swap(): return lax.ppermute(block, 'blk', [(i, i ^ bit) for i in range(n)])  17.8 us
    ppermute x12, waiting for transfers between devices, swap(): return lax.ppermute(block, 'blk', [(i, i ^ bit) for i in range(n)])  9.7 us
    pallas_call x2, Pallas kernels, grad_pair_of(): pl.pallas_call(functools.partial(pair_kernel, part * rows), out_shape=out...  9.61 us
    pallas_call x1, Pallas kernels, shards(): pl.pallas_call(expert_kernel, out_shape=[jax.ShapeDtypeStruct((half, wide...  9.24 us
    pallas_call x1, Pallas kernels, grad_down_of(): pl.pallas_call(down_kernel, out_shape=jax.ShapeDtypeStruct((hidden, width...  4.32 us
    pallas_call x1, Pallas kernels, shards(): pl.pallas_call(back_kernel, out_shape=jax.ShapeDtypeStruct((rows, hidden)...  3.5 us
    concatenate x6, other arithmetic, grow(): block = lax.optimization_barrier(jnp.concatenate([block, swap(block, bit)]))  1.73 us
    pallas_call x1, Pallas kernels, shards(): pl.pallas_call(router_kernel, out_shape=[jax.ShapeDtypeStruct((slots, wid...  1.52 us
  transfers between devices with their start and end apart: 12, of which 8 were waited for; matrix products, arithmetic and copies ran while one was open for 4% of the time, Pallas kernels for 32%

profile of v4, /device:TPU:0, one launch (start us, length us, event | category | flops | bytes accessed | tf_op | source)
XLA Modules:
  0.0 60.1 jit_solution(13934070527683036920)
XLA Ops:
  0.6 4.1 %collective-permute-start.4 = (bf16[1,4,6144]{2,1,0:T(4,128)(2,1)}, bf16[1,4,6144]{2,1,0:T(4,128)(2,1)S(1)}, u32[]{:S(2)}, u32[]{:S(2)}) collective-permute-start(bf16[1,4,6144]{2,1,0:T(4,128)(2,1)} %bitcast.16), channel_id=1, source_target_pairs={{0,8},{1,9},{2,10},{3,11},{4,12},{5,13},{6,14},{7,15},{8,0},{9,1},... | collective-permute-start | bytes 147464 | tf_op jit(solution)/shard_map/ppermute | solution.py:299
  4.7 1.5 %shard_map.135 = (bf16[4,6272]{1,0:T(4,128)(2,1)S(1)}, f32[1,16]{1,0:T(1,128)}, f32[1,16]{1,0:T(1,128)}, f32[8,16]{1,0:T(8,128)S(1)}, f32[8,16]{1,0:T(8,128)S(1)}, /*index=5*/f32[16,16]{1,0:T(8,128)S(1)}) custom-call(bf16[16,6144]{1,0:T(8,128)(2,1)} %tokens_in.1, f32[8,16]{1,0:T(8,128)} %bitcast.18, f32[8,16]{1,0:T(8,128)} %bitcast.19, s32[2,16]{1,0:T(2,128)} %bitcast.20), custom_call_target="tpu_custom_call" | custom-call | flops 1048576 | bytes 262144 | tf_op jit(solution)/shard_map/pallas_call | solution.py:318
  6.3 0.1 collective-permute-start
  6.3 1.2 %collective-permute-done.4 = bf16[1,4,6144]{2,1,0:T(4,128)(2,1)S(1)} collective-permute-done((bf16[1,4,6144]{2,1,0:T(4,128)(2,1)}, bf16[1,4,6144]{2,1,0:T(4,128)(2,1)S(1)}, u32[]{:S(2)}, u32[]{:S(2)}) %collective-permute-start.4) | collective-permute-done | bytes 49184 | tf_op jit(solution)/shard_map/ppermute | solution.py:299
  7.5 0.9 %pad_maximum_fusion.5 = bf16[2,4,6144]{2,1,0:T(4,128)(2,1)S(1)} fusion(bf16[1,4,6144]{2,1,0:T(4,128)(2,1)S(1)} %collective-permute-done.4, bf16[1,4,6144]{2,1,0:T(4,128)(2,1)} %bitcast.17), kind=kLoop, calls=%fused_computation.6 | loop fusion | flops 49152 | bytes 196608 | tf_op jit(solution)/shard_map/concatenate | solution.py:304
  8.4 1.8 %collective-permute-start.5 = (bf16[2,4,6144]{2,1,0:T(4,128)(2,1)S(1)}, bf16[2,4,6144]{2,1,0:T(4,128)(2,1)S(1)}, u32[]{:S(2)}, u32[]{:S(2)}) collective-permute-start(bf16[2,4,6144]{2,1,0:T(4,128)(2,1)S(1)} %pad_maximum_fusion.5), channel_id=1, source_target_pairs={{0,2},{1,3},{2,0},{3,1},{4,6},{5,7},{6,4},{7,5},{8,10},{9,11},{10,... | collective-permute-start | bytes 294920 | tf_op jit(solution)/shard_map/ppermute | solution.py:299
  10.2 1.3 %collective-permute-done = bf16[1,4,6272]{2,1,0:T(4,128)(2,1)S(1)} collective-permute-done((bf16[1,4,6272]{2,1,0:T(4,128)(2,1)S(1)}, bf16[1,4,6272]{2,1,0:T(4,128)(2,1)S(1)}, u32[]{:S(2)}, u32[]{:S(2)}) %collective-permute-start) | collective-permute-done | bytes 50208 | tf_op jit(solution)/shard_map/ppermute | solution.py:299
  11.5 0.1 pad_maximum_fusion.4
  11.5 1.5 %collective-permute-start.1 = (bf16[2,4,6272]{2,1,0:T(4,128)(2,1)S(1)}, bf16[2,4,6272]{2,1,0:T(4,128)(2,1)S(1)}, u32[]{:S(2)}, u32[]{:S(2)}) collective-permute-start(bf16[2,4,6272]{2,1,0:T(4,128)(2,1)S(1)} %pad_maximum_fusion.4), channel_id=1, source_target_pairs={{0,4},{1,5},{2,6},{3,7},{4,0},{5,1},{6,2},{7,3},{8,12},{9,13},{10,... | collective-permute-start | bytes 301064 | tf_op jit(solution)/shard_map/ppermute | solution.py:299
  13.0 0.1 collective-permute-done.5
  13.1 0.1 pad_maximum_fusion.3
  13.2 2.6 %collective-permute-start.6 = (bf16[4,4,6144]{2,1,0:T(4,128)(2,1)S(1)}, bf16[4,4,6144]{2,1,0:T(4,128)(2,1)S(1)}, u32[]{:S(2)}, u32[]{:S(2)}) collective-permute-start(bf16[4,4,6144]{2,1,0:T(4,128)(2,1)S(1)} %pad_maximum_fusion.3), channel_id=1, source_target_pairs={{0,4},{1,5},{2,6},{3,7},{4,0},{5,1},{6,2},{7,3},{8,12},{9,13},{10,... | collective-permute-start | bytes 589832 | tf_op jit(solution)/shard_map/ppermute | solution.py:299
  15.8 1.3 %collective-permute-done.1 = bf16[2,4,6272]{2,1,0:T(4,128)(2,1)S(1)} collective-permute-done((bf16[2,4,6272]{2,1,0:T(4,128)(2,1)S(1)}, bf16[2,4,6272]{2,1,0:T(4,128)(2,1)S(1)}, u32[]{:S(2)}, u32[]{:S(2)}) %collective-permute-start.1) | collective-permute-done | bytes 100384 | tf_op jit(solution)/shard_map/ppermute | solution.py:299
  17.2 0.1 pad_maximum_fusion.2
  17.3 1.6 %collective-permute-start.2 = (bf16[4,4,6272]{2,1,0:T(4,128)(2,1)S(1)}, bf16[4,4,6272]{2,1,0:T(4,128)(2,1)S(1)}, u32[]{:S(2)}, u32[]{:S(2)}) collective-permute-start(bf16[4,4,6272]{2,1,0:T(4,128)(2,1)S(1)} %pad_maximum_fusion.2), channel_id=1, source_target_pairs={{0,2},{1,3},{2,0},{3,1},{4,6},{5,7},{6,4},{7,5},{8,10},{9,11},{10,... | collective-permute-start | bytes 602120 | tf_op jit(solution)/shard_map/ppermute | solution.py:299
  18.9 0.6 collective-permute-done.6
  19.5 0.3 pad_maximum_fusion.1
  19.7 0.1 copy.19
  19.9 0.1 reshape.31
  20.0 0.1 collective-permute-start.7
  20.1 3.0 %collective-permute-done.2 = bf16[4,4,6272]{2,1,0:T(4,128)(2,1)S(1)} collective-permute-done((bf16[4,4,6272]{2,1,0:T(4,128)(2,1)S(1)}, bf16[4,4,6272]{2,1,0:T(4,128)(2,1)S(1)}, u32[]{:S(2)}, u32[]{:S(2)}) %collective-permute-start.2) | collective-permute-done | bytes 200736 | tf_op jit(solution)/shard_map/ppermute | solution.py:299
  23.1 0.3 pad_maximum_fusion
  23.3 0.1 reshape.29
  23.5 0.1 collective-permute-start.3
  23.6 0.0 collective-permute-done.7
  23.6 3.5 %shard_map.136.back = f32[64,512]{1,0:T(8,128)S(1)} custom-call(bf16[64,6144]{1,0:T(8,128)(2,1)S(1)} %constant_dynamic-update-slice_fusion.2.y, bf16[512,6144]{1,0:T(8,128)(2,1)} %down_in.1), custom_call_target="tpu_custom_call" | custom-call | flops 1610612736 | bytes 6291456 | tf_op jit(solution)/shard_map/pallas_call | solution.py:351
  27.1 0.0 collective-permute-done.3
  27.2 9.2 %shard_map.137 = (bf16[32,6272]{1,0:T(8,128)(2,1)S(1)}, f32[32,6272]{1,0:T(8,128)S(1)}, bf16[64,512]{1,0:T(8,128)(2,1)S(1)}, bf16[64,1024]{1,0:T(8,128)(2,1)S(1)}) custom-call(bf16[64,6272]{1,0:T(8,128)(2,1)S(1)} %constant_dynamic-update-slice_fusion.x, f32[64,512]{1,0:T(8,128)S(1)} %shard_map.136.back, bf16[6144,512]{1,0:T(8,128)(2,1)} %gate_in.1, ...), custom_call_target="tpu_custom_call" | custom-call | flops 6442450944 | bytes 12582912 | tf_op jit(solution)/shard_map/pallas_call | solution.py:366
  36.4 0.6 collective-permute-start.8
  37.0 1.4 %collective-permute-done.8.got = bf16[32,6272]{1,0:T(8,128)(2,1)S(1)} collective-permute-done((bf16[32,6272]{1,0:T(8,128)(2,1)S(1)}, bf16[32,6272]{1,0:T(8,128)(2,1)S(1)}, u32[]{:S(2)}, u32[]{:S(2)}) %collective-permute-start.8) | collective-permute-done | bytes 401440 | tf_op jit(solution)/shard_map/ppermute | solution.py:299
  38.3 0.2 shard_map.141
  38.5 1.6 %collective-permute-start.9 = (bf16[16,6272]{1,0:T(8,128)(2,1)S(1)}, bf16[16,6272]{1,0:T(8,128)(2,1)S(1)}, u32[]{:S(2)}, u32[]{:S(2)}) collective-permute-start(bf16[16,6272]{1,0:T(8,128)(2,1)S(1)} %get-tuple-element.39), channel_id=1, source_target_pairs={{0,2},{1,3},{2,0},{3,1},{4,6},{5,7},{6,4},{7,5},{8,10},{9,11},{10,... | collective-permute-start | bytes 602120 | tf_op jit(solution)/shard_map/ppermute | solution.py:299
  40.1 4.8 %shard_map.138 = (bf16[6144,512]{1,0:T(8,128)(2,1)}, bf16[6144,512]{1,0:T(8,128)(2,1)}) custom-call(bf16[64,6272]{1,0:T(8,128)(2,1)S(1)} %constant_dynamic-update-slice_fusion.x, bf16[64,1024]{1,0:T(8,128)(2,1)S(1)} %get-tuple-element.30.d_both), custom_call_target="tpu_custom_call" | custom-call | flops 1610612736 | bytes 6291456 | tf_op jit(solution)/shard_map/pallas_call | solution.py:270
  44.9 0.9 %collective-permute-done.9.got = bf16[16,6272]{1,0:T(8,128)(2,1)S(1)} collective-permute-done((bf16[16,6272]{1,0:T(8,128)(2,1)S(1)}, bf16[16,6272]{1,0:T(8,128)(2,1)S(1)}, u32[]{:S(2)}, u32[]{:S(2)}) %collective-permute-start.9) | collective-permute-done | bytes 200736 | tf_op jit(solution)/shard_map/ppermute | solution.py:299
  45.8 0.1 shard_map.142
  46.0 1.2 %collective-permute-start.10 = (bf16[8,6272]{1,0:T(8,128)(2,1)S(1)}, bf16[8,6272]{1,0:T(8,128)(2,1)S(1)}, u32[]{:S(2)}, u32[]{:S(2)}) collective-permute-start(bf16[8,6272]{1,0:T(8,128)(2,1)S(1)} %get-tuple-element.41), channel_id=1, source_target_pairs={{0,4},{1,5},{2,6},{3,7},{4,0},{5,1},{6,2},{7,3},{8,12},{9,13},{10,... | collective-permute-start | bytes 301064 | tf_op jit(solution)/shard_map/ppermute | solution.py:299
  47.1 4.3 %shard_map.140 = bf16[512,6144]{1,0:T(8,128)(2,1)} custom-call(bf16[64,512]{1,0:T(8,128)(2,1)S(1)} %get-tuple-element.35.weighted, bf16[64,6144]{1,0:T(8,128)(2,1)S(1)} %constant_dynamic-update-slice_fusion.2.y), custom_call_target="tpu_custom_call" | custom-call | flops 1610612736 | bytes 6291456 | tf_op jit(solution)/shard_map/pallas_call | solution.py:247
  51.5 0.0 collective-permute-done.10.got
  51.5 0.2 shard_map.143
  51.6 2.7 %collective-permute-start.11 = (bf16[4,6272]{1,0:T(4,128)(2,1)S(1)}, bf16[4,6272]{1,0:T(4,128)(2,1)S(1)}, u32[]{:S(2)}, u32[]{:S(2)}) collective-permute-start(bf16[4,6272]{1,0:T(4,128)(2,1)S(1)} %get-tuple-element.43), channel_id=1, source_target_pairs={{0,8},{1,9},{2,10},{3,11},{4,12},{5,13},{6,14},{7,15},{8,0},{9,1},... | collective-permute-start | bytes 150536 | tf_op jit(solution)/shard_map/ppermute | solution.py:299
  54.3 4.8 %shard_map.139 = (bf16[6144,512]{1,0:T(8,128)(2,1)}, bf16[6144,512]{1,0:T(8,128)(2,1)}) custom-call(bf16[64,6272]{1,0:T(8,128)(2,1)S(1)} %constant_dynamic-update-slice_fusion.x, bf16[64,1024]{1,0:T(8,128)(2,1)S(1)} %get-tuple-element.30.d_both, bf16[6144,512]{1,0:T(8,128)(2,1)} %get-tuple-element.31.refs_0_, ...), custom_call_target="tpu_custom_call", output_to_operand_aliasing={{0}: (2, {}), {1}: (3, {})} | custom-call | flops 1610612736 | bytes 6291456 | tf_op jit(solution)/shard_map/pallas_call | solution.py:270
  59.2 0.0 collective-permute-done.11.got
  59.2 0.9 %shard_map.144 = (bf16[16,6144]{1,0:T(8,128)(2,1)}, f32[8,16]{1,0:T(8,128)}) custom-call(f32[4,6272]{1,0:T(4,128)S(1)} %get-tuple-element.42.have, bf16[4,6272]{1,0:T(4,128)(2,1)S(1)} %collective-permute-done.11.got, f32[16,16]{1,0:T(8,128)S(1)} %get-tuple-element.44.select, f32[8,16]{1,0:T(8,128)S(1)} %get-tuple-element.45.base, ...), custom_call_target="tpu_custom_call" | custom-call | flops 1048576 | bytes 262144 | tf_op jit(solution)/shard_map/pallas_call | solution.py:25
  (4 shorter events, 0.1 us)
Async XLA Ops:
  0.6 6.9 %collective-permute-start.4 = (bf16[1,4,6144]{2,1,0:T(4,128)(2,1)}, bf16[1,4,6144]{2,1,0:T(4,128)(2,1)S(1)}, u32[]{:S(2)}, u32[]{:S(2)}) collective-permute-start(bf16[1,4,6144]{2,1,0:T(4,128)(2,1)} %bitcast.16), channel_id=1, source_target_pairs={{0,8},{1,9},{2,10},{3,11},{4,12},{5,13},{6,14},{7,15},{8,0},{9,1},... | collective-permute-start | bytes 147464 | tf_op jit(solution)/shard_map/ppermute | solution.py:299
  6.3 5.2 %collective-permute-start = (bf16[1,4,6272]{2,1,0:T(4,128)(2,1)S(1)}, bf16[1,4,6272]{2,1,0:T(4,128)(2,1)S(1)}, u32[]{:S(2)}, u32[]{:S(2)}) collective-permute-start(bf16[1,4,6272]{2,1,0:T(4,128)(2,1)S(1)} %bitcast.12), channel_id=1, source_target_pairs={{0,8},{1,9},{2,10},{3,11},{4,12},{5,13},{6,14},{7,15},{8,0},{9,1},... | collective-permute-start | bytes 150536 | tf_op jit(solution)/shard_map/ppermute | solution.py:299
  8.4 4.7 %collective-permute-start.5 = (bf16[2,4,6144]{2,1,0:T(4,128)(2,1)S(1)}, bf16[2,4,6144]{2,1,0:T(4,128)(2,1)S(1)}, u32[]{:S(2)}, u32[]{:S(2)}) collective-permute-start(bf16[2,4,6144]{2,1,0:T(4,128)(2,1)S(1)} %pad_maximum_fusion.5), channel_id=1, source_target_pairs={{0,2},{1,3},{2,0},{3,1},{4,6},{5,7},{6,4},{7,5},{8,10},{9,11},{10,... | collective-permute-start | bytes 294920 | tf_op jit(solution)/shard_map/ppermute | solution.py:299
  11.5 5.6 %collective-permute-start.1 = (bf16[2,4,6272]{2,1,0:T(4,128)(2,1)S(1)}, bf16[2,4,6272]{2,1,0:T(4,128)(2,1)S(1)}, u32[]{:S(2)}, u32[]{:S(2)}) collective-permute-start(bf16[2,4,6272]{2,1,0:T(4,128)(2,1)S(1)} %pad_maximum_fusion.4), channel_id=1, source_target_pairs={{0,4},{1,5},{2,6},{3,7},{4,0},{5,1},{6,2},{7,3},{8,12},{9,13},{10,... | collective-permute-start | bytes 301064 | tf_op jit(solution)/shard_map/ppermute | solution.py:299
  13.2 6.3 %collective-permute-start.6 = (bf16[4,4,6144]{2,1,0:T(4,128)(2,1)S(1)}, bf16[4,4,6144]{2,1,0:T(4,128)(2,1)S(1)}, u32[]{:S(2)}, u32[]{:S(2)}) collective-permute-start(bf16[4,4,6144]{2,1,0:T(4,128)(2,1)S(1)} %pad_maximum_fusion.3), channel_id=1, source_target_pairs={{0,4},{1,5},{2,6},{3,7},{4,0},{5,1},{6,2},{7,3},{8,12},{9,13},{10,... | collective-permute-start | bytes 589832 | tf_op jit(solution)/shard_map/ppermute | solution.py:299
  17.3 5.8 %collective-permute-start.2 = (bf16[4,4,6272]{2,1,0:T(4,128)(2,1)S(1)}, bf16[4,4,6272]{2,1,0:T(4,128)(2,1)S(1)}, u32[]{:S(2)}, u32[]{:S(2)}) collective-permute-start(bf16[4,4,6272]{2,1,0:T(4,128)(2,1)S(1)} %pad_maximum_fusion.2), channel_id=1, source_target_pairs={{0,2},{1,3},{2,0},{3,1},{4,6},{5,7},{6,4},{7,5},{8,10},{9,11},{10,... | collective-permute-start | bytes 602120 | tf_op jit(solution)/shard_map/ppermute | solution.py:299
  20.0 3.5 %collective-permute-start.7 = (bf16[32,6144]{1,0:T(8,128)(2,1)S(1)}, bf16[32,6144]{1,0:T(8,128)(2,1)S(1)}, u32[]{:S(2)}, u32[]{:S(2)}) collective-permute-start(bf16[32,6144]{1,0:T(8,128)(2,1)S(1)} %reshape.31), channel_id=1, source_target_pairs={{0,1},{1,0},{2,3},{3,2},{4,5},{5,4},{6,7},{7,6},{8,9},{9,8},{10,11... | collective-permute-start | bytes 1179656 | tf_op jit(solution)/shard_map/ppermute | solution.py:299
  23.5 3.6 %collective-permute-start.3 = (bf16[32,6272]{1,0:T(8,128)(2,1)S(1)}, bf16[32,6272]{1,0:T(8,128)(2,1)S(1)}, u32[]{:S(2)}, u32[]{:S(2)}) collective-permute-start(bf16[32,6272]{1,0:T(8,128)(2,1)S(1)} %reshape.29), channel_id=1, source_target_pairs={{0,1},{1,0},{2,3},{3,2},{4,5},{5,4},{6,7},{7,6},{8,9},{9,8},{10,11... | collective-permute-start | bytes 1204232 | tf_op jit(solution)/shard_map/ppermute | solution.py:299
  36.4 1.9 %collective-permute-start.8 = (bf16[32,6272]{1,0:T(8,128)(2,1)S(1)}, bf16[32,6272]{1,0:T(8,128)(2,1)S(1)}, u32[]{:S(2)}, u32[]{:S(2)}) collective-permute-start(bf16[32,6272]{1,0:T(8,128)(2,1)S(1)} %get-tuple-element.37), channel_id=1, source_target_pairs={{0,1},{1,0},{2,3},{3,2},{4,5},{5,4},{6,7},{7,6},{8,9},{9,8},{10,11... | collective-permute-start | bytes 1204232 | tf_op jit(solution)/shard_map/ppermute | solution.py:299
  38.5 7.3 %collective-permute-start.9 = (bf16[16,6272]{1,0:T(8,128)(2,1)S(1)}, bf16[16,6272]{1,0:T(8,128)(2,1)S(1)}, u32[]{:S(2)}, u32[]{:S(2)}) collective-permute-start(bf16[16,6272]{1,0:T(8,128)(2,1)S(1)} %get-tuple-element.39), channel_id=1, source_target_pairs={{0,2},{1,3},{2,0},{3,1},{4,6},{5,7},{6,4},{7,5},{8,10},{9,11},{10,... | collective-permute-start | bytes 602120 | tf_op jit(solution)/shard_map/ppermute | solution.py:299
  46.0 5.5 %collective-permute-start.10 = (bf16[8,6272]{1,0:T(8,128)(2,1)S(1)}, bf16[8,6272]{1,0:T(8,128)(2,1)S(1)}, u32[]{:S(2)}, u32[]{:S(2)}) collective-permute-start(bf16[8,6272]{1,0:T(8,128)(2,1)S(1)} %get-tuple-element.41), channel_id=1, source_target_pairs={{0,4},{1,5},{2,6},{3,7},{4,0},{5,1},{6,2},{7,3},{8,12},{9,13},{10,... | collective-permute-start | bytes 301064 | tf_op jit(solution)/shard_map/ppermute | solution.py:299
  51.6 7.5 %collective-permute-start.11 = (bf16[4,6272]{1,0:T(4,128)(2,1)S(1)}, bf16[4,6272]{1,0:T(4,128)(2,1)S(1)}, u32[]{:S(2)}, u32[]{:S(2)}) collective-permute-start(bf16[4,6272]{1,0:T(4,128)(2,1)S(1)} %get-tuple-element.43), channel_id=1, source_target_pairs={{0,8},{1,9},{2,10},{3,11},{4,12},{5,13},{6,14},{7,15},{8,0},{9,1},... | collective-permute-start | bytes 150536 | tf_op jit(solution)/shard_map/ppermute | solution.py:299

commit v5 on v4

--- a/solution.py
+++ b/solution.py
@@ -123,7 +123,7 @@
 
 
 def expert_kernel(
-    x, back, gate_in, up_in, send, keep, weighted, d_both, both_w, acc, sems
+    x, back, gate_in, up_in, send, keep, weighted, d_gate, d_up, both_w, d_both, acc, sems
 ):
     rows, width, hidden_dim = x.shape[0], both_w.shape[0], gate_in.shape[1]
     half = rows // 2
@@ -153,10 +153,10 @@
     weighted[...] = (g * hidden).astype(BF16)
     products = jnp.sum(hidden * back[...], axis=1, keepdims=True)
     scaled = g * back[...]
-    d_both[:, :hidden_dim] = (
-        scaled * pre_up * sig * (1.0 + pre_gate * (1.0 - sig))
-    ).astype(BF16)
-    d_both[:, hidden_dim:] = (scaled * act).astype(BF16)
+    d_gate[...] = (scaled * pre_up * sig * (1.0 + pre_gate * (1.0 - sig))).astype(BF16)
+    d_up[...] = (scaled * act).astype(BF16)
+    d_both[:, :hidden_dim] = d_gate[...]
+    d_both[:, hidden_dim:] = d_up[...]
     keep[:, width:] = lane_pair(half, products[:half], 0.0)
     send[:, width:] = split_pair(products[half:]).astype(BF16)
     wide = 1024
@@ -192,99 +192,43 @@
     grad_logits[...] = base[...] + coef[...] * token_products
 
 
-def down_kernel(weighted, y, out, buf, turned, sems):
-    chunks, _, step = buf.shape
-
-    def copy(i):
-        at = pl.ds(pl.multiple_of(i * step, step), step)
-        return pltpu.make_async_copy(buf.at[i], out.at[:, at], sems.at[i])
+def down_kernel(weighted, y, out, turned):
+    step = 512
+    turned[...] = weighted[...].astype(F32).T.astype(BF16)
 
     def body(i, carry):
         at = pl.ds(pl.multiple_of(i * step, step), step)
-        buf[i] = dot(turned[...], y[:, at], ((1,), (0,))).astype(BF16)
-        copy(i).start()
+        out[:, at] = dot(turned[...], y[:, at], ((1,), (0,))).astype(BF16)
         return carry
 
-    def finish(i, carry):
-        copy(i).wait()
+    lax.fori_loop(0, out.shape[1] // step, body, 0)
+
+
+def rows_kernel(x, d, out):
+    step = 512
+
+    def body(i, carry):
+        at = pl.ds(pl.multiple_of(i * step, step), step)
+        out[at, :] = dot(x[:, at], d[...], ((0,), (0,))).astype(BF16)
         return carry
 
-    turned[...] = weighted[...].astype(F32).T.astype(BF16)
-    lax.fori_loop(0, chunks, body, 0)
-    lax.fori_loop(0, chunks, finish, 0)
-
-
-def pair_kernel(first_row, x, d_both, *refs):
-    gate_out, up_out, gate_buf, up_buf, sems = refs[-5:]
-    chunks, step, cols = gate_buf.shape
-
-    def copy(k, i):
-        at = pl.ds(pl.multiple_of(first_row + i * step, step), step)
-        source, target = ((gate_buf, gate_out), (up_buf, up_out))[k]
-        return pltpu.make_async_copy(source.at[i], target.at[at], sems.at[k, i])
-
-    def body(i, carry):
-        at = pl.ds(pl.multiple_of(first_row + i * step, step), step)
-        both = dot(x[:, at], d_both[...], ((0,), (0,))).astype(BF16)
-        gate_buf[i] = both[:, :cols]
-        up_buf[i] = both[:, cols:]
-        copy(0, i).start()
-        copy(1, i).start()
-        return carry
-
-    def finish(i, carry):
-        copy(0, i).wait()
-        copy(1, i).wait()
-        return carry
-
-    lax.fori_loop(0, chunks, body, 0)
-    lax.fori_loop(0, chunks, finish, 0)
-
-
-def grad_down_of(weighted, y):
-    hidden, width = weighted.shape[1], y.shape[1]
-    step = 512
+    lax.fori_loop(0, out.shape[0] // step, body, 0)
+
+
+def grad_of(kernel, left, right, shape, scratch):
     return pl.pallas_call(
-        down_kernel,
-        out_shape=jax.ShapeDtypeStruct((hidden, width), BF16),
+        kernel,
+        out_shape=pltpu.VMEM(shape, BF16),
         in_specs=whole(2),
-        out_specs=pl.BlockSpec(memory_space=pl.ANY),
-        scratch_shapes=[
-            pltpu.VMEM((width // step, hidden, step), BF16),
-            pltpu.VMEM((hidden, weighted.shape[0]), BF16),
-            pltpu.SemaphoreType.DMA((width // step,)),
-        ],
-        compiler_params=pltpu.CompilerParams(vmem_limit_bytes=16 * MIB),
+        out_specs=pl.BlockSpec(memory_space=pltpu.VMEM),
+        scratch_shapes=scratch,
+        compiler_params=pltpu.CompilerParams(vmem_limit_bytes=8 * MIB),
         cost_estimate=pl.CostEstimate(
-            flops=8 * weighted.size * width, bytes_accessed=2 * hidden * width, transcendentals=0
-        ),
-    )(weighted, y)
-
-
-def grad_pair_of(x, d_both, width, part, parts, before):
-    cols = d_both.shape[1] // 2
-    step = 256
-    rows = width // parts
-    outs = [jax.ShapeDtypeStruct((width, cols), BF16)] * 2
-    anywhere = pl.BlockSpec(memory_space=pl.ANY)
-    return pl.pallas_call(
-        functools.partial(pair_kernel, part * rows),
-        out_shape=outs,
-        in_specs=whole(2) + [anywhere] * len(before),
-        out_specs=[anywhere] * 2,
-        scratch_shapes=[
-            pltpu.VMEM((rows // step, step, cols), BF16),
-            pltpu.VMEM((rows // step, step, cols), BF16),
-            pltpu.SemaphoreType.DMA((2, rows // step)),
-        ],
-        input_output_aliases={2 + i: i for i in range(len(before))},
-        compiler_params=pltpu.CompilerParams(vmem_limit_bytes=16 * MIB),
-        cost_estimate=pl.CostEstimate(
-            flops=8 * x.shape[0] * rows * 2 * cols,
-            bytes_accessed=4 * rows * cols,
+            flops=8 * left.shape[0] * shape[0] * shape[1],
+            bytes_accessed=2 * shape[0] * shape[1],
             transcendentals=0,
         ),
-    )(x, d_both, *before)
+    )(left, right)
 
 
 def make_shards(n):
@@ -363,18 +307,20 @@
             ),
         )(y_all, in_hbm(down_weight))
         half = rows // 2
-        low, keep, weighted, d_both = pl.pallas_call(
+        low, keep, weighted, d_gate, d_up = pl.pallas_call(
             expert_kernel,
             out_shape=[
                 jax.ShapeDtypeStruct((half, wide), BF16),
                 jax.ShapeDtypeStruct((half, wide), F32),
                 jax.ShapeDtypeStruct((rows, hidden), BF16),
-                jax.ShapeDtypeStruct((rows, 2 * hidden), BF16),
+                jax.ShapeDtypeStruct((rows, hidden), BF16),
+                jax.ShapeDtypeStruct((rows, hidden), BF16),
             ],
             in_specs=whole(2) + [anywhere] * 2,
-            out_specs=whole(4),
+            out_specs=whole(5),
             scratch_shapes=[
                 pltpu.VMEM((width, 2 * hidden), BF16),
+                pltpu.VMEM((rows, 2 * hidden), BF16),
                 pltpu.VMEM((rows, 2 * hidden), F32),
                 pltpu.SemaphoreType.DMA((2, 4)),
             ],
@@ -397,11 +343,11 @@
                 16 * half * wide,
             )
 
-        grad_down = grad_down_of(weighted, y_all)
-        grad_pair = ()
-        for part in range(2):
-            grad_pair = grad_pair_of(x_all, d_both, width, part, 2, grad_pair)
-        grad_gate, grad_up = grad_pair
+        grad_down = grad_of(
+            down_kernel, weighted, y_all, (hidden, width), [pltpu.VMEM((hidden, rows), BF16)]
+        )
+        grad_gate = grad_of(rows_kernel, x_all, d_gate, (width, hidden), [])
+        grad_up = grad_of(rows_kernel, x_all, d_up, (width, hidden), [])
 
         grad_tokens, grad_logits = call(
             home_kernel,

time: 60.3 us -> 66.9 us (1.11)
  local copies, waits for them, and re-layouts: 0.44 us -> 8.55 us
  Pallas kernels: 29.6 us -> 26.7 us
  waiting for transfers between devices: 9.7 us -> 11.1 us
    unnamed x2 -> x5, local copies, waits for them, and re-layouts: 0.06 us -> 8.17 us
    pallas_call x3, Pallas kernels: 13.9 us -> 11.1 us  [grad_of(): pl.pallas_call(kernel, out_shape=pltpu.VMEM(shape, BF16), in_specs=whole(...]
    ppermute x12, waiting for transfers between devices: 9.7 us -> 11.1 us  [swap(): return lax.ppermute(block, 'blk', [(i, i ^ bit) for i in range(n)])]
  transfers between devices with their start and end apart: 12 -> 12, of which waited for: 8 -> 8; matrix products, arithmetic and copies ran while one was open for 4% -> 15% of each run, Pallas kernels for 32% -> 24%
where the time goes in v5:
time: 66.9 us; the launch traced here: 66.7 us
  Pallas kernels  26.7 us (40%)
  starting transfers between devices  17.9 us (27%)
  waiting for transfers between devices  11.1 us (17%)
  local copies, waits for them, and re-layouts  8.55 us (13%)
  other arithmetic  1.73 us (3%)
  between operations  0.8 us (1%)
    ppermute x12, starting transfers between devices, swap(): return lax.ppermute(block, 'blk', [(i, i ^ bit) for i in range(n)])  17.9 us
    ppermute x12, waiting for transfers between devices, swap(): return lax.ppermute(block, 'blk', [(i, i ^ bit) for i in range(n)])  11.1 us
    pallas_call x3, Pallas kernels, grad_of(): pl.pallas_call(kernel, out_shape=pltpu.VMEM(shape, BF16), in_specs=whole(...  11.1 us
    pallas_call x1, Pallas kernels, shards(): pl.pallas_call(expert_kernel, out_shape=[jax.ShapeDtypeStruct((half, wide...  9.22 us
    unnamed x5, local copies, waits for them, and re-layouts  8.17 us
    pallas_call x1, Pallas kernels, shards(): pl.pallas_call(back_kernel, out_shape=jax.ShapeDtypeStruct((rows, hidden)...  3.5 us
    concatenate x6, other arithmetic, grow(): block = lax.optimization_barrier(jnp.concatenate([block, swap(block, bit)]))  1.73 us
    pallas_call x1, Pallas kernels, shards(): pl.pallas_call(router_kernel, out_shape=[jax.ShapeDtypeStruct((slots, wid...  1.52 us
  transfers between devices with their start and end apart: 12, of which 8 were waited for; matrix products, arithmetic and copies ran while one was open for 15% of the time, Pallas kernels for 24%

profile of v5, /device:TPU:0, one launch (start us, length us, event | category | flops | bytes accessed | tf_op | source)
XLA Modules:
  0.0 66.7 jit_solution(5402804747252762376)
XLA Ops:
  0.6 4.1 %collective-permute-start.4 = (bf16[1,4,6144]{2,1,0:T(4,128)(2,1)}, bf16[1,4,6144]{2,1,0:T(4,128)(2,1)S(1)}, u32[]{:S(2)}, u32[]{:S(2)}) collective-permute-start(bf16[1,4,6144]{2,1,0:T(4,128)(2,1)} %bitcast.16), channel_id=1, source_target_pairs={{0,8},{1,9},{2,10},{3,11},{4,12},{5,13},{6,14},{7,15},{8,0},{9,1},... | collective-permute-start | bytes 147464 | tf_op jit(solution)/shard_map/ppermute | solution.py:243
  4.7 1.5 %shard_map.135 = (bf16[4,6272]{1,0:T(4,128)(2,1)S(1)}, f32[1,16]{1,0:T(1,128)}, f32[1,16]{1,0:T(1,128)}, f32[8,16]{1,0:T(8,128)S(1)}, f32[8,16]{1,0:T(8,128)S(1)}, /*index=5*/f32[16,16]{1,0:T(8,128)S(1)}) custom-call(bf16[16,6144]{1,0:T(8,128)(2,1)} %tokens_in.1, f32[8,16]{1,0:T(8,128)} %bitcast.18, f32[8,16]{1,0:T(8,128)} %bitcast.19, s32[2,16]{1,0:T(2,128)} %bitcast.20), custom_call_target="tpu_custom_call" | custom-call | flops 1048576 | bytes 262144 | tf_op jit(solution)/shard_map/pallas_call | solution.py:262
  6.3 0.1 collective-permute-start
  6.3 1.2 %collective-permute-done.4 = bf16[1,4,6144]{2,1,0:T(4,128)(2,1)S(1)} collective-permute-done((bf16[1,4,6144]{2,1,0:T(4,128)(2,1)}, bf16[1,4,6144]{2,1,0:T(4,128)(2,1)S(1)}, u32[]{:S(2)}, u32[]{:S(2)}) %collective-permute-start.4) | collective-permute-done | bytes 49184 | tf_op jit(solution)/shard_map/ppermute | solution.py:243
  7.5 0.9 %pad_maximum_fusion.5 = bf16[2,4,6144]{2,1,0:T(4,128)(2,1)S(1)} fusion(bf16[1,4,6144]{2,1,0:T(4,128)(2,1)S(1)} %collective-permute-done.4, bf16[1,4,6144]{2,1,0:T(4,128)(2,1)} %bitcast.17), kind=kLoop, calls=%fused_computation.6 | loop fusion | flops 49152 | bytes 196608 | tf_op jit(solution)/shard_map/concatenate | solution.py:248
  8.4 1.8 %collective-permute-start.5 = (bf16[2,4,6144]{2,1,0:T(4,128)(2,1)S(1)}, bf16[2,4,6144]{2,1,0:T(4,128)(2,1)S(1)}, u32[]{:S(2)}, u32[]{:S(2)}) collective-permute-start(bf16[2,4,6144]{2,1,0:T(4,128)(2,1)S(1)} %pad_maximum_fusion.5), channel_id=1, source_target_pairs={{0,2},{1,3},{2,0},{3,1},{4,6},{5,7},{6,4},{7,5},{8,10},{9,11},{10,... | collective-permute-start | bytes 294920 | tf_op jit(solution)/shard_map/ppermute | solution.py:243
  10.2 1.3 %collective-permute-done = bf16[1,4,6272]{2,1,0:T(4,128)(2,1)S(1)} collective-permute-done((bf16[1,4,6272]{2,1,0:T(4,128)(2,1)S(1)}, bf16[1,4,6272]{2,1,0:T(4,128)(2,1)S(1)}, u32[]{:S(2)}, u32[]{:S(2)}) %collective-permute-start) | collective-permute-done | bytes 50208 | tf_op jit(solution)/shard_map/ppermute | solution.py:243
  11.5 0.1 pad_maximum_fusion.4
  11.5 1.5 %collective-permute-start.1 = (bf16[2,4,6272]{2,1,0:T(4,128)(2,1)S(1)}, bf16[2,4,6272]{2,1,0:T(4,128)(2,1)S(1)}, u32[]{:S(2)}, u32[]{:S(2)}) collective-permute-start(bf16[2,4,6272]{2,1,0:T(4,128)(2,1)S(1)} %pad_maximum_fusion.4), channel_id=1, source_target_pairs={{0,4},{1,5},{2,6},{3,7},{4,0},{5,1},{6,2},{7,3},{8,12},{9,13},{10,... | collective-permute-start | bytes 301064 | tf_op jit(solution)/shard_map/ppermute | solution.py:243
  13.0 0.1 collective-permute-done.5
  13.1 0.1 pad_maximum_fusion.3
  13.2 2.6 %collective-permute-start.6 = (bf16[4,4,6144]{2,1,0:T(4,128)(2,1)S(1)}, bf16[4,4,6144]{2,1,0:T(4,128)(2,1)S(1)}, u32[]{:S(2)}, u32[]{:S(2)}) collective-permute-start(bf16[4,4,6144]{2,1,0:T(4,128)(2,1)S(1)} %pad_maximum_fusion.3), channel_id=1, source_target_pairs={{0,4},{1,5},{2,6},{3,7},{4,0},{5,1},{6,2},{7,3},{8,12},{9,13},{10,... | collective-permute-start | bytes 589832 | tf_op jit(solution)/shard_map/ppermute | solution.py:243
  15.8 1.3 %collective-permute-done.1 = bf16[2,4,6272]{2,1,0:T(4,128)(2,1)S(1)} collective-permute-done((bf16[2,4,6272]{2,1,0:T(4,128)(2,1)S(1)}, bf16[2,4,6272]{2,1,0:T(4,128)(2,1)S(1)}, u32[]{:S(2)}, u32[]{:S(2)}) %collective-permute-start.1) | collective-permute-done | bytes 100384 | tf_op jit(solution)/shard_map/ppermute | solution.py:243
  17.2 0.1 pad_maximum_fusion.2
  17.3 1.6 %collective-permute-start.2 = (bf16[4,4,6272]{2,1,0:T(4,128)(2,1)S(1)}, bf16[4,4,6272]{2,1,0:T(4,128)(2,1)S(1)}, u32[]{:S(2)}, u32[]{:S(2)}) collective-permute-start(bf16[4,4,6272]{2,1,0:T(4,128)(2,1)S(1)} %pad_maximum_fusion.2), channel_id=1, source_target_pairs={{0,2},{1,3},{2,0},{3,1},{4,6},{5,7},{6,4},{7,5},{8,10},{9,11},{10,... | collective-permute-start | bytes 602120 | tf_op jit(solution)/shard_map/ppermute | solution.py:243
  18.9 0.6 collective-permute-done.6
  19.5 0.3 pad_maximum_fusion.1
  19.7 0.1 copy.17
  19.9 0.1 reshape.31
  20.0 0.1 collective-permute-start.7
  20.1 3.0 %collective-permute-done.2 = bf16[4,4,6272]{2,1,0:T(4,128)(2,1)S(1)} collective-permute-done((bf16[4,4,6272]{2,1,0:T(4,128)(2,1)S(1)}, bf16[4,4,6272]{2,1,0:T(4,128)(2,1)S(1)}, u32[]{:S(2)}, u32[]{:S(2)}) %collective-permute-start.2) | collective-permute-done | bytes 200736 | tf_op jit(solution)/shard_map/ppermute | solution.py:243
  23.1 0.3 pad_maximum_fusion
  23.3 0.1 reshape.29
  23.4 0.1 collective-permute-start.3
  23.6 0.0 collective-permute-done.7
  23.6 3.5 %shard_map.136.back = f32[64,512]{1,0:T(8,128)S(1)} custom-call(bf16[64,6144]{1,0:T(8,128)(2,1)S(1)} %constant_dynamic-update-slice_fusion.2.y, bf16[512,6144]{1,0:T(8,128)(2,1)} %down_in.1), custom_call_target="tpu_custom_call" | custom-call | flops 1610612736 | bytes 6291456 | tf_op jit(solution)/shard_map/pallas_call | solution.py:295
  27.1 0.0 collective-permute-done.3
  27.2 9.2 %shard_map.137 = (bf16[32,6272]{1,0:T(8,128)(2,1)S(1)}, f32[32,6272]{1,0:T(8,128)S(1)}, bf16[64,512]{1,0:T(8,128)(2,1)S(1)}, bf16[64,512]{1,0:T(8,128)(2,1)S(1)}, bf16[64,512]{1,0:T(8,128)(2,1)S(1)}) custom-call(bf16[64,6272]{1,0:T(8,128)(2,1)S(1)} %constant_dynamic-update-slice_fusion.x, f32[64,512]{1,0:T(8,128)S(1)} %shard_map.136.back, ...), custom_call_target="tpu_custom_call" | custom-call | flops 6442450944 | bytes 12582912 | tf_op jit(solution)/shard_map/pallas_call | solution.py:310
  36.4 0.6 collective-permute-start.8
  36.9 1.4 %collective-permute-done.8.got = bf16[32,6272]{1,0:T(8,128)(2,1)S(1)} collective-permute-done((bf16[32,6272]{1,0:T(8,128)(2,1)S(1)}, bf16[32,6272]{1,0:T(8,128)(2,1)S(1)}, u32[]{:S(2)}, u32[]{:S(2)}) %collective-permute-start.8) | collective-permute-done | bytes 401440 | tf_op jit(solution)/shard_map/ppermute | solution.py:243
  38.3 0.2 shard_map.141
  38.5 1.6 %collective-permute-start.9 = (bf16[16,6272]{1,0:T(8,128)(2,1)S(1)}, bf16[16,6272]{1,0:T(8,128)(2,1)S(1)}, u32[]{:S(2)}, u32[]{:S(2)}) collective-permute-start(bf16[16,6272]{1,0:T(8,128)(2,1)S(1)} %get-tuple-element.33), channel_id=1, source_target_pairs={{0,2},{1,3},{2,0},{3,1},{4,6},{5,7},{6,4},{7,5},{8,10},{9,11},{10,... | collective-permute-start | bytes 602120 | tf_op jit(solution)/shard_map/ppermute | solution.py:243
  40.1 3.4 %shard_map.140 = bf16[512,6144]{1,0:T(8,128)(2,1)S(1)} custom-call(bf16[64,512]{1,0:T(8,128)(2,1)S(1)} %get-tuple-element.29.weighted, bf16[64,6144]{1,0:T(8,128)(2,1)S(1)} %constant_dynamic-update-slice_fusion.2.y), custom_call_target="tpu_custom_call" | custom-call | flops 1610612736 | bytes 6291456 | tf_op jit(solution)/shard_map/pallas_call | solution.py:219
  43.5 2.3 %collective-permute-done.9.got = bf16[16,6272]{1,0:T(8,128)(2,1)S(1)} collective-permute-done((bf16[16,6272]{1,0:T(8,128)(2,1)S(1)}, bf16[16,6272]{1,0:T(8,128)(2,1)S(1)}, u32[]{:S(2)}, u32[]{:S(2)}) %collective-permute-start.9) | collective-permute-done | bytes 200736 | tf_op jit(solution)/shard_map/ppermute | solution.py:243
  45.8 0.1 shard_map.142
  46.0 1.2 %collective-permute-start.10 = (bf16[8,6272]{1,0:T(8,128)(2,1)S(1)}, bf16[8,6272]{1,0:T(8,128)(2,1)S(1)}, u32[]{:S(2)}, u32[]{:S(2)}) collective-permute-start(bf16[8,6272]{1,0:T(8,128)(2,1)S(1)} %get-tuple-element.35), channel_id=1, source_target_pairs={{0,4},{1,5},{2,6},{3,7},{4,0},{5,1},{6,2},{7,3},{8,12},{9,13},{10,... | collective-permute-start | bytes 301064 | tf_op jit(solution)/shard_map/ppermute | solution.py:243
  47.1 3.8 %shard_map.138 = bf16[6144,512]{1,0:T(8,128)(2,1)S(1)} custom-call(bf16[64,6272]{1,0:T(8,128)(2,1)S(1)} %constant_dynamic-update-slice_fusion.x, bf16[64,512]{1,0:T(8,128)(2,1)S(1)} %get-tuple-element.27.d), custom_call_target="tpu_custom_call" | custom-call | flops 1610612736 | bytes 6291456 | tf_op jit(solution)/shard_map/pallas_call | solution.py:219
  51.0 0.0 collective-permute-done.10.got
  51.0 0.2 shard_map.143
  51.1 2.7 %collective-permute-start.11 = (bf16[4,6272]{1,0:T(4,128)(2,1)S(1)}, bf16[4,6272]{1,0:T(4,128)(2,1)S(1)}, u32[]{:S(2)}, u32[]{:S(2)}) collective-permute-start(bf16[4,6272]{1,0:T(4,128)(2,1)S(1)} %get-tuple-element.37), channel_id=1, source_target_pairs={{0,8},{1,9},{2,10},{3,11},{4,12},{5,13},{6,14},{7,15},{8,0},{9,1},... | collective-permute-start | bytes 150536 | tf_op jit(solution)/shard_map/ppermute | solution.py:243
  53.8 3.8 %shard_map.139 = bf16[6144,512]{1,0:T(8,128)(2,1)S(1)} custom-call(bf16[64,6272]{1,0:T(8,128)(2,1)S(1)} %constant_dynamic-update-slice_fusion.x, bf16[64,512]{1,0:T(8,128)(2,1)S(1)} %get-tuple-element.28.d), custom_call_target="tpu_custom_call" | custom-call | flops 1610612736 | bytes 6291456 | tf_op jit(solution)/shard_map/pallas_call | solution.py:219
  57.7 2.7 %copy.22 = bf16[512,6144]{1,0:T(8,128)(2,1)} copy(bf16[512,6144]{1,0:T(8,128)(2,1)S(1)} %shard_map.140) | data formatting | bytes 12582912
  60.4 2.7 %copy.20 = bf16[6144,512]{1,0:T(8,128)(2,1)} copy(bf16[6144,512]{1,0:T(8,128)(2,1)S(1)} %shard_map.138) | data formatting | bytes 12582912
  63.1 2.7 %copy.21 = bf16[6144,512]{1,0:T(8,128)(2,1)} copy(bf16[6144,512]{1,0:T(8,128)(2,1)S(1)} %shard_map.139) | data formatting | bytes 12582912
  65.8 0.0 collective-permute-done.11.got
  65.8 0.9 %shard_map.144 = (bf16[16,6144]{1,0:T(8,128)(2,1)}, f32[8,16]{1,0:T(8,128)}) custom-call(f32[4,6272]{1,0:T(4,128)S(1)} %get-tuple-element.36.have, bf16[4,6272]{1,0:T(4,128)(2,1)S(1)} %collective-permute-done.11.got, f32[16,16]{1,0:T(8,128)S(1)} %get-tuple-element.38.select, f32[8,16]{1,0:T(8,128)S(1)} %get-tuple-element.39.base, ...), custom_call_target="tpu_custom_call" | custom-call | flops 1048576 | bytes 262144 | tf_op jit(solution)/shard_map/pallas_call | solution.py:25
  (4 shorter events, 0.1 us)
Async XLA Ops:
  0.6 6.9 %collective-permute-start.4 = (bf16[1,4,6144]{2,1,0:T(4,128)(2,1)}, bf16[1,4,6144]{2,1,0:T(4,128)(2,1)S(1)}, u32[]{:S(2)}, u32[]{:S(2)}) collective-permute-start(bf16[1,4,6144]{2,1,0:T(4,128)(2,1)} %bitcast.16), channel_id=1, source_target_pairs={{0,8},{1,9},{2,10},{3,11},{4,12},{5,13},{6,14},{7,15},{8,0},{9,1},... | collective-permute-start | bytes 147464 | tf_op jit(solution)/shard_map/ppermute | solution.py:243
  6.3 5.2 %collective-permute-start = (bf16[1,4,6272]{2,1,0:T(4,128)(2,1)S(1)}, bf16[1,4,6272]{2,1,0:T(4,128)(2,1)S(1)}, u32[]{:S(2)}, u32[]{:S(2)}) collective-permute-start(bf16[1,4,6272]{2,1,0:T(4,128)(2,1)S(1)} %bitcast.12), channel_id=1, source_target_pairs={{0,8},{1,9},{2,10},{3,11},{4,12},{5,13},{6,14},{7,15},{8,0},{9,1},... | collective-permute-start | bytes 150536 | tf_op jit(solution)/shard_map/ppermute | solution.py:243
  8.4 4.7 %collective-permute-start.5 = (bf16[2,4,6144]{2,1,0:T(4,128)(2,1)S(1)}, bf16[2,4,6144]{2,1,0:T(4,128)(2,1)S(1)}, u32[]{:S(2)}, u32[]{:S(2)}) collective-permute-start(bf16[2,4,6144]{2,1,0:T(4,128)(2,1)S(1)} %pad_maximum_fusion.5), channel_id=1, source_target_pairs={{0,2},{1,3},{2,0},{3,1},{4,6},{5,7},{6,4},{7,5},{8,10},{9,11},{10,... | collective-permute-start | bytes 294920 | tf_op jit(solution)/shard_map/ppermute | solution.py:243
  11.5 5.6 %collective-permute-start.1 = (bf16[2,4,6272]{2,1,0:T(4,128)(2,1)S(1)}, bf16[2,4,6272]{2,1,0:T(4,128)(2,1)S(1)}, u32[]{:S(2)}, u32[]{:S(2)}) collective-permute-start(bf16[2,4,6272]{2,1,0:T(4,128)(2,1)S(1)} %pad_maximum_fusion.4), channel_id=1, source_target_pairs={{0,4},{1,5},{2,6},{3,7},{4,0},{5,1},{6,2},{7,3},{8,12},{9,13},{10,... | collective-permute-start | bytes 301064 | tf_op jit(solution)/shard_map/ppermute | solution.py:243
  13.2 6.3 %collective-permute-start.6 = (bf16[4,4,6144]{2,1,0:T(4,128)(2,1)S(1)}, bf16[4,4,6144]{2,1,0:T(4,128)(2,1)S(1)}, u32[]{:S(2)}, u32[]{:S(2)}) collective-permute-start(bf16[4,4,6144]{2,1,0:T(4,128)(2,1)S(1)} %pad_maximum_fusion.3), channel_id=1, source_target_pairs={{0,4},{1,5},{2,6},{3,7},{4,0},{5,1},{6,2},{7,3},{8,12},{9,13},{10,... | collective-permute-start | bytes 589832 | tf_op jit(solution)/shard_map/ppermute | solution.py:243
  17.3 5.8 %collective-permute-start.2 = (bf16[4,4,6272]{2,1,0:T(4,128)(2,1)S(1)}, bf16[4,4,6272]{2,1,0:T(4,128)(2,1)S(1)}, u32[]{:S(2)}, u32[]{:S(2)}) collective-permute-start(bf16[4,4,6272]{2,1,0:T(4,128)(2,1)S(1)} %pad_maximum_fusion.2), channel_id=1, source_target_pairs={{0,2},{1,3},{2,0},{3,1},{4,6},{5,7},{6,4},{7,5},{8,10},{9,11},{10,... | collective-permute-start | bytes 602120 | tf_op jit(solution)/shard_map/ppermute | solution.py:243
  20.0 3.6 %collective-permute-start.7 = (bf16[32,6144]{1,0:T(8,128)(2,1)S(1)}, bf16[32,6144]{1,0:T(8,128)(2,1)S(1)}, u32[]{:S(2)}, u32[]{:S(2)}) collective-permute-start(bf16[32,6144]{1,0:T(8,128)(2,1)S(1)} %reshape.31), channel_id=1, source_target_pairs={{0,1},{1,0},{2,3},{3,2},{4,5},{5,4},{6,7},{7,6},{8,9},{9,8},{10,11... | collective-permute-start | bytes 1179656 | tf_op jit(solution)/shard_map/ppermute | solution.py:243
  23.4 3.7 %collective-permute-start.3 = (bf16[32,6272]{1,0:T(8,128)(2,1)S(1)}, bf16[32,6272]{1,0:T(8,128)(2,1)S(1)}, u32[]{:S(2)}, u32[]{:S(2)}) collective-permute-start(bf16[32,6272]{1,0:T(8,128)(2,1)S(1)} %reshape.29), channel_id=1, source_target_pairs={{0,1},{1,0},{2,3},{3,2},{4,5},{5,4},{6,7},{7,6},{8,9},{9,8},{10,11... | collective-permute-start | bytes 1204232 | tf_op jit(solution)/shard_map/ppermute | solution.py:243
  36.4 1.9 %collective-permute-start.8 = (bf16[32,6272]{1,0:T(8,128)(2,1)S(1)}, bf16[32,6272]{1,0:T(8,128)(2,1)S(1)}, u32[]{:S(2)}, u32[]{:S(2)}) collective-permute-start(bf16[32,6272]{1,0:T(8,128)(2,1)S(1)} %get-tuple-element.31), channel_id=1, source_target_pairs={{0,1},{1,0},{2,3},{3,2},{4,5},{5,4},{6,7},{7,6},{8,9},{9,8},{10,11... | collective-permute-start | bytes 1204232 | tf_op jit(solution)/shard_map/ppermute | solution.py:243
  38.5 7.3 %collective-permute-start.9 = (bf16[16,6272]{1,0:T(8,128)(2,1)S(1)}, bf16[16,6272]{1,0:T(8,128)(2,1)S(1)}, u32[]{:S(2)}, u32[]{:S(2)}) collective-permute-start(bf16[16,6272]{1,0:T(8,128)(2,1)S(1)} %get-tuple-element.33), channel_id=1, source_target_pairs={{0,2},{1,3},{2,0},{3,1},{4,6},{5,7},{6,4},{7,5},{8,10},{9,11},{10,... | collective-permute-start | bytes 602120 | tf_op jit(solution)/shard_map/ppermute | solution.py:243
  46.0 5.0 %collective-permute-start.10 = (bf16[8,6272]{1,0:T(8,128)(2,1)S(1)}, bf16[8,6272]{1,0:T(8,128)(2,1)S(1)}, u32[]{:S(2)}, u32[]{:S(2)}) collective-permute-start(bf16[8,6272]{1,0:T(8,128)(2,1)S(1)} %get-tuple-element.35), channel_id=1, source_target_pairs={{0,4},{1,5},{2,6},{3,7},{4,0},{5,1},{6,2},{7,3},{8,12},{9,13},{10,... | collective-permute-start | bytes 301064 | tf_op jit(solution)/shard_map/ppermute | solution.py:243
  51.1 14.7 %collective-permute-start.11 = (bf16[4,6272]{1,0:T(4,128)(2,1)S(1)}, bf16[4,6272]{1,0:T(4,128)(2,1)S(1)}, u32[]{:S(2)}, u32[]{:S(2)}) collective-permute-start(bf16[4,6272]{1,0:T(4,128)(2,1)S(1)} %get-tuple-element.37), channel_id=1, source_target_pairs={{0,8},{1,9},{2,10},{3,11},{4,12},{5,13},{6,14},{7,15},{8,0},{9,1},... | collective-permute-start | bytes 150536 | tf_op jit(solution)/shard_map/ppermute | solution.py:243

commit v6 on v4

--- a/solution.py
+++ b/solution.py
@@ -123,7 +123,7 @@
 
 
 def expert_kernel(
-    x, back, gate_in, up_in, send, keep, weighted, d_both, both_w, acc, sems
+    x, back, gate_in, up_in, send, keep, weighted_t, d_both, x_t, both_w, acc, sems
 ):
     rows, width, hidden_dim = x.shape[0], both_w.shape[0], gate_in.shape[1]
     half = rows // 2
@@ -139,6 +139,8 @@
     for i in range(chunks):
         copy(0, i).start()
         copy(1, i).start()
+    for c in range(0, width, LANES):
+        x_t[c : c + LANES, :] = x[:, c : c + LANES].astype(F32).T.astype(BF16)
     for i in range(chunks):
         at = pl.ds(i * step, step)
         copy(0, i).wait()
@@ -150,7 +152,7 @@
     sig = jax.nn.sigmoid(pre_gate)
     act = pre_gate * sig
     hidden = act * pre_up
-    weighted[...] = (g * hidden).astype(BF16)
+    weighted_t[...] = (g * hidden).T.astype(BF16)
     products = jnp.sum(hidden * back[...], axis=1, keepdims=True)
     scaled = g * back[...]
     d_both[:, :hidden_dim] = (
@@ -192,7 +194,14 @@
     grad_logits[...] = base[...] + coef[...] * token_products
 
 
-def down_kernel(weighted, y, out, buf, turned, sems):
+def tiles(out, left, right):
+    for c in range(0, right.shape[1], 256):
+        for r in range(0, left.shape[0], 128):
+            part = dot(left[r : r + 128], right[:, c : c + 256], ((1,), (0,)))
+            out[r : r + 128, c : c + 256] = part.astype(BF16)
+
+
+def down_kernel(weighted_t, y, out, buf, sems):
     chunks, _, step = buf.shape
 
     def copy(i):
@@ -201,7 +210,7 @@
 
     def body(i, carry):
         at = pl.ds(pl.multiple_of(i * step, step), step)
-        buf[i] = dot(turned[...], y[:, at], ((1,), (0,))).astype(BF16)
+        tiles(buf.at[i], weighted_t, y.at[:, at])
         copy(i).start()
         return carry
 
@@ -209,12 +218,11 @@
         copy(i).wait()
         return carry
 
-    turned[...] = weighted[...].astype(F32).T.astype(BF16)
     lax.fori_loop(0, chunks, body, 0)
     lax.fori_loop(0, chunks, finish, 0)
 
 
-def pair_kernel(first_row, x, d_both, *refs):
+def pair_kernel(first_row, x_t, d_both, *refs):
     gate_out, up_out, gate_buf, up_buf, sems = refs[-5:]
     chunks, step, cols = gate_buf.shape
 
@@ -225,10 +233,9 @@
 
     def body(i, carry):
         at = pl.ds(pl.multiple_of(first_row + i * step, step), step)
-        both = dot(x[:, at], d_both[...], ((0,), (0,))).astype(BF16)
-        gate_buf[i] = both[:, :cols]
-        up_buf[i] = both[:, cols:]
+        tiles(gate_buf.at[i], x_t.at[at], d_both.at[:, pl.ds(0, cols)])
         copy(0, i).start()
+        tiles(up_buf.at[i], x_t.at[at], d_both.at[:, pl.ds(cols, cols)])
         copy(1, i).start()
         return carry
 
@@ -241,9 +248,9 @@
     lax.fori_loop(0, chunks, finish, 0)
 
 
-def grad_down_of(weighted, y):
-    hidden, width = weighted.shape[1], y.shape[1]
-    step = 512
+def grad_down_of(weighted_t, y):
+    hidden, width = weighted_t.shape[0], y.shape[1]
+    step = 1024
     return pl.pallas_call(
         down_kernel,
         out_shape=jax.ShapeDtypeStruct((hidden, width), BF16),
@@ -251,19 +258,20 @@
         out_specs=pl.BlockSpec(memory_space=pl.ANY),
         scratch_shapes=[
             pltpu.VMEM((width // step, hidden, step), BF16),
-            pltpu.VMEM((hidden, weighted.shape[0]), BF16),
             pltpu.SemaphoreType.DMA((width // step,)),
         ],
         compiler_params=pltpu.CompilerParams(vmem_limit_bytes=16 * MIB),
         cost_estimate=pl.CostEstimate(
-            flops=8 * weighted.size * width, bytes_accessed=2 * hidden * width, transcendentals=0
+            flops=8 * weighted_t.size * width,
+            bytes_accessed=2 * hidden * width,
+            transcendentals=0,
         ),
-    )(weighted, y)
-
-
-def grad_pair_of(x, d_both, width, part, parts, before):
-    cols = d_both.shape[1] // 2
-    step = 256
+    )(weighted_t, y)
+
+
+def grad_pair_of(x_t, d_both, part, parts, before):
+    width, cols = x_t.shape[0], d_both.shape[1] // 2
+    step = 512
     rows = width // parts
     outs = [jax.ShapeDtypeStruct((width, cols), BF16)] * 2
     anywhere = pl.BlockSpec(memory_space=pl.ANY)
@@ -280,29 +288,31 @@
         input_output_aliases={2 + i: i for i in range(len(before))},
         compiler_params=pltpu.CompilerParams(vmem_limit_bytes=16 * MIB),
         cost_estimate=pl.CostEstimate(
-            flops=8 * x.shape[0] * rows * 2 * cols,
+            flops=8 * x_t.shape[1] * rows * 2 * cols,
             bytes_accessed=4 * rows * cols,
             transcendentals=0,
         ),
-    )(x, d_both, *before)
+    )(x_t, d_both, *before)
 
 
 def make_shards(n):
-    z_bits = []
+    levels = []
     bit = n // 2
-    while bit >= 4:
-        z_bits.append(bit)
+    while bit > 4:
+        levels.append((bit, bit))
         bit //= 2
-    nz = n // 4
-
-    def swap(block, bit):
-        return lax.ppermute(block, "blk", [(i, i ^ bit) for i in range(n)])
-
-    def grow(block, bits):
+    levels += [(4, 2), (2, 4)]
+
+    def swap(block, bits):
+        return lax.ppermute(block, "blk", [(i, i ^ bits[i % 2]) for i in range(n)])
+
+    def gather(block):
+        rows = n // 2 * block.shape[0]
         block = block[None]
-        for bit in bits:
-            block = lax.optimization_barrier(jnp.concatenate([block, swap(block, bit)]))
-        return block
+        for bits in levels:
+            block = lax.optimization_barrier(jnp.concatenate([block, swap(block, bits)]))
+        block = block.reshape(rows, block.shape[2])
+        return jnp.concatenate([block, swap(block, (1, 1))])
 
     def shards(
         tokens, cotangent, gate_weight, up_weight, down_weight, logits, ref_logits, routes
@@ -340,12 +350,8 @@
             ),
         )(in_hbm(tokens), in_hbm(logits.T), in_hbm(ref_logits.T), in_hbm(routes.T))
 
-        y_part = grow(cotangent, z_bits[:-1] + [2, z_bits[-1]])
-        y_part = y_part.reshape(2, 2, nz // 2, slots, width).transpose(1, 0, 2, 3, 4)
-        y_part = y_part.reshape(rows // 2, width)
-        y_all = jnp.concatenate([y_part, swap(y_part, 1)])
-        x_part = grow(send, z_bits + [2]).reshape(rows // 2, wide)
-        x_all = jnp.concatenate([x_part, swap(x_part, 1)])
+        y_all = gather(cotangent)
+        x_all = gather(send)
 
         work = 2 * rows * width * hidden
         back = pl.pallas_call(
@@ -363,16 +369,17 @@
             ),
         )(y_all, in_hbm(down_weight))
         half = rows // 2
-        low, keep, weighted, d_both = pl.pallas_call(
+        low, keep, weighted_t, d_both, x_t = pl.pallas_call(
             expert_kernel,
             out_shape=[
                 jax.ShapeDtypeStruct((half, wide), BF16),
                 jax.ShapeDtypeStruct((half, wide), F32),
-                jax.ShapeDtypeStruct((rows, hidden), BF16),
+                jax.ShapeDtypeStruct((hidden, rows), BF16),
                 jax.ShapeDtypeStruct((rows, 2 * hidden), BF16),
+                jax.ShapeDtypeStruct((width, rows), BF16),
             ],
             in_specs=whole(2) + [anywhere] * 2,
-            out_specs=whole(4),
+            out_specs=whole(5),
             scratch_shapes=[
                 pltpu.VMEM((width, 2 * hidden), BF16),
                 pltpu.VMEM((rows, 2 * hidden), F32),
@@ -384,9 +391,9 @@
             ),
         )(x_all, back, in_hbm(gate_weight), in_hbm(up_weight))
 
-        for bit in [1, 2] + z_bits[::-1]:
-            got = swap(low, bit)
-            if bit == z_bits[0]:
+        for bits in [(1, 1)] + levels[::-1]:
+            got = swap(low, bits)
+            if bits == levels[0]:
                 break
             half //= 2
             keep, low = call(
@@ -397,10 +404,10 @@
                 16 * half * wide,
             )
 
-        grad_down = grad_down_of(weighted, y_all)
+        grad_down = grad_down_of(weighted_t, y_all)
         grad_pair = ()
         for part in range(2):
-            grad_pair = grad_pair_of(x_all, d_both, width, part, 2, grad_pair)
+            grad_pair = grad_pair_of(x_t, d_both, part, 2, grad_pair)
         grad_gate, grad_up = grad_pair
 
         grad_tokens, grad_logits = call(

time: 60.3 us -> 57.6 us (0.955)
  Pallas kernels: 29.6 us -> 26 us
  waiting for transfers between devices: 9.7 us -> 11.6 us
  starting transfers between devices: 17.8 us -> 17.1 us
    pallas_call x2, Pallas kernels: 9.61 us -> 6.79 us  [grad_pair_of(): pl.pallas_call(functools.partial(pair_kernel, part * rows), out_shape=out...]
    ppermute x12, waiting for transfers between devices: 9.7 us -> 11.6 us  [swap(): return lax.ppermute(block, 'blk', [(i, i ^ bits[i % 2]) for i in range(n)])]
    pallas_call x1, Pallas kernels: 4.32 us -> 3.52 us  [grad_down_of(): pl.pallas_call(down_kernel, out_shape=jax.ShapeDtypeStruct((hidden, width...]
    ppermute x12, starting transfers between devices: 17.8 us -> 17.1 us  [swap(): return lax.ppermute(block, 'blk', [(i, i ^ bits[i % 2]) for i in range(n)])]
    concatenate x6 -> x7, other arithmetic: 1.73 us -> 1.79 us  [the longest x6 1.73 us: gather(): jnp.concatenate([block, swap(block, bits)])]
  transfers between devices with their start and end apart: 12 -> 12, of which waited for: 8 -> 8; matrix products, arithmetic and copies ran while one was open for 4% -> 3% of each run, Pallas kernels for 32% -> 27%
where the time goes in v6:
time: 57.6 us; the launch traced here: 57.4 us
  Pallas kernels  26 us (45%)
  starting transfers between devices  17.1 us (30%)
  waiting for transfers between devices  11.6 us (20%)
  other arithmetic  1.79 us (3%)
  between operations  0.79 us (1%)
    ppermute x12, starting transfers between devices, swap(): return lax.ppermute(block, 'blk', [(i, i ^ bits[i % 2]) for i in range(n)])  17.1 us
    ppermute x12, waiting for transfers between devices, swap(): return lax.ppermute(block, 'blk', [(i, i ^ bits[i % 2]) for i in range(n)])  11.6 us
    pallas_call x1, Pallas kernels, shards(): pl.pallas_call(expert_kernel, out_shape=[jax.ShapeDtypeStruct((half, wide...  9.24 us
    pallas_call x2, Pallas kernels, grad_pair_of(): pl.pallas_call(functools.partial(pair_kernel, part * rows), out_shape=out...  6.79 us
    pallas_call x1, Pallas kernels, grad_down_of(): pl.pallas_call(down_kernel, out_shape=jax.ShapeDtypeStruct((hidden, width...  3.52 us
    pallas_call x1, Pallas kernels, shards(): pl.pallas_call(back_kernel, out_shape=jax.ShapeDtypeStruct((rows, hidden)...  3.49 us
    concatenate x6, other arithmetic, gather(): jnp.concatenate([block, swap(block, bits)])  1.73 us
    pallas_call x1, Pallas kernels, shards(): pl.pallas_call(router_kernel, out_shape=[jax.ShapeDtypeStruct((slots, wid...  1.52 us
  transfers between devices with their start and end apart: 12, of which 8 were waited for; matrix products, arithmetic and copies ran while one was open for 3% of the time, Pallas kernels for 27%

profile of v6, /device:TPU:0, one launch (start us, length us, event | category | flops | bytes accessed | tf_op | source)
XLA Modules:
  0.0 57.4 jit_solution(2366488823452686190)
XLA Ops:
  0.6 4.1 %collective-permute-start.4 = (bf16[1,4,6144]{2,1,0:T(4,128)(2,1)}, bf16[1,4,6144]{2,1,0:T(4,128)(2,1)S(1)}, u32[]{:S(2)}, u32[]{:S(2)}) collective-permute-start(bf16[1,4,6144]{2,1,0:T(4,128)(2,1)} %bitcast.10), channel_id=1, source_target_pairs={{0,8},{1,9},{2,10},{3,11},{4,12},{5,13},{6,14},{7,15},{8,0},{9,1},... | collective-permute-start | bytes 147464 | tf_op jit(solution)/shard_map/ppermute | solution.py:307
  4.7 1.5 %shard_map.135 = (bf16[4,6272]{1,0:T(4,128)(2,1)S(1)}, f32[1,16]{1,0:T(1,128)}, f32[1,16]{1,0:T(1,128)}, f32[8,16]{1,0:T(8,128)S(1)}, f32[8,16]{1,0:T(8,128)S(1)}, /*index=5*/f32[16,16]{1,0:T(8,128)S(1)}) custom-call(bf16[16,6144]{1,0:T(8,128)(2,1)} %tokens_in.1, f32[8,16]{1,0:T(8,128)} %bitcast.12, f32[8,16]{1,0:T(8,128)} %bitcast.13, s32[2,16]{1,0:T(2,128)} %bitcast.14), custom_call_target="tpu_custom_call" | custom-call | flops 1048576 | bytes 262144 | tf_op jit(solution)/shard_map/pallas_call | solution.py:328
  6.3 0.1 collective-permute-start
  6.3 1.2 %collective-permute-done.4 = bf16[1,4,6144]{2,1,0:T(4,128)(2,1)S(1)} collective-permute-done((bf16[1,4,6144]{2,1,0:T(4,128)(2,1)}, bf16[1,4,6144]{2,1,0:T(4,128)(2,1)S(1)}, u32[]{:S(2)}, u32[]{:S(2)}) %collective-permute-start.4) | collective-permute-done | bytes 49184 | tf_op jit(solution)/shard_map/ppermute | solution.py:307
  7.5 0.9 %pad_maximum_fusion.6 = bf16[2,4,6144]{2,1,0:T(4,128)(2,1)S(1)} fusion(bf16[1,4,6144]{2,1,0:T(4,128)(2,1)S(1)} %collective-permute-done.4, bf16[1,4,6144]{2,1,0:T(4,128)(2,1)} %bitcast.11), kind=kLoop, calls=%fused_computation.6 | loop fusion | flops 49152 | bytes 196608 | tf_op jit(solution)/shard_map/concatenate | solution.py:313
  8.4 2.6 %collective-permute-start.5 = (bf16[2,4,6144]{2,1,0:T(4,128)(2,1)S(1)}, bf16[2,4,6144]{2,1,0:T(4,128)(2,1)S(1)}, u32[]{:S(2)}, u32[]{:S(2)}) collective-permute-start(bf16[2,4,6144]{2,1,0:T(4,128)(2,1)S(1)} %pad_maximum_fusion.6), channel_id=1, source_target_pairs={{0,4},{1,3},{2,6},{3,1},{4,0},{5,7},{6,2},{7,5},{8,12},{9,11},{10,... | collective-permute-start | bytes 294920 | tf_op jit(solution)/shard_map/ppermute | solution.py:307
  11.0 0.4 collective-permute-done
  11.5 0.1 pad_maximum_fusion.5
  11.5 1.5 %collective-permute-start.1 = (bf16[2,4,6272]{2,1,0:T(4,128)(2,1)S(1)}, bf16[2,4,6272]{2,1,0:T(4,128)(2,1)S(1)}, u32[]{:S(2)}, u32[]{:S(2)}) collective-permute-start(bf16[2,4,6272]{2,1,0:T(4,128)(2,1)S(1)} %pad_maximum_fusion.5), channel_id=1, source_target_pairs={{0,4},{1,3},{2,6},{3,1},{4,0},{5,7},{6,2},{7,5},{8,12},{9,11},{10,... | collective-permute-start | bytes 301064 | tf_op jit(solution)/shard_map/ppermute | solution.py:307
  13.0 0.6 collective-permute-done.5
  13.6 0.1 pad_maximum_fusion.4
  13.7 1.4 %collective-permute-start.6 = (bf16[4,4,6144]{2,1,0:T(4,128)(2,1)S(1)}, bf16[4,4,6144]{2,1,0:T(4,128)(2,1)S(1)}, u32[]{:S(2)}, u32[]{:S(2)}) collective-permute-start(bf16[4,4,6144]{2,1,0:T(4,128)(2,1)S(1)} %pad_maximum_fusion.4), channel_id=1, source_target_pairs={{0,2},{1,5},{2,0},{3,7},{4,6},{5,1},{6,4},{7,3},{8,10},{9,13},{10,... | collective-permute-start | bytes 589832 | tf_op jit(solution)/shard_map/ppermute | solution.py:307
  15.1 2.2 %collective-permute-done.1 = bf16[2,4,6272]{2,1,0:T(4,128)(2,1)S(1)} collective-permute-done((bf16[2,4,6272]{2,1,0:T(4,128)(2,1)S(1)}, bf16[2,4,6272]{2,1,0:T(4,128)(2,1)S(1)}, u32[]{:S(2)}, u32[]{:S(2)}) %collective-permute-start.1) | collective-permute-done | bytes 100384 | tf_op jit(solution)/shard_map/ppermute | solution.py:307
  17.3 0.1 pad_maximum_fusion.3
  17.5 0.9 %collective-permute-start.2 = (bf16[4,4,6272]{2,1,0:T(4,128)(2,1)S(1)}, bf16[4,4,6272]{2,1,0:T(4,128)(2,1)S(1)}, u32[]{:S(2)}, u32[]{:S(2)}) collective-permute-start(bf16[4,4,6272]{2,1,0:T(4,128)(2,1)S(1)} %pad_maximum_fusion.3), channel_id=1, source_target_pairs={{0,2},{1,5},{2,0},{3,7},{4,6},{5,1},{6,4},{7,3},{8,10},{9,13},{10,... | collective-permute-start | bytes 602120 | tf_op jit(solution)/shard_map/ppermute | solution.py:307
  18.4 1.1 %collective-permute-done.6 = bf16[4,4,6144]{2,1,0:T(4,128)(2,1)S(1)} collective-permute-done((bf16[4,4,6144]{2,1,0:T(4,128)(2,1)S(1)}, bf16[4,4,6144]{2,1,0:T(4,128)(2,1)S(1)}, u32[]{:S(2)}, u32[]{:S(2)}) %collective-permute-start.6) | collective-permute-done | bytes 196640 | tf_op jit(solution)/shard_map/ppermute | solution.py:307
  19.5 0.3 pad_maximum_fusion.2
  19.7 0.1 reshape.27
  19.9 0.1 collective-permute-start.7
  20.0 3.3 %collective-permute-done.2 = bf16[4,4,6272]{2,1,0:T(4,128)(2,1)S(1)} collective-permute-done((bf16[4,4,6272]{2,1,0:T(4,128)(2,1)S(1)}, bf16[4,4,6272]{2,1,0:T(4,128)(2,1)S(1)}, u32[]{:S(2)}, u32[]{:S(2)}) %collective-permute-start.2) | collective-permute-done | bytes 200736 | tf_op jit(solution)/shard_map/ppermute | solution.py:307
  23.3 0.3 pad_maximum_fusion.1
  23.5 0.1 reshape.26
  23.6 0.1 collective-permute-start.3
  23.7 0.0 collective-permute-done.7
  23.8 3.5 %shard_map.136.back = f32[64,512]{1,0:T(8,128)S(1)} custom-call(bf16[64,6144]{1,0:T(8,128)(2,1)S(1)} %constant_dynamic-update-slice_fusion.y, bf16[512,6144]{1,0:T(8,128)(2,1)} %down_in.1), custom_call_target="tpu_custom_call" | custom-call | flops 1610612736 | bytes 6291456 | tf_op jit(solution)/shard_map/pallas_call | solution.py:357
  27.3 0.0 collective-permute-done.3
  27.3 0.1 pad_maximum_fusion.x
  27.3 9.2 %shard_map.137 = (bf16[32,6272]{1,0:T(8,128)(2,1)S(1)}, f32[32,6272]{1,0:T(8,128)S(1)}, bf16[512,64]{1,0:T(8,128)(2,1)S(1)}, bf16[64,1024]{1,0:T(8,128)(2,1)S(1)}, bf16[6144,64]{1,0:T(8,128)(2,1)S(1)}) custom-call(bf16[64,6272]{1,0:T(8,128)(2,1)S(1)} %pad_maximum_fusion.x, f32[64,512]{1,0:T(8,128)S(1)} %shard_map.136.back, bf16[6144,512]{1,0:T(8,128)(2,1)} %gate_in.1, ...), custom_call_target="tpu_custom_call" | custom-call | flops 6442450944 | bytes 12582912 | tf_op jit(solution)/shard_map/pallas_call | solution.py:372
  36.6 0.6 collective-permute-start.8
  37.1 1.4 %collective-permute-done.8.got = bf16[32,6272]{1,0:T(8,128)(2,1)S(1)} collective-permute-done((bf16[32,6272]{1,0:T(8,128)(2,1)S(1)}, bf16[32,6272]{1,0:T(8,128)(2,1)S(1)}, u32[]{:S(2)}, u32[]{:S(2)}) %collective-permute-start.8) | collective-permute-done | bytes 401440 | tf_op jit(solution)/shard_map/ppermute | solution.py:307
  38.5 0.2 shard_map.141
  38.7 0.9 %collective-permute-start.9 = (bf16[16,6272]{1,0:T(8,128)(2,1)S(1)}, bf16[16,6272]{1,0:T(8,128)(2,1)S(1)}, u32[]{:S(2)}, u32[]{:S(2)}) collective-permute-start(bf16[16,6272]{1,0:T(8,128)(2,1)S(1)} %get-tuple-element.41), channel_id=1, source_target_pairs={{0,2},{1,5},{2,0},{3,7},{4,6},{5,1},{6,4},{7,3},{8,10},{9,13},{10,... | collective-permute-start | bytes 602120 | tf_op jit(solution)/shard_map/ppermute | solution.py:307
  39.6 3.5 %shard_map.140 = bf16[512,6144]{1,0:T(8,128)(2,1)} custom-call(bf16[512,64]{1,0:T(8,128)(2,1)S(1)} %get-tuple-element.37.weighted_t, bf16[64,6144]{1,0:T(8,128)(2,1)S(1)} %constant_dynamic-update-slice_fusion.y), custom_call_target="tpu_custom_call" | custom-call | flops 1610612736 | bytes 6291456 | tf_op jit(solution)/shard_map/pallas_call | solution.py:254
  43.1 1.4 %collective-permute-done.9.got = bf16[16,6272]{1,0:T(8,128)(2,1)S(1)} collective-permute-done((bf16[16,6272]{1,0:T(8,128)(2,1)S(1)}, bf16[16,6272]{1,0:T(8,128)(2,1)S(1)}, u32[]{:S(2)}, u32[]{:S(2)}) %collective-permute-start.9) | collective-permute-done | bytes 200736 | tf_op jit(solution)/shard_map/ppermute | solution.py:307
  44.4 0.1 shard_map.142
  44.6 1.5 %collective-permute-start.10 = (bf16[8,6272]{1,0:T(8,128)(2,1)S(1)}, bf16[8,6272]{1,0:T(8,128)(2,1)S(1)}, u32[]{:S(2)}, u32[]{:S(2)}) collective-permute-start(bf16[8,6272]{1,0:T(8,128)(2,1)S(1)} %get-tuple-element.43), channel_id=1, source_target_pairs={{0,4},{1,3},{2,6},{3,1},{4,0},{5,7},{6,2},{7,5},{8,12},{9,11},{10,... | collective-permute-start | bytes 301064 | tf_op jit(solution)/shard_map/ppermute | solution.py:307
  46.0 3.4 %shard_map.138 = (bf16[6144,512]{1,0:T(8,128)(2,1)}, bf16[6144,512]{1,0:T(8,128)(2,1)}) custom-call(bf16[6144,64]{1,0:T(8,128)(2,1)S(1)} %get-tuple-element.31.x_t, bf16[64,1024]{1,0:T(8,128)(2,1)S(1)} %get-tuple-element.32.d_both), custom_call_target="tpu_custom_call" | custom-call | flops 1610612736 | bytes 6291456 | tf_op jit(solution)/shard_map/pallas_call | solution.py:278
  49.4 0.0 collective-permute-done.10.got
  49.5 0.2 shard_map.143
  49.6 3.5 %collective-permute-start.11 = (bf16[4,6272]{1,0:T(4,128)(2,1)S(1)}, bf16[4,6272]{1,0:T(4,128)(2,1)S(1)}, u32[]{:S(2)}, u32[]{:S(2)}) collective-permute-start(bf16[4,6272]{1,0:T(4,128)(2,1)S(1)} %get-tuple-element.45), channel_id=1, source_target_pairs={{0,8},{1,9},{2,10},{3,11},{4,12},{5,13},{6,14},{7,15},{8,0},{9,1},... | collective-permute-start | bytes 150536 | tf_op jit(solution)/shard_map/ppermute | solution.py:307
  53.1 3.4 %shard_map.139 = (bf16[6144,512]{1,0:T(8,128)(2,1)}, bf16[6144,512]{1,0:T(8,128)(2,1)}) custom-call(bf16[6144,64]{1,0:T(8,128)(2,1)S(1)} %get-tuple-element.31.x_t, bf16[64,1024]{1,0:T(8,128)(2,1)S(1)} %get-tuple-element.32.d_both, bf16[6144,512]{1,0:T(8,128)(2,1)} %get-tuple-element.33.refs_0_, ...), custom_call_target="tpu_custom_call", output_to_operand_aliasing={{0}: (2, {}), {1}: (3, {})} | custom-call | flops 1610612736 | bytes 6291456 | tf_op jit(solution)/shard_map/pallas_call | solution.py:278
  56.5 0.0 collective-permute-done.11.got
  56.5 0.9 %shard_map.144 = (bf16[16,6144]{1,0:T(8,128)(2,1)}, f32[8,16]{1,0:T(8,128)}) custom-call(f32[4,6272]{1,0:T(4,128)S(1)} %get-tuple-element.44.have, bf16[4,6272]{1,0:T(4,128)(2,1)S(1)} %collective-permute-done.11.got, f32[16,16]{1,0:T(8,128)S(1)} %get-tuple-element.46.select, f32[8,16]{1,0:T(8,128)S(1)} %get-tuple-element.47.base, ...), custom_call_target="tpu_custom_call" | custom-call | flops 1048576 | bytes 262144 | tf_op jit(solution)/shard_map/pallas_call | solution.py:25
  (2 shorter events, 0.1 us)
Async XLA Ops:
  0.6 6.9 %collective-permute-start.4 = (bf16[1,4,6144]{2,1,0:T(4,128)(2,1)}, bf16[1,4,6144]{2,1,0:T(4,128)(2,1)S(1)}, u32[]{:S(2)}, u32[]{:S(2)}) collective-permute-start(bf16[1,4,6144]{2,1,0:T(4,128)(2,1)} %bitcast.10), channel_id=1, source_target_pairs={{0,8},{1,9},{2,10},{3,11},{4,12},{5,13},{6,14},{7,15},{8,0},{9,1},... | collective-permute-start | bytes 147464 | tf_op jit(solution)/shard_map/ppermute | solution.py:307
  6.3 5.2 %collective-permute-start = (bf16[1,4,6272]{2,1,0:T(4,128)(2,1)S(1)}, bf16[1,4,6272]{2,1,0:T(4,128)(2,1)S(1)}, u32[]{:S(2)}, u32[]{:S(2)}) collective-permute-start(bf16[1,4,6272]{2,1,0:T(4,128)(2,1)S(1)} %bitcast.8), channel_id=1, source_target_pairs={{0,8},{1,9},{2,10},{3,11},{4,12},{5,13},{6,14},{7,15},{8,0},{9,1},... | collective-permute-start | bytes 150536 | tf_op jit(solution)/shard_map/ppermute | solution.py:307
  8.4 5.2 %collective-permute-start.5 = (bf16[2,4,6144]{2,1,0:T(4,128)(2,1)S(1)}, bf16[2,4,6144]{2,1,0:T(4,128)(2,1)S(1)}, u32[]{:S(2)}, u32[]{:S(2)}) collective-permute-start(bf16[2,4,6144]{2,1,0:T(4,128)(2,1)S(1)} %pad_maximum_fusion.6), channel_id=1, source_target_pairs={{0,4},{1,3},{2,6},{3,1},{4,0},{5,7},{6,2},{7,5},{8,12},{9,11},{10,... | collective-permute-start | bytes 294920 | tf_op jit(solution)/shard_map/ppermute | solution.py:307
  11.5 5.8 %collective-permute-start.1 = (bf16[2,4,6272]{2,1,0:T(4,128)(2,1)S(1)}, bf16[2,4,6272]{2,1,0:T(4,128)(2,1)S(1)}, u32[]{:S(2)}, u32[]{:S(2)}) collective-permute-start(bf16[2,4,6272]{2,1,0:T(4,128)(2,1)S(1)} %pad_maximum_fusion.5), channel_id=1, source_target_pairs={{0,4},{1,3},{2,6},{3,1},{4,0},{5,7},{6,2},{7,5},{8,12},{9,11},{10,... | collective-permute-start | bytes 301064 | tf_op jit(solution)/shard_map/ppermute | solution.py:307
  13.7 5.7 %collective-permute-start.6 = (bf16[4,4,6144]{2,1,0:T(4,128)(2,1)S(1)}, bf16[4,4,6144]{2,1,0:T(4,128)(2,1)S(1)}, u32[]{:S(2)}, u32[]{:S(2)}) collective-permute-start(bf16[4,4,6144]{2,1,0:T(4,128)(2,1)S(1)} %pad_maximum_fusion.4), channel_id=1, source_target_pairs={{0,2},{1,5},{2,0},{3,7},{4,6},{5,1},{6,4},{7,3},{8,10},{9,13},{10,... | collective-permute-start | bytes 589832 | tf_op jit(solution)/shard_map/ppermute | solution.py:307
  17.5 5.8 %collective-permute-start.2 = (bf16[4,4,6272]{2,1,0:T(4,128)(2,1)S(1)}, bf16[4,4,6272]{2,1,0:T(4,128)(2,1)S(1)}, u32[]{:S(2)}, u32[]{:S(2)}) collective-permute-start(bf16[4,4,6272]{2,1,0:T(4,128)(2,1)S(1)} %pad_maximum_fusion.3), channel_id=1, source_target_pairs={{0,2},{1,5},{2,0},{3,7},{4,6},{5,1},{6,4},{7,3},{8,10},{9,13},{10,... | collective-permute-start | bytes 602120 | tf_op jit(solution)/shard_map/ppermute | solution.py:307
  19.9 3.8 %collective-permute-start.7 = (bf16[32,6144]{1,0:T(8,128)(2,1)S(1)}, bf16[32,6144]{1,0:T(8,128)(2,1)S(1)}, u32[]{:S(2)}, u32[]{:S(2)}) collective-permute-start(bf16[32,6144]{1,0:T(8,128)(2,1)S(1)} %reshape.27), channel_id=1, source_target_pairs={{0,1},{1,0},{2,3},{3,2},{4,5},{5,4},{6,7},{7,6},{8,9},{9,8},{10,11... | collective-permute-start | bytes 1179656 | tf_op jit(solution)/shard_map/ppermute | solution.py:307
  23.6 3.6 %collective-permute-start.3 = (bf16[32,6272]{1,0:T(8,128)(2,1)S(1)}, bf16[32,6272]{1,0:T(8,128)(2,1)S(1)}, u32[]{:S(2)}, u32[]{:S(2)}) collective-permute-start(bf16[32,6272]{1,0:T(8,128)(2,1)S(1)} %reshape.26), channel_id=1, source_target_pairs={{0,1},{1,0},{2,3},{3,2},{4,5},{5,4},{6,7},{7,6},{8,9},{9,8},{10,11... | collective-permute-start | bytes 1204232 | tf_op jit(solution)/shard_map/ppermute | solution.py:307
  36.6 1.9 %collective-permute-start.8 = (bf16[32,6272]{1,0:T(8,128)(2,1)S(1)}, bf16[32,6272]{1,0:T(8,128)(2,1)S(1)}, u32[]{:S(2)}, u32[]{:S(2)}) collective-permute-start(bf16[32,6272]{1,0:T(8,128)(2,1)S(1)} %get-tuple-element.39), channel_id=1, source_target_pairs={{0,1},{1,0},{2,3},{3,2},{4,5},{5,4},{6,7},{7,6},{8,9},{9,8},{10,11... | collective-permute-start | bytes 1204232 | tf_op jit(solution)/shard_map/ppermute | solution.py:307
  38.7 5.8 %collective-permute-start.9 = (bf16[16,6272]{1,0:T(8,128)(2,1)S(1)}, bf16[16,6272]{1,0:T(8,128)(2,1)S(1)}, u32[]{:S(2)}, u32[]{:S(2)}) collective-permute-start(bf16[16,6272]{1,0:T(8,128)(2,1)S(1)} %get-tuple-element.41), channel_id=1, source_target_pairs={{0,2},{1,5},{2,0},{3,7},{4,6},{5,1},{6,4},{7,3},{8,10},{9,13},{10,... | collective-permute-start | bytes 602120 | tf_op jit(solution)/shard_map/ppermute | solution.py:307
  44.6 4.9 %collective-permute-start.10 = (bf16[8,6272]{1,0:T(8,128)(2,1)S(1)}, bf16[8,6272]{1,0:T(8,128)(2,1)S(1)}, u32[]{:S(2)}, u32[]{:S(2)}) collective-permute-start(bf16[8,6272]{1,0:T(8,128)(2,1)S(1)} %get-tuple-element.43), channel_id=1, source_target_pairs={{0,4},{1,3},{2,6},{3,1},{4,0},{5,7},{6,2},{7,5},{8,12},{9,11},{10,... | collective-permute-start | bytes 301064 | tf_op jit(solution)/shard_map/ppermute | solution.py:307
  49.6 6.9 %collective-permute-start.11 = (bf16[4,6272]{1,0:T(4,128)(2,1)S(1)}, bf16[4,6272]{1,0:T(4,128)(2,1)S(1)}, u32[]{:S(2)}, u32[]{:S(2)}) collective-permute-start(bf16[4,6272]{1,0:T(4,128)(2,1)S(1)} %get-tuple-element.45), channel_id=1, source_target_pairs={{0,8},{1,9},{2,10},{3,11},{4,12},{5,13},{6,14},{7,15},{8,0},{9,1},... | collective-permute-start | bytes 150536 | tf_op jit(solution)/shard_map/ppermute | solution.py:307

commit v7 on v6

--- a/solution.py
+++ b/solution.py
@@ -309,9 +309,11 @@
     def gather(block):
         rows = n // 2 * block.shape[0]
         block = block[None]
-        for bits in levels:
+        for bits in levels[:-2]:
             block = lax.optimization_barrier(jnp.concatenate([block, swap(block, bits)]))
-        block = block.reshape(rows, block.shape[2])
+        near = swap(block, levels[-2])
+        parts = [block, near, swap(block, levels[-1]), swap(near, levels[-1])]
+        block = jnp.concatenate(parts).reshape(rows, block.shape[2])
         return jnp.concatenate([block, swap(block, (1, 1))])
 
     def shards(
@@ -360,8 +362,8 @@
             in_specs=whole(1) + [anywhere],
             out_specs=whole(1)[0],
             scratch_shapes=[
-                pltpu.VMEM((4, hidden, width // 4), BF16),
-                pltpu.SemaphoreType.DMA((4,)),
+                pltpu.VMEM((6, hidden, width // 6), BF16),
+                pltpu.SemaphoreType.DMA((6,)),
             ],
             compiler_params=pltpu.CompilerParams(vmem_limit_bytes=24 * MIB),
             cost_estimate=pl.CostEstimate(
@@ -383,7 +385,7 @@
             scratch_shapes=[
                 pltpu.VMEM((width, 2 * hidden), BF16),
                 pltpu.VMEM((rows, 2 * hidden), F32),
-                pltpu.SemaphoreType.DMA((2, 4)),
+                pltpu.SemaphoreType.DMA((2, 8)),
             ],
             compiler_params=pltpu.CompilerParams(vmem_limit_bytes=32 * MIB),
             cost_estimate=pl.CostEstimate(

time: 57.6 us -> 56.5 us (0.981)
  waiting for transfers between devices: 11.6 us -> 6.86 us
  starting transfers between devices: 17.1 us -> 21.3 us
    ppermute x12 -> x14, waiting for transfers between devices: 11.6 us -> 6.86 us  [swap(): return lax.ppermute(block, 'blk', [(i, i ^ bits[i % 2]) for i in range(n)])]
    ppermute x12 -> x14, starting transfers between devices: 17.1 us -> 21.3 us  [swap(): return lax.ppermute(block, 'blk', [(i, i ^ bits[i % 2]) for i in range(n)])]
    concatenate x6 -> x2, other arithmetic: 1.73 us -> 0.94 us  [gather(): jnp.concatenate([block, swap(block, bits)])]
    concatenate x0 -> x2, other arithmetic: none -> 0.59 us  [gather(): block = jnp.concatenate(parts).reshape(rows, block.shape[2])]
  transfers between devices with their start and end apart: 12 -> 14, of which waited for: 8 -> 8; matrix products, arithmetic and copies ran while one was open for 3% -> 3% of each run, Pallas kernels for 27% -> 27%
where the time goes in v7:
time: 56.5 us; the launch traced here: 56.3 us
  Pallas kernels  25.6 us (45%)
  starting transfers between devices  21.3 us (38%)
  waiting for transfers between devices  6.86 us (12%)
  other arithmetic  1.59 us (3%)
  between operations  0.78 us (1%)
    ppermute x14, starting transfers between devices, swap(): return lax.ppermute(block, 'blk', [(i, i ^ bits[i % 2]) for i in range(n)])  21.3 us
    pallas_call x1, Pallas kernels, shards(): pl.pallas_call(expert_kernel, out_shape=[jax.ShapeDtypeStruct((half, wide...  8.98 us
    ppermute x14, waiting for transfers between devices, swap(): return lax.ppermute(block, 'blk', [(i, i ^ bits[i % 2]) for i in range(n)])  6.86 us
    pallas_call x2, Pallas kernels, grad_pair_of(): pl.pallas_call(functools.partial(pair_kernel, part * rows), out_shape=out...  6.79 us
    pallas_call x1, Pallas kernels, grad_down_of(): pl.pallas_call(down_kernel, out_shape=jax.ShapeDtypeStruct((hidden, width...  3.54 us
    pallas_call x1, Pallas kernels, shards(): pl.pallas_call(back_kernel, out_shape=jax.ShapeDtypeStruct((rows, hidden)...  3.38 us
    pallas_call x1, Pallas kernels, shards(): pl.pallas_call(router_kernel, out_shape=[jax.ShapeDtypeStruct((slots, wid...  1.52 us
    pallas_call x4, Pallas kernels, call(): pl.pallas_call(kernel, out_shape=[jax.ShapeDtypeStruct(s, t) for s, t in...  1.38 us
  transfers between devices with their start and end apart: 14, of which 8 were waited for; matrix products, arithmetic and copies ran while one was open for 3% of the time, Pallas kernels for 27%

profile of v7, /device:TPU:0, one launch (start us, length us, event | category | flops | bytes accessed | tf_op | source)
XLA Modules:
  0.0 56.3 jit_solution(3371855896271060757)
XLA Ops:
  0.6 4.1 %collective-permute-start.5 = (bf16[1,4,6144]{2,1,0:T(4,128)(2,1)}, bf16[1,4,6144]{2,1,0:T(4,128)(2,1)S(1)}, u32[]{:S(2)}, u32[]{:S(2)}) collective-permute-start(bf16[1,4,6144]{2,1,0:T(4,128)(2,1)} %bitcast.10), channel_id=1, source_target_pairs={{0,8},{1,9},{2,10},{3,11},{4,12},{5,13},{6,14},{7,15},{8,0},{9,1},... | collective-permute-start | bytes 147464 | tf_op jit(solution)/shard_map/ppermute | solution.py:307
  4.7 1.5 %shard_map.135 = (bf16[4,6272]{1,0:T(4,128)(2,1)S(1)}, f32[1,16]{1,0:T(1,128)}, f32[1,16]{1,0:T(1,128)}, f32[8,16]{1,0:T(8,128)S(1)}, f32[8,16]{1,0:T(8,128)S(1)}, /*index=5*/f32[16,16]{1,0:T(8,128)S(1)}) custom-call(bf16[16,6144]{1,0:T(8,128)(2,1)} %tokens_in.1, f32[8,16]{1,0:T(8,128)} %bitcast.12, f32[8,16]{1,0:T(8,128)} %bitcast.13, s32[2,16]{1,0:T(2,128)} %bitcast.14), custom_call_target="tpu_custom_call" | custom-call | flops 1048576 | bytes 262144 | tf_op jit(solution)/shard_map/pallas_call | solution.py:330
  6.3 0.1 collective-permute-start
  6.3 1.2 %collective-permute-done.5 = bf16[1,4,6144]{2,1,0:T(4,128)(2,1)S(1)} collective-permute-done((bf16[1,4,6144]{2,1,0:T(4,128)(2,1)}, bf16[1,4,6144]{2,1,0:T(4,128)(2,1)S(1)}, u32[]{:S(2)}, u32[]{:S(2)}) %collective-permute-start.5) | collective-permute-done | bytes 49184 | tf_op jit(solution)/shard_map/ppermute | solution.py:307
  7.5 0.9 %pad_maximum_fusion.4 = bf16[2,4,6144]{2,1,0:T(4,128)(2,1)S(1)} fusion(bf16[1,4,6144]{2,1,0:T(4,128)(2,1)S(1)} %collective-permute-done.5, bf16[1,4,6144]{2,1,0:T(4,128)(2,1)} %bitcast.11), kind=kLoop, calls=%fused_computation.4 | loop fusion | flops 49152 | bytes 196608 | tf_op jit(solution)/shard_map/concatenate | solution.py:313
  8.4 2.6 %collective-permute-start.6 = (bf16[2,4,6144]{2,1,0:T(4,128)(2,1)S(1)}, bf16[2,4,6144]{2,1,0:T(4,128)(2,1)S(1)}, u32[]{:S(2)}, u32[]{:S(2)}) collective-permute-start(bf16[2,4,6144]{2,1,0:T(4,128)(2,1)S(1)} %pad_maximum_fusion.4), channel_id=1, source_target_pairs={{0,4},{1,3},{2,6},{3,1},{4,0},{5,7},{6,2},{7,5},{8,12},{9,11},{10,... | collective-permute-start | bytes 294920 | tf_op jit(solution)/shard_map/ppermute | solution.py:307
  11.0 0.5 collective-permute-done
  11.5 0.1 pad_maximum_fusion.3
  11.5 1.5 %collective-permute-start.1 = (bf16[2,4,6272]{2,1,0:T(4,128)(2,1)S(1)}, bf16[2,4,6272]{2,1,0:T(4,128)(2,1)S(1)}, u32[]{:S(2)}, u32[]{:S(2)}) collective-permute-start(bf16[2,4,6272]{2,1,0:T(4,128)(2,1)S(1)} %pad_maximum_fusion.3), channel_id=1, source_target_pairs={{0,4},{1,3},{2,6},{3,1},{4,0},{5,7},{6,2},{7,5},{8,12},{9,11},{10,... | collective-permute-start | bytes 301064 | tf_op jit(solution)/shard_map/ppermute | solution.py:307
  13.0 1.5 %collective-permute-start.7 = (bf16[2,4,6144]{2,1,0:T(4,128)(2,1)S(1)}, bf16[2,4,6144]{2,1,0:T(4,128)(2,1)S(1)}, u32[]{:S(2)}, u32[]{:S(2)}) collective-permute-start(bf16[2,4,6144]{2,1,0:T(4,128)(2,1)S(1)} %pad_maximum_fusion.4), channel_id=1, source_target_pairs={{0,2},{1,5},{2,0},{3,7},{4,6},{5,1},{6,4},{7,3},{8,10},{9,13},{10,... | collective-permute-start | bytes 294920 | tf_op jit(solution)/shard_map/ppermute | solution.py:307
  14.6 0.0 collective-permute-done.6
  14.6 0.9 %collective-permute-start.8 = (bf16[2,4,6144]{2,1,0:T(4,128)(2,1)S(1)}, bf16[2,4,6144]{2,1,0:T(4,128)(2,1)S(1)}, u32[]{:S(2)}, u32[]{:S(2)}) collective-permute-start(bf16[2,4,6144]{2,1,0:T(4,128)(2,1)S(1)} %collective-permute-done.6), channel_id=1, source_target_pairs={{0,2},{1,5},{2,0},{3,7},{4,6},{5,1},{6,4},{7,3},{8,10},{9,13},{10,... | collective-permute-start | bytes 294920 | tf_op jit(solution)/shard_map/ppermute | solution.py:307
  15.5 1.1 %collective-permute-start.2 = (bf16[2,4,6272]{2,1,0:T(4,128)(2,1)S(1)}, bf16[2,4,6272]{2,1,0:T(4,128)(2,1)S(1)}, u32[]{:S(2)}, u32[]{:S(2)}) collective-permute-start(bf16[2,4,6272]{2,1,0:T(4,128)(2,1)S(1)} %pad_maximum_fusion.3), channel_id=1, source_target_pairs={{0,2},{1,5},{2,0},{3,7},{4,6},{5,1},{6,4},{7,3},{8,10},{9,13},{10,... | collective-permute-start | bytes 301064 | tf_op jit(solution)/shard_map/ppermute | solution.py:307
  16.6 0.7 %collective-permute-done.1 = bf16[2,4,6272]{2,1,0:T(4,128)(2,1)S(1)} collective-permute-done((bf16[2,4,6272]{2,1,0:T(4,128)(2,1)S(1)}, bf16[2,4,6272]{2,1,0:T(4,128)(2,1)S(1)}, u32[]{:S(2)}, u32[]{:S(2)}) %collective-permute-start.1) | collective-permute-done | bytes 100384 | tf_op jit(solution)/shard_map/ppermute | solution.py:307
  17.3 1.6 %collective-permute-start.3 = (bf16[2,4,6272]{2,1,0:T(4,128)(2,1)S(1)}, bf16[2,4,6272]{2,1,0:T(4,128)(2,1)S(1)}, u32[]{:S(2)}, u32[]{:S(2)}) collective-permute-start(bf16[2,4,6272]{2,1,0:T(4,128)(2,1)S(1)} %collective-permute-done.1), channel_id=1, source_target_pairs={{0,2},{1,5},{2,0},{3,7},{4,6},{5,1},{6,4},{7,3},{8,10},{9,13},{10,... | collective-permute-start | bytes 301064 | tf_op jit(solution)/shard_map/ppermute | solution.py:307
  18.9 0.0 collective-permute-done.7
  18.9 0.3 collective-permute-done.8
  19.2 0.3 pad_maximum_fusion.2
  19.5 0.1 reshape.27
  19.6 0.1 collective-permute-start.9
  19.7 0.6 %collective-permute-done.2 = bf16[2,4,6272]{2,1,0:T(4,128)(2,1)S(1)} collective-permute-done((bf16[2,4,6272]{2,1,0:T(4,128)(2,1)S(1)}, bf16[2,4,6272]{2,1,0:T(4,128)(2,1)S(1)}, u32[]{:S(2)}, u32[]{:S(2)}) %collective-permute-start.2) | collective-permute-done | bytes 100384 | tf_op jit(solution)/shard_map/ppermute | solution.py:307
  20.3 1.7 %collective-permute-done.3 = bf16[2,4,6272]{2,1,0:T(4,128)(2,1)S(1)} collective-permute-done((bf16[2,4,6272]{2,1,0:T(4,128)(2,1)S(1)}, bf16[2,4,6272]{2,1,0:T(4,128)(2,1)S(1)}, u32[]{:S(2)}, u32[]{:S(2)}) %collective-permute-start.3) | collective-permute-done | bytes 100384 | tf_op jit(solution)/shard_map/ppermute | solution.py:307
  22.0 0.3 pad_maximum_fusion.1
  22.3 0.1 reshape.26
  22.3 0.1 collective-permute-start.4
  22.4 0.0 collective-permute-done.9
  22.5 3.4 %shard_map.136.back = f32[64,512]{1,0:T(8,128)S(1)} custom-call(bf16[64,6144]{1,0:T(8,128)(2,1)S(1)} %constant_dynamic-update-slice_fusion.y, bf16[512,6144]{1,0:T(8,128)(2,1)} %down_in.1), custom_call_target="tpu_custom_call" | custom-call | flops 1610612736 | bytes 6291456 | tf_op jit(solution)/shard_map/pallas_call | solution.py:359
  25.9 0.0 collective-permute-done.4
  25.9 0.1 pad_maximum_fusion.x
  25.9 9.0 %shard_map.137 = (bf16[32,6272]{1,0:T(8,128)(2,1)S(1)}, f32[32,6272]{1,0:T(8,128)S(1)}, bf16[512,64]{1,0:T(8,128)(2,1)S(1)}, bf16[64,1024]{1,0:T(8,128)(2,1)S(1)}, bf16[6144,64]{1,0:T(8,128)(2,1)S(1)}) custom-call(bf16[64,6272]{1,0:T(8,128)(2,1)S(1)} %pad_maximum_fusion.x, f32[64,512]{1,0:T(8,128)S(1)} %shard_map.136.back, bf16[6144,512]{1,0:T(8,128)(2,1)} %gate_in.1, ...), custom_call_target="tpu_custom_call" | custom-call | flops 6442450944 | bytes 12582912 | tf_op jit(solution)/shard_map/pallas_call | solution.py:374
  34.9 0.6 collective-permute-start.10
  35.5 1.4 %collective-permute-done.10.got = bf16[32,6272]{1,0:T(8,128)(2,1)S(1)} collective-permute-done((bf16[32,6272]{1,0:T(8,128)(2,1)S(1)}, bf16[32,6272]{1,0:T(8,128)(2,1)S(1)}, u32[]{:S(2)}, u32[]{:S(2)}) %collective-permute-start.10) | collective-permute-done | bytes 401440 | tf_op jit(solution)/shard_map/ppermute | solution.py:307
  36.8 0.2 shard_map.141
  37.0 1.7 %collective-permute-start.11 = (bf16[16,6272]{1,0:T(8,128)(2,1)S(1)}, bf16[16,6272]{1,0:T(8,128)(2,1)S(1)}, u32[]{:S(2)}, u32[]{:S(2)}) collective-permute-start(bf16[16,6272]{1,0:T(8,128)(2,1)S(1)} %get-tuple-element.41), channel_id=1, source_target_pairs={{0,2},{1,5},{2,0},{3,7},{4,6},{5,1},{6,4},{7,3},{8,10},{9,13},{10,... | collective-permute-start | bytes 602120 | tf_op jit(solution)/shard_map/ppermute | solution.py:307
  38.7 3.5 %shard_map.140 = bf16[512,6144]{1,0:T(8,128)(2,1)} custom-call(bf16[512,64]{1,0:T(8,128)(2,1)S(1)} %get-tuple-element.37.weighted_t, bf16[64,6144]{1,0:T(8,128)(2,1)S(1)} %constant_dynamic-update-slice_fusion.y), custom_call_target="tpu_custom_call" | custom-call | flops 1610612736 | bytes 6291456 | tf_op jit(solution)/shard_map/pallas_call | solution.py:254
  42.2 0.6 %collective-permute-done.11.got = bf16[16,6272]{1,0:T(8,128)(2,1)S(1)} collective-permute-done((bf16[16,6272]{1,0:T(8,128)(2,1)S(1)}, bf16[16,6272]{1,0:T(8,128)(2,1)S(1)}, u32[]{:S(2)}, u32[]{:S(2)}) %collective-permute-start.11) | collective-permute-done | bytes 200736 | tf_op jit(solution)/shard_map/ppermute | solution.py:307
  42.8 0.1 shard_map.142
  42.9 1.5 %collective-permute-start.12 = (bf16[8,6272]{1,0:T(8,128)(2,1)S(1)}, bf16[8,6272]{1,0:T(8,128)(2,1)S(1)}, u32[]{:S(2)}, u32[]{:S(2)}) collective-permute-start(bf16[8,6272]{1,0:T(8,128)(2,1)S(1)} %get-tuple-element.43), channel_id=1, source_target_pairs={{0,4},{1,3},{2,6},{3,1},{4,0},{5,7},{6,2},{7,5},{8,12},{9,11},{10,... | collective-permute-start | bytes 301064 | tf_op jit(solution)/shard_map/ppermute | solution.py:307
  44.5 3.4 %shard_map.138 = (bf16[6144,512]{1,0:T(8,128)(2,1)}, bf16[6144,512]{1,0:T(8,128)(2,1)}) custom-call(bf16[6144,64]{1,0:T(8,128)(2,1)S(1)} %get-tuple-element.31.x_t, bf16[64,1024]{1,0:T(8,128)(2,1)S(1)} %get-tuple-element.32.d_both), custom_call_target="tpu_custom_call" | custom-call | flops 1610612736 | bytes 6291456 | tf_op jit(solution)/shard_map/pallas_call | solution.py:278
  47.9 0.0 collective-permute-done.12.got
  47.9 0.2 shard_map.143
  48.0 4.0 %collective-permute-start.13 = (bf16[4,6272]{1,0:T(4,128)(2,1)S(1)}, bf16[4,6272]{1,0:T(4,128)(2,1)S(1)}, u32[]{:S(2)}, u32[]{:S(2)}) collective-permute-start(bf16[4,6272]{1,0:T(4,128)(2,1)S(1)} %get-tuple-element.45), channel_id=1, source_target_pairs={{0,8},{1,9},{2,10},{3,11},{4,12},{5,13},{6,14},{7,15},{8,0},{9,1},... | collective-permute-start | bytes 150536 | tf_op jit(solution)/shard_map/ppermute | solution.py:307
  52.0 3.4 %shard_map.139 = (bf16[6144,512]{1,0:T(8,128)(2,1)}, bf16[6144,512]{1,0:T(8,128)(2,1)}) custom-call(bf16[6144,64]{1,0:T(8,128)(2,1)S(1)} %get-tuple-element.31.x_t, bf16[64,1024]{1,0:T(8,128)(2,1)S(1)} %get-tuple-element.32.d_both, bf16[6144,512]{1,0:T(8,128)(2,1)} %get-tuple-element.33.refs_0_, ...), custom_call_target="tpu_custom_call", output_to_operand_aliasing={{0}: (2, {}), {1}: (3, {})} | custom-call | flops 1610612736 | bytes 6291456 | tf_op jit(solution)/shard_map/pallas_call | solution.py:278
  55.4 0.0 collective-permute-done.13.got
  55.4 0.9 %shard_map.144 = (bf16[16,6144]{1,0:T(8,128)(2,1)}, f32[8,16]{1,0:T(8,128)}) custom-call(f32[4,6272]{1,0:T(4,128)S(1)} %get-tuple-element.44.have, bf16[4,6272]{1,0:T(4,128)(2,1)S(1)} %collective-permute-done.13.got, f32[16,16]{1,0:T(8,128)S(1)} %get-tuple-element.46.select, f32[8,16]{1,0:T(8,128)S(1)} %get-tuple-element.47.base, ...), custom_call_target="tpu_custom_call" | custom-call | flops 1048576 | bytes 262144 | tf_op jit(solution)/shard_map/pallas_call | solution.py:25
  (2 shorter events, 0.1 us)
Async XLA Ops:
  0.6 6.9 %collective-permute-start.5 = (bf16[1,4,6144]{2,1,0:T(4,128)(2,1)}, bf16[1,4,6144]{2,1,0:T(4,128)(2,1)S(1)}, u32[]{:S(2)}, u32[]{:S(2)}) collective-permute-start(bf16[1,4,6144]{2,1,0:T(4,128)(2,1)} %bitcast.10), channel_id=1, source_target_pairs={{0,8},{1,9},{2,10},{3,11},{4,12},{5,13},{6,14},{7,15},{8,0},{9,1},... | collective-permute-start | bytes 147464 | tf_op jit(solution)/shard_map/ppermute | solution.py:307
  6.3 5.2 %collective-permute-start = (bf16[1,4,6272]{2,1,0:T(4,128)(2,1)S(1)}, bf16[1,4,6272]{2,1,0:T(4,128)(2,1)S(1)}, u32[]{:S(2)}, u32[]{:S(2)}) collective-permute-start(bf16[1,4,6272]{2,1,0:T(4,128)(2,1)S(1)} %bitcast.8), channel_id=1, source_target_pairs={{0,8},{1,9},{2,10},{3,11},{4,12},{5,13},{6,14},{7,15},{8,0},{9,1},... | collective-permute-start | bytes 150536 | tf_op jit(solution)/shard_map/ppermute | solution.py:307
  8.4 6.2 %collective-permute-start.6 = (bf16[2,4,6144]{2,1,0:T(4,128)(2,1)S(1)}, bf16[2,4,6144]{2,1,0:T(4,128)(2,1)S(1)}, u32[]{:S(2)}, u32[]{:S(2)}) collective-permute-start(bf16[2,4,6144]{2,1,0:T(4,128)(2,1)S(1)} %pad_maximum_fusion.4), channel_id=1, source_target_pairs={{0,4},{1,3},{2,6},{3,1},{4,0},{5,7},{6,2},{7,5},{8,12},{9,11},{10,... | collective-permute-start | bytes 294920 | tf_op jit(solution)/shard_map/ppermute | solution.py:307
  11.5 5.8 %collective-permute-start.1 = (bf16[2,4,6272]{2,1,0:T(4,128)(2,1)S(1)}, bf16[2,4,6272]{2,1,0:T(4,128)(2,1)S(1)}, u32[]{:S(2)}, u32[]{:S(2)}) collective-permute-start(bf16[2,4,6272]{2,1,0:T(4,128)(2,1)S(1)} %pad_maximum_fusion.3), channel_id=1, source_target_pairs={{0,4},{1,3},{2,6},{3,1},{4,0},{5,7},{6,2},{7,5},{8,12},{9,11},{10,... | collective-permute-start | bytes 301064 | tf_op jit(solution)/shard_map/ppermute | solution.py:307
  13.0 5.9 %collective-permute-start.7 = (bf16[2,4,6144]{2,1,0:T(4,128)(2,1)S(1)}, bf16[2,4,6144]{2,1,0:T(4,128)(2,1)S(1)}, u32[]{:S(2)}, u32[]{:S(2)}) collective-permute-start(bf16[2,4,6144]{2,1,0:T(4,128)(2,1)S(1)} %pad_maximum_fusion.4), channel_id=1, source_target_pairs={{0,2},{1,5},{2,0},{3,7},{4,6},{5,1},{6,4},{7,3},{8,10},{9,13},{10,... | collective-permute-start | bytes 294920 | tf_op jit(solution)/shard_map/ppermute | solution.py:307
  14.6 4.6 %collective-permute-start.8 = (bf16[2,4,6144]{2,1,0:T(4,128)(2,1)S(1)}, bf16[2,4,6144]{2,1,0:T(4,128)(2,1)S(1)}, u32[]{:S(2)}, u32[]{:S(2)}) collective-permute-start(bf16[2,4,6144]{2,1,0:T(4,128)(2,1)S(1)} %collective-permute-done.6), channel_id=1, source_target_pairs={{0,2},{1,5},{2,0},{3,7},{4,6},{5,1},{6,4},{7,3},{8,10},{9,13},{10,... | collective-permute-start | bytes 294920 | tf_op jit(solution)/shard_map/ppermute | solution.py:307
  15.5 4.8 %collective-permute-start.2 = (bf16[2,4,6272]{2,1,0:T(4,128)(2,1)S(1)}, bf16[2,4,6272]{2,1,0:T(4,128)(2,1)S(1)}, u32[]{:S(2)}, u32[]{:S(2)}) collective-permute-start(bf16[2,4,6272]{2,1,0:T(4,128)(2,1)S(1)} %pad_maximum_fusion.3), channel_id=1, source_target_pairs={{0,2},{1,5},{2,0},{3,7},{4,6},{5,1},{6,4},{7,3},{8,10},{9,13},{10,... | collective-permute-start | bytes 301064 | tf_op jit(solution)/shard_map/ppermute | solution.py:307
  17.3 4.6 %collective-permute-start.3 = (bf16[2,4,6272]{2,1,0:T(4,128)(2,1)S(1)}, bf16[2,4,6272]{2,1,0:T(4,128)(2,1)S(1)}, u32[]{:S(2)}, u32[]{:S(2)}) collective-permute-start(bf16[2,4,6272]{2,1,0:T(4,128)(2,1)S(1)} %collective-permute-done.1), channel_id=1, source_target_pairs={{0,2},{1,5},{2,0},{3,7},{4,6},{5,1},{6,4},{7,3},{8,10},{9,13},{10,... | collective-permute-start | bytes 301064 | tf_op jit(solution)/shard_map/ppermute | solution.py:307
  19.6 2.8 %collective-permute-start.9 = (bf16[32,6144]{1,0:T(8,128)(2,1)S(1)}, bf16[32,6144]{1,0:T(8,128)(2,1)S(1)}, u32[]{:S(2)}, u32[]{:S(2)}) collective-permute-start(bf16[32,6144]{1,0:T(8,128)(2,1)S(1)} %reshape.27), channel_id=1, source_target_pairs={{0,1},{1,0},{2,3},{3,2},{4,5},{5,4},{6,7},{7,6},{8,9},{9,8},{10,11... | collective-permute-start | bytes 1179656 | tf_op jit(solution)/shard_map/ppermute | solution.py:307
  22.3 3.5 %collective-permute-start.4 = (bf16[32,6272]{1,0:T(8,128)(2,1)S(1)}, bf16[32,6272]{1,0:T(8,128)(2,1)S(1)}, u32[]{:S(2)}, u32[]{:S(2)}) collective-permute-start(bf16[32,6272]{1,0:T(8,128)(2,1)S(1)} %reshape.26), channel_id=1, source_target_pairs={{0,1},{1,0},{2,3},{3,2},{4,5},{5,4},{6,7},{7,6},{8,9},{9,8},{10,11... | collective-permute-start | bytes 1204232 | tf_op jit(solution)/shard_map/ppermute | solution.py:307
  34.9 1.9 %collective-permute-start.10 = (bf16[32,6272]{1,0:T(8,128)(2,1)S(1)}, bf16[32,6272]{1,0:T(8,128)(2,1)S(1)}, u32[]{:S(2)}, u32[]{:S(2)}) collective-permute-start(bf16[32,6272]{1,0:T(8,128)(2,1)S(1)} %get-tuple-element.39), channel_id=1, source_target_pairs={{0,1},{1,0},{2,3},{3,2},{4,5},{5,4},{6,7},{7,6},{8,9},{9,8},{10,11... | collective-permute-start | bytes 1204232 | tf_op jit(solution)/shard_map/ppermute | solution.py:307
  37.0 5.8 %collective-permute-start.11 = (bf16[16,6272]{1,0:T(8,128)(2,1)S(1)}, bf16[16,6272]{1,0:T(8,128)(2,1)S(1)}, u32[]{:S(2)}, u32[]{:S(2)}) collective-permute-start(bf16[16,6272]{1,0:T(8,128)(2,1)S(1)} %get-tuple-element.41), channel_id=1, source_target_pairs={{0,2},{1,5},{2,0},{3,7},{4,6},{5,1},{6,4},{7,3},{8,10},{9,13},{10,... | collective-permute-start | bytes 602120 | tf_op jit(solution)/shard_map/ppermute | solution.py:307
  42.9 4.9 %collective-permute-start.12 = (bf16[8,6272]{1,0:T(8,128)(2,1)S(1)}, bf16[8,6272]{1,0:T(8,128)(2,1)S(1)}, u32[]{:S(2)}, u32[]{:S(2)}) collective-permute-start(bf16[8,6272]{1,0:T(8,128)(2,1)S(1)} %get-tuple-element.43), channel_id=1, source_target_pairs={{0,4},{1,3},{2,6},{3,1},{4,0},{5,7},{6,2},{7,5},{8,12},{9,11},{10,... | collective-permute-start | bytes 301064 | tf_op jit(solution)/shard_map/ppermute | solution.py:307
  48.0 7.4 %collective-permute-start.13 = (bf16[4,6272]{1,0:T(4,128)(2,1)S(1)}, bf16[4,6272]{1,0:T(4,128)(2,1)S(1)}, u32[]{:S(2)}, u32[]{:S(2)}) collective-permute-start(bf16[4,6272]{1,0:T(4,128)(2,1)S(1)} %get-tuple-element.45), channel_id=1, source_target_pairs={{0,8},{1,9},{2,10},{3,11},{4,12},{5,13},{6,14},{7,15},{8,0},{9,1},... | collective-permute-start | bytes 150536 | tf_op jit(solution)/shard_map/ppermute | solution.py:307

commit v8 on v6

--- a/solution.py
+++ b/solution.py
@@ -34,6 +34,10 @@
 
 def in_hbm(array):
     return pltpu.with_memory_space_constraint(array, pltpu.HBM)
+
+
+def in_vmem(array):
+    return pltpu.with_memory_space_constraint(array, pltpu.VMEM)
 
 
 def lane_pair(rows, first, second):
@@ -108,46 +112,50 @@
     send[:, :width] = x_slots[:slots].astype(BF16)
 
 
-def back_kernel(y, down_in, back, down, sems):
-    chunks, _, step = down.shape
-
-    def copy(i):
-        return pltpu.make_async_copy(down_in.at[:, pl.ds(i * step, step)], down.at[i], sems.at[i])
-
-    for i in range(chunks):
-        copy(i).start()
-    for i in range(chunks):
-        copy(i).wait()
-        part = dot(y[:, i * step : (i + 1) * step], down[i], ((1,), (1,)))
-        back[...] = part if i == 0 else back[...] + part
+def fetch_kernel(source, after, target, sems):
+    parts = sems.shape[0]
+    step = source.shape[0] // parts
+    copies = [
+        pltpu.make_async_copy(
+            source.at[pl.ds(i * step, step)], target.at[pl.ds(i * step, step)], sems.at[i]
+        )
+        for i in range(parts)
+    ]
+    for copy in copies:
+        copy.start()
+    for copy in copies:
+        copy.wait()
+
+
+def fetch(weight, after):
+    anywhere = pl.BlockSpec(memory_space=pl.ANY)
+    weight_in_vmem = pl.pallas_call(
+        fetch_kernel,
+        out_shape=pltpu.VMEM(weight.shape, weight.dtype),
+        in_specs=[anywhere] * 2,
+        out_specs=pl.BlockSpec(memory_space=pltpu.VMEM),
+        scratch_shapes=[pltpu.SemaphoreType.DMA((4,))],
+        compiler_params=pltpu.CompilerParams(vmem_limit_bytes=8 * MIB),
+        cost_estimate=pl.CostEstimate(
+            flops=0, bytes_accessed=2 * weight.size, transcendentals=0
+        ),
+    )(in_hbm(weight), after)
+    return in_vmem(weight_in_vmem)
+
+
+def back_kernel(y, down, back):
+    back[...] = dot(y[...], down[...], ((1,), (1,)))
 
 
 def expert_kernel(
-    x, back, gate_in, up_in, send, keep, weighted_t, d_both, x_t, both_w, acc, sems
+    x, back, gate_w, up_w, send, keep, weighted_t, d_both, x_t
 ):
-    rows, width, hidden_dim = x.shape[0], both_w.shape[0], gate_in.shape[1]
+    rows, width, hidden_dim = x.shape[0], gate_w.shape[0], gate_w.shape[1]
     half = rows // 2
-    chunks = sems.shape[1]
-    step = width // chunks
-
-    def copy(k, i):
-        at = pl.ds(i * step, step)
-        source = (gate_in, up_in)[k]
-        target = both_w.at[at, pl.ds(k * hidden_dim, hidden_dim)]
-        return pltpu.make_async_copy(source.at[at], target, sems.at[k, i])
-
-    for i in range(chunks):
-        copy(0, i).start()
-        copy(1, i).start()
     for c in range(0, width, LANES):
         x_t[c : c + LANES, :] = x[:, c : c + LANES].astype(F32).T.astype(BF16)
-    for i in range(chunks):
-        at = pl.ds(i * step, step)
-        copy(0, i).wait()
-        copy(1, i).wait()
-        part = dot(x[:, at], both_w[at, :], ((1,), (0,)))
-        acc[...] = part if i == 0 else acc[...] + part
-    pre_gate, pre_up = acc[:, :hidden_dim], acc[:, hidden_dim:]
+    pre_gate = dot(x[:, :width], gate_w[...], ((1,), (0,)))
+    pre_up = dot(x[:, :width], up_w[...], ((1,), (0,)))
     g = x[:, width:][:, 0:1].astype(F32)
     sig = jax.nn.sigmoid(pre_gate)
     act = pre_gate * sig
@@ -164,7 +172,8 @@
     wide = 1024
     for i in range(width // wide):
         at = pl.ds(i * wide, wide)
-        part = dot(d_both[...], both_w[at, :], ((1,), (1,)))
+        part = dot(d_both[:, :hidden_dim], gate_w[at, :], ((1,), (1,)))
+        part += dot(d_both[:, hidden_dim:], up_w[at, :], ((1,), (1,)))
         keep[:, at] = part[:half]
         send[:, at] = part[half:].astype(BF16)
 
@@ -195,34 +204,22 @@
 
 
 def tiles(out, left, right):
+    tall = 256 if left.shape[0] % 256 == 0 else 128
     for c in range(0, right.shape[1], 256):
-        for r in range(0, left.shape[0], 128):
-            part = dot(left[r : r + 128], right[:, c : c + 256], ((1,), (0,)))
-            out[r : r + 128, c : c + 256] = part.astype(BF16)
-
-
-def down_kernel(weighted_t, y, out, buf, sems):
-    chunks, _, step = buf.shape
-
-    def copy(i):
-        at = pl.ds(pl.multiple_of(i * step, step), step)
-        return pltpu.make_async_copy(buf.at[i], out.at[:, at], sems.at[i])
-
-    def body(i, carry):
-        at = pl.ds(pl.multiple_of(i * step, step), step)
-        tiles(buf.at[i], weighted_t, y.at[:, at])
-        copy(i).start()
+        for r in range(0, left.shape[0], tall):
+            part = dot(left[r : r + tall], right[:, c : c + 256], ((1,), (0,)))
+            out[r : r + tall, c : c + 256] = part.astype(BF16)
+
+
+def loop(count, body):
+    def step(i, carry):
+        body(i)
         return carry
 
-    def finish(i, carry):
-        copy(i).wait()
-        return carry
-
-    lax.fori_loop(0, chunks, body, 0)
-    lax.fori_loop(0, chunks, finish, 0)
-
-
-def pair_kernel(first_row, x_t, d_both, *refs):
+    lax.fori_loop(0, count, step, 0)
+
+
+def grads_kernel(first_row, x_t, d_both, *refs):
     gate_out, up_out, gate_buf, up_buf, sems = refs[-5:]
     chunks, step, cols = gate_buf.shape
 
@@ -231,68 +228,72 @@
         source, target = ((gate_buf, gate_out), (up_buf, up_out))[k]
         return pltpu.make_async_copy(source.at[i], target.at[at], sems.at[k, i])
 
-    def body(i, carry):
+    def body(i):
         at = pl.ds(pl.multiple_of(first_row + i * step, step), step)
         tiles(gate_buf.at[i], x_t.at[at], d_both.at[:, pl.ds(0, cols)])
         copy(0, i).start()
         tiles(up_buf.at[i], x_t.at[at], d_both.at[:, pl.ds(cols, cols)])
         copy(1, i).start()
-        return carry
-
-    def finish(i, carry):
+
+    def finish(i):
         copy(0, i).wait()
         copy(1, i).wait()
-        return carry
-
-    lax.fori_loop(0, chunks, body, 0)
-    lax.fori_loop(0, chunks, finish, 0)
-
-
-def grad_down_of(weighted_t, y):
-    hidden, width = weighted_t.shape[0], y.shape[1]
-    step = 1024
+
+    loop(chunks, body)
+    loop(chunks, finish)
+
+
+def first_kernel(weighted_t, y, x_t, d_both, down_out, gate_out, up_out, *scratch):
+    down_buf, down_sems = scratch[:2]
+    chunks, _, step = down_buf.shape
+
+    def copy(i):
+        at = pl.ds(pl.multiple_of(i * step, step), step)
+        return pltpu.make_async_copy(down_buf.at[i], down_out.at[:, at], down_sems.at[i])
+
+    def body(i):
+        at = pl.ds(pl.multiple_of(i * step, step), step)
+        tiles(down_buf.at[i], weighted_t, y.at[:, at])
+        copy(i).start()
+
+    loop(chunks, body)
+    grads_kernel(0, x_t, d_both, gate_out, up_out, *scratch[2:])
+    loop(chunks, lambda i: copy(i).wait())
+
+
+def grads_of(x_t, d_both, first_row, rows, before, down=()):
+    width, slots = x_t.shape
+    cols = d_both.shape[1] // 2
+    step = 256
+    outs = [jax.ShapeDtypeStruct((width, cols), BF16)] * 2
+    scratch = [
+        pltpu.VMEM((rows // step, step, cols), BF16),
+        pltpu.VMEM((rows // step, step, cols), BF16),
+        pltpu.SemaphoreType.DMA((2, rows // step)),
+    ]
+    kernel = functools.partial(grads_kernel, first_row)
+    if down:
+        kernel = first_kernel
+        wide = 1024
+        outs = [jax.ShapeDtypeStruct((cols, width), BF16)] + outs
+        scratch = [
+            pltpu.VMEM((width // wide, cols, wide), BF16),
+            pltpu.SemaphoreType.DMA((width // wide,)),
+        ] + scratch
+    anywhere = pl.BlockSpec(memory_space=pl.ANY)
+    elements = 2 * rows * cols + (width * cols if down else 0)
     return pl.pallas_call(
-        down_kernel,
-        out_shape=jax.ShapeDtypeStruct((hidden, width), BF16),
-        in_specs=whole(2),
-        out_specs=pl.BlockSpec(memory_space=pl.ANY),
-        scratch_shapes=[
-            pltpu.VMEM((width // step, hidden, step), BF16),
-            pltpu.SemaphoreType.DMA((width // step,)),
-        ],
-        compiler_params=pltpu.CompilerParams(vmem_limit_bytes=16 * MIB),
+        kernel,
+        out_shape=outs,
+        in_specs=whole(2 + len(down)) + [anywhere] * len(before),
+        out_specs=[anywhere] * len(outs),
+        scratch_shapes=scratch,
+        input_output_aliases={2 + i: i for i in range(len(before))},
+        compiler_params=pltpu.CompilerParams(vmem_limit_bytes=20 * MIB),
         cost_estimate=pl.CostEstimate(
-            flops=8 * weighted_t.size * width,
-            bytes_accessed=2 * hidden * width,
-            transcendentals=0,
+            flops=8 * slots * elements, bytes_accessed=2 * elements, transcendentals=0
         ),
-    )(weighted_t, y)
-
-
-def grad_pair_of(x_t, d_both, part, parts, before):
-    width, cols = x_t.shape[0], d_both.shape[1] // 2
-    step = 512
-    rows = width // parts
-    outs = [jax.ShapeDtypeStruct((width, cols), BF16)] * 2
-    anywhere = pl.BlockSpec(memory_space=pl.ANY)
-    return pl.pallas_call(
-        functools.partial(pair_kernel, part * rows),
-        out_shape=outs,
-        in_specs=whole(2) + [anywhere] * len(before),
-        out_specs=[anywhere] * 2,
-        scratch_shapes=[
-            pltpu.VMEM((rows // step, step, cols), BF16),
-            pltpu.VMEM((rows // step, step, cols), BF16),
-            pltpu.SemaphoreType.DMA((2, rows // step)),
-        ],
-        input_output_aliases={2 + i: i for i in range(len(before))},
-        compiler_params=pltpu.CompilerParams(vmem_limit_bytes=16 * MIB),
-        cost_estimate=pl.CostEstimate(
-            flops=8 * x_t.shape[1] * rows * 2 * cols,
-            bytes_accessed=4 * rows * cols,
-            transcendentals=0,
-        ),
-    )(x_t, d_both, *before)
+    )(*down, x_t, d_both, *before)
 
 
 def make_shards(n):
@@ -306,12 +307,9 @@
     def swap(block, bits):
         return lax.ppermute(block, "blk", [(i, i ^ bits[i % 2]) for i in range(n)])
 
-    def gather(block):
-        rows = n // 2 * block.shape[0]
-        block = block[None]
-        for bits in levels:
-            block = lax.optimization_barrier(jnp.concatenate([block, swap(block, bits)]))
-        block = block.reshape(rows, block.shape[2])
+    def join(parts):
+        block = jnp.concatenate(parts)
+        block = block.reshape(block.shape[0] * block.shape[1], block.shape[2])
         return jnp.concatenate([block, swap(block, (1, 1))])
 
     def shards(
@@ -350,24 +348,36 @@
             ),
         )(in_hbm(tokens), in_hbm(logits.T), in_hbm(ref_logits.T), in_hbm(routes.T))
 
-        y_all = gather(cotangent)
-        x_all = gather(send)
+        x_own, y_own = send[None], cotangent[None]
+        y_own = jnp.concatenate([y_own, swap(y_own, levels[0])])
+        x_own = jnp.concatenate([x_own, swap(x_own, levels[0])])
+        own = jnp.concatenate([x_own, y_own], axis=2)
+        for bits in levels[1:-2]:
+            own = jnp.concatenate([own, swap(own, bits)])
+        own = lax.optimization_barrier(own)
+        near = swap(own, levels[-2])
+        far = swap(own, levels[-1])
+        down_w = fetch(down_weight, send)
+        gate_w = fetch(gate_weight, own)
+        up_w = fetch(up_weight, near)
+        y_all = join(
+            [own[..., wide:], near[..., wide:], far[..., wide:], swap(near[..., wide:], levels[-1])]
+        )
+        x_all = join(
+            [own[..., :wide], near[..., :wide], far[..., :wide], swap(near[..., :wide], levels[-1])]
+        )
 
         work = 2 * rows * width * hidden
         back = pl.pallas_call(
             back_kernel,
             out_shape=jax.ShapeDtypeStruct((rows, hidden), F32),
-            in_specs=whole(1) + [anywhere],
+            in_specs=whole(2),
             out_specs=whole(1)[0],
-            scratch_shapes=[
-                pltpu.VMEM((4, hidden, width // 4), BF16),
-                pltpu.SemaphoreType.DMA((4,)),
-            ],
-            compiler_params=pltpu.CompilerParams(vmem_limit_bytes=24 * MIB),
+            compiler_params=pltpu.CompilerParams(vmem_limit_bytes=8 * MIB),
             cost_estimate=pl.CostEstimate(
                 flops=4 * work, bytes_accessed=2 * width * hidden, transcendentals=0
             ),
-        )(y_all, in_hbm(down_weight))
+        )(y_all, down_w)
         half = rows // 2
         low, keep, weighted_t, d_both, x_t = pl.pallas_call(
             expert_kernel,
@@ -378,18 +388,13 @@
                 jax.ShapeDtypeStruct((rows, 2 * hidden), BF16),
                 jax.ShapeDtypeStruct((width, rows), BF16),
             ],
-            in_specs=whole(2) + [anywhere] * 2,
+            in_specs=whole(4),
             out_specs=whole(5),
-            scratch_shapes=[
-                pltpu.VMEM((width, 2 * hidden), BF16),
-                pltpu.VMEM((rows, 2 * hidden), F32),
-                pltpu.SemaphoreType.DMA((2, 4)),
-            ],
-            compiler_params=pltpu.CompilerParams(vmem_limit_bytes=32 * MIB),
+            compiler_params=pltpu.CompilerParams(vmem_limit_bytes=8 * MIB),
             cost_estimate=pl.CostEstimate(
                 flops=16 * work, bytes_accessed=4 * width * hidden, transcendentals=0
             ),
-        )(x_all, back, in_hbm(gate_weight), in_hbm(up_weight))
+        )(x_all, back, gate_w, up_w)
 
         for bits in [(1, 1)] + levels[::-1]:
             got = swap(low, bits)
@@ -404,11 +409,11 @@
                 16 * half * wide,
             )
 
-        grad_down = grad_down_of(weighted_t, y_all)
-        grad_pair = ()
-        for part in range(2):
-            grad_pair = grad_pair_of(x_t, d_both, part, 2, grad_pair)
-        grad_gate, grad_up = grad_pair
+        cuts = (0, width // 4, width * 5 // 8, width)
+        grad_down, *pair = grads_of(x_t, d_both, 0, cuts[1], (), (weighted_t, y_all))
+        for start, stop in zip(cuts[1:], cuts[2:]):
+            pair = grads_of(x_t, d_both, start, stop - start, tuple(pair))
+        grad_gate, grad_up = pair
 
         grad_tokens, grad_logits = call(
             home_kernel,

time: 57.6 us -> 79.3 us (1.38)
  local copies, waits for them, and re-layouts: 0.24 us -> 18 us
  Pallas kernels: 26 us -> 31.3 us
  starting transfers between devices: 17.1 us -> 14.6 us
    unnamed x1 -> x15, local copies, waits for them, and re-layouts: 0.03 us -> 14.8 us
    pallas_call x3 -> x6, Pallas kernels: 10.3 us -> 20.3 us  [the longest x3 11.7 us: grads_of(): pl.pallas_call(kernel, out_shape=outs, in_specs=whole(2 + len(down)) + [a...]
    pallas_call x1, Pallas kernels: 9.24 us -> 6.06 us  [shards(): pl.pallas_call(expert_kernel, out_shape=[jax.ShapeDtypeStruct((half, wide...]
    ppermute x12, starting transfers between devices: 17.1 us -> 14.6 us  [swap(): return lax.ppermute(block, 'blk', [(i, i ^ bits[i % 2]) for i in range(n)])]
    reshape x2, local copies, waits for them, and re-layouts: 0.18 us -> 1.93 us  [join(): block = block.reshape(block.shape[0] * block.shape[1], block.shape[2])]
    pallas_call x1, Pallas kernels: 3.49 us -> 2.01 us  [shards(): pl.pallas_call(back_kernel, out_shape=jax.ShapeDtypeStruct((rows, hidden)...]
    concatenate x1, local copies, waits for them, and re-layouts: 0.03 us -> 1.02 us  [join(): return jnp.concatenate([block, swap(block, (1, 1))])]
    concatenate x7 -> x4, other arithmetic: 1.79 us -> 2.29 us  [the longest x2 1.35 us: join(): block = jnp.concatenate(parts)]
  transfers between devices with their start and end apart: 12 -> 12, of which waited for: 8 -> 4; matrix products, arithmetic and copies ran while one was open for 3% -> 7% of each run, Pallas kernels for 27% -> 28%
where the time goes in v8:
time: 79.3 us; the launch traced here: 78.9 us
  Pallas kernels  31.3 us (39%)
  local copies, waits for them, and re-layouts  18 us (23%)
  starting transfers between devices  14.6 us (18%)
  waiting for transfers between devices  12 us (15%)
  other arithmetic  2.29 us (3%)
  between operations  0.85 us (1%)
    unnamed x15, local copies, waits for them, and re-layouts  14.8 us
    ppermute x12, starting transfers between devices, swap(): return lax.ppermute(block, 'blk', [(i, i ^ bits[i % 2]) for i in range(n)])  14.6 us
    ppermute x12, waiting for transfers between devices, swap(): return lax.ppermute(block, 'blk', [(i, i ^ bits[i % 2]) for i in range(n)])  12 us
    pallas_call x3, Pallas kernels, grads_of(): pl.pallas_call(kernel, out_shape=outs, in_specs=whole(2 + len(down)) + [a...  11.7 us
    pallas_call x3, Pallas kernels, fetch(): pl.pallas_call(fetch_kernel, out_shape=pltpu.VMEM(weight.shape, weight.dt...  8.61 us
    pallas_call x1, Pallas kernels, shards(): pl.pallas_call(expert_kernel, out_shape=[jax.ShapeDtypeStruct((half, wide...  6.06 us
    pallas_call x1, Pallas kernels, shards(): pl.pallas_call(back_kernel, out_shape=jax.ShapeDtypeStruct((rows, hidden)...  2.01 us
    reshape x2, local copies, waits for them, and re-layouts, join(): block = block.reshape(block.shape[0] * block.shape[1], block.shape[2])  1.93 us
  transfers between devices with their start and end apart: 12, of which 4 were waited for; matrix products, arithmetic and copies ran while one was open for 7% of the time, Pallas kernels for 28%

profile of v8, /device:TPU:0, one launch (start us, length us, event | category | flops | bytes accessed | tf_op | source)
XLA Modules:
  0.0 78.9 jit_solution(4465805540937991782)
XLA Ops:
  0.6 1.5 %shard_map.135 = (bf16[4,6272]{1,0:T(4,128)(2,1)S(1)}, f32[1,16]{1,0:T(1,128)}, f32[1,16]{1,0:T(1,128)}, f32[8,16]{1,0:T(8,128)S(1)}, f32[8,16]{1,0:T(8,128)S(1)}, /*index=5*/f32[16,16]{1,0:T(8,128)S(1)}) custom-call(bf16[16,6144]{1,0:T(8,128)(2,1)} %tokens_in.1, f32[8,16]{1,0:T(8,128)} %bitcast.14, f32[8,16]{1,0:T(8,128)} %bitcast.15, s32[2,16]{1,0:T(2,128)} %bitcast.16), custom_call_target="tpu_custom_call" | custom-call | flops 1048576 | bytes 262144 | tf_op jit(solution)/shard_map/pallas_call | solution.py:326
  2.2 4.1 %collective-permute-start = (bf16[1,4,6272]{2,1,0:T(4,128)(2,1)S(1)}, bf16[1,4,6272]{2,1,0:T(4,128)(2,1)S(1)}, u32[]{:S(2)}, u32[]{:S(2)}) collective-permute-start(bf16[1,4,6272]{2,1,0:T(4,128)(2,1)S(1)} %bitcast.10), channel_id=1, source_target_pairs={{0,8},{1,9},{2,10},{3,11},{4,12},{5,13},{6,14},{7,15},{8,0},{9,1},... | collective-permute-start | bytes 150536 | tf_op jit(solution)/shard_map/ppermute | solution.py:308
  6.3 0.1 collective-permute-start.1
  6.3 5.2 %collective-permute-done.1 = bf16[1,4,6144]{2,1,0:T(4,128)(2,1)S(1)} collective-permute-done((bf16[1,4,6144]{2,1,0:T(4,128)(2,1)}, bf16[1,4,6144]{2,1,0:T(4,128)(2,1)S(1)}, u32[]{:S(2)}, u32[]{:S(2)}) %collective-permute-start.1) | collective-permute-done | bytes 49184 | tf_op jit(solution)/shard_map/ppermute | solution.py:308
  11.6 0.9 %maximum_maximum_fusion.after = bf16[2,4,12416]{2,1,0:T(4,128)(2,1)S(1)} fusion(bf16[1,4,6144]{2,1,0:T(4,128)(2,1)S(1)} %collective-permute-done.1, bf16[1,4,6144]{2,1,0:T(4,128)(2,1)} %bitcast.13, bf16[1,4,6272]{2,1,0:T(4,128)(2,1)S(1)} %collective-permute-done, bf16[1,4,6272]{2,1,0:T(4,128)(2,1)S(1)} %bitcast.11), kind=kLoop, calls=%fused_computation.3 | loop fusion | flops 794624 | bytes 397312 | tf_op jit(solution)/shard_map/concatenate | solution.py:354
  12.5 1.5 %collective-permute-start.2 = (bf16[2,4,12416]{2,1,0:T(4,128)(2,1)S(1)}, bf16[2,4,12416]{2,1,0:T(4,128)(2,1)S(1)}, u32[]{:S(2)}, u32[]{:S(2)}) collective-permute-start(bf16[2,4,12416]{2,1,0:T(4,128)(2,1)S(1)} %maximum_maximum_fusion.after), channel_id=1, source_target_pairs={{0,4},{1,3},{2,6},{3,1},{4,0},{5,7},{6,2},{7,5},{8,12},{9,11},{10,... | collective-permute-start | bytes 595976 | tf_op jit(solution)/shard_map/ppermute | solution.py:308
  14.0 1.5 %collective-permute-start.3 = (bf16[2,4,12416]{2,1,0:T(4,128)(2,1)S(1)}, bf16[2,4,12416]{2,1,0:T(4,128)(2,1)S(1)}, u32[]{:S(2)}, u32[]{:S(2)}) collective-permute-start(bf16[2,4,12416]{2,1,0:T(4,128)(2,1)S(1)} %maximum_maximum_fusion.after), channel_id=1, source_target_pairs={{0,2},{1,5},{2,0},{3,7},{4,6},{5,1},{6,4},{7,3},{8,10},{9,13},{10,... | collective-permute-start | bytes 595976 | tf_op jit(solution)/shard_map/ppermute | solution.py:308
  15.5 4.3 %collective-permute-done.2.after = bf16[2,4,12416]{2,1,0:T(4,128)(2,1)S(1)} collective-permute-done((bf16[2,4,12416]{2,1,0:T(4,128)(2,1)S(1)}, bf16[2,4,12416]{2,1,0:T(4,128)(2,1)S(1)}, u32[]{:S(2)}, u32[]{:S(2)}) %collective-permute-start.2) | collective-permute-done | bytes 198688 | tf_op jit(solution)/shard_map/ppermute | solution.py:308
  19.9 0.1 collective-permute-start.6
  20.0 2.9 %shard_map.136.down = bf16[512,6144]{1,0:T(8,128)(2,1)S(1)} custom-call(bf16[512,6144]{1,0:T(8,128)(2,1)} %source.3, bf16[4,6272]{1,0:T(4,128)(2,1)S(1)} %get-tuple-element.33.after), custom_call_target="tpu_custom_call" | custom-call | bytes 6291456 | tf_op jit(solution)/shard_map/pallas_call | solution.py:132
  22.9 0.0 copy-start
  22.9 2.7 %copy-done = bf16[512,6144]{1,0:T(8,128)(2,1)} copy-done((bf16[512,6144]{1,0:T(8,128)(2,1)}, bf16[512,6144]{1,0:T(8,128)(2,1)S(1)}, u32[]{:S(2)}) %copy-start) | copy-done | bytes 6291480
  25.6 2.9 %shard_map.138.gate_w = bf16[6144,512]{1,0:T(8,128)(2,1)S(1)} custom-call(bf16[6144,512]{1,0:T(8,128)(2,1)} %source.4, bf16[2,4,12416]{2,1,0:T(4,128)(2,1)S(1)} %maximum_maximum_fusion.after), custom_call_target="tpu_custom_call" | custom-call | bytes 6291456 | tf_op jit(solution)/shard_map/pallas_call | solution.py:132
  28.5 0.0 copy-start.2
  28.5 2.7 %copy-done.2 = bf16[6144,512]{1,0:T(8,128)(2,1)} copy-done((bf16[6144,512]{1,0:T(8,128)(2,1)}, bf16[6144,512]{1,0:T(8,128)(2,1)S(1)}, u32[]{:S(2)}) %copy-start.2) | copy-done | bytes 6291480
  31.3 2.1 %collective-permute-start.4 = (bf16[2,4,6272]{2,1,0:T(4,128)(2,1)S(1)}, bf16[2,4,6272]{2,1,0:T(4,128)(2,1)S(1)}, u32[]{:S(2)}, u32[]{:S(2)}) collective-permute-start(bf16[2,4,6272]{2,1,0:T(4,128)(2,1)S(1)} %slice.27), channel_id=1, source_target_pairs={{0,2},{1,5},{2,0},{3,7},{4,6},{5,1},{6,4},{7,3},{8,10},{9,13},{10,... | collective-permute-start | bytes 301064 | tf_op jit(solution)/shard_map/ppermute | solution.py:308
  33.4 2.9 %shard_map.139.up_w = bf16[6144,512]{1,0:T(8,128)(2,1)S(1)} custom-call(bf16[6144,512]{1,0:T(8,128)(2,1)} %source.5, bf16[2,4,12416]{2,1,0:T(4,128)(2,1)S(1)} %collective-permute-done.2.after), custom_call_target="tpu_custom_call" | custom-call | bytes 6291456 | tf_op jit(solution)/shard_map/pallas_call | solution.py:132
  36.3 0.0 copy-start.3
  36.3 2.7 %copy-done.3 = bf16[6144,512]{1,0:T(8,128)(2,1)} copy-done((bf16[6144,512]{1,0:T(8,128)(2,1)}, bf16[6144,512]{1,0:T(8,128)(2,1)S(1)}, u32[]{:S(2)}) %copy-start.3) | copy-done | bytes 6291480
  39.0 0.0 collective-permute-done.6
  39.0 0.3 pad_maximum_fusion.2
  39.3 0.0 slice-start
  39.3 0.8 %reshape.27 = bf16[32,6144]{1,0:T(8,128)(2,1)} reshape(bf16[8,4,6144]{2,1,0:T(4,128)(2,1)S(1)} %pad_maximum_fusion.2) | data formatting | bytes 786432 | tf_op jit(solution)/shard_map/reshape | solution.py:312
  40.2 1.0 %constant_dynamic-update-slice_fusion.1 = bf16[64,6144]{1,0:T(8,128)(2,1)S(1)} fusion(bf16[32,6144]{1,0:T(8,128)(2,1)} %reshape.27), kind=kLoop, calls=%fused_computation.5 | loop fusion | bytes 786432
  41.2 1.1 %pad_maximum_fusion.1 = bf16[8,4,6272]{2,1,0:T(4,128)(2,1)} fusion(bf16[2,4,6272]{2,1,0:T(4,128)(2,1)S(1)} %collective-permute-done.4, bf16[2,4,6272]{2,1,0:T(4,128)(2,1)S(1)} %slice.28, bf16[2,4,6272]{2,1,0:T(4,128)(2,1)S(1)} %slice.27, bf16[2,4,6272]{2,1,0:T(4,128)(2,1)S(1)} %slice.26), kind=kLoop, calls=%fused_computation.1 | loop fusion | flops 602112 | bytes 802816 | tf_op jit(solution)/shard_map/concatenate | solution.py:311
  42.3 1.1 %reshape.26 = bf16[32,6272]{1,0:T(8,128)(2,1)S(1)} reshape(bf16[8,4,6272]{2,1,0:T(4,128)(2,1)} %pad_maximum_fusion.1) | data formatting | bytes 802816 | tf_op jit(solution)/shard_map/reshape | solution.py:312
  43.3 0.6 collective-permute-start.5
  43.9 1.0 %constant_dynamic-update-slice_fusion.y = bf16[64,6144]{1,0:T(8,128)(2,1)S(1)} fusion(bf16[64,6144]{1,0:T(8,128)(2,1)S(1)} %constant_dynamic-update-slice_fusion.1, bf16[32,6144]{1,0:T(8,128)(2,1)} %collective-permute-done.7), kind=kLoop, calls=%fused_computation.4 | loop fusion | bytes 786432 | tf_op jit(solution)/shard_map/concatenate | solution.py:313
  44.9 0.0 copy-start.1
  45.0 2.8 %copy-done.1 = bf16[512,6144]{1,0:T(8,128)(2,1)S(1)} copy-done((bf16[512,6144]{1,0:T(8,128)(2,1)S(1)}, bf16[512,6144]{1,0:T(8,128)(2,1)}, u32[]{:S(2)}) %copy-start.1) | copy-done | bytes 6291480
  47.7 2.0 %shard_map.137.back = f32[64,512]{1,0:T(8,128)S(1)} custom-call(bf16[64,6144]{1,0:T(8,128)(2,1)S(1)} %constant_dynamic-update-slice_fusion.y, bf16[512,6144]{1,0:T(8,128)(2,1)S(1)} %copy-done.1), custom_call_target="tpu_custom_call" | custom-call | flops 1610612736 | bytes 6291456 | tf_op jit(solution)/shard_map/pallas_call | solution.py:371
  49.8 0.1 pad_maximum_fusion.x
  49.8 0.1 slice-done.1
  49.9 2.8 %copy-done.4 = bf16[6144,512]{1,0:T(8,128)(2,1)S(1)} copy-done((bf16[6144,512]{1,0:T(8,128)(2,1)S(1)}, bf16[6144,512]{1,0:T(8,128)(2,1)}, u32[]{:S(2)}) %copy-start.4) | copy-done | bytes 6291480
  52.7 6.1 %shard_map.140 = (bf16[32,6272]{1,0:T(8,128)(2,1)S(1)}, f32[32,6272]{1,0:T(8,128)S(1)}, bf16[512,64]{1,0:T(8,128)(2,1)S(1)}, bf16[64,1024]{1,0:T(8,128)(2,1)S(1)}, bf16[6144,64]{1,0:T(8,128)(2,1)S(1)}) custom-call(bf16[64,6272]{1,0:T(8,128)(2,1)S(1)} %pad_maximum_fusion.x, f32[64,512]{1,0:T(8,128)S(1)} %shard_map.137.back, bf16[6144,512]{1,0:T(8,128)(2,1)S(1)} %bitcast.9, ...), custom_call_target="tpu_custom_call" | custom-call | flops 6442450944 | bytes 12582912 | tf_op jit(solution)/shard_map/pallas_call | solution.py:382
  58.8 0.1 collective-permute-start.8
  58.9 1.7 %collective-permute-done.8.got = bf16[32,6272]{1,0:T(8,128)(2,1)S(1)} collective-permute-done((bf16[32,6272]{1,0:T(8,128)(2,1)S(1)}, bf16[32,6272]{1,0:T(8,128)(2,1)S(1)}, u32[]{:S(2)}, u32[]{:S(2)}) %collective-permute-start.8) | collective-permute-done | bytes 401440 | tf_op jit(solution)/shard_map/ppermute | solution.py:308
  60.6 0.2 shard_map.144
  60.7 0.1 collective-permute-start.9
  60.8 5.0 %shard_map.141 = (bf16[512,6144]{1,0:T(8,128)(2,1)}, bf16[6144,512]{1,0:T(8,128)(2,1)}, bf16[6144,512]{1,0:T(8,128)(2,1)}) custom-call(bf16[512,64]{1,0:T(8,128)(2,1)S(1)} %get-tuple-element.36.weighted_t, bf16[64,6144]{1,0:T(8,128)(2,1)S(1)} %constant_dynamic-update-slice_fusion.y, bf16[6144,64]{1,0:T(8,128)(2,1)S(1)} %get-tuple-element.34.x_t, ...), custom_call_target="tpu_custom_call" | custom-call | flops 2415919104 | bytes 9437184 | tf_op jit(solution)/shard_map/pallas_call | solution.py:285
  65.9 0.7 collective-permute-done.9.got
  66.5 0.1 shard_map.145
  66.7 1.8 %collective-permute-start.10 = (bf16[8,6272]{1,0:T(8,128)(2,1)S(1)}, bf16[8,6272]{1,0:T(8,128)(2,1)S(1)}, u32[]{:S(2)}, u32[]{:S(2)}) collective-permute-start(bf16[8,6272]{1,0:T(8,128)(2,1)S(1)} %get-tuple-element.49), channel_id=1, source_target_pairs={{0,4},{1,3},{2,6},{3,1},{4,0},{5,7},{6,2},{7,5},{8,12},{9,11},{10,... | collective-permute-start | bytes 301064 | tf_op jit(solution)/shard_map/ppermute | solution.py:308
  68.5 3.3 %shard_map.142 = (bf16[6144,512]{1,0:T(8,128)(2,1)}, bf16[6144,512]{1,0:T(8,128)(2,1)}) custom-call(bf16[6144,64]{1,0:T(8,128)(2,1)S(1)} %get-tuple-element.34.x_t, bf16[64,1024]{1,0:T(8,128)(2,1)S(1)} %get-tuple-element.35.d_both, bf16[6144,512]{1,0:T(8,128)(2,1)} %get-tuple-element.37.refs_0_, ...), custom_call_target="tpu_custom_call", output_to_operand_aliasing={{0}: (2, {}), {1}: (3, {})} | custom-call | flops 1207959552 | bytes 4718592 | tf_op jit(solution)/shard_map/pallas_call | solution.py:285
  71.8 0.2 shard_map.146
  72.0 2.7 %collective-permute-start.11 = (bf16[4,6272]{1,0:T(4,128)(2,1)S(1)}, bf16[4,6272]{1,0:T(4,128)(2,1)S(1)}, u32[]{:S(2)}, u32[]{:S(2)}) collective-permute-start(bf16[4,6272]{1,0:T(4,128)(2,1)S(1)} %get-tuple-element.51), channel_id=1, source_target_pairs={{0,8},{1,9},{2,10},{3,11},{4,12},{5,13},{6,14},{7,15},{8,0},{9,1},... | collective-permute-start | bytes 150536 | tf_op jit(solution)/shard_map/ppermute | solution.py:308
  74.6 3.3 %shard_map.143 = (bf16[6144,512]{1,0:T(8,128)(2,1)}, bf16[6144,512]{1,0:T(8,128)(2,1)}) custom-call(bf16[6144,64]{1,0:T(8,128)(2,1)S(1)} %get-tuple-element.34.x_t, bf16[64,1024]{1,0:T(8,128)(2,1)S(1)} %get-tuple-element.35.d_both, bf16[6144,512]{1,0:T(8,128)(2,1)} %get-tuple-element.39.refs_0_, ...), custom_call_target="tpu_custom_call", output_to_operand_aliasing={{0}: (2, {}), {1}: (3, {})} | custom-call | flops 1207959552 | bytes 4718592 | tf_op jit(solution)/shard_map/pallas_call | solution.py:285
  78.0 0.9 %shard_map.147 = (bf16[16,6144]{1,0:T(8,128)(2,1)}, f32[8,16]{1,0:T(8,128)}) custom-call(f32[4,6272]{1,0:T(4,128)S(1)} %get-tuple-element.50.have, bf16[4,6272]{1,0:T(4,128)(2,1)S(1)} %collective-permute-done.11.got, f32[16,16]{1,0:T(8,128)S(1)} %get-tuple-element.52.select, f32[8,16]{1,0:T(8,128)S(1)} %get-tuple-element.53.base, ...), custom_call_target="tpu_custom_call" | custom-call | flops 1048576 | bytes 262144 | tf_op jit(solution)/shard_map/pallas_call | solution.py:25
  (18 shorter events, 0.2 us)
Async XLA Ops:
  2.2 9.4 %collective-permute-start = (bf16[1,4,6272]{2,1,0:T(4,128)(2,1)S(1)}, bf16[1,4,6272]{2,1,0:T(4,128)(2,1)S(1)}, u32[]{:S(2)}, u32[]{:S(2)}) collective-permute-start(bf16[1,4,6272]{2,1,0:T(4,128)(2,1)S(1)} %bitcast.10), channel_id=1, source_target_pairs={{0,8},{1,9},{2,10},{3,11},{4,12},{5,13},{6,14},{7,15},{8,0},{9,1},... | collective-permute-start | bytes 150536 | tf_op jit(solution)/shard_map/ppermute | solution.py:308
  6.3 5.3 %collective-permute-start.1 = (bf16[1,4,6144]{2,1,0:T(4,128)(2,1)}, bf16[1,4,6144]{2,1,0:T(4,128)(2,1)S(1)}, u32[]{:S(2)}, u32[]{:S(2)}) collective-permute-start(bf16[1,4,6144]{2,1,0:T(4,128)(2,1)} %bitcast.12), channel_id=1, source_target_pairs={{0,8},{1,9},{2,10},{3,11},{4,12},{5,13},{6,14},{7,15},{8,0},{9,1},... | collective-permute-start | bytes 147464 | tf_op jit(solution)/shard_map/ppermute | solution.py:308
  12.5 7.4 %collective-permute-start.2 = (bf16[2,4,12416]{2,1,0:T(4,128)(2,1)S(1)}, bf16[2,4,12416]{2,1,0:T(4,128)(2,1)S(1)}, u32[]{:S(2)}, u32[]{:S(2)}) collective-permute-start(bf16[2,4,12416]{2,1,0:T(4,128)(2,1)S(1)} %maximum_maximum_fusion.after), channel_id=1, source_target_pairs={{0,4},{1,3},{2,6},{3,1},{4,0},{5,7},{6,2},{7,5},{8,12},{9,11},{10,... | collective-permute-start | bytes 595976 | tf_op jit(solution)/shard_map/ppermute | solution.py:308
  14.0 19.3 %collective-permute-start.3 = (bf16[2,4,12416]{2,1,0:T(4,128)(2,1)S(1)}, bf16[2,4,12416]{2,1,0:T(4,128)(2,1)S(1)}, u32[]{:S(2)}, u32[]{:S(2)}) collective-permute-start(bf16[2,4,12416]{2,1,0:T(4,128)(2,1)S(1)} %maximum_maximum_fusion.after), channel_id=1, source_target_pairs={{0,2},{1,5},{2,0},{3,7},{4,6},{5,1},{6,4},{7,3},{8,10},{9,13},{10,... | collective-permute-start | bytes 595976 | tf_op jit(solution)/shard_map/ppermute | solution.py:308
  19.9 19.1 %collective-permute-start.6 = (bf16[2,4,6144]{2,1,0:T(4,128)(2,1)S(1)}, bf16[2,4,6144]{2,1,0:T(4,128)(2,1)S(1)}, u32[]{:S(2)}, u32[]{:S(2)}) collective-permute-start(bf16[2,4,6144]{2,1,0:T(4,128)(2,1)S(1)} %slice.30), channel_id=1, source_target_pairs={{0,2},{1,5},{2,0},{3,7},{4,6},{5,1},{6,4},{7,3},{8,10},{9,13},{10,... | collective-permute-start | bytes 294920 | tf_op jit(solution)/shard_map/ppermute | solution.py:308
  22.9 2.7 %copy-start = (bf16[512,6144]{1,0:T(8,128)(2,1)}, bf16[512,6144]{1,0:T(8,128)(2,1)S(1)}, u32[]{:S(2)}) copy-start(bf16[512,6144]{1,0:T(8,128)(2,1)S(1)} %shard_map.136.down) | copy-start | bytes 18874372
  28.5 2.7 %copy-start.2 = (bf16[6144,512]{1,0:T(8,128)(2,1)}, bf16[6144,512]{1,0:T(8,128)(2,1)S(1)}, u32[]{:S(2)}) copy-start(bf16[6144,512]{1,0:T(8,128)(2,1)S(1)} %shard_map.138.gate_w) | copy-start | bytes 18874372
  31.3 9.9 %collective-permute-start.4 = (bf16[2,4,6272]{2,1,0:T(4,128)(2,1)S(1)}, bf16[2,4,6272]{2,1,0:T(4,128)(2,1)S(1)}, u32[]{:S(2)}, u32[]{:S(2)}) collective-permute-start(bf16[2,4,6272]{2,1,0:T(4,128)(2,1)S(1)} %slice.27), channel_id=1, source_target_pairs={{0,2},{1,5},{2,0},{3,7},{4,6},{5,1},{6,4},{7,3},{8,10},{9,13},{10,... | collective-permute-start | bytes 301064 | tf_op jit(solution)/shard_map/ppermute | solution.py:308
  36.3 2.7 %copy-start.3 = (bf16[6144,512]{1,0:T(8,128)(2,1)}, bf16[6144,512]{1,0:T(8,128)(2,1)S(1)}, u32[]{:S(2)}) copy-start(bf16[6144,512]{1,0:T(8,128)(2,1)S(1)} %shard_map.139.up_w) | copy-start | bytes 18874372
  39.3 10.5 %slice-start = ((s8[6291456]{0:T(1024)(128)(4,1)}), s8[2097152]{0:T(1024)(128)(4,1)S(1)}, s32[]{:S(2)}) async-start(s8[6291456]{0:T(1024)(128)(4,1)} %bitcast.8), calls=%async_computation | async-start | bytes 4194304
  40.2 3.8 %collective-permute-start.7 = (bf16[32,6144]{1,0:T(8,128)(2,1)}, bf16[32,6144]{1,0:T(8,128)(2,1)}, u32[]{:S(2)}, u32[]{:S(2)}) collective-permute-start(bf16[32,6144]{1,0:T(8,128)(2,1)} %reshape.27), channel_id=1, source_target_pairs={{0,1},{1,0},{2,3},{3,2},{4,5},{5,4},{6,7},{7,6},{8,9},{9,8},{10,11... | collective-permute-start | bytes 1179656 | tf_op jit(solution)/shard_map/ppermute | solution.py:308
  43.3 6.4 %collective-permute-start.5 = (bf16[32,6272]{1,0:T(8,128)(2,1)S(1)}, bf16[32,6272]{1,0:T(8,128)(2,1)S(1)}, u32[]{:S(2)}, u32[]{:S(2)}) collective-permute-start(bf16[32,6272]{1,0:T(8,128)(2,1)S(1)} %reshape.26), channel_id=1, source_target_pairs={{0,1},{1,0},{2,3},{3,2},{4,5},{5,4},{6,7},{7,6},{8,9},{9,8},{10,11... | collective-permute-start | bytes 1204232 | tf_op jit(solution)/shard_map/ppermute | solution.py:308
  44.9 2.8 %copy-start.1 = (bf16[512,6144]{1,0:T(8,128)(2,1)S(1)}, bf16[512,6144]{1,0:T(8,128)(2,1)}, u32[]{:S(2)}) copy-start(bf16[512,6144]{1,0:T(8,128)(2,1)} %copy-done) | copy-start | bytes 18874372
  47.7 2.2 %slice-start.1 = ((s8[6291456]{0:T(1024)(128)(4,1)}), s8[4194304]{0:T(1024)(128)(4,1)S(1)}, s32[]{:S(2)}) async-start(s8[6291456]{0:T(1024)(128)(4,1)} %bitcast.8), calls=%async_computation.1 | async-start | bytes 8388608
  49.9 2.8 %copy-start.4 = (bf16[6144,512]{1,0:T(8,128)(2,1)S(1)}, bf16[6144,512]{1,0:T(8,128)(2,1)}, u32[]{:S(2)}) copy-start(bf16[6144,512]{1,0:T(8,128)(2,1)} %copy-done.3) | copy-start | bytes 18874372
  58.8 1.8 %collective-permute-start.8 = (bf16[32,6272]{1,0:T(8,128)(2,1)S(1)}, bf16[32,6272]{1,0:T(8,128)(2,1)S(1)}, u32[]{:S(2)}, u32[]{:S(2)}) collective-permute-start(bf16[32,6272]{1,0:T(8,128)(2,1)S(1)} %get-tuple-element.45), channel_id=1, source_target_pairs={{0,1},{1,0},{2,3},{3,2},{4,5},{5,4},{6,7},{7,6},{8,9},{9,8},{10,11... | collective-permute-start | bytes 1204232 | tf_op jit(solution)/shard_map/ppermute | solution.py:308
  60.7 5.8 %collective-permute-start.9 = (bf16[16,6272]{1,0:T(8,128)(2,1)S(1)}, bf16[16,6272]{1,0:T(8,128)(2,1)S(1)}, u32[]{:S(2)}, u32[]{:S(2)}) collective-permute-start(bf16[16,6272]{1,0:T(8,128)(2,1)S(1)} %get-tuple-element.47), channel_id=1, source_target_pairs={{0,2},{1,5},{2,0},{3,7},{4,6},{5,1},{6,4},{7,3},{8,10},{9,13},{10,... | collective-permute-start | bytes 602120 | tf_op jit(solution)/shard_map/ppermute | solution.py:308
  66.7 5.1 %collective-permute-start.10 = (bf16[8,6272]{1,0:T(8,128)(2,1)S(1)}, bf16[8,6272]{1,0:T(8,128)(2,1)S(1)}, u32[]{:S(2)}, u32[]{:S(2)}) collective-permute-start(bf16[8,6272]{1,0:T(8,128)(2,1)S(1)} %get-tuple-element.49), channel_id=1, source_target_pairs={{0,4},{1,3},{2,6},{3,1},{4,0},{5,7},{6,2},{7,5},{8,12},{9,11},{10,... | collective-permute-start | bytes 301064 | tf_op jit(solution)/shard_map/ppermute | solution.py:308
  72.0 6.0 %collective-permute-start.11 = (bf16[4,6272]{1,0:T(4,128)(2,1)S(1)}, bf16[4,6272]{1,0:T(4,128)(2,1)S(1)}, u32[]{:S(2)}, u32[]{:S(2)}) collective-permute-start(bf16[4,6272]{1,0:T(4,128)(2,1)S(1)} %get-tuple-element.51), channel_id=1, source_target_pairs={{0,8},{1,9},{2,10},{3,11},{4,12},{5,13},{6,14},{7,15},{8,0},{9,1},... | collective-permute-start | bytes 150536 | tf_op jit(solution)/shard_map/ppermute | solution.py:308

commit v9 on v8

--- a/solution.py
+++ b/solution.py
@@ -112,35 +112,60 @@
     send[:, :width] = x_slots[:slots].astype(BF16)
 
 
-def fetch_kernel(source, after, target, sems):
-    parts = sems.shape[0]
-    step = source.shape[0] // parts
-    copies = [
-        pltpu.make_async_copy(
-            source.at[pl.ds(i * step, step)], target.at[pl.ds(i * step, step)], sems.at[i]
-        )
-        for i in range(parts)
-    ]
+def fetch_copies(sources, targets, sems):
+    parts = sems.shape[1]
+    copies = []
+    for k, (source, target) in enumerate(zip(sources, targets)):
+        step = source.shape[0] // parts
+        for i in range(parts):
+            at = pl.ds(i * step, step)
+            copies.append(pltpu.make_async_copy(source.at[at], target.at[at], sems.at[k, i]))
+    return copies
+
+
+def fetch_kernel(count, has_block, *refs):
+    sources, refs = refs[:count], refs[count + 1 :]
+    if has_block:
+        block, refs = refs[0], refs[1:]
+    targets, refs = refs[:count], refs[count:]
+    copies = fetch_copies(sources, targets, refs[-1])
     for copy in copies:
         copy.start()
+    if has_block:
+        refs[0][...] = block[...]
     for copy in copies:
         copy.wait()
 
 
-def fetch(weight, after):
+def fetch(weights, after, block=None):
     anywhere = pl.BlockSpec(memory_space=pl.ANY)
-    weight_in_vmem = pl.pallas_call(
-        fetch_kernel,
-        out_shape=pltpu.VMEM(weight.shape, weight.dtype),
-        in_specs=[anywhere] * 2,
-        out_specs=pl.BlockSpec(memory_space=pltpu.VMEM),
-        scratch_shapes=[pltpu.SemaphoreType.DMA((4,))],
+    count, blocks = len(weights), [] if block is None else [block]
+    out = pl.pallas_call(
+        functools.partial(fetch_kernel, count, bool(blocks)),
+        out_shape=[pltpu.VMEM(w.shape, w.dtype) for w in weights]
+        + [jax.ShapeDtypeStruct(b.shape, b.dtype) for b in blocks],
+        in_specs=[anywhere] * (count + 1) + whole(len(blocks)),
+        out_specs=whole(count + len(blocks)),
+        scratch_shapes=[pltpu.SemaphoreType.DMA((count, 4))],
         compiler_params=pltpu.CompilerParams(vmem_limit_bytes=8 * MIB),
         cost_estimate=pl.CostEstimate(
-            flops=0, bytes_accessed=2 * weight.size, transcendentals=0
+            flops=0, bytes_accessed=2 * sum(w.size for w in weights), transcendentals=0
         ),
-    )(in_hbm(weight), after)
-    return in_vmem(weight_in_vmem)
+    )(*[in_hbm(w) for w in weights], after, *blocks)
+    return [in_vmem(w) for w in out[:count]] + list(out[count:])
+
+
+def split_kernel(block, after, left, right):
+    left[...] = block[:, : left.shape[1]]
+    right[...] = block[:, left.shape[1] :]
+
+
+def join_kernel(own, near, far, last_x, last_y, out_x, out_y):
+    wide = out_x.shape[1]
+    for out, last, first in ((out_x, last_x, 0), (out_y, last_y, wide)):
+        cols = out.shape[1]
+        parts = [ref[:, first : first + cols] for ref in (own, near, far)] + [last[...]]
+        out[...] = jnp.concatenate([part.astype(F32) for part in parts]).astype(BF16)
 
 
 def back_kernel(y, down, back):
@@ -204,7 +229,7 @@
 
 
 def tiles(out, left, right):
-    tall = 256 if left.shape[0] % 256 == 0 else 128
+    tall = 128
     for c in range(0, right.shape[1], 256):
         for r in range(0, left.shape[0], tall):
             part = dot(left[r : r + tall], right[:, c : c + 256], ((1,), (0,)))
@@ -212,11 +237,8 @@
 
 
 def loop(count, body):
-    def step(i, carry):
+    for i in range(count):
         body(i)
-        return carry
-
-    lax.fori_loop(0, count, step, 0)
 
 
 def grads_kernel(first_row, x_t, d_both, *refs):
@@ -224,12 +246,12 @@
     chunks, step, cols = gate_buf.shape
 
     def copy(k, i):
-        at = pl.ds(pl.multiple_of(first_row + i * step, step), step)
+        at = pl.ds(first_row + i * step, step)
         source, target = ((gate_buf, gate_out), (up_buf, up_out))[k]
         return pltpu.make_async_copy(source.at[i], target.at[at], sems.at[k, i])
 
     def body(i):
-        at = pl.ds(pl.multiple_of(first_row + i * step, step), step)
+        at = pl.ds(first_row + i * step, step)
         tiles(gate_buf.at[i], x_t.at[at], d_both.at[:, pl.ds(0, cols)])
         copy(0, i).start()
         tiles(up_buf.at[i], x_t.at[at], d_both.at[:, pl.ds(cols, cols)])
@@ -248,11 +270,11 @@
     chunks, _, step = down_buf.shape
 
     def copy(i):
-        at = pl.ds(pl.multiple_of(i * step, step), step)
+        at = pl.ds(i * step, step)
         return pltpu.make_async_copy(down_buf.at[i], down_out.at[:, at], down_sems.at[i])
 
     def body(i):
-        at = pl.ds(pl.multiple_of(i * step, step), step)
+        at = pl.ds(i * step, step)
         tiles(down_buf.at[i], weighted_t, y.at[:, at])
         copy(i).start()
 
@@ -307,11 +329,6 @@
     def swap(block, bits):
         return lax.ppermute(block, "blk", [(i, i ^ bits[i % 2]) for i in range(n)])
 
-    def join(parts):
-        block = jnp.concatenate(parts)
-        block = block.reshape(block.shape[0] * block.shape[1], block.shape[2])
-        return jnp.concatenate([block, swap(block, (1, 1))])
-
     def shards(
         tokens, cotangent, gate_weight, up_weight, down_weight, logits, ref_logits, routes
     ):
@@ -344,28 +361,47 @@
             ],
             compiler_params=pltpu.CompilerParams(vmem_limit_bytes=8 * MIB),
             cost_estimate=pl.CostEstimate(
-                flops=1 << 20, bytes_accessed=1 << 18, transcendentals=0
+                flops=1 << 20, bytes_accessed=1 << 24, transcendentals=0
             ),
         )(in_hbm(tokens), in_hbm(logits.T), in_hbm(ref_logits.T), in_hbm(routes.T))
 
-        x_own, y_own = send[None], cotangent[None]
-        y_own = jnp.concatenate([y_own, swap(y_own, levels[0])])
-        x_own = jnp.concatenate([x_own, swap(x_own, levels[0])])
-        own = jnp.concatenate([x_own, y_own], axis=2)
+        y_got = swap(cotangent, levels[0])
+        x_got = swap(send, levels[0])
+        gate_w, y_own = fetch([gate_weight], send, cotangent)
+        own = jnp.concatenate(
+            [jnp.concatenate([send, y_own], axis=1), jnp.concatenate([x_got, y_got], axis=1)]
+        )
         for bits in levels[1:-2]:
             own = jnp.concatenate([own, swap(own, bits)])
-        own = lax.optimization_barrier(own)
         near = swap(own, levels[-2])
         far = swap(own, levels[-1])
-        down_w = fetch(down_weight, send)
-        gate_w = fetch(gate_weight, own)
-        up_w = fetch(up_weight, near)
-        y_all = join(
-            [own[..., wide:], near[..., wide:], far[..., wide:], swap(near[..., wide:], levels[-1])]
+        up_w, down_w = fetch([up_weight, down_weight], own)
+        few = own.shape[0]
+        near_x, near_y = pl.pallas_call(
+            split_kernel,
+            out_shape=[
+                jax.ShapeDtypeStruct((few, wide), BF16),
+                jax.ShapeDtypeStruct((few, width), BF16),
+            ],
+            in_specs=whole(1) + [anywhere],
+            out_specs=whole(2),
+            compiler_params=pltpu.CompilerParams(vmem_limit_bytes=8 * MIB),
+            cost_estimate=pl.CostEstimate(
+                flops=0, bytes_accessed=1 << 18, transcendentals=0
+            ),
+        )(near, up_w)
+
+        last_y = swap(near_y, levels[-1])
+        last_x = swap(near_x, levels[-1])
+        x_half, y_half = call(
+            join_kernel,
+            [((rows // 2, wide), BF16), ((rows // 2, width), BF16)],
+            [own, near, far, last_x, last_y],
+            0,
+            1 << 18,
         )
-        x_all = join(
-            [own[..., :wide], near[..., :wide], far[..., :wide], swap(near[..., :wide], levels[-1])]
-        )
+        y_all = jnp.concatenate([y_half, swap(y_half, (1, 1))])
+        x_all = jnp.concatenate([x_half, swap(x_half, (1, 1))])
 
         work = 2 * rows * width * hidden
         back = pl.pallas_call(

time: 79.3 us -> 54.7 us (0.69)
  local copies, waits for them, and re-layouts: 18 us -> 0.88 us
  Pallas kernels: 31.3 us -> 27.8 us
  other arithmetic: 2.29 us -> 0.16 us
  waiting for transfers between devices: 12 us -> 10.6 us
    unnamed x15 -> x3, local copies, waits for them, and re-layouts: 14.8 us -> 0.86 us
    pallas_call x3, Pallas kernels: 11.7 us -> 9.19 us  [grads_of(): pl.pallas_call(kernel, out_shape=outs, in_specs=whole(2 + len(down)) + [a...]
    concatenate x4 -> x2, other arithmetic: 2.29 us -> 0.16 us  [the longest x1 0.1 us: shards(): jnp.concatenate([jnp.concatenate([send, y_own], axis=1), jnp.concatenate(...]
    reshape x2 -> x0, local copies, waits for them, and re-layouts: 1.93 us -> none  [join(): block = block.reshape(block.shape[0] * block.shape[1], block.shape[2])]
    ppermute x12, waiting for transfers between devices: 12 us -> 10.6 us  [swap(): return lax.ppermute(block, 'blk', [(i, i ^ bits[i % 2]) for i in range(n)])]
    pallas_call x3, Pallas kernels: 8.61 us -> 7.58 us  [the longest x2 7.56 us: fetch(): pl.pallas_call(functools.partial(fetch_kernel, count, bool(blocks)), out_...]
    concatenate x1, local copies, waits for them, and re-layouts: 1.02 us -> 0.03 us  [shards(): y_all = jnp.concatenate([y_half, swap(y_half, (1, 1))])]
  transfers between devices with their start and end apart: 12 -> 12, of which waited for: 4 -> 7; matrix products, arithmetic and copies ran while one was open for 7% -> 0% of each run, Pallas kernels for 28% -> 34%
where the time goes in v9:
time: 54.7 us; the launch traced here: 54.5 us
  Pallas kernels  27.8 us (51%)
  starting transfers between devices  14.3 us (26%)
  waiting for transfers between devices  10.6 us (19%)
  local copies, waits for them, and re-layouts  0.88 us (2%)
  between operations  0.75 us (1%)
    ppermute x12, starting transfers between devices, swap(): return lax.ppermute(block, 'blk', [(i, i ^ bits[i % 2]) for i in range(n)])  14.3 us
    ppermute x12, waiting for transfers between devices, swap(): return lax.ppermute(block, 'blk', [(i, i ^ bits[i % 2]) for i in range(n)])  10.6 us
    pallas_call x3, Pallas kernels, grads_of(): pl.pallas_call(kernel, out_shape=outs, in_specs=whole(2 + len(down)) + [a...  9.19 us
    pallas_call x2, Pallas kernels, fetch(): pl.pallas_call(functools.partial(fetch_kernel, count, bool(blocks)), out_...  7.56 us
    pallas_call x1, Pallas kernels, shards(): pl.pallas_call(expert_kernel, out_shape=[jax.ShapeDtypeStruct((half, wide...  6.07 us
    pallas_call x1, Pallas kernels, shards(): pl.pallas_call(back_kernel, out_shape=jax.ShapeDtypeStruct((rows, hidden)...  2.01 us
    pallas_call x1, Pallas kernels, shards(): pl.pallas_call(router_kernel, out_shape=[jax.ShapeDtypeStruct((slots, wid...  1.53 us
    pallas_call x5, Pallas kernels, call(): pl.pallas_call(kernel, out_shape=[jax.ShapeDtypeStruct(s, t) for s, t in...  1.44 us
  transfers between devices with their start and end apart: 12, of which 7 were waited for; matrix products, arithmetic and copies ran while one was open for 0% of the time, Pallas kernels for 34%

profile of v9, /device:TPU:0, one launch (start us, length us, event | category | flops | bytes accessed | tf_op | source)
XLA Modules:
  0.0 54.5 jit_solution(11988356375447399172)
XLA Ops:
  0.6 1.5 %shard_map.135 = (bf16[4,6272]{1,0:T(4,128)(2,1)S(1)}, f32[1,16]{1,0:T(1,128)}, f32[1,16]{1,0:T(1,128)}, f32[8,16]{1,0:T(8,128)S(1)}, f32[8,16]{1,0:T(8,128)S(1)}, /*index=5*/f32[16,16]{1,0:T(8,128)S(1)}) custom-call(bf16[16,6144]{1,0:T(8,128)(2,1)} %tokens_in.1, f32[8,16]{1,0:T(8,128)} %bitcast.6, f32[8,16]{1,0:T(8,128)} %bitcast.7, s32[2,16]{1,0:T(2,128)} %bitcast.8), custom_call_target="tpu_custom_call" | custom-call | flops 1048576 | bytes 16777216 | tf_op jit(solution)/shard_map/pallas_call | solution.py:343
  2.2 4.1 %collective-permute-start = (bf16[4,6272]{1,0:T(4,128)(2,1)S(1)}, bf16[4,6272]{1,0:T(4,128)(2,1)S(1)}, u32[]{:S(2)}, u32[]{:S(2)}) collective-permute-start(bf16[4,6272]{1,0:T(4,128)(2,1)S(1)} %get-tuple-element.41.refs_1_), channel_id=1, source_target_pairs={{0,8},{1,9},{2,10},{3,11},{4,12},{5,13},{6,14},{7,15},{8,0},{9,1},... | collective-permute-start | bytes 150536 | tf_op jit(solution)/shard_map/ppermute | solution.py:330
  6.3 0.1 collective-permute-start.1
  6.3 0.0 copy-start
  6.3 0.8 %copy-done = bf16[4,6144]{1,0:T(4,128)(2,1)S(1)} copy-done((bf16[4,6144]{1,0:T(4,128)(2,1)S(1)}, bf16[4,6144]{1,0:T(4,128)(2,1)}, u32[]{:S(2)}) %copy-start) | copy-done | bytes 49176
  7.2 2.9 %shard_map.136 = (bf16[6144,512]{1,0:T(8,128)(2,1)S(1)}, bf16[4,6144]{1,0:T(4,128)(2,1)S(1)}) custom-call(bf16[6144,512]{1,0:T(8,128)(2,1)} %refs_0_.2, bf16[4,6272]{1,0:T(4,128)(2,1)S(1)} %get-tuple-element.41.refs_1_, bf16[4,6144]{1,0:T(4,128)(2,1)S(1)} %copy-done), custom_call_target="tpu_custom_call" | custom-call | bytes 6291456 | tf_op jit(solution)/shard_map/pallas_call | solution.py:143
  10.1 1.5 %collective-permute-done.1 = bf16[4,6144]{1,0:T(4,128)(2,1)S(1)} collective-permute-done((bf16[4,6144]{1,0:T(4,128)(2,1)}, bf16[4,6144]{1,0:T(4,128)(2,1)S(1)}, u32[]{:S(2)}, u32[]{:S(2)}) %collective-permute-start.1) | collective-permute-done | bytes 49184 | tf_op jit(solution)/shard_map/ppermute | solution.py:330
  11.6 0.0 collective-permute-done
  11.6 0.1 maximum_maximum_fusion.refs_2_.own
  11.7 1.5 %collective-permute-start.2 = (bf16[8,12416]{1,0:T(8,128)(2,1)S(1)}, bf16[8,12416]{1,0:T(8,128)(2,1)S(1)}, u32[]{:S(2)}, u32[]{:S(2)}) collective-permute-start(bf16[8,12416]{1,0:T(8,128)(2,1)S(1)} %maximum_maximum_fusion.refs_2_.own), channel_id=1, source_target_pairs={{0,4},{1,3},{2,6},{3,1},{4,0},{5,7},{6,2},{7,5},{8,12},{9,11},{10,... | collective-permute-start | bytes 595976 | tf_op jit(solution)/shard_map/ppermute | solution.py:330
  13.2 1.5 %collective-permute-start.3 = (bf16[8,12416]{1,0:T(8,128)(2,1)S(1)}, bf16[8,12416]{1,0:T(8,128)(2,1)S(1)}, u32[]{:S(2)}, u32[]{:S(2)}) collective-permute-start(bf16[8,12416]{1,0:T(8,128)(2,1)S(1)} %maximum_maximum_fusion.refs_2_.own), channel_id=1, source_target_pairs={{0,2},{1,5},{2,0},{3,7},{4,6},{5,1},{6,4},{7,3},{8,10},{9,13},{10,... | collective-permute-start | bytes 595976 | tf_op jit(solution)/shard_map/ppermute | solution.py:330
  14.7 4.7 %shard_map.137 = (bf16[6144,512]{1,0:T(8,128)(2,1)S(1)}, bf16[512,6144]{1,0:T(8,128)(2,1)S(1)}) custom-call(bf16[6144,512]{1,0:T(8,128)(2,1)} %refs_0_.3, bf16[512,6144]{1,0:T(8,128)(2,1)} %refs_1_.1, bf16[8,12416]{1,0:T(8,128)(2,1)S(1)} %maximum_maximum_fusion.refs_2_.own), custom_call_target="tpu_custom_call" | custom-call | bytes 12582912 | tf_op jit(solution)/shard_map/pallas_call | solution.py:143
  19.4 0.0 collective-permute-done.2.block.near
  19.5 0.6 %collective-permute-start.4 = (bf16[8,6272]{1,0:T(8,128)(2,1)S(1)}, bf16[8,6272]{1,0:T(8,128)(2,1)S(1)}, u32[]{:S(2)}, u32[]{:S(2)}) collective-permute-start(bf16[8,6272]{1,0:T(8,128)(2,1)S(1)} %get-tuple-element.44), channel_id=1, source_target_pairs={{0,2},{1,5},{2,0},{3,7},{4,6},{5,1},{6,4},{7,3},{8,10},{9,13},{10,... | collective-permute-start | bytes 301064 | tf_op jit(solution)/shard_map/ppermute | solution.py:330
  20.1 1.5 %collective-permute-start.5 = (bf16[8,6144]{1,0:T(8,128)(2,1)S(1)}, bf16[8,6144]{1,0:T(8,128)(2,1)S(1)}, u32[]{:S(2)}, u32[]{:S(2)}) collective-permute-start(bf16[8,6144]{1,0:T(8,128)(2,1)S(1)} %get-tuple-element.45), channel_id=1, source_target_pairs={{0,2},{1,5},{2,0},{3,7},{4,6},{5,1},{6,4},{7,3},{8,10},{9,13},{10,... | collective-permute-start | bytes 294920 | tf_op jit(solution)/shard_map/ppermute | solution.py:330
  21.6 0.0 collective-permute-done.3.far
  21.6 3.7 %collective-permute-done.5.last_y = bf16[8,6144]{1,0:T(8,128)(2,1)S(1)} collective-permute-done((bf16[8,6144]{1,0:T(8,128)(2,1)S(1)}, bf16[8,6144]{1,0:T(8,128)(2,1)S(1)}, u32[]{:S(2)}, u32[]{:S(2)}) %collective-permute-start.5) | collective-permute-done | bytes 98336 | tf_op jit(solution)/shard_map/ppermute | solution.py:330
  25.2 0.0 collective-permute-done.4.last_x
  25.2 0.1 shard_map.139
  25.3 0.1 collective-permute-start.7
  25.4 0.5 collective-permute-start.6
  25.9 1.2 %collective-permute-done.7 = bf16[32,6144]{1,0:T(8,128)(2,1)S(1)} collective-permute-done((bf16[32,6144]{1,0:T(8,128)(2,1)S(1)}, bf16[32,6144]{1,0:T(8,128)(2,1)S(1)}, u32[]{:S(2)}, u32[]{:S(2)}) %collective-permute-start.7) | collective-permute-done | bytes 393248 | tf_op jit(solution)/shard_map/ppermute | solution.py:330
  27.1 2.0 %shard_map.140.back = f32[64,512]{1,0:T(8,128)S(1)} custom-call(bf16[64,6144]{1,0:T(8,128)(2,1)S(1)} %constant_dynamic-update-slice_fusion.y, bf16[512,6144]{1,0:T(8,128)(2,1)S(1)} %get-tuple-element.48.down), custom_call_target="tpu_custom_call" | custom-call | flops 1610612736 | bytes 6291456 | tf_op jit(solution)/shard_map/pallas_call | solution.py:407
  29.1 0.0 collective-permute-done.6
  29.1 0.1 pad_maximum_fusion.x
  29.2 6.1 %shard_map.141 = (bf16[32,6272]{1,0:T(8,128)(2,1)S(1)}, f32[32,6272]{1,0:T(8,128)S(1)}, bf16[512,64]{1,0:T(8,128)(2,1)S(1)}, bf16[64,1024]{1,0:T(8,128)(2,1)S(1)}, bf16[6144,64]{1,0:T(8,128)(2,1)S(1)}) custom-call(bf16[64,6272]{1,0:T(8,128)(2,1)S(1)} %pad_maximum_fusion.x, f32[64,512]{1,0:T(8,128)S(1)} %shard_map.140.back, ...), custom_call_target="tpu_custom_call" | custom-call | flops 6442450944 | bytes 12582912 | tf_op jit(solution)/shard_map/pallas_call | solution.py:418
  35.3 0.2 collective-permute-start.8
  35.5 1.6 %collective-permute-done.8.got = bf16[32,6272]{1,0:T(8,128)(2,1)S(1)} collective-permute-done((bf16[32,6272]{1,0:T(8,128)(2,1)S(1)}, bf16[32,6272]{1,0:T(8,128)(2,1)S(1)}, u32[]{:S(2)}, u32[]{:S(2)}) %collective-permute-start.8) | collective-permute-done | bytes 401440 | tf_op jit(solution)/shard_map/ppermute | solution.py:330
  37.1 0.2 shard_map.145
  37.2 1.0 %collective-permute-start.9 = (bf16[16,6272]{1,0:T(8,128)(2,1)S(1)}, bf16[16,6272]{1,0:T(8,128)(2,1)S(1)}, u32[]{:S(2)}, u32[]{:S(2)}) collective-permute-start(bf16[16,6272]{1,0:T(8,128)(2,1)S(1)} %get-tuple-element.63), channel_id=1, source_target_pairs={{0,2},{1,5},{2,0},{3,7},{4,6},{5,1},{6,4},{7,3},{8,10},{9,13},{10,... | collective-permute-start | bytes 602120 | tf_op jit(solution)/shard_map/ppermute | solution.py:330
  38.3 4.2 %shard_map.142 = (bf16[512,6144]{1,0:T(8,128)(2,1)}, bf16[6144,512]{1,0:T(8,128)(2,1)}, bf16[6144,512]{1,0:T(8,128)(2,1)}) custom-call(bf16[512,64]{1,0:T(8,128)(2,1)S(1)} %get-tuple-element.52.weighted_t, bf16[64,6144]{1,0:T(8,128)(2,1)S(1)} %constant_dynamic-update-slice_fusion.y, bf16[6144,64]{1,0:T(8,128)(2,1)S(1)} %get-tuple-element.50.x_t, ...), custom_call_target="tpu_custom_call" | custom-call | flops 2415919104 | bytes 9437184 | tf_op jit(solution)/shard_map/pallas_call | solution.py:307
  42.4 0.6 %collective-permute-done.9.got = bf16[16,6272]{1,0:T(8,128)(2,1)S(1)} collective-permute-done((bf16[16,6272]{1,0:T(8,128)(2,1)S(1)}, bf16[16,6272]{1,0:T(8,128)(2,1)S(1)}, u32[]{:S(2)}, u32[]{:S(2)}) %collective-permute-start.9) | collective-permute-done | bytes 200736 | tf_op jit(solution)/shard_map/ppermute | solution.py:330
  43.0 0.1 shard_map.146
  43.2 0.9 %collective-permute-start.10 = (bf16[8,6272]{1,0:T(8,128)(2,1)S(1)}, bf16[8,6272]{1,0:T(8,128)(2,1)S(1)}, u32[]{:S(2)}, u32[]{:S(2)}) collective-permute-start(bf16[8,6272]{1,0:T(8,128)(2,1)S(1)} %get-tuple-element.65), channel_id=1, source_target_pairs={{0,4},{1,3},{2,6},{3,1},{4,0},{5,7},{6,2},{7,5},{8,12},{9,11},{10,... | collective-permute-start | bytes 301064 | tf_op jit(solution)/shard_map/ppermute | solution.py:330
  44.1 2.5 %shard_map.143 = (bf16[6144,512]{1,0:T(8,128)(2,1)}, bf16[6144,512]{1,0:T(8,128)(2,1)}) custom-call(bf16[6144,64]{1,0:T(8,128)(2,1)S(1)} %get-tuple-element.50.x_t, bf16[64,1024]{1,0:T(8,128)(2,1)S(1)} %get-tuple-element.51.d_both, bf16[6144,512]{1,0:T(8,128)(2,1)} %get-tuple-element.53.refs_0_, ...), custom_call_target="tpu_custom_call", output_to_operand_aliasing={{0}: (2, {}), {1}: (3, {})} | custom-call | flops 1207959552 | bytes 4718592 | tf_op jit(solution)/shard_map/pallas_call | solution.py:307
  46.6 1.3 %collective-permute-done.10.got = bf16[8,6272]{1,0:T(8,128)(2,1)S(1)} collective-permute-done((bf16[8,6272]{1,0:T(8,128)(2,1)S(1)}, bf16[8,6272]{1,0:T(8,128)(2,1)S(1)}, u32[]{:S(2)}, u32[]{:S(2)}) %collective-permute-start.10) | collective-permute-done | bytes 100384 | tf_op jit(solution)/shard_map/ppermute | solution.py:330
  47.8 0.2 shard_map.147
  48.0 2.3 %collective-permute-start.11 = (bf16[4,6272]{1,0:T(4,128)(2,1)S(1)}, bf16[4,6272]{1,0:T(4,128)(2,1)S(1)}, u32[]{:S(2)}, u32[]{:S(2)}) collective-permute-start(bf16[4,6272]{1,0:T(4,128)(2,1)S(1)} %get-tuple-element.67), channel_id=1, source_target_pairs={{0,8},{1,9},{2,10},{3,11},{4,12},{5,13},{6,14},{7,15},{8,0},{9,1},... | collective-permute-start | bytes 150536 | tf_op jit(solution)/shard_map/ppermute | solution.py:330
  50.3 2.5 %shard_map.144 = (bf16[6144,512]{1,0:T(8,128)(2,1)}, bf16[6144,512]{1,0:T(8,128)(2,1)}) custom-call(bf16[6144,64]{1,0:T(8,128)(2,1)S(1)} %get-tuple-element.50.x_t, bf16[64,1024]{1,0:T(8,128)(2,1)S(1)} %get-tuple-element.51.d_both, bf16[6144,512]{1,0:T(8,128)(2,1)} %get-tuple-element.55.refs_0_, ...), custom_call_target="tpu_custom_call", output_to_operand_aliasing={{0}: (2, {}), {1}: (3, {})} | custom-call | flops 1207959552 | bytes 4718592 | tf_op jit(solution)/shard_map/pallas_call | solution.py:307
  52.8 0.7 %collective-permute-done.11.got = bf16[4,6272]{1,0:T(4,128)(2,1)S(1)} collective-permute-done((bf16[4,6272]{1,0:T(4,128)(2,1)S(1)}, bf16[4,6272]{1,0:T(4,128)(2,1)S(1)}, u32[]{:S(2)}, u32[]{:S(2)}) %collective-permute-start.11) | collective-permute-done | bytes 50208 | tf_op jit(solution)/shard_map/ppermute | solution.py:330
  53.6 0.9 %shard_map.148 = (bf16[16,6144]{1,0:T(8,128)(2,1)}, f32[8,16]{1,0:T(8,128)}) custom-call(f32[4,6272]{1,0:T(4,128)S(1)} %get-tuple-element.66.have, bf16[4,6272]{1,0:T(4,128)(2,1)S(1)} %collective-permute-done.11.got, f32[16,16]{1,0:T(8,128)S(1)} %get-tuple-element.68.select, f32[8,16]{1,0:T(8,128)S(1)} %get-tuple-element.69.base, ...), custom_call_target="tpu_custom_call" | custom-call | flops 1048576 | bytes 262144 | tf_op jit(solution)/shard_map/pallas_call | solution.py:25
  (3 shorter events, 0.1 us)
Async XLA Ops:
  2.2 9.4 %collective-permute-start = (bf16[4,6272]{1,0:T(4,128)(2,1)S(1)}, bf16[4,6272]{1,0:T(4,128)(2,1)S(1)}, u32[]{:S(2)}, u32[]{:S(2)}) collective-permute-start(bf16[4,6272]{1,0:T(4,128)(2,1)S(1)} %get-tuple-element.41.refs_1_), channel_id=1, source_target_pairs={{0,8},{1,9},{2,10},{3,11},{4,12},{5,13},{6,14},{7,15},{8,0},{9,1},... | collective-permute-start | bytes 150536 | tf_op jit(solution)/shard_map/ppermute | solution.py:330
  6.3 5.3 %collective-permute-start.1 = (bf16[4,6144]{1,0:T(4,128)(2,1)}, bf16[4,6144]{1,0:T(4,128)(2,1)S(1)}, u32[]{:S(2)}, u32[]{:S(2)}) collective-permute-start(bf16[4,6144]{1,0:T(4,128)(2,1)} %refs_2_.1), channel_id=1, source_target_pairs={{0,8},{1,9},{2,10},{3,11},{4,12},{5,13},{6,14},{7,15},{8,0},{9,1},... | collective-permute-start | bytes 147464 | tf_op jit(solution)/shard_map/ppermute | solution.py:330
  6.3 0.8 %copy-start = (bf16[4,6144]{1,0:T(4,128)(2,1)S(1)}, bf16[4,6144]{1,0:T(4,128)(2,1)}, u32[]{:S(2)}) copy-start(bf16[4,6144]{1,0:T(4,128)(2,1)} %refs_2_.1) | copy-start | bytes 147460
  11.7 7.7 %collective-permute-start.2 = (bf16[8,12416]{1,0:T(8,128)(2,1)S(1)}, bf16[8,12416]{1,0:T(8,128)(2,1)S(1)}, u32[]{:S(2)}, u32[]{:S(2)}) collective-permute-start(bf16[8,12416]{1,0:T(8,128)(2,1)S(1)} %maximum_maximum_fusion.refs_2_.own), channel_id=1, source_target_pairs={{0,4},{1,3},{2,6},{3,1},{4,0},{5,7},{6,2},{7,5},{8,12},{9,11},{10,... | collective-permute-start | bytes 595976 | tf_op jit(solution)/shard_map/ppermute | solution.py:330
  13.2 8.4 %collective-permute-start.3 = (bf16[8,12416]{1,0:T(8,128)(2,1)S(1)}, bf16[8,12416]{1,0:T(8,128)(2,1)S(1)}, u32[]{:S(2)}, u32[]{:S(2)}) collective-permute-start(bf16[8,12416]{1,0:T(8,128)(2,1)S(1)} %maximum_maximum_fusion.refs_2_.own), channel_id=1, source_target_pairs={{0,2},{1,5},{2,0},{3,7},{4,6},{5,1},{6,4},{7,3},{8,10},{9,13},{10,... | collective-permute-start | bytes 595976 | tf_op jit(solution)/shard_map/ppermute | solution.py:330
  19.5 5.8 %collective-permute-start.4 = (bf16[8,6272]{1,0:T(8,128)(2,1)S(1)}, bf16[8,6272]{1,0:T(8,128)(2,1)S(1)}, u32[]{:S(2)}, u32[]{:S(2)}) collective-permute-start(bf16[8,6272]{1,0:T(8,128)(2,1)S(1)} %get-tuple-element.44), channel_id=1, source_target_pairs={{0,2},{1,5},{2,0},{3,7},{4,6},{5,1},{6,4},{7,3},{8,10},{9,13},{10,... | collective-permute-start | bytes 301064 | tf_op jit(solution)/shard_map/ppermute | solution.py:330
  20.1 5.2 %collective-permute-start.5 = (bf16[8,6144]{1,0:T(8,128)(2,1)S(1)}, bf16[8,6144]{1,0:T(8,128)(2,1)S(1)}, u32[]{:S(2)}, u32[]{:S(2)}) collective-permute-start(bf16[8,6144]{1,0:T(8,128)(2,1)S(1)} %get-tuple-element.45), channel_id=1, source_target_pairs={{0,2},{1,5},{2,0},{3,7},{4,6},{5,1},{6,4},{7,3},{8,10},{9,13},{10,... | collective-permute-start | bytes 294920 | tf_op jit(solution)/shard_map/ppermute | solution.py:330
  25.3 1.8 %collective-permute-start.7 = (bf16[32,6144]{1,0:T(8,128)(2,1)S(1)}, bf16[32,6144]{1,0:T(8,128)(2,1)S(1)}, u32[]{:S(2)}, u32[]{:S(2)}) collective-permute-start(bf16[32,6144]{1,0:T(8,128)(2,1)S(1)} %get-tuple-element.47), channel_id=1, source_target_pairs={{0,1},{1,0},{2,3},{3,2},{4,5},{5,4},{6,7},{7,6},{8,9},{9,8},{10,11... | collective-permute-start | bytes 1179656 | tf_op jit(solution)/shard_map/ppermute | solution.py:330
  25.4 3.8 %collective-permute-start.6 = (bf16[32,6272]{1,0:T(8,128)(2,1)S(1)}, bf16[32,6272]{1,0:T(8,128)(2,1)S(1)}, u32[]{:S(2)}, u32[]{:S(2)}) collective-permute-start(bf16[32,6272]{1,0:T(8,128)(2,1)S(1)} %get-tuple-element.46), channel_id=1, source_target_pairs={{0,1},{1,0},{2,3},{3,2},{4,5},{5,4},{6,7},{7,6},{8,9},{9,8},{10,11... | collective-permute-start | bytes 1204232 | tf_op jit(solution)/shard_map/ppermute | solution.py:330
  35.3 1.8 %collective-permute-start.8 = (bf16[32,6272]{1,0:T(8,128)(2,1)S(1)}, bf16[32,6272]{1,0:T(8,128)(2,1)S(1)}, u32[]{:S(2)}, u32[]{:S(2)}) collective-permute-start(bf16[32,6272]{1,0:T(8,128)(2,1)S(1)} %get-tuple-element.61), channel_id=1, source_target_pairs={{0,1},{1,0},{2,3},{3,2},{4,5},{5,4},{6,7},{7,6},{8,9},{9,8},{10,11... | collective-permute-start | bytes 1204232 | tf_op jit(solution)/shard_map/ppermute | solution.py:330
  37.2 5.8 %collective-permute-start.9 = (bf16[16,6272]{1,0:T(8,128)(2,1)S(1)}, bf16[16,6272]{1,0:T(8,128)(2,1)S(1)}, u32[]{:S(2)}, u32[]{:S(2)}) collective-permute-start(bf16[16,6272]{1,0:T(8,128)(2,1)S(1)} %get-tuple-element.63), channel_id=1, source_target_pairs={{0,2},{1,5},{2,0},{3,7},{4,6},{5,1},{6,4},{7,3},{8,10},{9,13},{10,... | collective-permute-start | bytes 602120 | tf_op jit(solution)/shard_map/ppermute | solution.py:330
  43.2 4.7 %collective-permute-start.10 = (bf16[8,6272]{1,0:T(8,128)(2,1)S(1)}, bf16[8,6272]{1,0:T(8,128)(2,1)S(1)}, u32[]{:S(2)}, u32[]{:S(2)}) collective-permute-start(bf16[8,6272]{1,0:T(8,128)(2,1)S(1)} %get-tuple-element.65), channel_id=1, source_target_pairs={{0,4},{1,3},{2,6},{3,1},{4,0},{5,7},{6,2},{7,5},{8,12},{9,11},{10,... | collective-permute-start | bytes 301064 | tf_op jit(solution)/shard_map/ppermute | solution.py:330
  48.0 5.6 %collective-permute-start.11 = (bf16[4,6272]{1,0:T(4,128)(2,1)S(1)}, bf16[4,6272]{1,0:T(4,128)(2,1)S(1)}, u32[]{:S(2)}, u32[]{:S(2)}) collective-permute-start(bf16[4,6272]{1,0:T(4,128)(2,1)S(1)} %get-tuple-element.67), channel_id=1, source_target_pairs={{0,8},{1,9},{2,10},{3,11},{4,12},{5,13},{6,14},{7,15},{8,0},{9,1},... | collective-permute-start | bytes 150536 | tf_op jit(solution)/shard_map/ppermute | solution.py:330

commit v10 on v8

v10 whole, which is shorter than its diff:
```python
import functools

import jax
import jax.numpy as jnp
from jax import lax
from jax.experimental import pallas as pl
from jax.experimental.pallas import tpu as pltpu
from jax.sharding import PartitionSpec as P

F32 = jnp.float32
BF16 = jnp.bfloat16
LANES = 128
MIB = 1 << 20


def dot(left, right, dims):
    return lax.dot_general(left, right, (dims, ((), ())), preferred_element_type=F32)


def whole(count):
    return [pl.BlockSpec(memory_space=pltpu.VMEM)] * count


def call(kernel, outs, args, flops, moved, limit=8):
    return pl.pallas_call(
        kernel,
        out_shape=[jax.ShapeDtypeStruct(s, t) for s, t in outs],
        in_specs=whole(len(args)),
        out_specs=whole(len(outs)),
        compiler_params=pltpu.CompilerParams(vmem_limit_bytes=limit * MIB),
        cost_estimate=pl.CostEstimate(flops=flops, bytes_accessed=moved, transcendentals=0),
    )(*args)


def in_hbm(array):
    return pltpu.with_memory_space_constraint(array, pltpu.HBM)


def in_vmem(array):
    return pltpu.with_memory_space_constraint(array, pltpu.VMEM)


def lane_pair(rows, first, second):
    lane = lax.broadcasted_iota(jnp.int32, (rows, LANES), 1)
    return jnp.where(lane == 0, first, jnp.where(lane == 1, second, 0.0))


def split_pair(value):
    high = value.astype(BF16).astype(F32)
    return lane_pair(value.shape[0], high, value - high)


def router_kernel(
    tokens_in,
    logits_in,
    ref_in,
    routes_in,
    y_in,
    send,
    entropy,
    divergence,
    base,
    coef,
    select_out,
    tokens,
    logits,
    ref_logits,
    routes,
    y,
    sems,
):
    sources = (logits_in, ref_in, routes_in, tokens_in, y_in)
    targets = (logits, ref_logits, routes, tokens, y)
    copies = [
        pltpu.make_async_copy(s, t, sems.at[i]) for i, (s, t) in enumerate(zip(sources, targets))
    ]
    for copy in copies:
        copy.start()
    for copy in copies[:3]:
        copy.wait()
    slots, width = send.shape[0], tokens.shape[1]
    experts, count = logits.shape
    x, r = logits[...], ref_logits[...]
    shifted = x - jnp.max(x, axis=0, keepdims=True)
    policy_log = shifted - jnp.log(jnp.sum(jnp.exp(shifted), axis=0, keepdims=True))
    shifted = r - jnp.max(r, axis=0, keepdims=True)
    frozen_log = shifted - jnp.log(jnp.sum(jnp.exp(shifted), axis=0, keepdims=True))
    probs = jnp.exp(policy_log)
    ratio = policy_log - frozen_log
    div = jnp.sum(probs * ratio, axis=0, keepdims=True)
    entropy[...] = -jnp.sum(probs * policy_log, axis=0, keepdims=True)
    divergence[...] = div
    base[...] = probs * (ratio - div)
    first, second = routes[0:1, :], routes[1:2, :]
    routed = jnp.where((first == 0) | (second == 0), 1.0, 0.0)
    expert = lax.broadcasted_iota(jnp.int32, (experts, count), 0)
    partner_hot = jnp.where(expert == first + second, 1.0, 0.0)
    partner_logit = jnp.sum(x * partner_hot, axis=0, keepdims=True)
    gate = jnp.where(routed > 0.0, jax.nn.sigmoid(x[0:1, :] - partner_logit), 0.0)
    coef[...] = (jnp.where(expert == 0, 1.0, 0.0) - partner_hot) * (gate * (1.0 - gate))
    token = lax.broadcasted_iota(jnp.int32, (1, count), 1)
    position = jnp.full((1, count), -1.0, F32)
    for t in range(count):
        position += jnp.where(token >= t, routed[:, t : t + 1], 0.0)
    slot = lax.broadcasted_iota(jnp.int32, (count, count), 0)
    hit = (slot == position.astype(jnp.int32)) & (routed > 0.0) & (slot < slots)
    select = jnp.where(hit, 1.0, 0.0)
    select_out[...] = select
    gate_low = gate.astype(BF16).astype(F32)
    g_slots = jnp.sum(select * gate_low, axis=1, keepdims=True)
    wide = width + LANES
    send[:, width:wide] = jnp.broadcast_to(g_slots[:slots], (slots, LANES)).astype(BF16)
    copies[3].wait()
    x_slots = dot(select.astype(BF16), tokens[...], ((1,), (0,)))
    send[:, :width] = x_slots[:slots].astype(BF16)
    copies[4].wait()
    send[:, wide:] = y[...]


def fetch_copies(sources, targets, sems):
    parts = sems.shape[1]
    copies = []
    for k, (source, target) in enumerate(zip(sources, targets)):
        step = source.shape[0] // parts
        for i in range(parts):
            at = pl.ds(i * step, step)
            copies.append(pltpu.make_async_copy(source.at[at], target.at[at], sems.at[k, i]))
    return copies


def fetch_kernel(count, *refs):
    sources, block, refs = refs[:count], refs[count], refs[count + 1 :]
    targets, out, sems = refs[:count], refs[count], refs[count + 1]
    copies = fetch_copies(sources, targets, sems)
    for copy in copies:
        copy.start()
    out[...] = block[...]
    for copy in copies:
        copy.wait()


def fetch(weights, block):
    count = len(weights)
    out = pl.pallas_call(
        functools.partial(fetch_kernel, count),
        out_shape=[pltpu.VMEM(w.shape, w.dtype) for w in weights]
        + [jax.ShapeDtypeStruct(block.shape, block.dtype)],
        in_specs=[pl.BlockSpec(memory_space=pl.ANY)] * count + whole(1),
        out_specs=whole(count + 1),
        scratch_shapes=[pltpu.SemaphoreType.DMA((count, 4))],
        compiler_params=pltpu.CompilerParams(vmem_limit_bytes=8 * MIB),
        cost_estimate=pl.CostEstimate(
            flops=0, bytes_accessed=2 * sum(w.size for w in weights), transcendentals=0
        ),
    )(*[in_hbm(w) for w in weights], block)
    return [in_vmem(w) for w in out[:count]] + [out[count]]


def join_kernel(own, near, far, most):
    parts = [ref[...].astype(F32) for ref in (own, near, far)]
    most[...] = jnp.concatenate(parts).astype(BF16)


def split_kernel(near, far, near_x, far_y):
    near_x[...] = near[:, : near_x.shape[1]]
    far_y[...] = far[:, near_x.shape[1] :]


def expert_kernel(*refs):
    pieces, (down_w, gate_w, up_w), refs = refs[:6], refs[6:9], refs[9:]
    send, keep, weighted_t, d_both, x_t, y, x = refs
    rows, width, hidden_dim = x.shape[0], gate_w.shape[0], gate_w.shape[1]
    wide = width + LANES
    half = rows // 2
    own, last_x, last_y, other, other_x, other_y = pieces
    for c in range(0, wide, LANES):
        at = pl.ds(c, LANES)
        parts = [ref[:, at].astype(F32) for ref in (own, last_x, other, other_x)]
        block = jnp.concatenate(parts)
        x[:, at] = block.astype(BF16)
        if c < width:
            x_t[at, :] = block.T.astype(BF16)
    for c in range(0, width, LANES):
        at, from_wide = pl.ds(c, LANES), pl.ds(wide + c, LANES)
        parts = [own[:, from_wide], last_y[:, at], other[:, from_wide], other_y[:, at]]
        y[:, at] = jnp.concatenate([part.astype(F32) for part in parts]).astype(BF16)
    pre_gate = dot(x[:, :width], gate_w[...], ((1,), (0,)))
    pre_up = dot(x[:, :width], up_w[...], ((1,), (0,)))
    back = dot(y[...], down_w[...], ((1,), (1,)))
    g = x[:, width:][:, 0:1].astype(F32)
    sig = jax.nn.sigmoid(pre_gate)
    act = pre_gate * sig
    hidden = act * pre_up
    weighted_t[...] = (g * hidden).T.astype(BF16)
    products = jnp.sum(hidden * back, axis=1, keepdims=True)
    scaled = g * back
    d_both[:, :hidden_dim] = (
        scaled * pre_up * sig * (1.0 + pre_gate * (1.0 - sig))
    ).astype(BF16)
    d_both[:, hidden_dim:] = (scaled * act).astype(BF16)
    keep[:, width:] = lane_pair(half, products[:half], 0.0)
    send[:, width:] = split_pair(products[half:]).astype(BF16)
    wide = 1024
    for i in range(width // wide):
        at = pl.ds(i * wide, wide)
        part = dot(d_both[:, :hidden_dim], gate_w[at, :], ((1,), (1,)))
        part += dot(d_both[:, hidden_dim:], up_w[at, :], ((1,), (1,)))
        keep[:, at] = part[:half]
        send[:, at] = part[half:].astype(BF16)


def fold_kernel(have, got, keep, send):
    half = keep.shape[0]
    width = keep.shape[1] - LANES
    total = have[:, :width] + got[:, :width].astype(F32)
    keep[:, :width] = total[:half]
    send[:, :width] = total[half:].astype(BF16)
    tail = have[:, width:] + got[:, width:].astype(F32)
    value = tail[:, 0:1] + tail[:, 1:2]
    keep[:, width:] = lane_pair(half, value[:half], 0.0)
    send[:, width:] = split_pair(value[half:]).astype(BF16)


def home_kernel(
    row, have, got, select, base, coef, *refs
):
    rest, grad_tokens, grad_logits, gate_out, up_out, sems = refs[:2], *refs[-5:]
    late = late_copies(row, rest, (gate_out, up_out), sems)
    for copy in late:
        copy.start()
    slots = have.shape[0]
    width = have.shape[1] - LANES
    count = select.shape[0]
    total = (have[:, :width] + got[:, :width].astype(F32)).astype(BF16)
    padded = jnp.concatenate([total, jnp.zeros((count - slots, width), BF16)], axis=0)
    grad_tokens[...] = dot(select[...].astype(BF16), padded, ((0,), (0,))).astype(BF16)
    tail = have[:, width:] + got[:, width:].astype(F32)
    value = tail[:, 0:1] + tail[:, 1:2]
    token_products = jnp.sum(select[0:slots, :] * value, axis=0, keepdims=True)
    grad_logits[...] = base[...] + coef[...] * token_products
    for copy in late:
        copy.wait()


def tiles(out, left, right):
    tall = 128
    for c in range(0, right.shape[1], 256):
        for r in range(0, left.shape[0], tall):
            part = dot(left[r : r + tall], right[:, c : c + 256], ((1,), (0,)))
            out[r : r + tall, c : c + 256] = part.astype(BF16)


def loop(count, body):
    for i in range(count):
        body(i)


def late_copies(row, sources, targets, sems):
    step = sources[0].shape[0]
    return [
        pltpu.make_async_copy(source, target.at[pl.ds(row, step)], sems.at[k])
        for k, (source, target) in enumerate(zip(sources, targets))
    ]


def grads_kernel(first_row, x_t, d_both, *refs):
    gate_out, up_out, gate_left, up_left, gate_buf, up_buf, sems = refs[-7:]
    chunks, step, cols = gate_buf.shape
    copies = []
    if first_row:
        copies += late_copies(first_row - step, refs[:2], (gate_out, up_out), sems.at[chunks])
        for copy in copies:
            copy.start()
    for i in range(chunks + 1):
        at = pl.ds(first_row + i * step, step)
        outs = (gate_buf, up_buf) if i < chunks else (gate_left, up_left)
        for k, target in enumerate((gate_out, up_out)):
            tile = outs[k].at[i] if i < chunks else outs[k]
            tiles(tile, x_t.at[at], d_both.at[:, pl.ds(k * cols, cols)])
            if i < chunks:
                copy = pltpu.make_async_copy(tile, target.at[at], sems.at[i, k])
                copy.start()
                copies.append(copy)
    for copy in copies:
        copy.wait()


def first_kernel(weighted_t, y, x_t, d_both, down_out, *refs):
    down_buf, down_sems = refs[4:6]
    chunks, _, step = down_buf.shape
    copies = []
    for i in range(chunks):
        at = pl.ds(i * step, step)
        tiles(down_buf.at[i], weighted_t, y.at[:, at])
        copies.append(pltpu.make_async_copy(down_buf.at[i], down_out.at[:, at], down_sems.at[i]))
        copies[i].start()
    grads_kernel(0, x_t, d_both, *refs[:4], *refs[6:])
    for copy in copies:
        copy.wait()


def grads_of(x_t, d_both, first_row, rows, before, down=()):
    width, slots = x_t.shape
    cols = d_both.shape[1] // 2
    step = 256
    chunks = rows // step - 1
    anywhere = pl.BlockSpec(memory_space=pl.ANY)
    outs = [jax.ShapeDtypeStruct((width, cols), BF16)] * 2
    outs += [jax.ShapeDtypeStruct((step, cols), BF16)] * 2
    out_specs = [anywhere] * 2 + whole(2)
    scratch = [
        pltpu.VMEM((chunks, step, cols), BF16),
        pltpu.VMEM((chunks, step, cols), BF16),
        pltpu.SemaphoreType.DMA((chunks + 1, 2)),
    ]
    kernel = functools.partial(grads_kernel, first_row)
    if down:
        kernel = first_kernel
        wide = 1024
        outs = [jax.ShapeDtypeStruct((cols, width), BF16)] + outs
        out_specs = [anywhere] + out_specs
        scratch = [
            pltpu.VMEM((width // wide, cols, wide), BF16),
            pltpu.SemaphoreType.DMA((width // wide,)),
        ] + scratch
    elements = 2 * rows * cols + (width * cols if down else 0)
    return pl.pallas_call(
        kernel,
        out_shape=outs,
        in_specs=whole(2 + len(down)) + (whole(2) + [anywhere] * 2 if before else []),
        out_specs=out_specs,
        scratch_shapes=scratch,
        input_output_aliases={4: 0, 5: 1} if before else {},
        compiler_params=pltpu.CompilerParams(vmem_limit_bytes=20 * MIB),
        cost_estimate=pl.CostEstimate(
            flops=8 * slots * elements, bytes_accessed=2 * elements, transcendentals=0
        ),
    )(*down, x_t, d_both, *before[2:], *before[:2])


def make_shards(n):
    levels = []
    bit = n // 2
    while bit > 4:
        levels.append((bit, bit))
        bit //= 2
    levels += [(4, 2), (2, 4)]

    def swap(block, bits):
        return lax.ppermute(block, "blk", [(i, i ^ bits[i % 2]) for i in range(n)])

    def shards(
        tokens, cotangent, gate_weight, up_weight, down_weight, logits, ref_logits, routes
    ):
        count, width = tokens.shape
        slots = cotangent.shape[0]
        experts = logits.shape[1]
        hidden = down_weight.shape[0]
        rows = n * slots
        wide = width + LANES
        anywhere = pl.BlockSpec(memory_space=pl.ANY)

        send, entropy, divergence, base, coef, select = pl.pallas_call(
            router_kernel,
            out_shape=[
                jax.ShapeDtypeStruct((slots, wide + width), BF16),
                jax.ShapeDtypeStruct((1, count), F32),
                jax.ShapeDtypeStruct((1, count), F32),
                jax.ShapeDtypeStruct((experts, count), F32),
                jax.ShapeDtypeStruct((experts, count), F32),
                jax.ShapeDtypeStruct((count, count), F32),
            ],
            in_specs=[anywhere] * 5,
            out_specs=whole(6),
            scratch_shapes=[
                pltpu.VMEM((count, width), BF16),
                pltpu.VMEM((experts, count), F32),
                pltpu.VMEM((experts, count), F32),
                pltpu.VMEM((2, count), jnp.int32),
                pltpu.VMEM((slots, width), BF16),
                pltpu.SemaphoreType.DMA((5,)),
            ],
            compiler_params=pltpu.CompilerParams(vmem_limit_bytes=8 * MIB),
            cost_estimate=pl.CostEstimate(
                flops=1 << 20, bytes_accessed=1 << 24, transcendentals=0
            ),
        )(*[in_hbm(a) for a in (tokens, logits.T, ref_logits.T, routes.T, cotangent)])

        got = swap(send, levels[0])
        gate_w, own = fetch([gate_weight], send)
        own = jnp.concatenate([own, got])
        for bits in levels[1:-2]:
            own = jnp.concatenate([own, swap(own, bits)])
        near = swap(own, levels[-2])
        far = swap(own, levels[-1])
        up_w, down_w, own = fetch([up_weight, down_weight], own)
        few = own.shape[0]
        near_x, far_y = call(
            split_kernel, [((few, wide), BF16), ((few, width), BF16)], [near, far], 0, 1 << 18
        )
        (most,) = call(
            join_kernel, [((3 * few, wide + width), BF16)], [own, near, far], 0, 1 << 23
        )
        last_x = swap(near_x, levels[-1])
        last_y = swap(far_y, levels[-2])
        pieces = [most, last_x, last_y]
        pieces += [swap(piece, (1, 1)) for piece in pieces]

        work = 2 * rows * width * hidden
        half = rows // 2
        low, keep, weighted_t, d_both, x_t, y_all = pl.pallas_call(
            expert_kernel,
            out_shape=[
                jax.ShapeDtypeStruct((half, wide), BF16),
                jax.ShapeDtypeStruct((half, wide), F32),
                jax.ShapeDtypeStruct((hidden, rows), BF16),
                jax.ShapeDtypeStruct((rows, 2 * hidden), BF16),
                jax.ShapeDtypeStruct((width, rows), BF16),
                jax.ShapeDtypeStruct((rows, width), BF16),
            ],
            in_specs=whole(9),
            out_specs=whole(6),
            scratch_shapes=[pltpu.VMEM((rows, wide), BF16)],
            compiler_params=pltpu.CompilerParams(vmem_limit_bytes=16 * MIB),
            cost_estimate=pl.CostEstimate(
                flops=16 * work, bytes_accessed=4 * width * hidden, transcendentals=0
            ),
        )(*pieces, down_w, gate_w, up_w)

        for bits in [(1, 1)] + levels[::-1]:
            got = swap(low, bits)
            if bits == levels[0]:
                break
            half //= 2
            keep, low = call(
                fold_kernel,
                [((half, wide), F32), ((half, wide), BF16)],
                [keep, got],
                4 * half * wide,
                16 * half * wide,
            )

        cuts = [0, width // 3, 2 * width // 3, width]
        grad_down, *pair = grads_of(x_t, d_both, 0, cuts[1], (), (weighted_t, y_all))
        for start, stop in zip(cuts[1:], cuts[2:]):
            pair = grads_of(x_t, d_both, start, stop - start, tuple(pair))
        grad_gate, grad_up, *rest = pair

        grad_tokens, grad_logits, grad_gate, grad_up = pl.pallas_call(
            functools.partial(home_kernel, width - rest[0].shape[0]),
            out_shape=[
                jax.ShapeDtypeStruct((count, width), BF16),
                jax.ShapeDtypeStruct((experts, count), F32),
                jax.ShapeDtypeStruct(grad_gate.shape, BF16),
                jax.ShapeDtypeStruct(grad_up.shape, BF16),
            ],
            in_specs=whole(7) + [anywhere] * 2,
            out_specs=whole(2) + [anywhere] * 2,
            scratch_shapes=[pltpu.SemaphoreType.DMA((2,))],
            input_output_aliases={7: 2, 8: 3},
            compiler_params=pltpu.CompilerParams(vmem_limit_bytes=8 * MIB),
            cost_estimate=pl.CostEstimate(
                flops=1 << 20, bytes_accessed=1 << 18, transcendentals=0
            ),
        )(keep, got, select, base, coef, *rest, grad_gate, grad_up)
        return (
            grad_gate,
            grad_up,
            grad_down,
            grad_tokens,
            grad_logits.T,
            entropy.reshape(count),
            divergence.reshape(count),
        )

    return shards


def solution(mesh):
    in_specs = (
        P(("grp", "blk"), None),
        P(("grp", "blk"), None),
        P(None, "blk"),
        P(None, "blk"),
        P("blk", None),
        P(("grp", "blk"), None),
        P(("grp", "blk"), None),
        P(("grp", "blk"), None),
    )
    out_specs = (
        P("grp", "blk"),
        P("grp", "blk"),
        P(("grp", "blk"), None),
        P(("grp", "blk"), None),
        P(("grp", "blk"), None),
        P(("grp", "blk")),
        P(("grp", "blk")),
    )
    return jax.shard_map(
        make_shards(mesh.shape["blk"]),
        mesh=mesh,
        in_specs=in_specs,
        out_specs=out_specs,
        check_vma=False,
    )
```

time: 79.3 us -> 54.7 us (0.69)
  local copies, waits for them, and re-layouts: 18 us -> 0 us
  Pallas kernels: 31.3 us -> 28.2 us
  other arithmetic: 2.29 us -> 0.1 us
  starting transfers between devices: 14.6 us -> 12.6 us
  waiting for transfers between devices: 12 us -> 12.9 us
    unnamed x15 -> x0, local copies, waits for them, and re-layouts: 14.8 us -> none
    pallas_call x7 -> x6, Pallas kernels: 22.3 us -> 17.7 us  [the longest x3 8.69 us: grads_of(): pl.pallas_call(kernel, out_shape=outs, in_specs=whole(2 + len(down)) + (w...]
    concatenate x4 -> x1, other arithmetic: 2.29 us -> 0.1 us  [shards(): own = jnp.concatenate([own, got])]
    pallas_call x1, Pallas kernels: 6.06 us -> 8.19 us  [shards(): pl.pallas_call(expert_kernel, out_shape=[jax.ShapeDtypeStruct((half, wide...]
    reshape x2 -> x0, local copies, waits for them, and re-layouts: 1.93 us -> none  [join(): block = block.reshape(block.shape[0] * block.shape[1], block.shape[2])]
    ppermute x12, starting transfers between devices: 14.6 us -> 12.6 us  [swap(): return lax.ppermute(block, 'blk', [(i, i ^ bits[i % 2]) for i in range(n)])]
    concatenate x1 -> x0, local copies, waits for them, and re-layouts: 1.02 us -> none  [join(): return jnp.concatenate([block, swap(block, (1, 1))])]
    ppermute x12, waiting for transfers between devices: 12 us -> 12.9 us  [swap(): return lax.ppermute(block, 'blk', [(i, i ^ bits[i % 2]) for i in range(n)])]
  transfers between devices with their start and end apart: 12 -> 12, of which waited for: 4 -> 9; matrix products, arithmetic and copies ran while one was open for 7% -> 0% of each run, Pallas kernels for 28% -> 30%
where the time goes in v10:
time: 54.7 us; the launch traced here: 54.5 us
  Pallas kernels  28.2 us (52%)
  waiting for transfers between devices  12.9 us (24%)
  starting transfers between devices  12.6 us (23%)
  between operations  0.72 us (1%)
    ppermute x12, waiting for transfers between devices, swap(): return lax.ppermute(block, 'blk', [(i, i ^ bits[i % 2]) for i in range(n)])  12.9 us
    ppermute x12, starting transfers between devices, swap(): return lax.ppermute(block, 'blk', [(i, i ^ bits[i % 2]) for i in range(n)])  12.6 us
    pallas_call x3, Pallas kernels, grads_of(): pl.pallas_call(kernel, out_shape=outs, in_specs=whole(2 + len(down)) + (w...  8.69 us
    pallas_call x1, Pallas kernels, shards(): pl.pallas_call(expert_kernel, out_shape=[jax.ShapeDtypeStruct((half, wide...  8.19 us
    pallas_call x2, Pallas kernels, fetch(): pl.pallas_call(functools.partial(fetch_kernel, count), out_shape=[pltpu.V...  7.57 us
    pallas_call x1, Pallas kernels, shards(): pl.pallas_call(router_kernel, out_shape=[jax.ShapeDtypeStruct((slots, wid...  1.72 us
    pallas_call x1, Pallas kernels, shards(): pl.pallas_call(functools.partial(home_kernel, width - rest[0].shape[0]),...  1.49 us
  transfers between devices with their start and end apart: 12, of which 9 were waited for; matrix products, arithmetic and copies ran while one was open for 0% of the time, Pallas kernels for 30%

profile of v10, /device:TPU:0, one launch (start us, length us, event | category | flops | bytes accessed | tf_op | source)
XLA Modules:
  0.0 54.5 jit_solution(6832206681383443304)
XLA Ops:
  0.6 1.7 %shard_map.135 = (bf16[4,12416]{1,0:T(4,128)(2,1)S(1)}, f32[1,16]{1,0:T(1,128)}, f32[1,16]{1,0:T(1,128)}, f32[8,16]{1,0:T(8,128)S(1)}, f32[8,16]{1,0:T(8,128)S(1)}, /*index=5*/f32[16,16]{1,0:T(8,128)S(1)}) custom-call(bf16[16,6144]{1,0:T(8,128)(2,1)} %tokens_in.1, f32[8,16]{1,0:T(8,128)} %bitcast.6, f32[8,16]{1,0:T(8,128)} %bitcast.7, s32[2,16]{1,0:T(2,128)} %bitcast.8, ...), custom_call_target="tpu_custom_call" | custom-call | flops 1048576 | bytes 16777216 | tf_op jit(solution)/shard_map/pallas_call | solution.py:363
  2.4 4.1 %collective-permute-start = (bf16[4,12416]{1,0:T(4,128)(2,1)S(1)}, bf16[4,12416]{1,0:T(4,128)(2,1)S(1)}, u32[]{:S(2)}, u32[]{:S(2)}) collective-permute-start(bf16[4,12416]{1,0:T(4,128)(2,1)S(1)} %get-tuple-element.49.refs_1_), channel_id=1, source_target_pairs={{0,8},{1,9},{2,10},{3,11},{4,12},{5,13},{6,14},{7,15},{8,0},{9,1},... | collective-permute-start | bytes 297992 | tf_op jit(solution)/shard_map/ppermute | solution.py:350
  6.5 2.9 %shard_map.136 = (bf16[6144,512]{1,0:T(8,128)(2,1)S(1)}, bf16[4,12416]{1,0:T(4,128)(2,1)S(1)}) custom-call(bf16[6144,512]{1,0:T(8,128)(2,1)} %refs_0_.2, bf16[4,12416]{1,0:T(4,128)(2,1)S(1)} %get-tuple-element.49.refs_1_), custom_call_target="tpu_custom_call" | custom-call | bytes 6291456 | tf_op jit(solution)/shard_map/pallas_call | solution.py:144
  9.3 2.1 %collective-permute-done = bf16[4,12416]{1,0:T(4,128)(2,1)S(1)} collective-permute-done((bf16[4,12416]{1,0:T(4,128)(2,1)S(1)}, bf16[4,12416]{1,0:T(4,128)(2,1)S(1)}, u32[]{:S(2)}, u32[]{:S(2)}) %collective-permute-start) | collective-permute-done | bytes 99360 | tf_op jit(solution)/shard_map/ppermute | solution.py:350
  11.4 0.1 pad_maximum_fusion.refs_2_
  11.5 1.6 %collective-permute-start.2 = (bf16[8,12416]{1,0:T(8,128)(2,1)S(1)}, bf16[8,12416]{1,0:T(8,128)(2,1)S(1)}, u32[]{:S(2)}, u32[]{:S(2)}) collective-permute-start(bf16[8,12416]{1,0:T(8,128)(2,1)S(1)} %pad_maximum_fusion.refs_2_), channel_id=1, source_target_pairs={{0,2},{1,5},{2,0},{3,7},{4,6},{5,1},{6,4},{7,3},{8,10},{9,13},{10,... | collective-permute-start | bytes 595976 | tf_op jit(solution)/shard_map/ppermute | solution.py:350
  13.1 0.7 %collective-permute-start.1 = (bf16[8,12416]{1,0:T(8,128)(2,1)S(1)}, bf16[8,12416]{1,0:T(8,128)(2,1)S(1)}, u32[]{:S(2)}, u32[]{:S(2)}) collective-permute-start(bf16[8,12416]{1,0:T(8,128)(2,1)S(1)} %pad_maximum_fusion.refs_2_), channel_id=1, source_target_pairs={{0,4},{1,3},{2,6},{3,1},{4,0},{5,7},{6,2},{7,5},{8,12},{9,11},{10,... | collective-permute-start | bytes 595976 | tf_op jit(solution)/shard_map/ppermute | solution.py:350
  13.8 4.7 %shard_map.137 = (bf16[6144,512]{1,0:T(8,128)(2,1)S(1)}, bf16[512,6144]{1,0:T(8,128)(2,1)S(1)}, bf16[8,12416]{1,0:T(8,128)(2,1)S(1)}) custom-call(bf16[6144,512]{1,0:T(8,128)(2,1)} %refs_0_.3, bf16[512,6144]{1,0:T(8,128)(2,1)} %refs_1_.1, bf16[8,12416]{1,0:T(8,128)(2,1)S(1)} %pad_maximum_fusion.refs_2_), custom_call_target="tpu_custom_call" | custom-call | bytes 12582912 | tf_op jit(solution)/shard_map/pallas_call | solution.py:144
  18.5 0.4 collective-permute-done.2.far
  18.9 0.0 collective-permute-done.1.near
  18.9 0.1 collective-permute-start.5
  19.0 1.6 %collective-permute-start.3 = (bf16[8,6272]{1,0:T(8,128)(2,1)S(1)}, bf16[8,6272]{1,0:T(8,128)(2,1)S(1)}, u32[]{:S(2)}, u32[]{:S(2)}) collective-permute-start(bf16[8,6272]{1,0:T(8,128)(2,1)S(1)} %get-tuple-element.52), channel_id=1, source_target_pairs={{0,2},{1,5},{2,0},{3,7},{4,6},{5,1},{6,4},{7,3},{8,10},{9,13},{10,... | collective-permute-start | bytes 301064 | tf_op jit(solution)/shard_map/ppermute | solution.py:350
  20.6 0.3 collective-permute-start.4
  21.0 3.6 %collective-permute-done.3.refs_1_ = bf16[8,6272]{1,0:T(8,128)(2,1)S(1)} collective-permute-done((bf16[8,6272]{1,0:T(8,128)(2,1)S(1)}, bf16[8,6272]{1,0:T(8,128)(2,1)S(1)}, u32[]{:S(2)}, u32[]{:S(2)}) %collective-permute-start.3) | collective-permute-done | bytes 100384 | tf_op jit(solution)/shard_map/ppermute | solution.py:350
  24.6 0.0 collective-permute-start.6
  24.6 0.7 %collective-permute-done.4.refs_2_ = bf16[8,6144]{1,0:T(8,128)(2,1)S(1)} collective-permute-done((bf16[8,6144]{1,0:T(8,128)(2,1)S(1)}, bf16[8,6144]{1,0:T(8,128)(2,1)S(1)}, u32[]{:S(2)}, u32[]{:S(2)}) %collective-permute-start.4) | collective-permute-done | bytes 98336 | tf_op jit(solution)/shard_map/ppermute | solution.py:350
  25.3 0.0 collective-permute-start.7
  25.3 1.3 %collective-permute-done.7.refs_5_ = bf16[8,6144]{1,0:T(8,128)(2,1)S(1)} collective-permute-done((bf16[8,6144]{1,0:T(8,128)(2,1)S(1)}, bf16[8,6144]{1,0:T(8,128)(2,1)S(1)}, u32[]{:S(2)}, u32[]{:S(2)}) %collective-permute-start.7) | collective-permute-done | bytes 98336 | tf_op jit(solution)/shard_map/ppermute | solution.py:350
  26.6 0.0 collective-permute-done.6.refs_4_
  26.6 0.0 collective-permute-done.5.refs_3_
  26.6 8.2 %shard_map.140 = (bf16[32,6272]{1,0:T(8,128)(2,1)S(1)}, f32[32,6272]{1,0:T(8,128)S(1)}, bf16[512,64]{1,0:T(8,128)(2,1)S(1)}, bf16[64,1024]{1,0:T(8,128)(2,1)S(1)...) custom-call(bf16[24,12416]{1,0:T(8,128)(2,1)S(1)} %shard_map.138.refs_0_, ...), custom_call_target="tpu_custom_call" | custom-call | flops 6442450944 | bytes 12582912 | tf_op jit(solution)/shard_map/pallas_call | solution.py:411
  34.8 0.2 collective-permute-start.8
  35.0 1.6 %collective-permute-done.8.got = bf16[32,6272]{1,0:T(8,128)(2,1)S(1)} collective-permute-done((bf16[32,6272]{1,0:T(8,128)(2,1)S(1)}, bf16[32,6272]{1,0:T(8,128)(2,1)S(1)}, u32[]{:S(2)}, u32[]{:S(2)}) %collective-permute-start.8) | collective-permute-done | bytes 401440 | tf_op jit(solution)/shard_map/ppermute | solution.py:350
  36.6 0.2 shard_map.141
  36.7 0.9 %collective-permute-start.9 = (bf16[16,6272]{1,0:T(8,128)(2,1)S(1)}, bf16[16,6272]{1,0:T(8,128)(2,1)S(1)}, u32[]{:S(2)}, u32[]{:S(2)}) collective-permute-start(bf16[16,6272]{1,0:T(8,128)(2,1)S(1)} %get-tuple-element.60), channel_id=1, source_target_pairs={{0,2},{1,5},{2,0},{3,7},{4,6},{5,1},{6,4},{7,3},{8,10},{9,13},{10,... | collective-permute-start | bytes 602120 | tf_op jit(solution)/shard_map/ppermute | solution.py:350
  37.6 4.4 %shard_map.144 = (bf16[512,6144]{1,0:T(8,128)(2,1)}, bf16[6144,512]{1,0:T(8,128)(2,1)}, bf16[6144,512]{1,0:T(8,128)(2,1)}, bf16[256,512]{1,0:T(8,128)(2,1)S(1)}, bf16[256,512]{1,0:T(8,128)(2,1)S(1)}) custom-call(bf16[512,64]{1,0:T(8,128)(2,1)S(1)} %get-tuple-element.70.weighted_t, bf16[64,6144]{1,0:T(8,128)(2,1)S(1)} %get-tuple-element.71.y, ...), custom_call_target="tpu_custom_call" | custom-call | flops 2684354560 | bytes 10485760 | tf_op jit(solution)/shard_map/pallas_call | solution.py:327
  42.0 0.5 collective-permute-done.9.got
  42.5 0.1 shard_map.142
  42.7 0.5 collective-permute-start.10
  43.2 2.2 %shard_map.145 = (bf16[6144,512]{1,0:T(8,128)(2,1)}, bf16[6144,512]{1,0:T(8,128)(2,1)}, bf16[256,512]{1,0:T(8,128)(2,1)S(1)}, bf16[256,512]{1,0:T(8,128)(2,1)S(1)}) custom-call(bf16[6144,64]{1,0:T(8,128)(2,1)S(1)} %get-tuple-element.68.x_t, bf16[64,1024]{1,0:T(8,128)(2,1)S(1)} %get-tuple-element.69.d_both, ...), custom_call_target="tpu_custom_call", output_to_operand_aliasing={{0}: (4, {}), {1}: (5, {})} | custom-call | flops 1073741824 | bytes 4194304 | tf_op jit(solution)/shard_map/pallas_call | solution.py:327
  45.3 2.0 %collective-permute-done.10.got = bf16[8,6272]{1,0:T(8,128)(2,1)S(1)} collective-permute-done((bf16[8,6272]{1,0:T(8,128)(2,1)S(1)}, bf16[8,6272]{1,0:T(8,128)(2,1)S(1)}, u32[]{:S(2)}, u32[]{:S(2)}) %collective-permute-start.10) | collective-permute-done | bytes 100384 | tf_op jit(solution)/shard_map/ppermute | solution.py:350
  47.3 0.2 shard_map.143
  47.5 2.6 %collective-permute-start.11 = (bf16[4,6272]{1,0:T(4,128)(2,1)S(1)}, bf16[4,6272]{1,0:T(4,128)(2,1)S(1)}, u32[]{:S(2)}, u32[]{:S(2)}) collective-permute-start(bf16[4,6272]{1,0:T(4,128)(2,1)S(1)} %get-tuple-element.64), channel_id=1, source_target_pairs={{0,8},{1,9},{2,10},{3,11},{4,12},{5,13},{6,14},{7,15},{8,0},{9,1},... | collective-permute-start | bytes 150536 | tf_op jit(solution)/shard_map/ppermute | solution.py:350
  50.1 2.2 %shard_map.146 = (bf16[6144,512]{1,0:T(8,128)(2,1)}, bf16[6144,512]{1,0:T(8,128)(2,1)}, bf16[256,512]{1,0:T(8,128)(2,1)S(1)}, bf16[256,512]{1,0:T(8,128)(2,1)S(1)}) custom-call(bf16[6144,64]{1,0:T(8,128)(2,1)S(1)} %get-tuple-element.68.x_t, bf16[64,1024]{1,0:T(8,128)(2,1)S(1)} %get-tuple-element.69.d_both, ...), custom_call_target="tpu_custom_call", output_to_operand_aliasing={{0}: (4, {}), {1}: (5, {})} | custom-call | flops 1073741824 | bytes 4194304 | tf_op jit(solution)/shard_map/pallas_call | solution.py:327
  52.2 0.8 %collective-permute-done.11.got = bf16[4,6272]{1,0:T(4,128)(2,1)S(1)} collective-permute-done((bf16[4,6272]{1,0:T(4,128)(2,1)S(1)}, bf16[4,6272]{1,0:T(4,128)(2,1)S(1)}, u32[]{:S(2)}, u32[]{:S(2)}) %collective-permute-start.11) | collective-permute-done | bytes 50208 | tf_op jit(solution)/shard_map/ppermute | solution.py:350
  53.0 1.5 %shard_map.147 = (bf16[16,6144]{1,0:T(8,128)(2,1)}, f32[8,16]{1,0:T(8,128)}, bf16[6144,512]{1,0:T(8,128)(2,1)}, bf16[6144,512]{1,0:T(8,128)(2,1)}) custom-call(f32[4,6272]{1,0:T(4,128)S(1)} %get-tuple-element.63.have, bf16[4,6272]{1,0:T(4,128)(2,1)S(1)} %collective-permute-done.11.got, ...), custom_call_target="tpu_custom_call", output_to_operand_aliasing={{2}: (7, {}), {3}: (8, {})} | custom-call | flops 1048576 | bytes 262144 | tf_op jit(solution)/shard_map/pallas_call | solution.py:449
  (2 shorter events, 0.1 us)
Async XLA Ops:
  2.4 9.1 %collective-permute-start = (bf16[4,12416]{1,0:T(4,128)(2,1)S(1)}, bf16[4,12416]{1,0:T(4,128)(2,1)S(1)}, u32[]{:S(2)}, u32[]{:S(2)}) collective-permute-start(bf16[4,12416]{1,0:T(4,128)(2,1)S(1)} %get-tuple-element.49.refs_1_), channel_id=1, source_target_pairs={{0,8},{1,9},{2,10},{3,11},{4,12},{5,13},{6,14},{7,15},{8,0},{9,1},... | collective-permute-start | bytes 297992 | tf_op jit(solution)/shard_map/ppermute | solution.py:350
  11.5 7.4 %collective-permute-start.2 = (bf16[8,12416]{1,0:T(8,128)(2,1)S(1)}, bf16[8,12416]{1,0:T(8,128)(2,1)S(1)}, u32[]{:S(2)}, u32[]{:S(2)}) collective-permute-start(bf16[8,12416]{1,0:T(8,128)(2,1)S(1)} %pad_maximum_fusion.refs_2_), channel_id=1, source_target_pairs={{0,2},{1,5},{2,0},{3,7},{4,6},{5,1},{6,4},{7,3},{8,10},{9,13},{10,... | collective-permute-start | bytes 595976 | tf_op jit(solution)/shard_map/ppermute | solution.py:350
  13.1 5.7 %collective-permute-start.1 = (bf16[8,12416]{1,0:T(8,128)(2,1)S(1)}, bf16[8,12416]{1,0:T(8,128)(2,1)S(1)}, u32[]{:S(2)}, u32[]{:S(2)}) collective-permute-start(bf16[8,12416]{1,0:T(8,128)(2,1)S(1)} %pad_maximum_fusion.refs_2_), channel_id=1, source_target_pairs={{0,4},{1,3},{2,6},{3,1},{4,0},{5,7},{6,2},{7,5},{8,12},{9,11},{10,... | collective-permute-start | bytes 595976 | tf_op jit(solution)/shard_map/ppermute | solution.py:350
  18.9 7.6 %collective-permute-start.5 = (bf16[24,12416]{1,0:T(8,128)(2,1)S(1)}, bf16[24,12416]{1,0:T(8,128)(2,1)S(1)}, u32[]{:S(2)}, u32[]{:S(2)}) collective-permute-start(bf16[24,12416]{1,0:T(8,128)(2,1)S(1)} %shard_map.138.refs_0_), channel_id=1, source_target_pairs={{0,1},{1,0},{2,3},{3,2},{4,5},{5,4},{6,7},{7,6},{8,9},{9,8},{10,11... | collective-permute-start | bytes 1787912 | tf_op jit(solution)/shard_map/ppermute | solution.py:350
  19.0 5.5 %collective-permute-start.3 = (bf16[8,6272]{1,0:T(8,128)(2,1)S(1)}, bf16[8,6272]{1,0:T(8,128)(2,1)S(1)}, u32[]{:S(2)}, u32[]{:S(2)}) collective-permute-start(bf16[8,6272]{1,0:T(8,128)(2,1)S(1)} %get-tuple-element.52), channel_id=1, source_target_pairs={{0,2},{1,5},{2,0},{3,7},{4,6},{5,1},{6,4},{7,3},{8,10},{9,13},{10,... | collective-permute-start | bytes 301064 | tf_op jit(solution)/shard_map/ppermute | solution.py:350
  20.6 4.6 %collective-permute-start.4 = (bf16[8,6144]{1,0:T(8,128)(2,1)S(1)}, bf16[8,6144]{1,0:T(8,128)(2,1)S(1)}, u32[]{:S(2)}, u32[]{:S(2)}) collective-permute-start(bf16[8,6144]{1,0:T(8,128)(2,1)S(1)} %get-tuple-element.53), channel_id=1, source_target_pairs={{0,4},{1,3},{2,6},{3,1},{4,0},{5,7},{6,2},{7,5},{8,12},{9,11},{10,... | collective-permute-start | bytes 294920 | tf_op jit(solution)/shard_map/ppermute | solution.py:350
  24.6 2.0 %collective-permute-start.6 = (bf16[8,6272]{1,0:T(8,128)(2,1)S(1)}, bf16[8,6272]{1,0:T(8,128)(2,1)S(1)}, u32[]{:S(2)}, u32[]{:S(2)}) collective-permute-start(bf16[8,6272]{1,0:T(8,128)(2,1)S(1)} %collective-permute-done.3.refs_1_), channel_id=1, source_target_pairs={{0,1},{1,0},{2,3},{3,2},{4,5},{5,4},{6,7},{7,6},{8,9},{9,8},{10,11... | collective-permute-start | bytes 301064 | tf_op jit(solution)/shard_map/ppermute | solution.py:350
  25.3 1.3 %collective-permute-start.7 = (bf16[8,6144]{1,0:T(8,128)(2,1)S(1)}, bf16[8,6144]{1,0:T(8,128)(2,1)S(1)}, u32[]{:S(2)}, u32[]{:S(2)}) collective-permute-start(bf16[8,6144]{1,0:T(8,128)(2,1)S(1)} %collective-permute-done.4.refs_2_), channel_id=1, source_target_pairs={{0,1},{1,0},{2,3},{3,2},{4,5},{5,4},{6,7},{7,6},{8,9},{9,8},{10,11... | collective-permute-start | bytes 294920 | tf_op jit(solution)/shard_map/ppermute | solution.py:350
  34.8 1.8 %collective-permute-start.8 = (bf16[32,6272]{1,0:T(8,128)(2,1)S(1)}, bf16[32,6272]{1,0:T(8,128)(2,1)S(1)}, u32[]{:S(2)}, u32[]{:S(2)}) collective-permute-start(bf16[32,6272]{1,0:T(8,128)(2,1)S(1)} %get-tuple-element.58), channel_id=1, source_target_pairs={{0,1},{1,0},{2,3},{3,2},{4,5},{5,4},{6,7},{7,6},{8,9},{9,8},{10,11... | collective-permute-start | bytes 1204232 | tf_op jit(solution)/shard_map/ppermute | solution.py:350
  36.7 5.8 %collective-permute-start.9 = (bf16[16,6272]{1,0:T(8,128)(2,1)S(1)}, bf16[16,6272]{1,0:T(8,128)(2,1)S(1)}, u32[]{:S(2)}, u32[]{:S(2)}) collective-permute-start(bf16[16,6272]{1,0:T(8,128)(2,1)S(1)} %get-tuple-element.60), channel_id=1, source_target_pairs={{0,2},{1,5},{2,0},{3,7},{4,6},{5,1},{6,4},{7,3},{8,10},{9,13},{10,... | collective-permute-start | bytes 602120 | tf_op jit(solution)/shard_map/ppermute | solution.py:350
  42.7 4.7 %collective-permute-start.10 = (bf16[8,6272]{1,0:T(8,128)(2,1)S(1)}, bf16[8,6272]{1,0:T(8,128)(2,1)S(1)}, u32[]{:S(2)}, u32[]{:S(2)}) collective-permute-start(bf16[8,6272]{1,0:T(8,128)(2,1)S(1)} %get-tuple-element.62), channel_id=1, source_target_pairs={{0,4},{1,3},{2,6},{3,1},{4,0},{5,7},{6,2},{7,5},{8,12},{9,11},{10,... | collective-permute-start | bytes 301064 | tf_op jit(solution)/shard_map/ppermute | solution.py:350
  47.5 5.6 %collective-permute-start.11 = (bf16[4,6272]{1,0:T(4,128)(2,1)S(1)}, bf16[4,6272]{1,0:T(4,128)(2,1)S(1)}, u32[]{:S(2)}, u32[]{:S(2)}) collective-permute-start(bf16[4,6272]{1,0:T(4,128)(2,1)S(1)} %get-tuple-element.64), channel_id=1, source_target_pairs={{0,8},{1,9},{2,10},{3,11},{4,12},{5,13},{6,14},{7,15},{8,0},{9,1},... | collective-permute-start | bytes 150536 | tf_op jit(solution)/shard_map/ppermute | solution.py:350

commit v11 on v10

--- a/solution.py
+++ b/solution.py
@@ -128,64 +128,69 @@
     return copies
 
 
-def fetch_kernel(count, *refs):
-    sources, block, refs = refs[:count], refs[count], refs[count + 1 :]
-    targets, out, sems = refs[:count], refs[count], refs[count + 1]
-    copies = fetch_copies(sources, targets, sems)
+def fetch_kernel(source, after, target, sems):
+    copies = fetch_copies([source], [target], sems)
     for copy in copies:
         copy.start()
-    out[...] = block[...]
     for copy in copies:
         copy.wait()
 
 
-def fetch(weights, block):
-    count = len(weights)
+def fetch(weight, after):
+    anywhere = pl.BlockSpec(memory_space=pl.ANY)
     out = pl.pallas_call(
-        functools.partial(fetch_kernel, count),
-        out_shape=[pltpu.VMEM(w.shape, w.dtype) for w in weights]
-        + [jax.ShapeDtypeStruct(block.shape, block.dtype)],
-        in_specs=[pl.BlockSpec(memory_space=pl.ANY)] * count + whole(1),
-        out_specs=whole(count + 1),
-        scratch_shapes=[pltpu.SemaphoreType.DMA((count, 4))],
+        fetch_kernel,
+        out_shape=pltpu.VMEM(weight.shape, weight.dtype),
+        in_specs=[anywhere] * 2,
+        out_specs=whole(1)[0],
+        scratch_shapes=[pltpu.SemaphoreType.DMA((1, 4))],
         compiler_params=pltpu.CompilerParams(vmem_limit_bytes=8 * MIB),
         cost_estimate=pl.CostEstimate(
-            flops=0, bytes_accessed=2 * sum(w.size for w in weights), transcendentals=0
+            flops=0, bytes_accessed=2 * weight.size, transcendentals=0
         ),
-    )(*[in_hbm(w) for w in weights], block)
-    return [in_vmem(w) for w in out[:count]] + [out[count]]
-
-
-def join_kernel(own, near, far, most):
-    parts = [ref[...].astype(F32) for ref in (own, near, far)]
-    most[...] = jnp.concatenate(parts).astype(BF16)
-
-
-def split_kernel(near, far, near_x, far_y):
-    near_x[...] = near[:, : near_x.shape[1]]
-    far_y[...] = far[:, near_x.shape[1] :]
+    )(in_hbm(weight), after)
+    return in_vmem(out)
+
+
+def relay_kernel(block, *refs):
+    refs[-1][...] = block[...]
+
+
+def relay(block, *after):
+    return pl.pallas_call(
+        relay_kernel,
+        out_shape=jax.ShapeDtypeStruct(block.shape, block.dtype),
+        in_specs=whole(1) + [pl.BlockSpec(memory_space=pl.ANY)] * len(after),
+        out_specs=whole(1)[0],
+        compiler_params=pltpu.CompilerParams(vmem_limit_bytes=8 * MIB),
+        cost_estimate=pl.CostEstimate(
+            flops=0, bytes_accessed=4 * block.size, transcendentals=0
+        ),
+    )(block, *after)
 
 
 def expert_kernel(*refs):
-    pieces, (down_w, gate_w, up_w), refs = refs[:6], refs[6:9], refs[9:]
-    send, keep, weighted_t, d_both, x_t, y, x = refs
+    pieces, (down_in, gate_w, up_w), refs = refs[:4], refs[4:7], refs[7:]
+    send, keep, weighted_t, d_both, x_t, y, x, down_w, sems = refs
     rows, width, hidden_dim = x.shape[0], gate_w.shape[0], gate_w.shape[1]
     wide = width + LANES
     half = rows // 2
-    own, last_x, last_y, other, other_x, other_y = pieces
+    copies = fetch_copies([down_in], [down_w], sems)
+    for copy in copies:
+        copy.start()
     for c in range(0, wide, LANES):
         at = pl.ds(c, LANES)
-        parts = [ref[:, at].astype(F32) for ref in (own, last_x, other, other_x)]
-        block = jnp.concatenate(parts)
+        block = jnp.concatenate([ref[:, at].astype(F32) for ref in pieces])
         x[:, at] = block.astype(BF16)
         if c < width:
             x_t[at, :] = block.T.astype(BF16)
-    for c in range(0, width, LANES):
-        at, from_wide = pl.ds(c, LANES), pl.ds(wide + c, LANES)
-        parts = [own[:, from_wide], last_y[:, at], other[:, from_wide], other_y[:, at]]
-        y[:, at] = jnp.concatenate([part.astype(F32) for part in parts]).astype(BF16)
+    quarter = rows // 4
+    for i, ref in enumerate(pieces):
+        y[i * quarter : (i + 1) * quarter, :] = ref[:, wide:]
     pre_gate = dot(x[:, :width], gate_w[...], ((1,), (0,)))
     pre_up = dot(x[:, :width], up_w[...], ((1,), (0,)))
+    for copy in copies:
+        copy.wait()
     back = dot(y[...], down_w[...], ((1,), (1,)))
     g = x[:, width:][:, 0:1].astype(F32)
     sig = jax.nn.sigmoid(pre_gate)
@@ -221,13 +226,7 @@
     send[:, width:] = split_pair(value[half:]).astype(BF16)
 
 
-def home_kernel(
-    row, have, got, select, base, coef, *refs
-):
-    rest, grad_tokens, grad_logits, gate_out, up_out, sems = refs[:2], *refs[-5:]
-    late = late_copies(row, rest, (gate_out, up_out), sems)
-    for copy in late:
-        copy.start()
+def home_kernel(have, got, select, base, coef, grad_tokens, grad_logits):
     slots = have.shape[0]
     width = have.shape[1] - LANES
     count = select.shape[0]
@@ -238,8 +237,6 @@
     value = tail[:, 0:1] + tail[:, 1:2]
     token_products = jnp.sum(select[0:slots, :] * value, axis=0, keepdims=True)
     grad_logits[...] = base[...] + coef[...] * token_products
-    for copy in late:
-        copy.wait()
 
 
 def tiles(out, left, right):
@@ -263,19 +260,19 @@
     ]
 
 
-def grads_kernel(first_row, x_t, d_both, *refs):
-    gate_out, up_out, gate_left, up_left, gate_buf, up_buf, sems = refs[-7:]
+def grads_kernel(first_row, last, x_t, d_both, *refs):
+    left = refs[:2] if first_row else ()
+    gate_buf, up_buf, sems = refs[-3:]
+    outs = refs[-5:-3] if last else refs[-7:-5]
+    kept = () if last else refs[-5:-3]
     chunks, step, cols = gate_buf.shape
-    copies = []
-    if first_row:
-        copies += late_copies(first_row - step, refs[:2], (gate_out, up_out), sems.at[chunks])
-        for copy in copies:
-            copy.start()
-    for i in range(chunks + 1):
+    copies = late_copies(first_row - step, left, outs, sems.at[chunks]) if left else []
+    for copy in copies:
+        copy.start()
+    for i in range(chunks if last else chunks + 1):
         at = pl.ds(first_row + i * step, step)
-        outs = (gate_buf, up_buf) if i < chunks else (gate_left, up_left)
-        for k, target in enumerate((gate_out, up_out)):
-            tile = outs[k].at[i] if i < chunks else outs[k]
+        for k, target in enumerate(outs):
+            tile = (gate_buf, up_buf)[k].at[i] if i < chunks else kept[k]
             tiles(tile, x_t.at[at], d_both.at[:, pl.ds(k * cols, cols)])
             if i < chunks:
                 copy = pltpu.make_async_copy(tile, target.at[at], sems.at[i, k])
@@ -294,7 +291,7 @@
         tiles(down_buf.at[i], weighted_t, y.at[:, at])
         copies.append(pltpu.make_async_copy(down_buf.at[i], down_out.at[:, at], down_sems.at[i]))
         copies[i].start()
-    grads_kernel(0, x_t, d_both, *refs[:4], *refs[6:])
+    grads_kernel(0, False, x_t, d_both, *refs[:4], *refs[6:])
     for copy in copies:
         copy.wait()
 
@@ -303,17 +300,18 @@
     width, slots = x_t.shape
     cols = d_both.shape[1] // 2
     step = 256
-    chunks = rows // step - 1
+    last = first_row + rows == width
+    chunks = rows // step - (0 if last else 1)
     anywhere = pl.BlockSpec(memory_space=pl.ANY)
     outs = [jax.ShapeDtypeStruct((width, cols), BF16)] * 2
-    outs += [jax.ShapeDtypeStruct((step, cols), BF16)] * 2
-    out_specs = [anywhere] * 2 + whole(2)
+    outs += [] if last else [jax.ShapeDtypeStruct((step, cols), BF16)] * 2
+    out_specs = [anywhere] * 2 + whole(len(outs) - 2)
     scratch = [
         pltpu.VMEM((chunks, step, cols), BF16),
         pltpu.VMEM((chunks, step, cols), BF16),
         pltpu.SemaphoreType.DMA((chunks + 1, 2)),
     ]
-    kernel = functools.partial(grads_kernel, first_row)
+    kernel = functools.partial(grads_kernel, first_row, last)
     if down:
         kernel = first_kernel
         wide = 1024
@@ -386,24 +384,24 @@
             ),
         )(*[in_hbm(a) for a in (tokens, logits.T, ref_logits.T, routes.T, cotangent)])
 
-        got = swap(send, levels[0])
-        gate_w, own = fetch([gate_weight], send)
-        own = jnp.concatenate([own, got])
-        for bits in levels[1:-2]:
+        own = send
+        for bits in levels[:-3]:
             own = jnp.concatenate([own, swap(own, bits)])
-        near = swap(own, levels[-2])
-        far = swap(own, levels[-1])
-        up_w, down_w, own = fetch([up_weight, down_weight], own)
-        few = own.shape[0]
-        near_x, far_y = call(
-            split_kernel, [((few, wide), BF16), ((few, width), BF16)], [near, far], 0, 1 << 18
-        )
-        (most,) = call(
-            join_kernel, [((3 * few, wide + width), BF16)], [own, near, far], 0, 1 << 23
-        )
-        last_x = swap(near_x, levels[-1])
-        last_y = swap(far_y, levels[-2])
-        pieces = [most, last_x, last_y]
+        first, second, third = levels[-3:]
+        block_1 = swap(own, first)
+        block_2 = swap(own, second)
+        block_3 = swap(own, third)
+        gate_w = fetch(gate_weight, own)
+        block_1 = relay(block_1, gate_w, block_2)
+        block_12 = swap(block_1, second)
+        block_13 = swap(block_1, third)
+        block_23 = swap(block_3, second)
+        up_w = fetch(up_weight, block_1)
+        block_12 = relay(block_12, up_w)
+        block_123 = swap(block_12, third)
+        low_half = jnp.concatenate([own, block_1, block_2, block_12])
+        high_half = jnp.concatenate([block_3, block_13, block_23, block_123])
+        pieces = [low_half, high_half]
         pieces += [swap(piece, (1, 1)) for piece in pieces]
 
         work = 2 * rows * width * hidden
@@ -418,14 +416,18 @@
                 jax.ShapeDtypeStruct((width, rows), BF16),
                 jax.ShapeDtypeStruct((rows, width), BF16),
             ],
-            in_specs=whole(9),
+            in_specs=whole(4) + [anywhere] + whole(2),
             out_specs=whole(6),
-            scratch_shapes=[pltpu.VMEM((rows, wide), BF16)],
-            compiler_params=pltpu.CompilerParams(vmem_limit_bytes=16 * MIB),
+            scratch_shapes=[
+                pltpu.VMEM((rows, wide), BF16),
+                pltpu.VMEM((hidden, width), BF16),
+                pltpu.SemaphoreType.DMA((1, 4)),
+            ],
+            compiler_params=pltpu.CompilerParams(vmem_limit_bytes=24 * MIB),
             cost_estimate=pl.CostEstimate(
                 flops=16 * work, bytes_accessed=4 * width * hidden, transcendentals=0
             ),
-        )(*pieces, down_w, gate_w, up_w)
+        )(*pieces, in_hbm(down_weight), gate_w, up_w)
 
         for bits in [(1, 1)] + levels[::-1]:
             got = swap(low, bits)
@@ -444,25 +446,15 @@
         grad_down, *pair = grads_of(x_t, d_both, 0, cuts[1], (), (weighted_t, y_all))
         for start, stop in zip(cuts[1:], cuts[2:]):
             pair = grads_of(x_t, d_both, start, stop - start, tuple(pair))
-        grad_gate, grad_up, *rest = pair
-
-        grad_tokens, grad_logits, grad_gate, grad_up = pl.pallas_call(
-            functools.partial(home_kernel, width - rest[0].shape[0]),
-            out_shape=[
-                jax.ShapeDtypeStruct((count, width), BF16),
-                jax.ShapeDtypeStruct((experts, count), F32),
-                jax.ShapeDtypeStruct(grad_gate.shape, BF16),
-                jax.ShapeDtypeStruct(grad_up.shape, BF16),
-            ],
-            in_specs=whole(7) + [anywhere] * 2,
-            out_specs=whole(2) + [anywhere] * 2,
-            scratch_shapes=[pltpu.SemaphoreType.DMA((2,))],
-            input_output_aliases={7: 2, 8: 3},
-            compiler_params=pltpu.CompilerParams(vmem_limit_bytes=8 * MIB),
-            cost_estimate=pl.CostEstimate(
-                flops=1 << 20, bytes_accessed=1 << 18, transcendentals=0
-            ),
-        )(keep, got, select, base, coef, *rest, grad_gate, grad_up)
+        grad_gate, grad_up = pair
+
+        grad_tokens, grad_logits = call(
+            home_kernel,
+            [((count, width), BF16), ((experts, count), F32)],
+            [keep, got, select, base, coef],
+            1 << 20,
+            1 << 18,
+        )
         return (
             grad_gate,
             grad_up,

time: 54.7 us -> 52.9 us (0.967)
  waiting for transfers between devices: 12.9 us -> 6.76 us
  starting transfers between devices: 12.6 us -> 18.2 us
  Pallas kernels: 28.2 us -> 26.5 us
    ppermute x12 -> x13, waiting for transfers between devices: 12.9 us -> 6.76 us  [swap(): return lax.ppermute(block, 'blk', [(i, i ^ bits[i % 2]) for i in range(n)])]
    ppermute x12 -> x13, starting transfers between devices: 12.6 us -> 18.2 us  [swap(): return lax.ppermute(block, 'blk', [(i, i ^ bits[i % 2]) for i in range(n)])]
    pallas_call x3 -> x4, Pallas kernels: 9.06 us -> 5.75 us  [the longest x2 5.73 us: fetch(): pl.pallas_call(fetch_kernel, out_shape=pltpu.VMEM(weight.shape, weight.dt...]
    pallas_call x5 -> x4, Pallas kernels: 0.52 us -> 1.39 us  [call(): pl.pallas_call(kernel, out_shape=[jax.ShapeDtypeStruct(s, t) for s, t in...]
    pallas_call x1, Pallas kernels: 8.19 us -> 8.78 us  [shards(): pl.pallas_call(expert_kernel, out_shape=[jax.ShapeDtypeStruct((half, wide...]
  transfers between devices with their start and end apart: 12 -> 13, of which waited for: 9 -> 5; matrix products, arithmetic and copies ran while one was open for 0% -> 1% of each run, Pallas kernels for 30% -> 28%
where the time goes in v11:
time: 52.9 us; the launch traced here: 52.7 us
  Pallas kernels  26.5 us (50%)
  starting transfers between devices  18.2 us (34%)
  waiting for transfers between devices  6.76 us (13%)
  between operations  0.78 us (1%)
    ppermute x13, starting transfers between devices, swap(): return lax.ppermute(block, 'blk', [(i, i ^ bits[i % 2]) for i in range(n)])  18.2 us
    pallas_call x3, Pallas kernels, grads_of(): pl.pallas_call(kernel, out_shape=outs, in_specs=whole(2 + len(down)) + (w...  8.87 us
    pallas_call x1, Pallas kernels, shards(): pl.pallas_call(expert_kernel, out_shape=[jax.ShapeDtypeStruct((half, wide...  8.78 us
    ppermute x13, waiting for transfers between devices, swap(): return lax.ppermute(block, 'blk', [(i, i ^ bits[i % 2]) for i in range(n)])  6.76 us
    pallas_call x2, Pallas kernels, fetch(): pl.pallas_call(fetch_kernel, out_shape=pltpu.VMEM(weight.shape, weight.dt...  5.73 us
    pallas_call x1, Pallas kernels, shards(): pl.pallas_call(router_kernel, out_shape=[jax.ShapeDtypeStruct((slots, wid...  1.72 us
    pallas_call x4, Pallas kernels, call(): pl.pallas_call(kernel, out_shape=[jax.ShapeDtypeStruct(s, t) for s, t in...  1.39 us
  transfers between devices with their start and end apart: 13, of which 5 were waited for; matrix products, arithmetic and copies ran while one was open for 1% of the time, Pallas kernels for 28%

profile of v11, /device:TPU:0, one launch (start us, length us, event | category | flops | bytes accessed | tf_op | source)
XLA Modules:
  0.0 52.7 jit_solution(12678998372667741816)
XLA Ops:
  0.6 1.7 %shard_map.135 = (bf16[4,12416]{1,0:T(4,128)(2,1)S(1)}, f32[1,16]{1,0:T(1,128)}, f32[1,16]{1,0:T(1,128)}, f32[8,16]{1,0:T(8,128)S(1)}, f32[8,16]{1,0:T(8,128)S(1)}, /*index=5*/f32[16,16]{1,0:T(8,128)S(1)}) custom-call(bf16[16,6144]{1,0:T(8,128)(2,1)} %tokens_in.1, f32[8,16]{1,0:T(8,128)} %bitcast.6, f32[8,16]{1,0:T(8,128)} %bitcast.7, s32[2,16]{1,0:T(2,128)} %bitcast.8, ...), custom_call_target="tpu_custom_call" | custom-call | flops 1048576 | bytes 16777216 | tf_op jit(solution)/shard_map/pallas_call | solution.py:361
  2.4 3.1 %collective-permute-start.1 = (bf16[4,12416]{1,0:T(4,128)(2,1)S(1)}, bf16[4,12416]{1,0:T(4,128)(2,1)S(1)}, u32[]{:S(2)}, u32[]{:S(2)}) collective-permute-start(bf16[4,12416]{1,0:T(4,128)(2,1)S(1)} %get-tuple-element.38.after), channel_id=1, source_target_pairs={{0,4},{1,3},{2,6},{3,1},{4,0},{5,7},{6,2},{7,5},{8,12},{9,11},{10,... | collective-permute-start | bytes 297992 | tf_op jit(solution)/shard_map/ppermute | solution.py:348
  5.5 2.6 %collective-permute-start = (bf16[4,12416]{1,0:T(4,128)(2,1)S(1)}, bf16[4,12416]{1,0:T(4,128)(2,1)S(1)}, u32[]{:S(2)}, u32[]{:S(2)}) collective-permute-start(bf16[4,12416]{1,0:T(4,128)(2,1)S(1)} %get-tuple-element.38.after), channel_id=1, source_target_pairs={{0,8},{1,9},{2,10},{3,11},{4,12},{5,13},{6,14},{7,15},{8,0},{9,1},... | collective-permute-start | bytes 297992 | tf_op jit(solution)/shard_map/ppermute | solution.py:348
  8.0 1.5 %collective-permute-start.3 = (bf16[4,12416]{1,0:T(4,128)(2,1)S(1)}, bf16[4,12416]{1,0:T(4,128)(2,1)S(1)}, u32[]{:S(2)}, u32[]{:S(2)}) collective-permute-start(bf16[4,12416]{1,0:T(4,128)(2,1)S(1)} %get-tuple-element.38.after), channel_id=1, source_target_pairs={{0,2},{1,5},{2,0},{3,7},{4,6},{5,1},{6,4},{7,3},{8,10},{9,13},{10,... | collective-permute-start | bytes 297992 | tf_op jit(solution)/shard_map/ppermute | solution.py:348
  9.6 2.9 %shard_map.136.refs_0_.refs_5_ = bf16[6144,512]{1,0:T(8,128)(2,1)S(1)} custom-call(bf16[6144,512]{1,0:T(8,128)(2,1)} %source.2, bf16[4,12416]{1,0:T(4,128)(2,1)S(1)} %get-tuple-element.38.after), custom_call_target="tpu_custom_call" | custom-call | bytes 6291456 | tf_op jit(solution)/shard_map/pallas_call | solution.py:141
  12.4 0.0 collective-permute-done.1.refs_1_
  12.4 0.0 collective-permute-done.block
  12.5 1.9 %collective-permute-start.2 = (bf16[4,12416]{1,0:T(4,128)(2,1)S(1)}, bf16[4,12416]{1,0:T(4,128)(2,1)S(1)}, u32[]{:S(2)}, u32[]{:S(2)}) collective-permute-start(bf16[4,12416]{1,0:T(4,128)(2,1)S(1)} %shard_map.137.after), channel_id=1, source_target_pairs={{0,4},{1,3},{2,6},{3,1},{4,0},{5,7},{6,2},{7,5},{8,12},{9,11},{10,... | collective-permute-start | bytes 297992 | tf_op jit(solution)/shard_map/ppermute | solution.py:348
  14.4 0.5 collective-permute-start.4
  14.9 2.9 %shard_map.138.refs_0_.refs_6_ = bf16[6144,512]{1,0:T(8,128)(2,1)S(1)} custom-call(bf16[6144,512]{1,0:T(8,128)(2,1)} %source.3, bf16[4,12416]{1,0:T(4,128)(2,1)S(1)} %shard_map.137.after), custom_call_target="tpu_custom_call" | custom-call | bytes 6291456 | tf_op jit(solution)/shard_map/pallas_call | solution.py:141
  17.7 0.0 collective-permute-done.3
  17.7 0.3 collective-permute-start.5
  18.0 0.0 collective-permute-done.2.block
  18.0 1.6 %collective-permute-start.6 = (bf16[4,12416]{1,0:T(4,128)(2,1)S(1)}, bf16[4,12416]{1,0:T(4,128)(2,1)S(1)}, u32[]{:S(2)}, u32[]{:S(2)}) collective-permute-start(bf16[4,12416]{1,0:T(4,128)(2,1)S(1)} %shard_map.139), channel_id=1, source_target_pairs={{0,2},{1,5},{2,0},{3,7},{4,6},{5,1},{6,4},{7,3},{8,10},{9,13},{10,... | collective-permute-start | bytes 297992 | tf_op jit(solution)/shard_map/ppermute | solution.py:348
  19.6 0.2 pad_maximum_fusion.refs_0_
  19.9 0.1 collective-permute-start.7
  19.9 2.5 %collective-permute-done.5 = bf16[4,12416]{1,0:T(4,128)(2,1)S(1)} collective-permute-done((bf16[4,12416]{1,0:T(4,128)(2,1)S(1)}, bf16[4,12416]{1,0:T(4,128)(2,1)S(1)}, u32[]{:S(2)}, u32[]{:S(2)}) %collective-permute-start.5) | collective-permute-done | bytes 99360 | tf_op jit(solution)/shard_map/ppermute | solution.py:348
  22.5 0.0 collective-permute-done.4
  22.5 0.2 collective-permute-done.6
  22.7 0.2 pad_maximum_fusion.1.refs_1_
  23.0 0.1 collective-permute-start.8
  23.0 0.0 collective-permute-done.7.refs_2_
  23.1 1.7 %collective-permute-done.8.refs_3_ = bf16[16,12416]{1,0:T(8,128)(2,1)S(1)} collective-permute-done((bf16[16,12416]{1,0:T(8,128)(2,1)S(1)}, bf16[16,12416]{1,0:T(8,128)(2,1)S(1)}, u32[]{:S(2)}, u32[]{:S(2)}) %collective-permute-start.8) | collective-permute-done | bytes 397344 | tf_op jit(solution)/shard_map/ppermute | solution.py:348
  24.8 8.8 %shard_map.140 = (bf16[32,6272]{1,0:T(8,128)(2,1)S(1)}, f32[32,6272]{1,0:T(8,128)S(1)}, bf16[512,64]{1,0:T(8,128)(2,1)S(1)}, bf16[64,1024]{1,0:T(8,128)(2,1)S(1)...) custom-call(bf16[16,12416]{1,0:T(8,128)(2,1)S(1)} %pad_maximum_fusion.refs_0_, ...), custom_call_target="tpu_custom_call" | custom-call | flops 6442450944 | bytes 12582912 | tf_op jit(solution)/shard_map/pallas_call | solution.py:409
  33.5 0.2 collective-permute-start.9
  33.7 1.6 %collective-permute-done.9.got = bf16[32,6272]{1,0:T(8,128)(2,1)S(1)} collective-permute-done((bf16[32,6272]{1,0:T(8,128)(2,1)S(1)}, bf16[32,6272]{1,0:T(8,128)(2,1)S(1)}, u32[]{:S(2)}, u32[]{:S(2)}) %collective-permute-start.9) | collective-permute-done | bytes 401440 | tf_op jit(solution)/shard_map/ppermute | solution.py:348
  35.3 0.2 shard_map.144
  35.5 1.6 %collective-permute-start.10 = (bf16[16,6272]{1,0:T(8,128)(2,1)S(1)}, bf16[16,6272]{1,0:T(8,128)(2,1)S(1)}, u32[]{:S(2)}, u32[]{:S(2)}) collective-permute-start(bf16[16,6272]{1,0:T(8,128)(2,1)S(1)} %get-tuple-element.57), channel_id=1, source_target_pairs={{0,2},{1,5},{2,0},{3,7},{4,6},{5,1},{6,4},{7,3},{8,10},{9,13},{10,... | collective-permute-start | bytes 602120 | tf_op jit(solution)/shard_map/ppermute | solution.py:348
  37.1 4.4 %shard_map.141 = (bf16[512,6144]{1,0:T(8,128)(2,1)}, bf16[6144,512]{1,0:T(8,128)(2,1)}, bf16[6144,512]{1,0:T(8,128)(2,1)}, bf16[256,512]{1,0:T(8,128)(2,1)S(1)}, bf16[256,512]{1,0:T(8,128)(2,1)S(1)}) custom-call(bf16[512,64]{1,0:T(8,128)(2,1)S(1)} %get-tuple-element.41.weighted_t, bf16[64,6144]{1,0:T(8,128)(2,1)S(1)} %get-tuple-element.42.y, ...), custom_call_target="tpu_custom_call" | custom-call | flops 2684354560 | bytes 10485760 | tf_op jit(solution)/shard_map/pallas_call | solution.py:325
  41.5 0.0 collective-permute-done.10.got
  41.5 0.1 shard_map.145
  41.6 1.8 %collective-permute-start.11 = (bf16[8,6272]{1,0:T(8,128)(2,1)S(1)}, bf16[8,6272]{1,0:T(8,128)(2,1)S(1)}, u32[]{:S(2)}, u32[]{:S(2)}) collective-permute-start(bf16[8,6272]{1,0:T(8,128)(2,1)S(1)} %get-tuple-element.59), channel_id=1, source_target_pairs={{0,4},{1,3},{2,6},{3,1},{4,0},{5,7},{6,2},{7,5},{8,12},{9,11},{10,... | collective-permute-start | bytes 301064 | tf_op jit(solution)/shard_map/ppermute | solution.py:348
  43.5 2.2 %shard_map.142 = (bf16[6144,512]{1,0:T(8,128)(2,1)}, bf16[6144,512]{1,0:T(8,128)(2,1)}, bf16[256,512]{1,0:T(8,128)(2,1)S(1)}, bf16[256,512]{1,0:T(8,128)(2,1)S(1)}) custom-call(bf16[6144,64]{1,0:T(8,128)(2,1)S(1)} %get-tuple-element.39.x_t, bf16[64,1024]{1,0:T(8,128)(2,1)S(1)} %get-tuple-element.40.d_both, ...), custom_call_target="tpu_custom_call", output_to_operand_aliasing={{0}: (4, {}), {1}: (5, {})} | custom-call | flops 1073741824 | bytes 4194304 | tf_op jit(solution)/shard_map/pallas_call | solution.py:325
  45.6 0.6 %collective-permute-done.11.got = bf16[8,6272]{1,0:T(8,128)(2,1)S(1)} collective-permute-done((bf16[8,6272]{1,0:T(8,128)(2,1)S(1)}, bf16[8,6272]{1,0:T(8,128)(2,1)S(1)}, u32[]{:S(2)}, u32[]{:S(2)}) %collective-permute-start.11) | collective-permute-done | bytes 100384 | tf_op jit(solution)/shard_map/ppermute | solution.py:348
  46.3 0.2 shard_map.146
  46.4 3.0 %collective-permute-start.12 = (bf16[4,6272]{1,0:T(4,128)(2,1)S(1)}, bf16[4,6272]{1,0:T(4,128)(2,1)S(1)}, u32[]{:S(2)}, u32[]{:S(2)}) collective-permute-start(bf16[4,6272]{1,0:T(4,128)(2,1)S(1)} %get-tuple-element.61), channel_id=1, source_target_pairs={{0,8},{1,9},{2,10},{3,11},{4,12},{5,13},{6,14},{7,15},{8,0},{9,1},... | collective-permute-start | bytes 150536 | tf_op jit(solution)/shard_map/ppermute | solution.py:348
  49.4 2.4 %shard_map.143 = (bf16[6144,512]{1,0:T(8,128)(2,1)}, bf16[6144,512]{1,0:T(8,128)(2,1)}) custom-call(bf16[6144,64]{1,0:T(8,128)(2,1)S(1)} %get-tuple-element.39.x_t, bf16[64,1024]{1,0:T(8,128)(2,1)S(1)} %get-tuple-element.40.d_both, bf16[256,512]{1,0:T(8,128)(2,1)S(1)} %get-tuple-element.47.refs_0_, ...), custom_call_target="tpu_custom_call", output_to_operand_aliasing={{0}: (4, {}), {1}: (5, {})} | custom-call | flops 1073741824 | bytes 4194304 | tf_op jit(solution)/shard_map/pallas_call | solution.py:325
  51.8 0.0 collective-permute-done.12.got
  51.8 0.9 %shard_map.147 = (bf16[16,6144]{1,0:T(8,128)(2,1)}, f32[8,16]{1,0:T(8,128)}) custom-call(f32[4,6272]{1,0:T(4,128)S(1)} %get-tuple-element.60.have, bf16[4,6272]{1,0:T(4,128)(2,1)S(1)} %collective-permute-done.12.got, f32[16,16]{1,0:T(8,128)S(1)} %get-tuple-element.62.select, f32[8,16]{1,0:T(8,128)S(1)} %get-tuple-element.63.base, ...), custom_call_target="tpu_custom_call" | custom-call | flops 1048576 | bytes 262144 | tf_op jit(solution)/shard_map/pallas_call | solution.py:25
  (2 shorter events, 0.0 us)
Async XLA Ops:
  2.4 10.1 %collective-permute-start.1 = (bf16[4,12416]{1,0:T(4,128)(2,1)S(1)}, bf16[4,12416]{1,0:T(4,128)(2,1)S(1)}, u32[]{:S(2)}, u32[]{:S(2)}) collective-permute-start(bf16[4,12416]{1,0:T(4,128)(2,1)S(1)} %get-tuple-element.38.after), channel_id=1, source_target_pairs={{0,4},{1,3},{2,6},{3,1},{4,0},{5,7},{6,2},{7,5},{8,12},{9,11},{10,... | collective-permute-start | bytes 297992 | tf_op jit(solution)/shard_map/ppermute | solution.py:348
  5.5 7.0 %collective-permute-start = (bf16[4,12416]{1,0:T(4,128)(2,1)S(1)}, bf16[4,12416]{1,0:T(4,128)(2,1)S(1)}, u32[]{:S(2)}, u32[]{:S(2)}) collective-permute-start(bf16[4,12416]{1,0:T(4,128)(2,1)S(1)} %get-tuple-element.38.after), channel_id=1, source_target_pairs={{0,8},{1,9},{2,10},{3,11},{4,12},{5,13},{6,14},{7,15},{8,0},{9,1},... | collective-permute-start | bytes 297992 | tf_op jit(solution)/shard_map/ppermute | solution.py:348
  8.0 9.7 %collective-permute-start.3 = (bf16[4,12416]{1,0:T(4,128)(2,1)S(1)}, bf16[4,12416]{1,0:T(4,128)(2,1)S(1)}, u32[]{:S(2)}, u32[]{:S(2)}) collective-permute-start(bf16[4,12416]{1,0:T(4,128)(2,1)S(1)} %get-tuple-element.38.after), channel_id=1, source_target_pairs={{0,2},{1,5},{2,0},{3,7},{4,6},{5,1},{6,4},{7,3},{8,10},{9,13},{10,... | collective-permute-start | bytes 297992 | tf_op jit(solution)/shard_map/ppermute | solution.py:348
  12.5 5.6 %collective-permute-start.2 = (bf16[4,12416]{1,0:T(4,128)(2,1)S(1)}, bf16[4,12416]{1,0:T(4,128)(2,1)S(1)}, u32[]{:S(2)}, u32[]{:S(2)}) collective-permute-start(bf16[4,12416]{1,0:T(4,128)(2,1)S(1)} %shard_map.137.after), channel_id=1, source_target_pairs={{0,4},{1,3},{2,6},{3,1},{4,0},{5,7},{6,2},{7,5},{8,12},{9,11},{10,... | collective-permute-start | bytes 297992 | tf_op jit(solution)/shard_map/ppermute | solution.py:348
  14.4 8.1 %collective-permute-start.4 = (bf16[4,12416]{1,0:T(4,128)(2,1)S(1)}, bf16[4,12416]{1,0:T(4,128)(2,1)S(1)}, u32[]{:S(2)}, u32[]{:S(2)}) collective-permute-start(bf16[4,12416]{1,0:T(4,128)(2,1)S(1)} %shard_map.137.after), channel_id=1, source_target_pairs={{0,2},{1,5},{2,0},{3,7},{4,6},{5,1},{6,4},{7,3},{8,10},{9,13},{10,... | collective-permute-start | bytes 297992 | tf_op jit(solution)/shard_map/ppermute | solution.py:348
  17.7 4.7 %collective-permute-start.5 = (bf16[4,12416]{1,0:T(4,128)(2,1)S(1)}, bf16[4,12416]{1,0:T(4,128)(2,1)S(1)}, u32[]{:S(2)}, u32[]{:S(2)}) collective-permute-start(bf16[4,12416]{1,0:T(4,128)(2,1)S(1)} %collective-permute-done.3), channel_id=1, source_target_pairs={{0,4},{1,3},{2,6},{3,1},{4,0},{5,7},{6,2},{7,5},{8,12},{9,11},{10,... | collective-permute-start | bytes 297992 | tf_op jit(solution)/shard_map/ppermute | solution.py:348
  18.0 4.7 %collective-permute-start.6 = (bf16[4,12416]{1,0:T(4,128)(2,1)S(1)}, bf16[4,12416]{1,0:T(4,128)(2,1)S(1)}, u32[]{:S(2)}, u32[]{:S(2)}) collective-permute-start(bf16[4,12416]{1,0:T(4,128)(2,1)S(1)} %shard_map.139), channel_id=1, source_target_pairs={{0,2},{1,5},{2,0},{3,7},{4,6},{5,1},{6,4},{7,3},{8,10},{9,13},{10,... | collective-permute-start | bytes 297992 | tf_op jit(solution)/shard_map/ppermute | solution.py:348
  19.9 3.2 %collective-permute-start.7 = (bf16[16,12416]{1,0:T(8,128)(2,1)S(1)}, bf16[16,12416]{1,0:T(8,128)(2,1)S(1)}, u32[]{:S(2)}, u32[]{:S(2)}) collective-permute-start(bf16[16,12416]{1,0:T(8,128)(2,1)S(1)} %pad_maximum_fusion.refs_0_), channel_id=1, source_target_pairs={{0,1},{1,0},{2,3},{3,2},{4,5},{5,4},{6,7},{7,6},{8,9},{9,8},{10,11... | collective-permute-start | bytes 1191944 | tf_op jit(solution)/shard_map/ppermute | solution.py:348
  23.0 1.8 %collective-permute-start.8 = (bf16[16,12416]{1,0:T(8,128)(2,1)S(1)}, bf16[16,12416]{1,0:T(8,128)(2,1)S(1)}, u32[]{:S(2)}, u32[]{:S(2)}) collective-permute-start(bf16[16,12416]{1,0:T(8,128)(2,1)S(1)} %pad_maximum_fusion.1.refs_1_), channel_id=1, source_target_pairs={{0,1},{1,0},{2,3},{3,2},{4,5},{5,4},{6,7},{7,6},{8,9},{9,8},{10,11... | collective-permute-start | bytes 1191944 | tf_op jit(solution)/shard_map/ppermute | solution.py:348
  33.5 1.8 %collective-permute-start.9 = (bf16[32,6272]{1,0:T(8,128)(2,1)S(1)}, bf16[32,6272]{1,0:T(8,128)(2,1)S(1)}, u32[]{:S(2)}, u32[]{:S(2)}) collective-permute-start(bf16[32,6272]{1,0:T(8,128)(2,1)S(1)} %get-tuple-element.55), channel_id=1, source_target_pairs={{0,1},{1,0},{2,3},{3,2},{4,5},{5,4},{6,7},{7,6},{8,9},{9,8},{10,11... | collective-permute-start | bytes 1204232 | tf_op jit(solution)/shard_map/ppermute | solution.py:348
  35.5 5.9 %collective-permute-start.10 = (bf16[16,6272]{1,0:T(8,128)(2,1)S(1)}, bf16[16,6272]{1,0:T(8,128)(2,1)S(1)}, u32[]{:S(2)}, u32[]{:S(2)}) collective-permute-start(bf16[16,6272]{1,0:T(8,128)(2,1)S(1)} %get-tuple-element.57), channel_id=1, source_target_pairs={{0,2},{1,5},{2,0},{3,7},{4,6},{5,1},{6,4},{7,3},{8,10},{9,13},{10,... | collective-permute-start | bytes 602120 | tf_op jit(solution)/shard_map/ppermute | solution.py:348
  41.6 4.7 %collective-permute-start.11 = (bf16[8,6272]{1,0:T(8,128)(2,1)S(1)}, bf16[8,6272]{1,0:T(8,128)(2,1)S(1)}, u32[]{:S(2)}, u32[]{:S(2)}) collective-permute-start(bf16[8,6272]{1,0:T(8,128)(2,1)S(1)} %get-tuple-element.59), channel_id=1, source_target_pairs={{0,4},{1,3},{2,6},{3,1},{4,0},{5,7},{6,2},{7,5},{8,12},{9,11},{10,... | collective-permute-start | bytes 301064 | tf_op jit(solution)/shard_map/ppermute | solution.py:348
  46.4 5.3 %collective-permute-start.12 = (bf16[4,6272]{1,0:T(4,128)(2,1)S(1)}, bf16[4,6272]{1,0:T(4,128)(2,1)S(1)}, u32[]{:S(2)}, u32[]{:S(2)}) collective-permute-start(bf16[4,6272]{1,0:T(4,128)(2,1)S(1)} %get-tuple-element.61), channel_id=1, source_target_pairs={{0,8},{1,9},{2,10},{3,11},{4,12},{5,13},{6,14},{7,15},{8,0},{9,1},... | collective-permute-start | bytes 150536 | tf_op jit(solution)/shard_map/ppermute | solution.py:348

commit v12 on v11

--- a/solution.py
+++ b/solution.py
@@ -21,15 +21,15 @@
     return [pl.BlockSpec(memory_space=pltpu.VMEM)] * count
 
 
-def call(kernel, outs, args, flops, moved, limit=8):
+def call(kernel, outs, args, flops, moved, limit=8, after=()):
     return pl.pallas_call(
         kernel,
         out_shape=[jax.ShapeDtypeStruct(s, t) for s, t in outs],
-        in_specs=whole(len(args)),
+        in_specs=whole(len(args)) + [pl.BlockSpec(memory_space=pl.ANY)] * len(after),
         out_specs=whole(len(outs)),
         compiler_params=pltpu.CompilerParams(vmem_limit_bytes=limit * MIB),
         cost_estimate=pl.CostEstimate(flops=flops, bytes_accessed=moved, transcendentals=0),
-    )(*args)
+    )(*args, *after)
 
 
 def in_hbm(array):
@@ -120,36 +120,43 @@
 def fetch_copies(sources, targets, sems):
     parts = sems.shape[1]
     copies = []
-    for k, (source, target) in enumerate(zip(sources, targets)):
-        step = source.shape[0] // parts
+    for k, ((source, row), target) in enumerate(zip(sources, targets)):
+        step = target.shape[0] // parts
         for i in range(parts):
-            at = pl.ds(i * step, step)
-            copies.append(pltpu.make_async_copy(source.at[at], target.at[at], sems.at[k, i]))
+            copies.append(
+                pltpu.make_async_copy(
+                    source.at[pl.ds(row + i * step, step)],
+                    target.at[pl.ds(i * step, step)],
+                    sems.at[k, i],
+                )
+            )
     return copies
 
 
-def fetch_kernel(source, after, target, sems):
-    copies = fetch_copies([source], [target], sems)
+def fetch_kernel(count, *refs):
+    sources, targets, sems = refs[:count], refs[count + 1 : -1], refs[-1]
+    copies = fetch_copies([(source, 0) for source in sources], targets, sems)
     for copy in copies:
         copy.start()
     for copy in copies:
         copy.wait()
 
 
-def fetch(weight, after):
+def fetch(weights, rows, after):
     anywhere = pl.BlockSpec(memory_space=pl.ANY)
+    count = len(weights)
     out = pl.pallas_call(
-        fetch_kernel,
-        out_shape=pltpu.VMEM(weight.shape, weight.dtype),
-        in_specs=[anywhere] * 2,
-        out_specs=whole(1)[0],
-        scratch_shapes=[pltpu.SemaphoreType.DMA((1, 4))],
+        functools.partial(fetch_kernel, count),
+        out_shape=[pltpu.VMEM((r, w.shape[1]), w.dtype) for w, r in zip(weights, rows)],
+        in_specs=[anywhere] * (count + 1),
+        out_specs=whole(count),
+        scratch_shapes=[pltpu.SemaphoreType.DMA((count, 4))],
         compiler_params=pltpu.CompilerParams(vmem_limit_bytes=8 * MIB),
         cost_estimate=pl.CostEstimate(
-            flops=0, bytes_accessed=2 * weight.size, transcendentals=0
+            flops=0, bytes_accessed=2 * sum(w.size for w in weights), transcendentals=0
         ),
-    )(in_hbm(weight), after)
-    return in_vmem(out)
+    )(*[in_hbm(w) for w in weights], after)
+    return [in_vmem(w) for w in out]
 
 
 def relay_kernel(block, *refs):
@@ -170,13 +177,14 @@
 
 
 def expert_kernel(*refs):
-    pieces, (down_in, gate_w, up_w), refs = refs[:4], refs[4:7], refs[7:]
-    send, keep, weighted_t, d_both, x_t, y, x, down_w, sems = refs
+    pieces, (down_in, up_in, gate_w, up_head), refs = refs[:4], refs[4:8], refs[8:]
+    send, keep, weighted_t, d_both, x_t, y, x, down_w, up_tail, up_sems, down_sems = refs
     rows, width, hidden_dim = x.shape[0], gate_w.shape[0], gate_w.shape[1]
-    wide = width + LANES
+    wide, cut = width + LANES, up_head.shape[0]
     half = rows // 2
-    copies = fetch_copies([down_in], [down_w], sems)
-    for copy in copies:
+    up_copies = fetch_copies([(up_in, cut)], [up_tail], up_sems)
+    down_copies = fetch_copies([(down_in, 0)], [down_w], down_sems)
+    for copy in up_copies + down_copies:
         copy.start()
     for c in range(0, wide, LANES):
         at = pl.ds(c, LANES)
@@ -184,14 +192,20 @@
         x[:, at] = block.astype(BF16)
         if c < width:
             x_t[at, :] = block.T.astype(BF16)
-    quarter = rows // 4
-    for i, ref in enumerate(pieces):
-        y[i * quarter : (i + 1) * quarter, :] = ref[:, wide:]
+    for c in range(0, width, LANES):
+        parts = [ref[:, wide + c : wide + c + LANES].astype(F32) for ref in pieces]
+        y[:, c : c + LANES] = jnp.concatenate(parts).astype(BF16)
     pre_gate = dot(x[:, :width], gate_w[...], ((1,), (0,)))
-    pre_up = dot(x[:, :width], up_w[...], ((1,), (0,)))
-    for copy in copies:
+    pre_up = dot(x[:, :cut], up_head[...], ((1,), (0,)))
+    for copy in up_copies:
         copy.wait()
-    back = dot(y[...], down_w[...], ((1,), (1,)))
+    pre_up += dot(x[:, cut:width], up_tail[...], ((1,), (0,)))
+    part = hidden_dim // len(down_copies)
+    back = []
+    for i, copy in enumerate(down_copies):
+        copy.wait()
+        back.append(dot(y[...], down_w[i * part : (i + 1) * part, :], ((1,), (1,))))
+    back = jnp.concatenate(back, axis=1)
     g = x[:, width:][:, 0:1].astype(F32)
     sig = jax.nn.sigmoid(pre_gate)
     act = pre_gate * sig
@@ -208,33 +222,73 @@
     wide = 1024
     for i in range(width // wide):
         at = pl.ds(i * wide, wide)
+        up_rows = up_head[at, :] if i * wide < cut else up_tail[pl.ds(i * wide - cut, wide), :]
         part = dot(d_both[:, :hidden_dim], gate_w[at, :], ((1,), (1,)))
-        part += dot(d_both[:, hidden_dim:], up_w[at, :], ((1,), (1,)))
+        part += dot(d_both[:, hidden_dim:], up_rows, ((1,), (1,)))
         keep[:, at] = part[:half]
         send[:, at] = part[half:].astype(BF16)
 
 
+def folded(have, got):
+    width = have.shape[1] - LANES
+    tail = have[:, width:] + got[:, width:].astype(F32)
+    return have[:, :width] + got[:, :width].astype(F32), tail[:, 0:1] + tail[:, 1:2]
+
+
+def put_keep(out, row, total, value):
+    rows, width = total.shape
+    out[row : row + rows, :width] = total
+    out[row : row + rows, width:] = lane_pair(rows, value, 0.0)
+
+
+def put_send(out, total, value):
+    width = total.shape[1]
+    out[:, :width] = total.astype(BF16)
+    out[:, width:] = split_pair(value).astype(BF16)
+
+
+def core_fold_kernel(have, got, *refs):
+    keep, over_second, over_third = refs[-3:]
+    total, value = folded(have, got)
+    half, part = have.shape[0] // 2, have.shape[0] // 4
+    put_keep(keep, 0, total[:half], value[:half])
+    put_send(over_second, total[half : half + part], value[half : half + part])
+    put_send(over_third, total[half + part :], value[half + part :])
+
+
+def pair_fold_kernel(have, got_second, got_third, *refs):
+    keep, over_second, over_third = refs[-3:]
+    half, part = have.shape[0] // 2, have.shape[0] // 4
+    total, value = folded(have[:half], got_second)
+    put_keep(keep, 0, total[:part], value[:part])
+    put_send(over_third, total[part:], value[part:])
+    total, value = folded(have[half:], got_third)
+    put_keep(keep, part, total[:part], value[:part])
+    put_send(over_second, total[part:], value[part:])
+
+
+def last_fold_kernel(have, got_second, got_third, *refs):
+    keep, over_first = refs[-2:]
+    part = have.shape[0] // 2
+    put_keep(keep, 0, *folded(have[:part], got_third))
+    put_send(over_first, *folded(have[part:], got_second))
+
+
 def fold_kernel(have, got, keep, send):
     half = keep.shape[0]
-    width = keep.shape[1] - LANES
-    total = have[:, :width] + got[:, :width].astype(F32)
-    keep[:, :width] = total[:half]
-    send[:, :width] = total[half:].astype(BF16)
-    tail = have[:, width:] + got[:, width:].astype(F32)
-    value = tail[:, 0:1] + tail[:, 1:2]
-    keep[:, width:] = lane_pair(half, value[:half], 0.0)
-    send[:, width:] = split_pair(value[half:]).astype(BF16)
+    total, value = folded(have, got)
+    put_keep(keep, 0, total[:half], value[:half])
+    put_send(send, total[half:], value[half:])
 
 
 def home_kernel(have, got, select, base, coef, grad_tokens, grad_logits):
     slots = have.shape[0]
     width = have.shape[1] - LANES
     count = select.shape[0]
-    total = (have[:, :width] + got[:, :width].astype(F32)).astype(BF16)
+    total, value = folded(have, got)
+    total = total.astype(BF16)
     padded = jnp.concatenate([total, jnp.zeros((count - slots, width), BF16)], axis=0)
     grad_tokens[...] = dot(select[...].astype(BF16), padded, ((0,), (0,))).astype(BF16)
-    tail = have[:, width:] + got[:, width:].astype(F32)
-    value = tail[:, 0:1] + tail[:, 1:2]
     token_products = jnp.sum(select[0:slots, :] * value, axis=0, keepdims=True)
     grad_logits[...] = base[...] + coef[...] * token_products
 
@@ -252,88 +306,86 @@
         body(i)
 
 
-def late_copies(row, sources, targets, sems):
-    step = sources[0].shape[0]
-    return [
-        pltpu.make_async_copy(source, target.at[pl.ds(row, step)], sems.at[k])
-        for k, (source, target) in enumerate(zip(sources, targets))
-    ]
-
-
-def grads_kernel(first_row, last, x_t, d_both, *refs):
-    left = refs[:2] if first_row else ()
-    gate_buf, up_buf, sems = refs[-3:]
-    outs = refs[-5:-3] if last else refs[-7:-5]
-    kept = () if last else refs[-5:-3]
-    chunks, step, cols = gate_buf.shape
-    copies = late_copies(first_row - step, left, outs, sems.at[chunks]) if left else []
-    for copy in copies:
-        copy.start()
-    for i in range(chunks if last else chunks + 1):
-        at = pl.ds(first_row + i * step, step)
-        for k, target in enumerate(outs):
-            tile = (gate_buf, up_buf)[k].at[i] if i < chunks else kept[k]
-            tiles(tile, x_t.at[at], d_both.at[:, pl.ds(k * cols, cols)])
-            if i < chunks:
-                copy = pltpu.make_async_copy(tile, target.at[at], sems.at[i, k])
-                copy.start()
-                copies.append(copy)
+def grads_kernel(plan, before, *refs):
+    (downs, downs_here), (pairs, pairs_here) = plan
+    weighted_t, y, x_t, d_both = refs[:4]
+    left_downs, left_pairs = refs[4:6] if before else (None, None)
+    down_buf, pair_buf, down_sems, pair_sems = refs[-4:]
+    down_out, gate_out, up_out, down_kept, pair_kept = refs[-9:-4]
+    wide, step, cols = down_buf.shape[2], pair_buf.shape[2], pair_buf.shape[3]
+    copies = []
+
+    def write_down(block, i):
+        at, sem = pl.ds(i * wide, wide), down_sems.at[len(copies)]
+        copies.append(pltpu.make_async_copy(block, down_out.at[:, at], sem))
+        copies[-1].start()
+
+    def write_pair(block, i):
+        for k, out in enumerate((gate_out, up_out)):
+            at, sem = pl.ds(i * step, step), pair_sems.at[len(copies)]
+            copies.append(pltpu.make_async_copy(block.at[k], out.at[at], sem))
+            copies[-1].start()
+
+    if before:
+        for j, i in enumerate(before[0]):
+            write_down(left_downs.at[j], i)
+        for j, i in enumerate(before[1]):
+            write_pair(left_pairs.at[j], i)
+    for j, i in enumerate(downs):
+        here = j < downs_here
+        block = down_buf.at[j] if here else down_kept.at[j - downs_here]
+        tiles(block, weighted_t, y.at[:, pl.ds(i * wide, wide)])
+        if here:
+            write_down(block, i)
+    for j, i in enumerate(pairs):
+        here = j < pairs_here
+        block = pair_buf.at[j] if here else pair_kept.at[j - pairs_here]
+        for k in range(2):
+            at = pl.ds(k * cols, cols)
+            tiles(block.at[k], x_t.at[pl.ds(i * step, step)], d_both.at[:, at])
+        if here:
+            write_pair(block, i)
     for copy in copies:
         copy.wait()
 
 
-def first_kernel(weighted_t, y, x_t, d_both, down_out, *refs):
-    down_buf, down_sems = refs[4:6]
-    chunks, _, step = down_buf.shape
-    copies = []
-    for i in range(chunks):
-        at = pl.ds(i * step, step)
-        tiles(down_buf.at[i], weighted_t, y.at[:, at])
-        copies.append(pltpu.make_async_copy(down_buf.at[i], down_out.at[:, at], down_sems.at[i]))
-        copies[i].start()
-    grads_kernel(0, False, x_t, d_both, *refs[:4], *refs[6:])
-    for copy in copies:
-        copy.wait()
-
-
-def grads_of(x_t, d_both, first_row, rows, before, down=()):
+def grads_of(weighted_t, y, x_t, d_both, wide, step, plan, before, state):
+    (downs, downs_here), (pairs, pairs_here) = plan
     width, slots = x_t.shape
-    cols = d_both.shape[1] // 2
-    step = 256
-    last = first_row + rows == width
-    chunks = rows // step - (0 if last else 1)
+    cols = weighted_t.shape[0]
     anywhere = pl.BlockSpec(memory_space=pl.ANY)
-    outs = [jax.ShapeDtypeStruct((width, cols), BF16)] * 2
-    outs += [] if last else [jax.ShapeDtypeStruct((step, cols), BF16)] * 2
-    out_specs = [anywhere] * 2 + whole(len(outs) - 2)
-    scratch = [
-        pltpu.VMEM((chunks, step, cols), BF16),
-        pltpu.VMEM((chunks, step, cols), BF16),
-        pltpu.SemaphoreType.DMA((chunks + 1, 2)),
-    ]
-    kernel = functools.partial(grads_kernel, first_row, last)
-    if down:
-        kernel = first_kernel
-        wide = 1024
-        outs = [jax.ShapeDtypeStruct((cols, width), BF16)] + outs
-        out_specs = [anywhere] + out_specs
-        scratch = [
-            pltpu.VMEM((width // wide, cols, wide), BF16),
-            pltpu.SemaphoreType.DMA((width // wide,)),
-        ] + scratch
-    elements = 2 * rows * cols + (width * cols if down else 0)
+
+    def down_blocks(count):
+        return (max(count, 1), cols, wide)
+
+    def pair_blocks(count):
+        return (max(count, 1), 2, step, cols)
+
+    kept = len(downs) - downs_here, len(pairs) - pairs_here
+    outs = [jax.ShapeDtypeStruct((cols, width), BF16)]
+    outs += [jax.ShapeDtypeStruct((width, cols), BF16)] * 2
+    outs += [jax.ShapeDtypeStruct(down_blocks(kept[0]), BF16)]
+    outs += [jax.ShapeDtypeStruct(pair_blocks(kept[1]), BF16)]
+    sems = 2 * (len(pairs) + len(downs) + sum(len(b) for b in before)) + 2
+    elements = len(downs) * cols * wide + 2 * len(pairs) * step * cols
+    operands = [weighted_t, y, x_t, d_both, *state[3:], *state[:3]]
     return pl.pallas_call(
-        kernel,
+        functools.partial(grads_kernel, plan, before),
         out_shape=outs,
-        in_specs=whole(2 + len(down)) + (whole(2) + [anywhere] * 2 if before else []),
-        out_specs=out_specs,
-        scratch_shapes=scratch,
-        input_output_aliases={4: 0, 5: 1} if before else {},
-        compiler_params=pltpu.CompilerParams(vmem_limit_bytes=20 * MIB),
+        in_specs=whole(4 + len(state[3:])) + [anywhere] * len(state[:3]),
+        out_specs=[anywhere] * 3 + whole(2),
+        scratch_shapes=[
+            pltpu.VMEM(down_blocks(downs_here), BF16),
+            pltpu.VMEM(pair_blocks(pairs_here), BF16),
+            pltpu.SemaphoreType.DMA((sems,)),
+            pltpu.SemaphoreType.DMA((sems,)),
+        ],
+        input_output_aliases={6: 0, 7: 1, 8: 2} if state else {},
+        compiler_params=pltpu.CompilerParams(vmem_limit_bytes=24 * MIB),
         cost_estimate=pl.CostEstimate(
             flops=8 * slots * elements, bytes_accessed=2 * elements, transcendentals=0
         ),
-    )(*down, x_t, d_both, *before[2:], *before[:2])
+    )(*operands)
 
 
 def make_shards(n):
@@ -391,17 +443,16 @@
         block_1 = swap(own, first)
         block_2 = swap(own, second)
         block_3 = swap(own, third)
-        gate_w = fetch(gate_weight, own)
+        cut = width // 3 * 2
+        gate_w, up_head = fetch([gate_weight, up_weight], [width, cut], own)
         block_1 = relay(block_1, gate_w, block_2)
         block_12 = swap(block_1, second)
         block_13 = swap(block_1, third)
         block_23 = swap(block_3, second)
-        up_w = fetch(up_weight, block_1)
-        block_12 = relay(block_12, up_w)
         block_123 = swap(block_12, third)
-        low_half = jnp.concatenate([own, block_1, block_2, block_12])
-        high_half = jnp.concatenate([block_3, block_13, block_23, block_123])
-        pieces = [low_half, high_half]
+        early = jnp.concatenate([own, block_3, block_1, block_12, block_2, block_23])
+        late = jnp.concatenate([block_13, block_123])
+        pieces = [early, late]
         pieces += [swap(piece, (1, 1)) for piece in pieces]
 
         work = 2 * rows * width * hidden
@@ -416,37 +467,58 @@
                 jax.ShapeDtypeStruct((width, rows), BF16),
                 jax.ShapeDtypeStruct((rows, width), BF16),
             ],
-            in_specs=whole(4) + [anywhere] + whole(2),
+            in_specs=whole(4) + [anywhere] * 2 + whole(2),
             out_specs=whole(6),
             scratch_shapes=[
                 pltpu.VMEM((rows, wide), BF16),
                 pltpu.VMEM((hidden, width), BF16),
-                pltpu.SemaphoreType.DMA((1, 4)),
+                pltpu.VMEM((width - cut, hidden), BF16),
+                pltpu.SemaphoreType.DMA((1, 2)),
+                pltpu.SemaphoreType.DMA((1, 2)),
             ],
-            compiler_params=pltpu.CompilerParams(vmem_limit_bytes=24 * MIB),
+            compiler_params=pltpu.CompilerParams(vmem_limit_bytes=28 * MIB),
             cost_estimate=pl.CostEstimate(
                 flops=16 * work, bytes_accessed=4 * width * hidden, transcendentals=0
             ),
-        )(*pieces, in_hbm(down_weight), gate_w, up_w)
-
-        for bits in [(1, 1)] + levels[::-1]:
+        )(*pieces, in_hbm(down_weight), in_hbm(up_weight), gate_w, up_head)
+
+        wide_block, step = width // 6, width // 24
+        plans = (
+            ((range(0, 4), 2), (range(0), 0)),
+            ((range(4, 6), 2), (range(0, 10), 6)),
+            ((range(0), 0), (range(10, 19), 5)),
+            ((range(0), 0), (range(19, 24), 5)),
+        )
+        state, before, states = (), (), []
+        for plan in plans:
+            state = grads_of(
+                weighted_t, y_all, x_t, d_both, wide_block, step, plan, before, tuple(state)
+            )
+            before = tuple(blocks[here:] for blocks, here in plan)
+            states.append(state[3])
+        grad_down, grad_gate, grad_up = state[:3]
+
+        few = own.shape[0]
+
+        def fold(kernel, kept, sent, args, after):
+            outs = [((kept, wide), F32)] + [((count, wide), BF16) for count in sent]
+            return call(kernel, outs, args, 4 * kept * wide, 16 * kept * wide, after=after)
+
+        got = swap(low, (1, 1))
+        keep, over_second, over_third = fold(
+            core_fold_kernel, 4 * few, (2 * few, 2 * few), [keep, got], [states[0]]
+        )
+        got = swap(over_second, second), swap(over_third, third)
+        keep, over_second, over_third = fold(
+            pair_fold_kernel, 2 * few, (few, few), [keep, *got], [states[1]]
+        )
+        got = swap(over_second, second), swap(over_third, third)
+        keep, low = fold(last_fold_kernel, few, (few,), [keep, *got], [states[2]])
+        got = swap(low, first)
+        for bits in levels[:-3][::-1]:
+            few //= 2
+            keep, low = fold(fold_kernel, few, (few,), [keep, got], [])
             got = swap(low, bits)
-            if bits == levels[0]:
-                break
-            half //= 2
-            keep, low = call(
-                fold_kernel,
-                [((half, wide), F32), ((half, wide), BF16)],
-                [keep, got],
-                4 * half * wide,
-                16 * half * wide,
-            )
-
-        cuts = [0, width // 3, 2 * width // 3, width]
-        grad_down, *pair = grads_of(x_t, d_both, 0, cuts[1], (), (weighted_t, y_all))
-        for start, stop in zip(cuts[1:], cuts[2:]):
-            pair = grads_of(x_t, d_both, start, stop - start, tuple(pair))
-        grad_gate, grad_up = pair
 
         grad_tokens, grad_logits = call(
             home_kernel,

time: 52.9 us -> 66.6 us (1.26)
  local copies, waits for them, and re-layouts: 0 us -> 12 us
  Pallas kernels: 26.5 us -> 30.1 us
  starting transfers between devices: 18.2 us -> 14.6 us
  waiting for transfers between devices: 6.76 us -> 8.86 us
    unnamed x0 -> x8, local copies, waits for them, and re-layouts: none -> 9.64 us
    ppermute x13 -> x15, starting transfers between devices: 18.2 us -> 14.6 us  [swap(): return lax.ppermute(block, 'blk', [(i, i ^ bits[i % 2]) for i in range(n)])]
    concatenate x0 -> x1, local copies, waits for them, and re-layouts: none -> 2.39 us  [shards(): jnp.concatenate([own, block_3, block_1, block_12, block_2, block_23])]
    pallas_call x1, Pallas kernels: 8.78 us -> 11 us  [shards(): pl.pallas_call(expert_kernel, out_shape=[jax.ShapeDtypeStruct((half, wide...]
    ppermute x13 -> x15, waiting for transfers between devices: 6.76 us -> 8.86 us  [swap(): return lax.ppermute(block, 'blk', [(i, i ^ bits[i % 2]) for i in range(n)])]
    pallas_call x5, Pallas kernels: 14.6 us -> 15.9 us  [the longest x4 11.8 us: grads_of(): pl.pallas_call(functools.partial(grads_kernel, plan, before), out_shape=o...]
  transfers between devices with their start and end apart: 13 -> 15, of which waited for: 5 -> 7; matrix products, arithmetic and copies ran while one was open for 1% -> 4% of each run, Pallas kernels for 28% -> 24%
where the time goes in v12:
time: 66.6 us; the launch traced here: 66.4 us
  Pallas kernels  30.1 us (45%)
  starting transfers between devices  14.6 us (22%)
  local copies, waits for them, and re-layouts  12 us (18%)
  waiting for transfers between devices  8.86 us (13%)
  between operations  0.78 us (1%)
    ppermute x15, starting transfers between devices, swap(): return lax.ppermute(block, 'blk', [(i, i ^ bits[i % 2]) for i in range(n)])  14.6 us
    pallas_call x4, Pallas kernels, grads_of(): pl.pallas_call(functools.partial(grads_kernel, plan, before), out_shape=o...  11.8 us
    pallas_call x1, Pallas kernels, shards(): pl.pallas_call(expert_kernel, out_shape=[jax.ShapeDtypeStruct((half, wide...  11 us
    unnamed x8, local copies, waits for them, and re-layouts  9.64 us
    ppermute x15, waiting for transfers between devices, swap(): return lax.ppermute(block, 'blk', [(i, i ^ bits[i % 2]) for i in range(n)])  8.86 us
    pallas_call x1, Pallas kernels, fetch(): pl.pallas_call(functools.partial(fetch_kernel, count), out_shape=[pltpu.V...  4.06 us
    concatenate x1, local copies, waits for them, and re-layouts, shards(): jnp.concatenate([own, block_3, block_1, block_12, block_2, block_23])  2.39 us
    pallas_call x1, Pallas kernels, shards(): pl.pallas_call(router_kernel, out_shape=[jax.ShapeDtypeStruct((slots, wid...  1.72 us
  transfers between devices with their start and end apart: 15, of which 7 were waited for; matrix products, arithmetic and copies ran while one was open for 4% of the time, Pallas kernels for 24%

profile of v12, /device:TPU:0, one launch (start us, length us, event | category | flops | bytes accessed | tf_op | source)
XLA Modules:
  0.0 66.4 jit_solution(13255566491430858153)
XLA Ops:
  0.6 1.7 %shard_map.135 = (bf16[4,12416]{1,0:T(4,128)(2,1)S(1)}, f32[1,16]{1,0:T(1,128)}, f32[1,16]{1,0:T(1,128)}, f32[8,16]{1,0:T(8,128)S(1)}, f32[8,16]{1,0:T(8,128)S(1)}, /*index=5*/f32[16,16]{1,0:T(8,128)S(1)}) custom-call(bf16[16,6144]{1,0:T(8,128)(2,1)} %tokens_in.1, f32[8,16]{1,0:T(8,128)} %bitcast.6, f32[8,16]{1,0:T(8,128)} %bitcast.7, s32[2,16]{1,0:T(2,128)} %bitcast.8, ...), custom_call_target="tpu_custom_call" | custom-call | flops 1048576 | bytes 16777216 | tf_op jit(solution)/shard_map/pallas_call | solution.py:413
  2.4 3.1 %collective-permute-start.2 = (bf16[4,12416]{1,0:T(4,128)(2,1)S(1)}, bf16[4,12416]{1,0:T(4,128)(2,1)S(1)}, u32[]{:S(2)}, u32[]{:S(2)}) collective-permute-start(bf16[4,12416]{1,0:T(4,128)(2,1)S(1)} %get-tuple-element.49.refs_2_), channel_id=1, source_target_pairs={{0,4},{1,3},{2,6},{3,1},{4,0},{5,7},{6,2},{7,5},{8,12},{9,11},{10,... | collective-permute-start | bytes 297992 | tf_op jit(solution)/shard_map/ppermute | solution.py:400
  5.5 2.6 %collective-permute-start.1 = (bf16[4,12416]{1,0:T(4,128)(2,1)S(1)}, bf16[4,12416]{1,0:T(4,128)(2,1)S(1)}, u32[]{:S(2)}, u32[]{:S(2)}) collective-permute-start(bf16[4,12416]{1,0:T(4,128)(2,1)S(1)} %get-tuple-element.49.refs_2_), channel_id=1, source_target_pairs={{0,8},{1,9},{2,10},{3,11},{4,12},{5,13},{6,14},{7,15},{8,0},{9,1},... | collective-permute-start | bytes 297992 | tf_op jit(solution)/shard_map/ppermute | solution.py:400
  8.0 1.5 %collective-permute-start = (bf16[4,12416]{1,0:T(4,128)(2,1)S(1)}, bf16[4,12416]{1,0:T(4,128)(2,1)S(1)}, u32[]{:S(2)}, u32[]{:S(2)}) collective-permute-start(bf16[4,12416]{1,0:T(4,128)(2,1)S(1)} %get-tuple-element.49.refs_2_), channel_id=1, source_target_pairs={{0,2},{1,5},{2,0},{3,7},{4,6},{5,1},{6,4},{7,3},{8,10},{9,13},{10,... | collective-permute-start | bytes 297992 | tf_op jit(solution)/shard_map/ppermute | solution.py:400
  9.6 4.1 %shard_map.136 = (bf16[6144,512]{1,0:T(8,128)(2,1)S(1)}, bf16[4096,512]{1,0:T(8,128)(2,1)S(1)}) custom-call(bf16[6144,512]{1,0:T(8,128)(2,1)} %refs_0_.1, bf16[6144,512]{1,0:T(8,128)(2,1)} %refs_5_.1, bf16[4,12416]{1,0:T(4,128)(2,1)S(1)} %get-tuple-element.49.refs_2_), custom_call_target="tpu_custom_call" | custom-call | bytes 12582912 | tf_op jit(solution)/shard_map/pallas_call | solution.py:148
  13.6 0.0 copy-start.2
  13.6 0.0 collective-permute-done.2.refs_1_
  13.7 0.0 collective-permute-done.1.block
  13.7 2.0 %copy-done.2 = bf16[4096,512]{1,0:T(8,128)(2,1)} copy-done((bf16[4096,512]{1,0:T(8,128)(2,1)}, bf16[4096,512]{1,0:T(8,128)(2,1)S(1)}, u32[]{:S(2)}) %copy-start.2) | copy-done | bytes 4194328
  15.6 2.7 %copy-done = bf16[6144,512]{1,0:T(8,128)(2,1)} copy-done((bf16[6144,512]{1,0:T(8,128)(2,1)}, bf16[6144,512]{1,0:T(8,128)(2,1)S(1)}, u32[]{:S(2)}) %copy-start) | copy-done | bytes 6291480
  18.3 0.4 collective-permute-start.3
  18.8 0.0 collective-permute-done
  18.8 1.6 %collective-permute-start.4 = (bf16[4,12416]{1,0:T(4,128)(2,1)S(1)}, bf16[4,12416]{1,0:T(4,128)(2,1)S(1)}, u32[]{:S(2)}, u32[]{:S(2)}) collective-permute-start(bf16[4,12416]{1,0:T(4,128)(2,1)S(1)} %collective-permute-done), channel_id=1, source_target_pairs={{0,4},{1,3},{2,6},{3,1},{4,0},{5,7},{6,2},{7,5},{8,12},{9,11},{10,... | collective-permute-start | bytes 297992 | tf_op jit(solution)/shard_map/ppermute | solution.py:400
  20.4 0.5 collective-permute-start.5
  20.9 2.7 %collective-permute-done.3 = bf16[4,12416]{1,0:T(4,128)(2,1)S(1)} collective-permute-done((bf16[4,12416]{1,0:T(4,128)(2,1)S(1)}, bf16[4,12416]{1,0:T(4,128)(2,1)S(1)}, u32[]{:S(2)}, u32[]{:S(2)}) %collective-permute-start.3) | collective-permute-done | bytes 99360 | tf_op jit(solution)/shard_map/ppermute | solution.py:400
  23.6 0.5 collective-permute-start.6
  24.1 1.6 %collective-permute-done.4 = bf16[4,12416]{1,0:T(4,128)(2,1)S(1)} collective-permute-done((bf16[4,12416]{1,0:T(4,128)(2,1)S(1)}, bf16[4,12416]{1,0:T(4,128)(2,1)S(1)}, u32[]{:S(2)}, u32[]{:S(2)}) %collective-permute-start.4) | collective-permute-done | bytes 99360 | tf_op jit(solution)/shard_map/ppermute | solution.py:400
  25.7 2.4 %concatenate.6.refs_0_ = bf16[24,12416]{1,0:T(8,128)(2,1)S(1)} concatenate(bf16[4,12416]{1,0:T(4,128)(2,1)S(1)} %get-tuple-element.49.refs_2_, bf16[4,12416]{1,0:T(4,128)(2,1)S(1)} %collective-permute-done, bf16[4,12416]{1,0:T(4,128)(2,1)S(1)} %shard_map.137, bf16[4,12416]{1,0:T(4,128)(2,1)S(1)} %collective-permute-done.3, bf16[4,12416]{1,0:T(4,128)(2,1)S(1)} %collective-permute-done.2.refs_1_, ...), dimensions={0} | concatenate | bytes 1191936 | tf_op jit(solution)/shard_map/concatenate | solution.py:453
  28.1 0.1 collective-permute-start.7
  28.1 0.0 collective-permute-done.5
  28.1 0.1 collective-permute-done.6
  28.2 0.1 pad_maximum_fusion.refs_1_
  28.3 0.5 collective-permute-start.8
  28.8 1.6 %collective-permute-done.8.refs_3_ = bf16[8,12416]{1,0:T(8,128)(2,1)S(1)} collective-permute-done((bf16[8,12416]{1,0:T(8,128)(2,1)S(1)}, bf16[8,12416]{1,0:T(8,128)(2,1)S(1)}, u32[]{:S(2)}, u32[]{:S(2)}) %collective-permute-start.8) | collective-permute-done | bytes 198688 | tf_op jit(solution)/shard_map/ppermute | solution.py:400
  30.4 0.0 collective-permute-done.7.refs_2_
  30.4 2.8 %copy-done.1 = bf16[6144,512]{1,0:T(8,128)(2,1)S(1)} copy-done((bf16[6144,512]{1,0:T(8,128)(2,1)S(1)}, bf16[6144,512]{1,0:T(8,128)(2,1)}, u32[]{:S(2)}) %copy-start.1) | copy-done | bytes 6291480
  33.2 2.2 %copy-done.3 = bf16[4096,512]{1,0:T(8,128)(2,1)S(1)} copy-done((bf16[4096,512]{1,0:T(8,128)(2,1)S(1)}, bf16[4096,512]{1,0:T(8,128)(2,1)}, u32[]{:S(2)}) %copy-start.3) | copy-done | bytes 4194328
  35.4 11.0 %shard_map.138 = (bf16[32,6272]{1,0:T(8,128)(2,1)S(1)}, f32[32,6272]{1,0:T(8,128)S(1)}, bf16[512,64]{1,0:T(8,128)(2,1)S(1)}, bf16[64,1024]{1,0:T(8,128)(2,1)S(1)...) custom-call(bf16[24,12416]{1,0:T(8,128)(2,1)S(1)} %concatenate.6.refs_0_, ...), custom_call_target="tpu_custom_call" | custom-call | flops 6442450944 | bytes 12582912 | tf_op jit(solution)/shard_map/pallas_call | solution.py:460
  46.5 0.2 collective-permute-start.9
  46.6 1.9 %shard_map.139 = (bf16[512,6144]{1,0:T(8,128)(2,1)}, bf16[6144,512]{1,0:T(8,128)(2,1)}, bf16[6144,512]{1,0:T(8,128)(2,1)}, bf16[2,512,1024]{2,1,0:T(8,128)(2,1)S(1)}, bf16[1,2,256,512]{3,2,1,0:T(8,128)(2,1)S(1)}) custom-call(bf16[512,64]{1,0:T(8,128)(2,1)S(1)} %get-tuple-element.52.refs_0_, bf16[64,6144]{1,0:T(8,128)(2,1)S(1)} %get-tuple-element.53.refs_1_, ...), custom_call_target="tpu_custom_call" | custom-call | flops 1073741824 | bytes 4194304 | tf_op jit(solution)/shard_map/pallas_call | solution.py:372
  48.6 0.0 collective-permute-done.9.got
  48.6 0.2 shard_map.143
  48.8 0.5 collective-permute-start.10
  49.3 0.5 collective-permute-start.11
  49.8 3.5 %shard_map.140 = (bf16[512,6144]{1,0:T(8,128)(2,1)}, bf16[6144,512]{1,0:T(8,128)(2,1)}, bf16[6144,512]{1,0:T(8,128)(2,1)}, bf16[1,512,1024]{2,1,0:T(8,128)(2,1)S(1)}, bf16[4,2,256,512]{3,2,1,0:T(8,128)(2,1)S(1)}) custom-call(bf16[512,64]{1,0:T(8,128)(2,1)S(1)} %get-tuple-element.52.refs_0_, ...), custom_call_target="tpu_custom_call", output_to_operand_aliasing={{0}: (6, {}), {1}: (7, {}), {2}: (8, {})} | custom-call | flops 1879048192 | bytes 7340032 | tf_op jit(solution)/shard_map/pallas_call | solution.py:372
  53.3 0.8 %collective-permute-done.10.got_second = bf16[8,6272]{1,0:T(8,128)(2,1)S(1)} collective-permute-done((bf16[8,6272]{1,0:T(8,128)(2,1)S(1)}, bf16[8,6272]{1,0:T(8,128)(2,1)S(1)}, u32[]{:S(2)}, u32[]{:S(2)}) %collective-permute-start.10) | collective-permute-done | bytes 100384 | tf_op jit(solution)/shard_map/ppermute | solution.py:400
  54.2 0.0 collective-permute-done.11.got_third
  54.2 0.2 shard_map.144
  54.3 1.4 %collective-permute-start.12 = (bf16[4,6272]{1,0:T(4,128)(2,1)S(1)}, bf16[4,6272]{1,0:T(4,128)(2,1)S(1)}, u32[]{:S(2)}, u32[]{:S(2)}) collective-permute-start(bf16[4,6272]{1,0:T(4,128)(2,1)S(1)} %get-tuple-element.80), channel_id=1, source_target_pairs={{0,4},{1,3},{2,6},{3,1},{4,0},{5,7},{6,2},{7,5},{8,12},{9,11},{10,... | collective-permute-start | bytes 150536 | tf_op jit(solution)/shard_map/ppermute | solution.py:400
  55.7 1.0 %collective-permute-start.13 = (bf16[4,6272]{1,0:T(4,128)(2,1)S(1)}, bf16[4,6272]{1,0:T(4,128)(2,1)S(1)}, u32[]{:S(2)}, u32[]{:S(2)}) collective-permute-start(bf16[4,6272]{1,0:T(4,128)(2,1)S(1)} %get-tuple-element.81), channel_id=1, source_target_pairs={{0,2},{1,5},{2,0},{3,7},{4,6},{5,1},{6,4},{7,3},{8,10},{9,13},{10,... | collective-permute-start | bytes 150536 | tf_op jit(solution)/shard_map/ppermute | solution.py:400
  56.7 2.7 %shard_map.141 = (bf16[512,6144]{1,0:T(8,128)(2,1)}, bf16[6144,512]{1,0:T(8,128)(2,1)}, bf16[6144,512]{1,0:T(8,128)(2,1)}, bf16[1,512,1024]{2,1,0:T(8,128)(2,1)S(1)}, bf16[4,2,256,512]{3,2,1,0:T(8,128)(2,1)S(1)}) custom-call(bf16[512,64]{1,0:T(8,128)(2,1)S(1)} %get-tuple-element.52.refs_0_, ...), custom_call_target="tpu_custom_call", output_to_operand_aliasing={{0}: (6, {}), {1}: (7, {}), {2}: (8, {})} | custom-call | flops 1207959552 | bytes 4718592 | tf_op jit(solution)/shard_map/pallas_call | solution.py:372
  59.3 0.0 collective-permute-done.12.got_second
  59.3 0.5 collective-permute-done.13.got_third
  59.8 0.2 shard_map.145
  60.0 0.2 collective-permute-start.14
  60.2 3.7 %shard_map.142 = (bf16[512,6144]{1,0:T(8,128)(2,1)}, bf16[6144,512]{1,0:T(8,128)(2,1)}, bf16[6144,512]{1,0:T(8,128)(2,1)}, bf16[1,512,1024]{2,1,0:T(8,128)(2,1)}, bf16[1,2,256,512]{3,2,1,0:T(8,128)(2,1)}) custom-call(bf16[512,64]{1,0:T(8,128)(2,1)S(1)} %get-tuple-element.52.refs_0_, ...), custom_call_target="tpu_custom_call", output_to_operand_aliasing={{0}: (6, {}), {1}: (7, {}), {2}: (8, {})} | custom-call | flops 671088640 | bytes 2621440 | tf_op jit(solution)/shard_map/pallas_call | solution.py:372
  63.9 1.6 %collective-permute-done.14.got = bf16[4,6272]{1,0:T(4,128)(2,1)S(1)} collective-permute-done((bf16[4,6272]{1,0:T(4,128)(2,1)S(1)}, bf16[4,6272]{1,0:T(4,128)(2,1)S(1)}, u32[]{:S(2)}, u32[]{:S(2)}) %collective-permute-start.14) | collective-permute-done | bytes 50208 | tf_op jit(solution)/shard_map/ppermute | solution.py:400
  65.5 0.9 %shard_map.146 = (bf16[16,6144]{1,0:T(8,128)(2,1)}, f32[8,16]{1,0:T(8,128)}) custom-call(f32[4,6272]{1,0:T(4,128)S(1)} %get-tuple-element.82.have, bf16[4,6272]{1,0:T(4,128)(2,1)S(1)} %collective-permute-done.14.got, f32[16,16]{1,0:T(8,128)S(1)} %get-tuple-element.84.select, f32[8,16]{1,0:T(8,128)S(1)} %get-tuple-element.85.base, ...), custom_call_target="tpu_custom_call" | custom-call | flops 1048576 | bytes 262144 | tf_op jit(solution)/shard_map/pallas_call | solution.py:25
  (4 shorter events, 0.0 us)
Async XLA Ops:
  2.4 11.3 %collective-permute-start.2 = (bf16[4,12416]{1,0:T(4,128)(2,1)S(1)}, bf16[4,12416]{1,0:T(4,128)(2,1)S(1)}, u32[]{:S(2)}, u32[]{:S(2)}) collective-permute-start(bf16[4,12416]{1,0:T(4,128)(2,1)S(1)} %get-tuple-element.49.refs_2_), channel_id=1, source_target_pairs={{0,4},{1,3},{2,6},{3,1},{4,0},{5,7},{6,2},{7,5},{8,12},{9,11},{10,... | collective-permute-start | bytes 297992 | tf_op jit(solution)/shard_map/ppermute | solution.py:400
  5.5 8.2 %collective-permute-start.1 = (bf16[4,12416]{1,0:T(4,128)(2,1)S(1)}, bf16[4,12416]{1,0:T(4,128)(2,1)S(1)}, u32[]{:S(2)}, u32[]{:S(2)}) collective-permute-start(bf16[4,12416]{1,0:T(4,128)(2,1)S(1)} %get-tuple-element.49.refs_2_), channel_id=1, source_target_pairs={{0,8},{1,9},{2,10},{3,11},{4,12},{5,13},{6,14},{7,15},{8,0},{9,1},... | collective-permute-start | bytes 297992 | tf_op jit(solution)/shard_map/ppermute | solution.py:400
  8.0 10.8 %collective-permute-start = (bf16[4,12416]{1,0:T(4,128)(2,1)S(1)}, bf16[4,12416]{1,0:T(4,128)(2,1)S(1)}, u32[]{:S(2)}, u32[]{:S(2)}) collective-permute-start(bf16[4,12416]{1,0:T(4,128)(2,1)S(1)} %get-tuple-element.49.refs_2_), channel_id=1, source_target_pairs={{0,2},{1,5},{2,0},{3,7},{4,6},{5,1},{6,4},{7,3},{8,10},{9,13},{10,... | collective-permute-start | bytes 297992 | tf_op jit(solution)/shard_map/ppermute | solution.py:400
  13.6 2.0 %copy-start.2 = (bf16[4096,512]{1,0:T(8,128)(2,1)}, bf16[4096,512]{1,0:T(8,128)(2,1)S(1)}, u32[]{:S(2)}) copy-start(bf16[4096,512]{1,0:T(8,128)(2,1)S(1)} %get-tuple-element.51.refs_7_) | copy-start | bytes 12582916
  15.6 2.7 %copy-start = (bf16[6144,512]{1,0:T(8,128)(2,1)}, bf16[6144,512]{1,0:T(8,128)(2,1)S(1)}, u32[]{:S(2)}) copy-start(bf16[6144,512]{1,0:T(8,128)(2,1)S(1)} %get-tuple-element.50.refs_0_.refs_6_) | copy-start | bytes 18874372
  18.3 5.2 %collective-permute-start.3 = (bf16[4,12416]{1,0:T(4,128)(2,1)S(1)}, bf16[4,12416]{1,0:T(4,128)(2,1)S(1)}, u32[]{:S(2)}, u32[]{:S(2)}) collective-permute-start(bf16[4,12416]{1,0:T(4,128)(2,1)S(1)} %shard_map.137), channel_id=1, source_target_pairs={{0,4},{1,3},{2,6},{3,1},{4,0},{5,7},{6,2},{7,5},{8,12},{9,11},{10,... | collective-permute-start | bytes 297992 | tf_op jit(solution)/shard_map/ppermute | solution.py:400
  18.8 6.9 %collective-permute-start.4 = (bf16[4,12416]{1,0:T(4,128)(2,1)S(1)}, bf16[4,12416]{1,0:T(4,128)(2,1)S(1)}, u32[]{:S(2)}, u32[]{:S(2)}) collective-permute-start(bf16[4,12416]{1,0:T(4,128)(2,1)S(1)} %collective-permute-done), channel_id=1, source_target_pairs={{0,4},{1,3},{2,6},{3,1},{4,0},{5,7},{6,2},{7,5},{8,12},{9,11},{10,... | collective-permute-start | bytes 297992 | tf_op jit(solution)/shard_map/ppermute | solution.py:400
  20.4 7.8 %collective-permute-start.5 = (bf16[4,12416]{1,0:T(4,128)(2,1)S(1)}, bf16[4,12416]{1,0:T(4,128)(2,1)S(1)}, u32[]{:S(2)}, u32[]{:S(2)}) collective-permute-start(bf16[4,12416]{1,0:T(4,128)(2,1)S(1)} %shard_map.137), channel_id=1, source_target_pairs={{0,2},{1,5},{2,0},{3,7},{4,6},{5,1},{6,4},{7,3},{8,10},{9,13},{10,... | collective-permute-start | bytes 297992 | tf_op jit(solution)/shard_map/ppermute | solution.py:400
  23.6 4.6 %collective-permute-start.6 = (bf16[4,12416]{1,0:T(4,128)(2,1)S(1)}, bf16[4,12416]{1,0:T(4,128)(2,1)S(1)}, u32[]{:S(2)}, u32[]{:S(2)}) collective-permute-start(bf16[4,12416]{1,0:T(4,128)(2,1)S(1)} %collective-permute-done.3), channel_id=1, source_target_pairs={{0,2},{1,5},{2,0},{3,7},{4,6},{5,1},{6,4},{7,3},{8,10},{9,13},{10,... | collective-permute-start | bytes 297992 | tf_op jit(solution)/shard_map/ppermute | solution.py:400
  28.1 2.4 %collective-permute-start.7 = (bf16[24,12416]{1,0:T(8,128)(2,1)S(1)}, bf16[24,12416]{1,0:T(8,128)(2,1)S(1)}, u32[]{:S(2)}, u32[]{:S(2)}) collective-permute-start(bf16[24,12416]{1,0:T(8,128)(2,1)S(1)} %concatenate.6.refs_0_), channel_id=1, source_target_pairs={{0,1},{1,0},{2,3},{3,2},{4,5},{5,4},{6,7},{7,6},{8,9},{9,8},{10,11... | collective-permute-start | bytes 1787912 | tf_op jit(solution)/shard_map/ppermute | solution.py:400
  28.3 2.1 %collective-permute-start.8 = (bf16[8,12416]{1,0:T(8,128)(2,1)S(1)}, bf16[8,12416]{1,0:T(8,128)(2,1)S(1)}, u32[]{:S(2)}, u32[]{:S(2)}) collective-permute-start(bf16[8,12416]{1,0:T(8,128)(2,1)S(1)} %pad_maximum_fusion.refs_1_), channel_id=1, source_target_pairs={{0,1},{1,0},{2,3},{3,2},{4,5},{5,4},{6,7},{7,6},{8,9},{9,8},{10,11... | collective-permute-start | bytes 595976 | tf_op jit(solution)/shard_map/ppermute | solution.py:400
  30.4 2.8 %copy-start.1 = (bf16[6144,512]{1,0:T(8,128)(2,1)S(1)}, bf16[6144,512]{1,0:T(8,128)(2,1)}, u32[]{:S(2)}) copy-start(bf16[6144,512]{1,0:T(8,128)(2,1)} %copy-done) | copy-start | bytes 18874372
  33.2 2.2 %copy-start.3 = (bf16[4096,512]{1,0:T(8,128)(2,1)S(1)}, bf16[4096,512]{1,0:T(8,128)(2,1)}, u32[]{:S(2)}) copy-start(bf16[4096,512]{1,0:T(8,128)(2,1)} %copy-done.2) | copy-start | bytes 12582916
  46.5 2.1 %collective-permute-start.9 = (bf16[32,6272]{1,0:T(8,128)(2,1)S(1)}, bf16[32,6272]{1,0:T(8,128)(2,1)S(1)}, u32[]{:S(2)}, u32[]{:S(2)}) collective-permute-start(bf16[32,6272]{1,0:T(8,128)(2,1)S(1)} %get-tuple-element.75), channel_id=1, source_target_pairs={{0,1},{1,0},{2,3},{3,2},{4,5},{5,4},{6,7},{7,6},{8,9},{9,8},{10,11... | collective-permute-start | bytes 1204232 | tf_op jit(solution)/shard_map/ppermute | solution.py:400
  48.8 5.4 %collective-permute-start.10 = (bf16[8,6272]{1,0:T(8,128)(2,1)S(1)}, bf16[8,6272]{1,0:T(8,128)(2,1)S(1)}, u32[]{:S(2)}, u32[]{:S(2)}) collective-permute-start(bf16[8,6272]{1,0:T(8,128)(2,1)S(1)} %get-tuple-element.77), channel_id=1, source_target_pairs={{0,4},{1,3},{2,6},{3,1},{4,0},{5,7},{6,2},{7,5},{8,12},{9,11},{10,... | collective-permute-start | bytes 301064 | tf_op jit(solution)/shard_map/ppermute | solution.py:400
  49.3 4.9 %collective-permute-start.11 = (bf16[8,6272]{1,0:T(8,128)(2,1)S(1)}, bf16[8,6272]{1,0:T(8,128)(2,1)S(1)}, u32[]{:S(2)}, u32[]{:S(2)}) collective-permute-start(bf16[8,6272]{1,0:T(8,128)(2,1)S(1)} %get-tuple-element.78), channel_id=1, source_target_pairs={{0,2},{1,5},{2,0},{3,7},{4,6},{5,1},{6,4},{7,3},{8,10},{9,13},{10,... | collective-permute-start | bytes 301064 | tf_op jit(solution)/shard_map/ppermute | solution.py:400
  54.3 5.0 %collective-permute-start.12 = (bf16[4,6272]{1,0:T(4,128)(2,1)S(1)}, bf16[4,6272]{1,0:T(4,128)(2,1)S(1)}, u32[]{:S(2)}, u32[]{:S(2)}) collective-permute-start(bf16[4,6272]{1,0:T(4,128)(2,1)S(1)} %get-tuple-element.80), channel_id=1, source_target_pairs={{0,4},{1,3},{2,6},{3,1},{4,0},{5,7},{6,2},{7,5},{8,12},{9,11},{10,... | collective-permute-start | bytes 150536 | tf_op jit(solution)/shard_map/ppermute | solution.py:400
  55.7 4.1 %collective-permute-start.13 = (bf16[4,6272]{1,0:T(4,128)(2,1)S(1)}, bf16[4,6272]{1,0:T(4,128)(2,1)S(1)}, u32[]{:S(2)}, u32[]{:S(2)}) collective-permute-start(bf16[4,6272]{1,0:T(4,128)(2,1)S(1)} %get-tuple-element.81), channel_id=1, source_target_pairs={{0,2},{1,5},{2,0},{3,7},{4,6},{5,1},{6,4},{7,3},{8,10},{9,13},{10,... | collective-permute-start | bytes 150536 | tf_op jit(solution)/shard_map/ppermute | solution.py:400
  60.0 5.5 %collective-permute-start.14 = (bf16[4,6272]{1,0:T(4,128)(2,1)S(1)}, bf16[4,6272]{1,0:T(4,128)(2,1)S(1)}, u32[]{:S(2)}, u32[]{:S(2)}) collective-permute-start(bf16[4,6272]{1,0:T(4,128)(2,1)S(1)} %get-tuple-element.83), channel_id=1, source_target_pairs={{0,8},{1,9},{2,10},{3,11},{4,12},{5,13},{6,14},{7,15},{8,0},{9,1},... | collective-permute-start | bytes 150536 | tf_op jit(solution)/shard_map/ppermute | solution.py:400

commit v13 on v11

--- a/solution.py
+++ b/solution.py
@@ -120,36 +120,43 @@
 def fetch_copies(sources, targets, sems):
     parts = sems.shape[1]
     copies = []
-    for k, (source, target) in enumerate(zip(sources, targets)):
-        step = source.shape[0] // parts
+    for k, ((source, row), target) in enumerate(zip(sources, targets)):
+        step = target.shape[0] // parts
         for i in range(parts):
-            at = pl.ds(i * step, step)
-            copies.append(pltpu.make_async_copy(source.at[at], target.at[at], sems.at[k, i]))
+            copies.append(
+                pltpu.make_async_copy(
+                    source.at[pl.ds(row + i * step, step)],
+                    target.at[pl.ds(i * step, step)],
+                    sems.at[k, i],
+                )
+            )
     return copies
 
 
-def fetch_kernel(source, after, target, sems):
-    copies = fetch_copies([source], [target], sems)
+def fetch_kernel(count, *refs):
+    sources, targets, sems = refs[:count], refs[count + 1 : -1], refs[-1]
+    copies = fetch_copies([(source, 0) for source in sources], targets, sems)
     for copy in copies:
         copy.start()
     for copy in copies:
         copy.wait()
 
 
-def fetch(weight, after):
+def fetch(weights, rows, after):
     anywhere = pl.BlockSpec(memory_space=pl.ANY)
+    count = len(weights)
     out = pl.pallas_call(
-        fetch_kernel,
-        out_shape=pltpu.VMEM(weight.shape, weight.dtype),
-        in_specs=[anywhere] * 2,
-        out_specs=whole(1)[0],
-        scratch_shapes=[pltpu.SemaphoreType.DMA((1, 4))],
+        functools.partial(fetch_kernel, count),
+        out_shape=[pltpu.VMEM((r, w.shape[1]), w.dtype) for w, r in zip(weights, rows)],
+        in_specs=[anywhere] * (count + 1),
+        out_specs=whole(count),
+        scratch_shapes=[pltpu.SemaphoreType.DMA((count, 4))],
         compiler_params=pltpu.CompilerParams(vmem_limit_bytes=8 * MIB),
         cost_estimate=pl.CostEstimate(
-            flops=0, bytes_accessed=2 * weight.size, transcendentals=0
+            flops=0, bytes_accessed=2 * sum(w.size for w in weights), transcendentals=0
         ),
-    )(in_hbm(weight), after)
-    return in_vmem(out)
+    )(*[in_hbm(w) for w in weights], after)
+    return [in_vmem(w) for w in out]
 
 
 def relay_kernel(block, *refs):
@@ -170,12 +177,12 @@
 
 
 def expert_kernel(*refs):
-    pieces, (down_in, gate_w, up_w), refs = refs[:4], refs[4:7], refs[7:]
+    pieces, (down_in, gate_w, up_w), refs = refs[:6], refs[6:9], refs[9:]
     send, keep, weighted_t, d_both, x_t, y, x, down_w, sems = refs
     rows, width, hidden_dim = x.shape[0], gate_w.shape[0], gate_w.shape[1]
     wide = width + LANES
     half = rows // 2
-    copies = fetch_copies([down_in], [down_w], sems)
+    copies = fetch_copies([(down_in, 0)], [down_w], sems)
     for copy in copies:
         copy.start()
     for c in range(0, wide, LANES):
@@ -184,9 +191,9 @@
         x[:, at] = block.astype(BF16)
         if c < width:
             x_t[at, :] = block.T.astype(BF16)
-    quarter = rows // 4
-    for i, ref in enumerate(pieces):
-        y[i * quarter : (i + 1) * quarter, :] = ref[:, wide:]
+    for c in range(0, width, LANES):
+        parts = [ref[:, wide + c : wide + c + LANES].astype(F32) for ref in pieces]
+        y[:, c : c + LANES] = jnp.concatenate(parts).astype(BF16)
     pre_gate = dot(x[:, :width], gate_w[...], ((1,), (0,)))
     pre_up = dot(x[:, :width], up_w[...], ((1,), (0,)))
     for copy in copies:
@@ -391,17 +398,17 @@
         block_1 = swap(own, first)
         block_2 = swap(own, second)
         block_3 = swap(own, third)
-        gate_w = fetch(gate_weight, own)
+        gate_w, up_w = fetch([gate_weight, up_weight], [width, width], own)
         block_1 = relay(block_1, gate_w, block_2)
         block_12 = swap(block_1, second)
         block_13 = swap(block_1, third)
         block_23 = swap(block_3, second)
-        up_w = fetch(up_weight, block_1)
-        block_12 = relay(block_12, up_w)
         block_123 = swap(block_12, third)
-        low_half = jnp.concatenate([own, block_1, block_2, block_12])
-        high_half = jnp.concatenate([block_3, block_13, block_23, block_123])
-        pieces = [low_half, high_half]
+        pieces = [
+            jnp.concatenate([own, block_1, block_2, block_12]),
+            jnp.concatenate([block_3, block_13]),
+            jnp.concatenate([block_23, block_123]),
+        ]
         pieces += [swap(piece, (1, 1)) for piece in pieces]
 
         work = 2 * rows * width * hidden
@@ -416,7 +423,7 @@
                 jax.ShapeDtypeStruct((width, rows), BF16),
                 jax.ShapeDtypeStruct((rows, width), BF16),
             ],
-            in_specs=whole(4) + [anywhere] + whole(2),
+            in_specs=whole(6) + [anywhere] + whole(2),
             out_specs=whole(6),
             scratch_shapes=[
                 pltpu.VMEM((rows, wide), BF16),

time: 52.9 us -> 55.5 us (1.049)
  waiting for transfers between devices: 6.76 us -> 11.3 us
  starting transfers between devices: 18.2 us -> 15.4 us
  Pallas kernels: 26.5 us -> 27.4 us
    ppermute x13 -> x14, waiting for transfers between devices: 6.76 us -> 11.3 us  [swap(): return lax.ppermute(block, 'blk', [(i, i ^ bits[i % 2]) for i in range(n)])]
    ppermute x13 -> x14, starting transfers between devices: 18.2 us -> 15.4 us  [swap(): return lax.ppermute(block, 'blk', [(i, i ^ bits[i % 2]) for i in range(n)])]
    pallas_call x1, Pallas kernels: 8.78 us -> 10.7 us  [shards(): pl.pallas_call(expert_kernel, out_shape=[jax.ShapeDtypeStruct((half, wide...]
    pallas_call x2 -> x1, Pallas kernels: 5.73 us -> 4.7 us  [fetch(): pl.pallas_call(functools.partial(fetch_kernel, count), out_shape=[pltpu.V...]
  transfers between devices with their start and end apart: 13 -> 14, of which waited for: 5 -> 6; matrix products, arithmetic and copies ran while one was open for 1% -> 1% of each run, Pallas kernels for 28% -> 25%
where the time goes in v13:
time: 55.5 us; the launch traced here: 55.3 us
  Pallas kernels  27.4 us (49%)
  starting transfers between devices  15.4 us (28%)
  waiting for transfers between devices  11.3 us (20%)
  between operations  0.78 us (1%)
    ppermute x14, starting transfers between devices, swap(): return lax.ppermute(block, 'blk', [(i, i ^ bits[i % 2]) for i in range(n)])  15.4 us
    ppermute x14, waiting for transfers between devices, swap(): return lax.ppermute(block, 'blk', [(i, i ^ bits[i % 2]) for i in range(n)])  11.3 us
    pallas_call x1, Pallas kernels, shards(): pl.pallas_call(expert_kernel, out_shape=[jax.ShapeDtypeStruct((half, wide...  10.7 us
    pallas_call x3, Pallas kernels, grads_of(): pl.pallas_call(kernel, out_shape=outs, in_specs=whole(2 + len(down)) + (w...  8.87 us
    pallas_call x1, Pallas kernels, fetch(): pl.pallas_call(functools.partial(fetch_kernel, count), out_shape=[pltpu.V...  4.7 us
    pallas_call x1, Pallas kernels, shards(): pl.pallas_call(router_kernel, out_shape=[jax.ShapeDtypeStruct((slots, wid...  1.72 us
    pallas_call x4, Pallas kernels, call(): pl.pallas_call(kernel, out_shape=[jax.ShapeDtypeStruct(s, t) for s, t in...  1.38 us
  transfers between devices with their start and end apart: 14, of which 6 were waited for; matrix products, arithmetic and copies ran while one was open for 1% of the time, Pallas kernels for 25%

profile of v13, /device:TPU:0, one launch (start us, length us, event | category | flops | bytes accessed | tf_op | source)
XLA Modules:
  0.0 55.3 jit_solution(16721084856013526962)
XLA Ops:
  0.6 1.7 %shard_map.135 = (bf16[4,12416]{1,0:T(4,128)(2,1)S(1)}, f32[1,16]{1,0:T(1,128)}, f32[1,16]{1,0:T(1,128)}, f32[8,16]{1,0:T(8,128)S(1)}, f32[8,16]{1,0:T(8,128)S(1)}, /*index=5*/f32[16,16]{1,0:T(8,128)S(1)}) custom-call(bf16[16,6144]{1,0:T(8,128)(2,1)} %tokens_in.1, f32[8,16]{1,0:T(8,128)} %bitcast.6, f32[8,16]{1,0:T(8,128)} %bitcast.7, s32[2,16]{1,0:T(2,128)} %bitcast.8, ...), custom_call_target="tpu_custom_call" | custom-call | flops 1048576 | bytes 16777216 | tf_op jit(solution)/shard_map/pallas_call | solution.py:368
  2.4 3.1 %collective-permute-start.1 = (bf16[4,12416]{1,0:T(4,128)(2,1)S(1)}, bf16[4,12416]{1,0:T(4,128)(2,1)S(1)}, u32[]{:S(2)}, u32[]{:S(2)}) collective-permute-start(bf16[4,12416]{1,0:T(4,128)(2,1)S(1)} %get-tuple-element.40.refs_2_), channel_id=1, source_target_pairs={{0,4},{1,3},{2,6},{3,1},{4,0},{5,7},{6,2},{7,5},{8,12},{9,11},{10,... | collective-permute-start | bytes 297992 | tf_op jit(solution)/shard_map/ppermute | solution.py:355
  5.5 2.6 %collective-permute-start = (bf16[4,12416]{1,0:T(4,128)(2,1)S(1)}, bf16[4,12416]{1,0:T(4,128)(2,1)S(1)}, u32[]{:S(2)}, u32[]{:S(2)}) collective-permute-start(bf16[4,12416]{1,0:T(4,128)(2,1)S(1)} %get-tuple-element.40.refs_2_), channel_id=1, source_target_pairs={{0,8},{1,9},{2,10},{3,11},{4,12},{5,13},{6,14},{7,15},{8,0},{9,1},... | collective-permute-start | bytes 297992 | tf_op jit(solution)/shard_map/ppermute | solution.py:355
  8.0 1.5 %collective-permute-start.3 = (bf16[4,12416]{1,0:T(4,128)(2,1)S(1)}, bf16[4,12416]{1,0:T(4,128)(2,1)S(1)}, u32[]{:S(2)}, u32[]{:S(2)}) collective-permute-start(bf16[4,12416]{1,0:T(4,128)(2,1)S(1)} %get-tuple-element.40.refs_2_), channel_id=1, source_target_pairs={{0,2},{1,5},{2,0},{3,7},{4,6},{5,1},{6,4},{7,3},{8,10},{9,13},{10,... | collective-permute-start | bytes 297992 | tf_op jit(solution)/shard_map/ppermute | solution.py:355
  9.6 4.7 %shard_map.136 = (bf16[6144,512]{1,0:T(8,128)(2,1)S(1)}, bf16[6144,512]{1,0:T(8,128)(2,1)S(1)}) custom-call(bf16[6144,512]{1,0:T(8,128)(2,1)} %refs_0_.1, bf16[6144,512]{1,0:T(8,128)(2,1)} %refs_1_.1, bf16[4,12416]{1,0:T(4,128)(2,1)S(1)} %get-tuple-element.40.refs_2_), custom_call_target="tpu_custom_call" | custom-call | bytes 12582912 | tf_op jit(solution)/shard_map/pallas_call | solution.py:148
  14.3 0.0 collective-permute-done.1.refs_1_
  14.3 0.0 collective-permute-done.block
  14.3 0.6 %collective-permute-start.4 = (bf16[4,12416]{1,0:T(4,128)(2,1)S(1)}, bf16[4,12416]{1,0:T(4,128)(2,1)S(1)}, u32[]{:S(2)}, u32[]{:S(2)}) collective-permute-start(bf16[4,12416]{1,0:T(4,128)(2,1)S(1)} %shard_map.137), channel_id=1, source_target_pairs={{0,2},{1,5},{2,0},{3,7},{4,6},{5,1},{6,4},{7,3},{8,10},{9,13},{10,... | collective-permute-start | bytes 297992 | tf_op jit(solution)/shard_map/ppermute | solution.py:355
  14.9 0.4 collective-permute-start.2
  15.3 0.0 collective-permute-done.3
  15.3 1.6 %collective-permute-start.5 = (bf16[4,12416]{1,0:T(4,128)(2,1)S(1)}, bf16[4,12416]{1,0:T(4,128)(2,1)S(1)}, u32[]{:S(2)}, u32[]{:S(2)}) collective-permute-start(bf16[4,12416]{1,0:T(4,128)(2,1)S(1)} %collective-permute-done.3), channel_id=1, source_target_pairs={{0,4},{1,3},{2,6},{3,1},{4,0},{5,7},{6,2},{7,5},{8,12},{9,11},{10,... | collective-permute-start | bytes 297992 | tf_op jit(solution)/shard_map/ppermute | solution.py:355
  16.9 2.4 %collective-permute-done.4 = bf16[4,12416]{1,0:T(4,128)(2,1)S(1)} collective-permute-done((bf16[4,12416]{1,0:T(4,128)(2,1)S(1)}, bf16[4,12416]{1,0:T(4,128)(2,1)S(1)}, u32[]{:S(2)}, u32[]{:S(2)}) %collective-permute-start.4) | collective-permute-done | bytes 99360 | tf_op jit(solution)/shard_map/ppermute | solution.py:355
  19.3 0.1 pad_maximum_fusion.1.refs_1_
  19.4 0.1 collective-permute-start.8
  19.5 0.0 collective-permute-done.2
  19.5 1.5 %collective-permute-start.6 = (bf16[4,12416]{1,0:T(4,128)(2,1)S(1)}, bf16[4,12416]{1,0:T(4,128)(2,1)S(1)}, u32[]{:S(2)}, u32[]{:S(2)}) collective-permute-start(bf16[4,12416]{1,0:T(4,128)(2,1)S(1)} %collective-permute-done.2), channel_id=1, source_target_pairs={{0,2},{1,5},{2,0},{3,7},{4,6},{5,1},{6,4},{7,3},{8,10},{9,13},{10,... | collective-permute-start | bytes 297992 | tf_op jit(solution)/shard_map/ppermute | solution.py:355
  21.0 0.2 pad_maximum_fusion.refs_0_
  21.3 0.1 collective-permute-start.7
  21.3 0.0 collective-permute-done.5
  21.4 2.9 %collective-permute-done.6 = bf16[4,12416]{1,0:T(4,128)(2,1)S(1)} collective-permute-done((bf16[4,12416]{1,0:T(4,128)(2,1)S(1)}, bf16[4,12416]{1,0:T(4,128)(2,1)S(1)}, u32[]{:S(2)}, u32[]{:S(2)}) %collective-permute-start.6) | collective-permute-done | bytes 99360 | tf_op jit(solution)/shard_map/ppermute | solution.py:355
  24.2 0.1 pad_maximum_fusion.2.refs_2_
  24.3 0.1 collective-permute-start.9
  24.4 0.0 collective-permute-done.8.refs_4_
  24.4 1.4 %collective-permute-done.9.refs_5_ = bf16[8,12416]{1,0:T(8,128)(2,1)S(1)} collective-permute-done((bf16[8,12416]{1,0:T(8,128)(2,1)S(1)}, bf16[8,12416]{1,0:T(8,128)(2,1)S(1)}, u32[]{:S(2)}, u32[]{:S(2)}) %collective-permute-start.9) | collective-permute-done | bytes 198688 | tf_op jit(solution)/shard_map/ppermute | solution.py:355
  25.8 0.0 collective-permute-done.7.refs_3_
  25.8 10.7 %shard_map.138 = (bf16[32,6272]{1,0:T(8,128)(2,1)S(1)}, f32[32,6272]{1,0:T(8,128)S(1)}, bf16[512,64]{1,0:T(8,128)(2,1)S(1)}, bf16[64,1024]{1,0:T(8,128)(2,1)S(1)...) custom-call(bf16[16,12416]{1,0:T(8,128)(2,1)S(1)} %pad_maximum_fusion.refs_0_, ...), custom_call_target="tpu_custom_call" | custom-call | flops 6442450944 | bytes 12582912 | tf_op jit(solution)/shard_map/pallas_call | solution.py:416
  36.6 0.2 collective-permute-start.10
  36.8 1.6 %collective-permute-done.10.got = bf16[32,6272]{1,0:T(8,128)(2,1)S(1)} collective-permute-done((bf16[32,6272]{1,0:T(8,128)(2,1)S(1)}, bf16[32,6272]{1,0:T(8,128)(2,1)S(1)}, u32[]{:S(2)}, u32[]{:S(2)}) %collective-permute-start.10) | collective-permute-done | bytes 401440 | tf_op jit(solution)/shard_map/ppermute | solution.py:355
  38.4 0.2 shard_map.142
  38.5 1.5 %collective-permute-start.11 = (bf16[16,6272]{1,0:T(8,128)(2,1)S(1)}, bf16[16,6272]{1,0:T(8,128)(2,1)S(1)}, u32[]{:S(2)}, u32[]{:S(2)}) collective-permute-start(bf16[16,6272]{1,0:T(8,128)(2,1)S(1)} %get-tuple-element.61), channel_id=1, source_target_pairs={{0,2},{1,5},{2,0},{3,7},{4,6},{5,1},{6,4},{7,3},{8,10},{9,13},{10,... | collective-permute-start | bytes 602120 | tf_op jit(solution)/shard_map/ppermute | solution.py:355
  40.0 4.4 %shard_map.139 = (bf16[512,6144]{1,0:T(8,128)(2,1)}, bf16[6144,512]{1,0:T(8,128)(2,1)}, bf16[6144,512]{1,0:T(8,128)(2,1)}, bf16[256,512]{1,0:T(8,128)(2,1)S(1)}, bf16[256,512]{1,0:T(8,128)(2,1)S(1)}) custom-call(bf16[512,64]{1,0:T(8,128)(2,1)S(1)} %get-tuple-element.45.weighted_t, bf16[64,6144]{1,0:T(8,128)(2,1)S(1)} %get-tuple-element.46.y, ...), custom_call_target="tpu_custom_call" | custom-call | flops 2684354560 | bytes 10485760 | tf_op jit(solution)/shard_map/pallas_call | solution.py:332
  44.4 0.0 collective-permute-done.11.got
  44.4 0.1 shard_map.143
  44.6 1.1 %collective-permute-start.12 = (bf16[8,6272]{1,0:T(8,128)(2,1)S(1)}, bf16[8,6272]{1,0:T(8,128)(2,1)S(1)}, u32[]{:S(2)}, u32[]{:S(2)}) collective-permute-start(bf16[8,6272]{1,0:T(8,128)(2,1)S(1)} %get-tuple-element.63), channel_id=1, source_target_pairs={{0,4},{1,3},{2,6},{3,1},{4,0},{5,7},{6,2},{7,5},{8,12},{9,11},{10,... | collective-permute-start | bytes 301064 | tf_op jit(solution)/shard_map/ppermute | solution.py:355
  45.6 2.2 %shard_map.140 = (bf16[6144,512]{1,0:T(8,128)(2,1)}, bf16[6144,512]{1,0:T(8,128)(2,1)}, bf16[256,512]{1,0:T(8,128)(2,1)S(1)}, bf16[256,512]{1,0:T(8,128)(2,1)S(1)}) custom-call(bf16[6144,64]{1,0:T(8,128)(2,1)S(1)} %get-tuple-element.43.x_t, bf16[64,1024]{1,0:T(8,128)(2,1)S(1)} %get-tuple-element.44.d_both, ...), custom_call_target="tpu_custom_call", output_to_operand_aliasing={{0}: (4, {}), {1}: (5, {})} | custom-call | flops 1073741824 | bytes 4194304 | tf_op jit(solution)/shard_map/pallas_call | solution.py:332
  47.8 1.4 %collective-permute-done.12.got = bf16[8,6272]{1,0:T(8,128)(2,1)S(1)} collective-permute-done((bf16[8,6272]{1,0:T(8,128)(2,1)S(1)}, bf16[8,6272]{1,0:T(8,128)(2,1)S(1)}, u32[]{:S(2)}, u32[]{:S(2)}) %collective-permute-start.12) | collective-permute-done | bytes 100384 | tf_op jit(solution)/shard_map/ppermute | solution.py:355
  49.2 0.2 shard_map.144
  49.4 1.1 %collective-permute-start.13 = (bf16[4,6272]{1,0:T(4,128)(2,1)S(1)}, bf16[4,6272]{1,0:T(4,128)(2,1)S(1)}, u32[]{:S(2)}, u32[]{:S(2)}) collective-permute-start(bf16[4,6272]{1,0:T(4,128)(2,1)S(1)} %get-tuple-element.65), channel_id=1, source_target_pairs={{0,8},{1,9},{2,10},{3,11},{4,12},{5,13},{6,14},{7,15},{8,0},{9,1},... | collective-permute-start | bytes 150536 | tf_op jit(solution)/shard_map/ppermute | solution.py:355
  50.5 2.3 %shard_map.141 = (bf16[6144,512]{1,0:T(8,128)(2,1)}, bf16[6144,512]{1,0:T(8,128)(2,1)}) custom-call(bf16[6144,64]{1,0:T(8,128)(2,1)S(1)} %get-tuple-element.43.x_t, bf16[64,1024]{1,0:T(8,128)(2,1)S(1)} %get-tuple-element.44.d_both, bf16[256,512]{1,0:T(8,128)(2,1)S(1)} %get-tuple-element.51.refs_0_, ...), custom_call_target="tpu_custom_call", output_to_operand_aliasing={{0}: (4, {}), {1}: (5, {})} | custom-call | flops 1073741824 | bytes 4194304 | tf_op jit(solution)/shard_map/pallas_call | solution.py:332
  52.8 1.6 %collective-permute-done.13.got = bf16[4,6272]{1,0:T(4,128)(2,1)S(1)} collective-permute-done((bf16[4,6272]{1,0:T(4,128)(2,1)S(1)}, bf16[4,6272]{1,0:T(4,128)(2,1)S(1)}, u32[]{:S(2)}, u32[]{:S(2)}) %collective-permute-start.13) | collective-permute-done | bytes 50208 | tf_op jit(solution)/shard_map/ppermute | solution.py:355
  54.4 0.9 %shard_map.145 = (bf16[16,6144]{1,0:T(8,128)(2,1)}, f32[8,16]{1,0:T(8,128)}) custom-call(f32[4,6272]{1,0:T(4,128)S(1)} %get-tuple-element.64.have, bf16[4,6272]{1,0:T(4,128)(2,1)S(1)} %collective-permute-done.13.got, f32[16,16]{1,0:T(8,128)S(1)} %get-tuple-element.66.select, f32[8,16]{1,0:T(8,128)S(1)} %get-tuple-element.67.base, ...), custom_call_target="tpu_custom_call" | custom-call | flops 1048576 | bytes 262144 | tf_op jit(solution)/shard_map/pallas_call | solution.py:25
  (1 shorter events, 0.0 us)
Async XLA Ops:
  2.4 11.9 %collective-permute-start.1 = (bf16[4,12416]{1,0:T(4,128)(2,1)S(1)}, bf16[4,12416]{1,0:T(4,128)(2,1)S(1)}, u32[]{:S(2)}, u32[]{:S(2)}) collective-permute-start(bf16[4,12416]{1,0:T(4,128)(2,1)S(1)} %get-tuple-element.40.refs_2_), channel_id=1, source_target_pairs={{0,4},{1,3},{2,6},{3,1},{4,0},{5,7},{6,2},{7,5},{8,12},{9,11},{10,... | collective-permute-start | bytes 297992 | tf_op jit(solution)/shard_map/ppermute | solution.py:355
  5.5 8.8 %collective-permute-start = (bf16[4,12416]{1,0:T(4,128)(2,1)S(1)}, bf16[4,12416]{1,0:T(4,128)(2,1)S(1)}, u32[]{:S(2)}, u32[]{:S(2)}) collective-permute-start(bf16[4,12416]{1,0:T(4,128)(2,1)S(1)} %get-tuple-element.40.refs_2_), channel_id=1, source_target_pairs={{0,8},{1,9},{2,10},{3,11},{4,12},{5,13},{6,14},{7,15},{8,0},{9,1},... | collective-permute-start | bytes 297992 | tf_op jit(solution)/shard_map/ppermute | solution.py:355
  8.0 7.3 %collective-permute-start.3 = (bf16[4,12416]{1,0:T(4,128)(2,1)S(1)}, bf16[4,12416]{1,0:T(4,128)(2,1)S(1)}, u32[]{:S(2)}, u32[]{:S(2)}) collective-permute-start(bf16[4,12416]{1,0:T(4,128)(2,1)S(1)} %get-tuple-element.40.refs_2_), channel_id=1, source_target_pairs={{0,2},{1,5},{2,0},{3,7},{4,6},{5,1},{6,4},{7,3},{8,10},{9,13},{10,... | collective-permute-start | bytes 297992 | tf_op jit(solution)/shard_map/ppermute | solution.py:355
  14.3 5.0 %collective-permute-start.4 = (bf16[4,12416]{1,0:T(4,128)(2,1)S(1)}, bf16[4,12416]{1,0:T(4,128)(2,1)S(1)}, u32[]{:S(2)}, u32[]{:S(2)}) collective-permute-start(bf16[4,12416]{1,0:T(4,128)(2,1)S(1)} %shard_map.137), channel_id=1, source_target_pairs={{0,2},{1,5},{2,0},{3,7},{4,6},{5,1},{6,4},{7,3},{8,10},{9,13},{10,... | collective-permute-start | bytes 297992 | tf_op jit(solution)/shard_map/ppermute | solution.py:355
  14.9 4.6 %collective-permute-start.2 = (bf16[4,12416]{1,0:T(4,128)(2,1)S(1)}, bf16[4,12416]{1,0:T(4,128)(2,1)S(1)}, u32[]{:S(2)}, u32[]{:S(2)}) collective-permute-start(bf16[4,12416]{1,0:T(4,128)(2,1)S(1)} %shard_map.137), channel_id=1, source_target_pairs={{0,4},{1,3},{2,6},{3,1},{4,0},{5,7},{6,2},{7,5},{8,12},{9,11},{10,... | collective-permute-start | bytes 297992 | tf_op jit(solution)/shard_map/ppermute | solution.py:355
  15.3 6.0 %collective-permute-start.5 = (bf16[4,12416]{1,0:T(4,128)(2,1)S(1)}, bf16[4,12416]{1,0:T(4,128)(2,1)S(1)}, u32[]{:S(2)}, u32[]{:S(2)}) collective-permute-start(bf16[4,12416]{1,0:T(4,128)(2,1)S(1)} %collective-permute-done.3), channel_id=1, source_target_pairs={{0,4},{1,3},{2,6},{3,1},{4,0},{5,7},{6,2},{7,5},{8,12},{9,11},{10,... | collective-permute-start | bytes 297992 | tf_op jit(solution)/shard_map/ppermute | solution.py:355
  19.4 5.0 %collective-permute-start.8 = (bf16[8,12416]{1,0:T(8,128)(2,1)S(1)}, bf16[8,12416]{1,0:T(8,128)(2,1)S(1)}, u32[]{:S(2)}, u32[]{:S(2)}) collective-permute-start(bf16[8,12416]{1,0:T(8,128)(2,1)S(1)} %pad_maximum_fusion.1.refs_1_), channel_id=1, source_target_pairs={{0,1},{1,0},{2,3},{3,2},{4,5},{5,4},{6,7},{7,6},{8,9},{9,8},{10,11... | collective-permute-start | bytes 595976 | tf_op jit(solution)/shard_map/ppermute | solution.py:355
  19.5 4.7 %collective-permute-start.6 = (bf16[4,12416]{1,0:T(4,128)(2,1)S(1)}, bf16[4,12416]{1,0:T(4,128)(2,1)S(1)}, u32[]{:S(2)}, u32[]{:S(2)}) collective-permute-start(bf16[4,12416]{1,0:T(4,128)(2,1)S(1)} %collective-permute-done.2), channel_id=1, source_target_pairs={{0,2},{1,5},{2,0},{3,7},{4,6},{5,1},{6,4},{7,3},{8,10},{9,13},{10,... | collective-permute-start | bytes 297992 | tf_op jit(solution)/shard_map/ppermute | solution.py:355
  21.3 4.6 %collective-permute-start.7 = (bf16[16,12416]{1,0:T(8,128)(2,1)S(1)}, bf16[16,12416]{1,0:T(8,128)(2,1)S(1)}, u32[]{:S(2)}, u32[]{:S(2)}) collective-permute-start(bf16[16,12416]{1,0:T(8,128)(2,1)S(1)} %pad_maximum_fusion.refs_0_), channel_id=1, source_target_pairs={{0,1},{1,0},{2,3},{3,2},{4,5},{5,4},{6,7},{7,6},{8,9},{9,8},{10,11... | collective-permute-start | bytes 1191944 | tf_op jit(solution)/shard_map/ppermute | solution.py:355
  24.3 1.5 %collective-permute-start.9 = (bf16[8,12416]{1,0:T(8,128)(2,1)S(1)}, bf16[8,12416]{1,0:T(8,128)(2,1)S(1)}, u32[]{:S(2)}, u32[]{:S(2)}) collective-permute-start(bf16[8,12416]{1,0:T(8,128)(2,1)S(1)} %pad_maximum_fusion.2.refs_2_), channel_id=1, source_target_pairs={{0,1},{1,0},{2,3},{3,2},{4,5},{5,4},{6,7},{7,6},{8,9},{9,8},{10,11... | collective-permute-start | bytes 595976 | tf_op jit(solution)/shard_map/ppermute | solution.py:355
  36.6 1.8 %collective-permute-start.10 = (bf16[32,6272]{1,0:T(8,128)(2,1)S(1)}, bf16[32,6272]{1,0:T(8,128)(2,1)S(1)}, u32[]{:S(2)}, u32[]{:S(2)}) collective-permute-start(bf16[32,6272]{1,0:T(8,128)(2,1)S(1)} %get-tuple-element.59), channel_id=1, source_target_pairs={{0,1},{1,0},{2,3},{3,2},{4,5},{5,4},{6,7},{7,6},{8,9},{9,8},{10,11... | collective-permute-start | bytes 1204232 | tf_op jit(solution)/shard_map/ppermute | solution.py:355
  38.5 5.9 %collective-permute-start.11 = (bf16[16,6272]{1,0:T(8,128)(2,1)S(1)}, bf16[16,6272]{1,0:T(8,128)(2,1)S(1)}, u32[]{:S(2)}, u32[]{:S(2)}) collective-permute-start(bf16[16,6272]{1,0:T(8,128)(2,1)S(1)} %get-tuple-element.61), channel_id=1, source_target_pairs={{0,2},{1,5},{2,0},{3,7},{4,6},{5,1},{6,4},{7,3},{8,10},{9,13},{10,... | collective-permute-start | bytes 602120 | tf_op jit(solution)/shard_map/ppermute | solution.py:355
  44.6 4.7 %collective-permute-start.12 = (bf16[8,6272]{1,0:T(8,128)(2,1)S(1)}, bf16[8,6272]{1,0:T(8,128)(2,1)S(1)}, u32[]{:S(2)}, u32[]{:S(2)}) collective-permute-start(bf16[8,6272]{1,0:T(8,128)(2,1)S(1)} %get-tuple-element.63), channel_id=1, source_target_pairs={{0,4},{1,3},{2,6},{3,1},{4,0},{5,7},{6,2},{7,5},{8,12},{9,11},{10,... | collective-permute-start | bytes 301064 | tf_op jit(solution)/shard_map/ppermute | solution.py:355
  49.4 5.0 %collective-permute-start.13 = (bf16[4,6272]{1,0:T(4,128)(2,1)S(1)}, bf16[4,6272]{1,0:T(4,128)(2,1)S(1)}, u32[]{:S(2)}, u32[]{:S(2)}) collective-permute-start(bf16[4,6272]{1,0:T(4,128)(2,1)S(1)} %get-tuple-element.65), channel_id=1, source_target_pairs={{0,8},{1,9},{2,10},{3,11},{4,12},{5,13},{6,14},{7,15},{8,0},{9,1},... | collective-permute-start | bytes 150536 | tf_op jit(solution)/shard_map/ppermute | solution.py:355

commit v14 on v11

--- a/solution.py
+++ b/solution.py
@@ -164,18 +164,18 @@
         out_specs=whole(1)[0],
         compiler_params=pltpu.CompilerParams(vmem_limit_bytes=8 * MIB),
         cost_estimate=pl.CostEstimate(
-            flops=0, bytes_accessed=4 * block.size, transcendentals=0
+            flops=0, bytes_accessed=4 * MIB, transcendentals=0
         ),
     )(block, *after)
 
 
 def expert_kernel(*refs):
-    pieces, (down_in, gate_w, up_w), refs = refs[:4], refs[4:7], refs[7:]
-    send, keep, weighted_t, d_both, x_t, y, x, down_w, sems = refs
+    pieces, (up_in, gate_w, down_w), refs = refs[:4], refs[4:7], refs[7:]
+    send, keep, weighted_t, d_both, x_t, y, x, up_w, sems = refs
     rows, width, hidden_dim = x.shape[0], gate_w.shape[0], gate_w.shape[1]
     wide = width + LANES
     half = rows // 2
-    copies = fetch_copies([down_in], [down_w], sems)
+    copies = fetch_copies([up_in], [up_w], sems)
     for copy in copies:
         copy.start()
     for c in range(0, wide, LANES):
@@ -188,10 +188,10 @@
     for i, ref in enumerate(pieces):
         y[i * quarter : (i + 1) * quarter, :] = ref[:, wide:]
     pre_gate = dot(x[:, :width], gate_w[...], ((1,), (0,)))
+    back = dot(y[...], down_w[...], ((1,), (1,)))
+    for copy in copies:
+        copy.wait()
     pre_up = dot(x[:, :width], up_w[...], ((1,), (0,)))
-    for copy in copies:
-        copy.wait()
-    back = dot(y[...], down_w[...], ((1,), (1,)))
     g = x[:, width:][:, 0:1].astype(F32)
     sig = jax.nn.sigmoid(pre_gate)
     act = pre_gate * sig
@@ -388,17 +388,18 @@
         for bits in levels[:-3]:
             own = jnp.concatenate([own, swap(own, bits)])
         first, second, third = levels[-3:]
-        block_1 = swap(own, first)
+        block_1 = relay(relay(swap(own, first)))
         block_2 = swap(own, second)
         block_3 = swap(own, third)
         gate_w = fetch(gate_weight, own)
-        block_1 = relay(block_1, gate_w, block_2)
+        block_1 = relay(block_1, gate_w, block_2, block_3)
         block_12 = swap(block_1, second)
-        block_13 = swap(block_1, third)
-        block_23 = swap(block_3, second)
-        up_w = fetch(up_weight, block_1)
-        block_12 = relay(block_12, up_w)
-        block_123 = swap(block_12, third)
+        again = relay(block_1)
+        block_13 = swap(again, third)
+        down_w = fetch(down_weight, again)
+        block_12 = relay(block_12, down_w)
+        block_123 = relay(swap(block_12, third))
+        block_23 = swap(relay(block_3, block_12), second)
         low_half = jnp.concatenate([own, block_1, block_2, block_12])
         high_half = jnp.concatenate([block_3, block_13, block_23, block_123])
         pieces = [low_half, high_half]
@@ -420,14 +421,14 @@
             out_specs=whole(6),
             scratch_shapes=[
                 pltpu.VMEM((rows, wide), BF16),
-                pltpu.VMEM((hidden, width), BF16),
+                pltpu.VMEM((width, hidden), BF16),
                 pltpu.SemaphoreType.DMA((1, 4)),
             ],
             compiler_params=pltpu.CompilerParams(vmem_limit_bytes=24 * MIB),
             cost_estimate=pl.CostEstimate(
                 flops=16 * work, bytes_accessed=4 * width * hidden, transcendentals=0
             ),
-        )(*pieces, in_hbm(down_weight), gate_w, up_w)
+        )(*pieces, in_hbm(up_weight), gate_w, down_w)
 
         for bits in [(1, 1)] + levels[::-1]:
             got = swap(low, bits)

time: 52.9 us -> 56.2 us (1.062)
  waiting for transfers between devices: 6.76 us -> 11.2 us
  starting transfers between devices: 18.2 us -> 14.9 us
  Pallas kernels: 26.5 us -> 28.6 us
    ppermute x13, waiting for transfers between devices: 6.76 us -> 11.2 us  [swap(): return lax.ppermute(block, 'blk', [(i, i ^ bits[i % 2]) for i in range(n)])]
    ppermute x13, starting transfers between devices: 18.2 us -> 14.9 us  [swap(): return lax.ppermute(block, 'blk', [(i, i ^ bits[i % 2]) for i in range(n)])]
    pallas_call x1, Pallas kernels: 8.78 us -> 10.9 us  [shards(): pl.pallas_call(expert_kernel, out_shape=[jax.ShapeDtypeStruct((half, wide...]
  transfers between devices with their start and end apart: 13 -> 13, of which waited for: 5 -> 9; matrix products, arithmetic and copies ran while one was open for 1% -> 1% of each run, Pallas kernels for 28% -> 26%
where the time goes in v14:
time: 56.2 us; the launch traced here: 56 us
  Pallas kernels  28.6 us (51%)
  starting transfers between devices  14.9 us (27%)
  waiting for transfers between devices  11.2 us (20%)
  between operations  0.79 us (1%)
    ppermute x13, starting transfers between devices, swap(): return lax.ppermute(block, 'blk', [(i, i ^ bits[i % 2]) for i in range(n)])  14.9 us
    ppermute x13, waiting for transfers between devices, swap(): return lax.ppermute(block, 'blk', [(i, i ^ bits[i % 2]) for i in range(n)])  11.2 us
    pallas_call x1, Pallas kernels, shards(): pl.pallas_call(expert_kernel, out_shape=[jax.ShapeDtypeStruct((half, wide...  10.9 us
    pallas_call x3, Pallas kernels, grads_of(): pl.pallas_call(kernel, out_shape=outs, in_specs=whole(2 + len(down)) + (w...  8.86 us
    pallas_call x2, Pallas kernels, fetch(): pl.pallas_call(fetch_kernel, out_shape=pltpu.VMEM(weight.shape, weight.dt...  5.73 us
    pallas_call x1, Pallas kernels, shards(): pl.pallas_call(router_kernel, out_shape=[jax.ShapeDtypeStruct((slots, wid...  1.72 us
    pallas_call x4, Pallas kernels, call(): pl.pallas_call(kernel, out_shape=[jax.ShapeDtypeStruct(s, t) for s, t in...  1.38 us
  transfers between devices with their start and end apart: 13, of which 9 were waited for; matrix products, arithmetic and copies ran while one was open for 1% of the time, Pallas kernels for 26%

profile of v14, /device:TPU:0, one launch (start us, length us, event | category | flops | bytes accessed | tf_op | source)
XLA Modules:
  0.0 56.0 jit_solution(14166554795313251542)
XLA Ops:
  0.6 1.7 %shard_map.135 = (bf16[4,12416]{1,0:T(4,128)(2,1)S(1)}, f32[1,16]{1,0:T(1,128)}, f32[1,16]{1,0:T(1,128)}, f32[8,16]{1,0:T(8,128)S(1)}, f32[8,16]{1,0:T(8,128)S(1)}, /*index=5*/f32[16,16]{1,0:T(8,128)S(1)}) custom-call(bf16[16,6144]{1,0:T(8,128)(2,1)} %tokens_in.1, f32[8,16]{1,0:T(8,128)} %bitcast.6, f32[8,16]{1,0:T(8,128)} %bitcast.7, s32[2,16]{1,0:T(2,128)} %bitcast.8, ...), custom_call_target="tpu_custom_call" | custom-call | flops 1048576 | bytes 16777216 | tf_op jit(solution)/shard_map/pallas_call | solution.py:361
  2.4 4.1 %collective-permute-start = (bf16[4,12416]{1,0:T(4,128)(2,1)S(1)}, bf16[4,12416]{1,0:T(4,128)(2,1)S(1)}, u32[]{:S(2)}, u32[]{:S(2)}) collective-permute-start(bf16[4,12416]{1,0:T(4,128)(2,1)S(1)} %get-tuple-element.38.after), channel_id=1, source_target_pairs={{0,8},{1,9},{2,10},{3,11},{4,12},{5,13},{6,14},{7,15},{8,0},{9,1},... | collective-permute-start | bytes 297992 | tf_op jit(solution)/shard_map/ppermute | solution.py:348
  6.5 1.5 %collective-permute-start.2 = (bf16[4,12416]{1,0:T(4,128)(2,1)S(1)}, bf16[4,12416]{1,0:T(4,128)(2,1)S(1)}, u32[]{:S(2)}, u32[]{:S(2)}) collective-permute-start(bf16[4,12416]{1,0:T(4,128)(2,1)S(1)} %get-tuple-element.38.after), channel_id=1, source_target_pairs={{0,2},{1,5},{2,0},{3,7},{4,6},{5,1},{6,4},{7,3},{8,10},{9,13},{10,... | collective-permute-start | bytes 297992 | tf_op jit(solution)/shard_map/ppermute | solution.py:348
  8.0 1.6 %collective-permute-start.1 = (bf16[4,12416]{1,0:T(4,128)(2,1)S(1)}, bf16[4,12416]{1,0:T(4,128)(2,1)S(1)}, u32[]{:S(2)}, u32[]{:S(2)}) collective-permute-start(bf16[4,12416]{1,0:T(4,128)(2,1)S(1)} %get-tuple-element.38.after), channel_id=1, source_target_pairs={{0,4},{1,3},{2,6},{3,1},{4,0},{5,7},{6,2},{7,5},{8,12},{9,11},{10,... | collective-permute-start | bytes 297992 | tf_op jit(solution)/shard_map/ppermute | solution.py:348
  9.6 2.9 %shard_map.138.refs_0_.refs_5_ = bf16[6144,512]{1,0:T(8,128)(2,1)S(1)} custom-call(bf16[6144,512]{1,0:T(8,128)(2,1)} %source.2, bf16[4,12416]{1,0:T(4,128)(2,1)S(1)} %get-tuple-element.38.after), custom_call_target="tpu_custom_call" | custom-call | bytes 6291456 | tf_op jit(solution)/shard_map/pallas_call | solution.py:141
  12.4 0.0 collective-permute-done.block
  12.5 0.0 collective-permute-done.2.refs_2_.block
  12.5 0.1 collective-permute-done.1.refs_1_
  12.6 1.6 %collective-permute-start.3 = (bf16[4,12416]{1,0:T(4,128)(2,1)S(1)}, bf16[4,12416]{1,0:T(4,128)(2,1)S(1)}, u32[]{:S(2)}, u32[]{:S(2)}) collective-permute-start(bf16[4,12416]{1,0:T(4,128)(2,1)S(1)} %shard_map.139.block), channel_id=1, source_target_pairs={{0,4},{1,3},{2,6},{3,1},{4,0},{5,7},{6,2},{7,5},{8,12},{9,11},{10,... | collective-permute-start | bytes 297992 | tf_op jit(solution)/shard_map/ppermute | solution.py:348
  14.3 0.6 %collective-permute-start.4 = (bf16[4,12416]{1,0:T(4,128)(2,1)S(1)}, bf16[4,12416]{1,0:T(4,128)(2,1)S(1)}, u32[]{:S(2)}, u32[]{:S(2)}) collective-permute-start(bf16[4,12416]{1,0:T(4,128)(2,1)S(1)} %shard_map.140.after), channel_id=1, source_target_pairs={{0,2},{1,5},{2,0},{3,7},{4,6},{5,1},{6,4},{7,3},{8,10},{9,13},{10,... | collective-permute-start | bytes 297992 | tf_op jit(solution)/shard_map/ppermute | solution.py:348
  14.9 2.9 %shard_map.141.refs_0_.refs_6_ = bf16[512,6144]{1,0:T(8,128)(2,1)S(1)} custom-call(bf16[512,6144]{1,0:T(8,128)(2,1)} %source.3, bf16[4,12416]{1,0:T(4,128)(2,1)S(1)} %shard_map.140.after), custom_call_target="tpu_custom_call" | custom-call | bytes 6291456 | tf_op jit(solution)/shard_map/pallas_call | solution.py:141
  17.8 0.4 collective-permute-done.3.block
  18.2 1.2 %collective-permute-start.6 = (bf16[4,12416]{1,0:T(4,128)(2,1)S(1)}, bf16[4,12416]{1,0:T(4,128)(2,1)S(1)}, u32[]{:S(2)}, u32[]{:S(2)}) collective-permute-start(bf16[4,12416]{1,0:T(4,128)(2,1)S(1)} %shard_map.142.refs_0_), channel_id=1, source_target_pairs={{0,2},{1,5},{2,0},{3,7},{4,6},{5,1},{6,4},{7,3},{8,10},{9,13},{10,... | collective-permute-start | bytes 297992 | tf_op jit(solution)/shard_map/ppermute | solution.py:348
  19.3 0.5 collective-permute-start.5
  19.9 0.2 pad_maximum_fusion.refs_0_
  20.1 0.1 collective-permute-start.7
  20.2 2.7 %collective-permute-done.6.block = bf16[4,12416]{1,0:T(4,128)(2,1)S(1)} collective-permute-done((bf16[4,12416]{1,0:T(4,128)(2,1)S(1)}, bf16[4,12416]{1,0:T(4,128)(2,1)S(1)}, u32[]{:S(2)}, u32[]{:S(2)}) %collective-permute-start.6) | collective-permute-done | bytes 99360 | tf_op jit(solution)/shard_map/ppermute | solution.py:348
  22.9 0.0 collective-permute-done.4
  22.9 1.2 %collective-permute-done.5 = bf16[4,12416]{1,0:T(4,128)(2,1)S(1)} collective-permute-done((bf16[4,12416]{1,0:T(4,128)(2,1)S(1)}, bf16[4,12416]{1,0:T(4,128)(2,1)S(1)}, u32[]{:S(2)}, u32[]{:S(2)}) %collective-permute-start.5) | collective-permute-done | bytes 99360 | tf_op jit(solution)/shard_map/ppermute | solution.py:348
  24.0 0.2 pad_maximum_fusion.1.refs_1_
  24.3 0.1 collective-permute-start.8
  24.4 0.0 collective-permute-done.7.refs_2_
  24.4 1.7 %collective-permute-done.8.refs_3_ = bf16[16,12416]{1,0:T(8,128)(2,1)S(1)} collective-permute-done((bf16[16,12416]{1,0:T(8,128)(2,1)S(1)}, bf16[16,12416]{1,0:T(8,128)(2,1)S(1)}, u32[]{:S(2)}, u32[]{:S(2)}) %collective-permute-start.8) | collective-permute-done | bytes 397344 | tf_op jit(solution)/shard_map/ppermute | solution.py:348
  26.1 10.9 %shard_map.145 = (bf16[32,6272]{1,0:T(8,128)(2,1)S(1)}, f32[32,6272]{1,0:T(8,128)S(1)}, bf16[512,64]{1,0:T(8,128)(2,1)S(1)}, bf16[64,1024]{1,0:T(8,128)(2,1)S(1)...) custom-call(bf16[16,12416]{1,0:T(8,128)(2,1)S(1)} %pad_maximum_fusion.refs_0_, ...), custom_call_target="tpu_custom_call" | custom-call | flops 6442450944 | bytes 12582912 | tf_op jit(solution)/shard_map/pallas_call | solution.py:410
  37.0 0.2 collective-permute-start.9
  37.2 1.6 %collective-permute-done.9.got = bf16[32,6272]{1,0:T(8,128)(2,1)S(1)} collective-permute-done((bf16[32,6272]{1,0:T(8,128)(2,1)S(1)}, bf16[32,6272]{1,0:T(8,128)(2,1)S(1)}, u32[]{:S(2)}, u32[]{:S(2)}) %collective-permute-start.9) | collective-permute-done | bytes 401440 | tf_op jit(solution)/shard_map/ppermute | solution.py:348
  38.8 0.2 shard_map.149
  38.9 1.0 %collective-permute-start.10 = (bf16[16,6272]{1,0:T(8,128)(2,1)S(1)}, bf16[16,6272]{1,0:T(8,128)(2,1)S(1)}, u32[]{:S(2)}, u32[]{:S(2)}) collective-permute-start(bf16[16,6272]{1,0:T(8,128)(2,1)S(1)} %get-tuple-element.57), channel_id=1, source_target_pairs={{0,2},{1,5},{2,0},{3,7},{4,6},{5,1},{6,4},{7,3},{8,10},{9,13},{10,... | collective-permute-start | bytes 602120 | tf_op jit(solution)/shard_map/ppermute | solution.py:348
  39.9 4.3 %shard_map.146 = (bf16[512,6144]{1,0:T(8,128)(2,1)}, bf16[6144,512]{1,0:T(8,128)(2,1)}, bf16[6144,512]{1,0:T(8,128)(2,1)}, bf16[256,512]{1,0:T(8,128)(2,1)S(1)}, bf16[256,512]{1,0:T(8,128)(2,1)S(1)}) custom-call(bf16[512,64]{1,0:T(8,128)(2,1)S(1)} %get-tuple-element.41.weighted_t, bf16[64,6144]{1,0:T(8,128)(2,1)S(1)} %get-tuple-element.42.y, ...), custom_call_target="tpu_custom_call" | custom-call | flops 2684354560 | bytes 10485760 | tf_op jit(solution)/shard_map/pallas_call | solution.py:325
  44.3 0.4 collective-permute-done.10.got
  44.7 0.1 shard_map.150
  44.9 0.5 collective-permute-start.11
  45.3 2.2 %shard_map.147 = (bf16[6144,512]{1,0:T(8,128)(2,1)}, bf16[6144,512]{1,0:T(8,128)(2,1)}, bf16[256,512]{1,0:T(8,128)(2,1)S(1)}, bf16[256,512]{1,0:T(8,128)(2,1)S(1)}) custom-call(bf16[6144,64]{1,0:T(8,128)(2,1)S(1)} %get-tuple-element.39.x_t, bf16[64,1024]{1,0:T(8,128)(2,1)S(1)} %get-tuple-element.40.d_both, ...), custom_call_target="tpu_custom_call", output_to_operand_aliasing={{0}: (4, {}), {1}: (5, {})} | custom-call | flops 1073741824 | bytes 4194304 | tf_op jit(solution)/shard_map/pallas_call | solution.py:325
  47.5 2.0 %collective-permute-done.11.got = bf16[8,6272]{1,0:T(8,128)(2,1)S(1)} collective-permute-done((bf16[8,6272]{1,0:T(8,128)(2,1)S(1)}, bf16[8,6272]{1,0:T(8,128)(2,1)S(1)}, u32[]{:S(2)}, u32[]{:S(2)}) %collective-permute-start.11) | collective-permute-done | bytes 100384 | tf_op jit(solution)/shard_map/ppermute | solution.py:348
  49.5 0.2 shard_map.151
  49.7 2.0 %collective-permute-start.12 = (bf16[4,6272]{1,0:T(4,128)(2,1)S(1)}, bf16[4,6272]{1,0:T(4,128)(2,1)S(1)}, u32[]{:S(2)}, u32[]{:S(2)}) collective-permute-start(bf16[4,6272]{1,0:T(4,128)(2,1)S(1)} %get-tuple-element.61), channel_id=1, source_target_pairs={{0,8},{1,9},{2,10},{3,11},{4,12},{5,13},{6,14},{7,15},{8,0},{9,1},... | collective-permute-start | bytes 150536 | tf_op jit(solution)/shard_map/ppermute | solution.py:348
  51.6 2.4 %shard_map.148 = (bf16[6144,512]{1,0:T(8,128)(2,1)}, bf16[6144,512]{1,0:T(8,128)(2,1)}) custom-call(bf16[6144,64]{1,0:T(8,128)(2,1)S(1)} %get-tuple-element.39.x_t, bf16[64,1024]{1,0:T(8,128)(2,1)S(1)} %get-tuple-element.40.d_both, bf16[256,512]{1,0:T(8,128)(2,1)S(1)} %get-tuple-element.47.refs_0_, ...), custom_call_target="tpu_custom_call", output_to_operand_aliasing={{0}: (4, {}), {1}: (5, {})} | custom-call | flops 1073741824 | bytes 4194304 | tf_op jit(solution)/shard_map/pallas_call | solution.py:325
  54.0 1.1 %collective-permute-done.12.got = bf16[4,6272]{1,0:T(4,128)(2,1)S(1)} collective-permute-done((bf16[4,6272]{1,0:T(4,128)(2,1)S(1)}, bf16[4,6272]{1,0:T(4,128)(2,1)S(1)}, u32[]{:S(2)}, u32[]{:S(2)}) %collective-permute-start.12) | collective-permute-done | bytes 50208 | tf_op jit(solution)/shard_map/ppermute | solution.py:348
  55.1 0.9 %shard_map.152 = (bf16[16,6144]{1,0:T(8,128)(2,1)}, f32[8,16]{1,0:T(8,128)}) custom-call(f32[4,6272]{1,0:T(4,128)S(1)} %get-tuple-element.60.have, bf16[4,6272]{1,0:T(4,128)(2,1)S(1)} %collective-permute-done.12.got, f32[16,16]{1,0:T(8,128)S(1)} %get-tuple-element.62.select, f32[8,16]{1,0:T(8,128)S(1)} %get-tuple-element.63.base, ...), custom_call_target="tpu_custom_call" | custom-call | flops 1048576 | bytes 262144 | tf_op jit(solution)/shard_map/pallas_call | solution.py:25
  (7 shorter events, 0.1 us)
Async XLA Ops:
  2.4 10.1 %collective-permute-start = (bf16[4,12416]{1,0:T(4,128)(2,1)S(1)}, bf16[4,12416]{1,0:T(4,128)(2,1)S(1)}, u32[]{:S(2)}, u32[]{:S(2)}) collective-permute-start(bf16[4,12416]{1,0:T(4,128)(2,1)S(1)} %get-tuple-element.38.after), channel_id=1, source_target_pairs={{0,8},{1,9},{2,10},{3,11},{4,12},{5,13},{6,14},{7,15},{8,0},{9,1},... | collective-permute-start | bytes 297992 | tf_op jit(solution)/shard_map/ppermute | solution.py:348
  6.5 6.0 %collective-permute-start.2 = (bf16[4,12416]{1,0:T(4,128)(2,1)S(1)}, bf16[4,12416]{1,0:T(4,128)(2,1)S(1)}, u32[]{:S(2)}, u32[]{:S(2)}) collective-permute-start(bf16[4,12416]{1,0:T(4,128)(2,1)S(1)} %get-tuple-element.38.after), channel_id=1, source_target_pairs={{0,2},{1,5},{2,0},{3,7},{4,6},{5,1},{6,4},{7,3},{8,10},{9,13},{10,... | collective-permute-start | bytes 297992 | tf_op jit(solution)/shard_map/ppermute | solution.py:348
  8.0 4.6 %collective-permute-start.1 = (bf16[4,12416]{1,0:T(4,128)(2,1)S(1)}, bf16[4,12416]{1,0:T(4,128)(2,1)S(1)}, u32[]{:S(2)}, u32[]{:S(2)}) collective-permute-start(bf16[4,12416]{1,0:T(4,128)(2,1)S(1)} %get-tuple-element.38.after), channel_id=1, source_target_pairs={{0,4},{1,3},{2,6},{3,1},{4,0},{5,7},{6,2},{7,5},{8,12},{9,11},{10,... | collective-permute-start | bytes 297992 | tf_op jit(solution)/shard_map/ppermute | solution.py:348
  12.6 5.5 %collective-permute-start.3 = (bf16[4,12416]{1,0:T(4,128)(2,1)S(1)}, bf16[4,12416]{1,0:T(4,128)(2,1)S(1)}, u32[]{:S(2)}, u32[]{:S(2)}) collective-permute-start(bf16[4,12416]{1,0:T(4,128)(2,1)S(1)} %shard_map.139.block), channel_id=1, source_target_pairs={{0,4},{1,3},{2,6},{3,1},{4,0},{5,7},{6,2},{7,5},{8,12},{9,11},{10,... | collective-permute-start | bytes 297992 | tf_op jit(solution)/shard_map/ppermute | solution.py:348
  14.3 8.6 %collective-permute-start.4 = (bf16[4,12416]{1,0:T(4,128)(2,1)S(1)}, bf16[4,12416]{1,0:T(4,128)(2,1)S(1)}, u32[]{:S(2)}, u32[]{:S(2)}) collective-permute-start(bf16[4,12416]{1,0:T(4,128)(2,1)S(1)} %shard_map.140.after), channel_id=1, source_target_pairs={{0,2},{1,5},{2,0},{3,7},{4,6},{5,1},{6,4},{7,3},{8,10},{9,13},{10,... | collective-permute-start | bytes 297992 | tf_op jit(solution)/shard_map/ppermute | solution.py:348
  18.2 4.7 %collective-permute-start.6 = (bf16[4,12416]{1,0:T(4,128)(2,1)S(1)}, bf16[4,12416]{1,0:T(4,128)(2,1)S(1)}, u32[]{:S(2)}, u32[]{:S(2)}) collective-permute-start(bf16[4,12416]{1,0:T(4,128)(2,1)S(1)} %shard_map.142.refs_0_), channel_id=1, source_target_pairs={{0,2},{1,5},{2,0},{3,7},{4,6},{5,1},{6,4},{7,3},{8,10},{9,13},{10,... | collective-permute-start | bytes 297992 | tf_op jit(solution)/shard_map/ppermute | solution.py:348
  19.3 4.7 %collective-permute-start.5 = (bf16[4,12416]{1,0:T(4,128)(2,1)S(1)}, bf16[4,12416]{1,0:T(4,128)(2,1)S(1)}, u32[]{:S(2)}, u32[]{:S(2)}) collective-permute-start(bf16[4,12416]{1,0:T(4,128)(2,1)S(1)} %shard_map.143), channel_id=1, source_target_pairs={{0,4},{1,3},{2,6},{3,1},{4,0},{5,7},{6,2},{7,5},{8,12},{9,11},{10,... | collective-permute-start | bytes 297992 | tf_op jit(solution)/shard_map/ppermute | solution.py:348
  20.1 4.3 %collective-permute-start.7 = (bf16[16,12416]{1,0:T(8,128)(2,1)S(1)}, bf16[16,12416]{1,0:T(8,128)(2,1)S(1)}, u32[]{:S(2)}, u32[]{:S(2)}) collective-permute-start(bf16[16,12416]{1,0:T(8,128)(2,1)S(1)} %pad_maximum_fusion.refs_0_), channel_id=1, source_target_pairs={{0,1},{1,0},{2,3},{3,2},{4,5},{5,4},{6,7},{7,6},{8,9},{9,8},{10,11... | collective-permute-start | bytes 1191944 | tf_op jit(solution)/shard_map/ppermute | solution.py:348
  24.3 1.8 %collective-permute-start.8 = (bf16[16,12416]{1,0:T(8,128)(2,1)S(1)}, bf16[16,12416]{1,0:T(8,128)(2,1)S(1)}, u32[]{:S(2)}, u32[]{:S(2)}) collective-permute-start(bf16[16,12416]{1,0:T(8,128)(2,1)S(1)} %pad_maximum_fusion.1.refs_1_), channel_id=1, source_target_pairs={{0,1},{1,0},{2,3},{3,2},{4,5},{5,4},{6,7},{7,6},{8,9},{9,8},{10,11... | collective-permute-start | bytes 1191944 | tf_op jit(solution)/shard_map/ppermute | solution.py:348
  37.0 1.8 %collective-permute-start.9 = (bf16[32,6272]{1,0:T(8,128)(2,1)S(1)}, bf16[32,6272]{1,0:T(8,128)(2,1)S(1)}, u32[]{:S(2)}, u32[]{:S(2)}) collective-permute-start(bf16[32,6272]{1,0:T(8,128)(2,1)S(1)} %get-tuple-element.55), channel_id=1, source_target_pairs={{0,1},{1,0},{2,3},{3,2},{4,5},{5,4},{6,7},{7,6},{8,9},{9,8},{10,11... | collective-permute-start | bytes 1204232 | tf_op jit(solution)/shard_map/ppermute | solution.py:348
  38.9 5.8 %collective-permute-start.10 = (bf16[16,6272]{1,0:T(8,128)(2,1)S(1)}, bf16[16,6272]{1,0:T(8,128)(2,1)S(1)}, u32[]{:S(2)}, u32[]{:S(2)}) collective-permute-start(bf16[16,6272]{1,0:T(8,128)(2,1)S(1)} %get-tuple-element.57), channel_id=1, source_target_pairs={{0,2},{1,5},{2,0},{3,7},{4,6},{5,1},{6,4},{7,3},{8,10},{9,13},{10,... | collective-permute-start | bytes 602120 | tf_op jit(solution)/shard_map/ppermute | solution.py:348
  44.9 4.7 %collective-permute-start.11 = (bf16[8,6272]{1,0:T(8,128)(2,1)S(1)}, bf16[8,6272]{1,0:T(8,128)(2,1)S(1)}, u32[]{:S(2)}, u32[]{:S(2)}) collective-permute-start(bf16[8,6272]{1,0:T(8,128)(2,1)S(1)} %get-tuple-element.59), channel_id=1, source_target_pairs={{0,4},{1,3},{2,6},{3,1},{4,0},{5,7},{6,2},{7,5},{8,12},{9,11},{10,... | collective-permute-start | bytes 301064 | tf_op jit(solution)/shard_map/ppermute | solution.py:348
  49.7 5.4 %collective-permute-start.12 = (bf16[4,6272]{1,0:T(4,128)(2,1)S(1)}, bf16[4,6272]{1,0:T(4,128)(2,1)S(1)}, u32[]{:S(2)}, u32[]{:S(2)}) collective-permute-start(bf16[4,6272]{1,0:T(4,128)(2,1)S(1)} %get-tuple-element.61), channel_id=1, source_target_pairs={{0,8},{1,9},{2,10},{3,11},{4,12},{5,13},{6,14},{7,15},{8,0},{9,1},... | collective-permute-start | bytes 150536 | tf_op jit(solution)/shard_map/ppermute | solution.py:348

commit v15 on v13

--- a/solution.py
+++ b/solution.py
@@ -50,54 +50,37 @@
     return lane_pair(value.shape[0], high, value - high)
 
 
-def router_kernel(
-    tokens_in,
-    logits_in,
-    ref_in,
-    routes_in,
-    y_in,
-    send,
-    entropy,
-    divergence,
-    base,
-    coef,
-    select_out,
-    tokens,
-    logits,
-    ref_logits,
-    routes,
-    y,
-    sems,
-):
-    sources = (logits_in, ref_in, routes_in, tokens_in, y_in)
-    targets = (logits, ref_logits, routes, tokens, y)
+def start_all(sources, targets, sems):
     copies = [
         pltpu.make_async_copy(s, t, sems.at[i]) for i, (s, t) in enumerate(zip(sources, targets))
     ]
     for copy in copies:
         copy.start()
-    for copy in copies[:3]:
-        copy.wait()
-    slots, width = send.shape[0], tokens.shape[1]
-    experts, count = logits.shape
-    x, r = logits[...], ref_logits[...]
-    shifted = x - jnp.max(x, axis=0, keepdims=True)
-    policy_log = shifted - jnp.log(jnp.sum(jnp.exp(shifted), axis=0, keepdims=True))
-    shifted = r - jnp.max(r, axis=0, keepdims=True)
-    frozen_log = shifted - jnp.log(jnp.sum(jnp.exp(shifted), axis=0, keepdims=True))
-    probs = jnp.exp(policy_log)
-    ratio = policy_log - frozen_log
-    div = jnp.sum(probs * ratio, axis=0, keepdims=True)
-    entropy[...] = -jnp.sum(probs * policy_log, axis=0, keepdims=True)
-    divergence[...] = div
-    base[...] = probs * (ratio - div)
+    return copies
+
+
+def gates(logits, routes):
     first, second = routes[0:1, :], routes[1:2, :]
     routed = jnp.where((first == 0) | (second == 0), 1.0, 0.0)
-    expert = lax.broadcasted_iota(jnp.int32, (experts, count), 0)
+    expert = lax.broadcasted_iota(jnp.int32, logits.shape, 0)
     partner_hot = jnp.where(expert == first + second, 1.0, 0.0)
-    partner_logit = jnp.sum(x * partner_hot, axis=0, keepdims=True)
-    gate = jnp.where(routed > 0.0, jax.nn.sigmoid(x[0:1, :] - partner_logit), 0.0)
-    coef[...] = (jnp.where(expert == 0, 1.0, 0.0) - partner_hot) * (gate * (1.0 - gate))
+    partner_logit = jnp.sum(logits * partner_hot, axis=0, keepdims=True)
+    gate = jnp.where(routed > 0.0, jax.nn.sigmoid(logits[0:1, :] - partner_logit), 0.0)
+    window_hot = jnp.where(expert == 0, 1.0, 0.0)
+    return routed, gate, (window_hot - partner_hot) * (gate * (1.0 - gate))
+
+
+def select_kernel(
+    logits_in, routes_in, tokens_in, y_in, send, select_out, logits, routes, tokens, y, sems
+):
+    copies = start_all(
+        (logits_in, routes_in, tokens_in, y_in), (logits, routes, tokens, y), sems
+    )
+    slots, width = send.shape[0], tokens.shape[1]
+    count = logits.shape[1]
+    for copy in copies[:2]:
+        copy.wait()
+    routed, gate, _ = gates(logits[...], routes[...])
     token = lax.broadcasted_iota(jnp.int32, (1, count), 1)
     position = jnp.full((1, count), -1.0, F32)
     for t in range(count):
@@ -110,11 +93,42 @@
     g_slots = jnp.sum(select * gate_low, axis=1, keepdims=True)
     wide = width + LANES
     send[:, width:wide] = jnp.broadcast_to(g_slots[:slots], (slots, LANES)).astype(BF16)
-    copies[3].wait()
+    for copy in copies[2:]:
+        copy.wait()
     x_slots = dot(select.astype(BF16), tokens[...], ((1,), (0,)))
     send[:, :width] = x_slots[:slots].astype(BF16)
-    copies[4].wait()
     send[:, wide:] = y[...]
+
+
+def router_kernel(
+    logits_in,
+    ref_in,
+    routes_in,
+    after,
+    entropy,
+    divergence,
+    base,
+    coef,
+    logits,
+    ref_logits,
+    routes,
+    sems,
+):
+    copies = start_all((logits_in, ref_in, routes_in), (logits, ref_logits, routes), sems)
+    for copy in copies:
+        copy.wait()
+    x, r = logits[...], ref_logits[...]
+    shifted = x - jnp.max(x, axis=0, keepdims=True)
+    policy_log = shifted - jnp.log(jnp.sum(jnp.exp(shifted), axis=0, keepdims=True))
+    shifted = r - jnp.max(r, axis=0, keepdims=True)
+    frozen_log = shifted - jnp.log(jnp.sum(jnp.exp(shifted), axis=0, keepdims=True))
+    probs = jnp.exp(policy_log)
+    ratio = policy_log - frozen_log
+    div = jnp.sum(probs * ratio, axis=0, keepdims=True)
+    entropy[...] = -jnp.sum(probs * policy_log, axis=0, keepdims=True)
+    divergence[...] = div
+    base[...] = probs * (ratio - div)
+    coef[...] = gates(x, routes[...])[2]
 
 
 def fetch_copies(sources, targets, sems):
@@ -171,13 +185,13 @@
         out_specs=whole(1)[0],
         compiler_params=pltpu.CompilerParams(vmem_limit_bytes=8 * MIB),
         cost_estimate=pl.CostEstimate(
-            flops=0, bytes_accessed=4 * block.size, transcendentals=0
+            flops=0, bytes_accessed=4 * MIB, transcendentals=0
         ),
     )(block, *after)
 
 
 def expert_kernel(*refs):
-    pieces, (down_in, gate_w, up_w), refs = refs[:6], refs[6:9], refs[9:]
+    pieces, (down_in, gate_w, up_w), refs = refs[:4], refs[4:7], refs[7:]
     send, keep, weighted_t, d_both, x_t, y, x, down_w, sems = refs
     rows, width, hidden_dim = x.shape[0], gate_w.shape[0], gate_w.shape[1]
     wide = width + LANES
@@ -191,9 +205,9 @@
         x[:, at] = block.astype(BF16)
         if c < width:
             x_t[at, :] = block.T.astype(BF16)
-    for c in range(0, width, LANES):
-        parts = [ref[:, wide + c : wide + c + LANES].astype(F32) for ref in pieces]
-        y[:, c : c + LANES] = jnp.concatenate(parts).astype(BF16)
+    quarter = rows // 4
+    for i, ref in enumerate(pieces):
+        y[i * quarter : (i + 1) * quarter, :] = ref[:, wide:]
     pre_gate = dot(x[:, :width], gate_w[...], ((1,), (0,)))
     pre_up = dot(x[:, :width], up_w[...], ((1,), (0,)))
     for copy in copies:
@@ -365,51 +379,67 @@
         wide = width + LANES
         anywhere = pl.BlockSpec(memory_space=pl.ANY)
 
-        send, entropy, divergence, base, coef, select = pl.pallas_call(
+        small = [in_hbm(a) for a in (logits.T, ref_logits.T, routes.T)]
+        send, select = pl.pallas_call(
+            select_kernel,
+            out_shape=[
+                jax.ShapeDtypeStruct((slots, wide + width), BF16),
+                jax.ShapeDtypeStruct((count, count), F32),
+            ],
+            in_specs=[anywhere] * 4,
+            out_specs=whole(2),
+            scratch_shapes=[
+                pltpu.VMEM((experts, count), F32),
+                pltpu.VMEM((2, count), jnp.int32),
+                pltpu.VMEM((count, width), BF16),
+                pltpu.VMEM((slots, width), BF16),
+                pltpu.SemaphoreType.DMA((4,)),
+            ],
+            compiler_params=pltpu.CompilerParams(vmem_limit_bytes=8 * MIB),
+            cost_estimate=pl.CostEstimate(
+                flops=1 << 20, bytes_accessed=1 << 22, transcendentals=0
+            ),
+        )(small[0], small[2], in_hbm(tokens), in_hbm(cotangent))
+
+        own = send
+        for bits in levels[:-3]:
+            own = jnp.concatenate([own, swap(own, bits)])
+        first, second, third = levels[-3:]
+        block_1 = relay(relay(swap(own, first)))
+        block_2 = swap(own, second)
+        block_3 = swap(own, third)
+        gate_w, up_w = fetch([gate_weight, up_weight], [width, width], own)
+        block_1 = relay(block_1, gate_w, block_2, block_3)
+        block_12 = swap(block_1, second)
+        block_13 = swap(relay(block_1), third)
+        block_23 = swap(block_3, second)
+        block_123 = swap(relay(block_12), third)
+        low_half = jnp.concatenate([own, block_1, block_2, block_12])
+        high_half = jnp.concatenate([block_3, block_13, block_23, block_123])
+        pieces = [low_half, high_half]
+        pieces += [swap(piece, (1, 1)) for piece in pieces]
+
+        entropy, divergence, base, coef = pl.pallas_call(
             router_kernel,
             out_shape=[
-                jax.ShapeDtypeStruct((slots, wide + width), BF16),
                 jax.ShapeDtypeStruct((1, count), F32),
                 jax.ShapeDtypeStruct((1, count), F32),
                 jax.ShapeDtypeStruct((experts, count), F32),
                 jax.ShapeDtypeStruct((experts, count), F32),
-                jax.ShapeDtypeStruct((count, count), F32),
             ],
-            in_specs=[anywhere] * 5,
-            out_specs=whole(6),
+            in_specs=[anywhere] * 4,
+            out_specs=whole(4),
             scratch_shapes=[
-                pltpu.VMEM((count, width), BF16),
                 pltpu.VMEM((experts, count), F32),
                 pltpu.VMEM((experts, count), F32),
                 pltpu.VMEM((2, count), jnp.int32),
-                pltpu.VMEM((slots, width), BF16),
-                pltpu.SemaphoreType.DMA((5,)),
+                pltpu.SemaphoreType.DMA((3,)),
             ],
             compiler_params=pltpu.CompilerParams(vmem_limit_bytes=8 * MIB),
             cost_estimate=pl.CostEstimate(
-                flops=1 << 20, bytes_accessed=1 << 24, transcendentals=0
+                flops=1 << 20, bytes_accessed=1 << 22, transcendentals=0
             ),
-        )(*[in_hbm(a) for a in (tokens, logits.T, ref_logits.T, routes.T, cotangent)])
-
-        own = send
-        for bits in levels[:-3]:
-            own = jnp.concatenate([own, swap(own, bits)])
-        first, second, third = levels[-3:]
-        block_1 = swap(own, first)
-        block_2 = swap(own, second)
-        block_3 = swap(own, third)
-        gate_w, up_w = fetch([gate_weight, up_weight], [width, width], own)
-        block_1 = relay(block_1, gate_w, block_2)
-        block_12 = swap(block_1, second)
-        block_13 = swap(block_1, third)
-        block_23 = swap(block_3, second)
-        block_123 = swap(block_12, third)
-        pieces = [
-            jnp.concatenate([own, block_1, block_2, block_12]),
-            jnp.concatenate([block_3, block_13]),
-            jnp.concatenate([block_23, block_123]),
-        ]
-        pieces += [swap(piece, (1, 1)) for piece in pieces]
+        )(*small, high_half)
 
         work = 2 * rows * width * hidden
         half = rows // 2
@@ -423,7 +453,7 @@
                 jax.ShapeDtypeStruct((width, rows), BF16),
                 jax.ShapeDtypeStruct((rows, width), BF16),
             ],
-            in_specs=whole(6) + [anywhere] + whole(2),
+            in_specs=whole(4) + [anywhere] + whole(2),
             out_specs=whole(6),
             scratch_shapes=[
                 pltpu.VMEM((rows, wide), BF16),

time: 55.5 us -> 53.3 us (0.960)
  starting transfers between devices: 15.4 us -> 13.6 us
  Pallas kernels: 27.4 us -> 26.3 us
  waiting for transfers between devices: 11.3 us -> 12 us
    pallas_call x1, Pallas kernels: 10.7 us -> 8.8 us  [shards(): pl.pallas_call(expert_kernel, out_shape=[jax.ShapeDtypeStruct((half, wide...]
    ppermute x14 -> x13, starting transfers between devices: 15.4 us -> 13.6 us  [swap(): return lax.ppermute(block, 'blk', [(i, i ^ bits[i % 2]) for i in range(n)])]
    pallas_call x1 -> x2, Pallas kernels: 1.72 us -> 2.48 us  [the longest x1 1.3 us: shards(): pl.pallas_call(router_kernel, out_shape=[jax.ShapeDtypeStruct((1, count),...]
    ppermute x14 -> x13, waiting for transfers between devices: 11.3 us -> 12 us  [swap(): return lax.ppermute(block, 'blk', [(i, i ^ bits[i % 2]) for i in range(n)])]
  transfers between devices with their start and end apart: 14 -> 13, of which waited for: 6 -> 8; matrix products, arithmetic and copies ran while one was open for 1% -> 1% of each run, Pallas kernels for 25% -> 28%
where the time goes in v15:
time: 53.3 us; the launch traced here: 53.1 us
  Pallas kernels  26.3 us (49%)
  starting transfers between devices  13.6 us (26%)
  waiting for transfers between devices  12 us (23%)
  between operations  0.79 us (1%)
    ppermute x13, starting transfers between devices, swap(): return lax.ppermute(block, 'blk', [(i, i ^ bits[i % 2]) for i in range(n)])  13.6 us
    ppermute x13, waiting for transfers between devices, swap(): return lax.ppermute(block, 'blk', [(i, i ^ bits[i % 2]) for i in range(n)])  12 us
    pallas_call x3, Pallas kernels, grads_of(): pl.pallas_call(kernel, out_shape=outs, in_specs=whole(2 + len(down)) + (w...  8.86 us
    pallas_call x1, Pallas kernels, shards(): pl.pallas_call(expert_kernel, out_shape=[jax.ShapeDtypeStruct((half, wide...  8.8 us
    pallas_call x1, Pallas kernels, fetch(): pl.pallas_call(functools.partial(fetch_kernel, count), out_shape=[pltpu.V...  4.7 us
    pallas_call x4, Pallas kernels, call(): pl.pallas_call(kernel, out_shape=[jax.ShapeDtypeStruct(s, t) for s, t in...  1.38 us
    pallas_call x1, Pallas kernels, shards(): pl.pallas_call(router_kernel, out_shape=[jax.ShapeDtypeStruct((1, count),...  1.3 us
    pallas_call x1, Pallas kernels, shards(): pl.pallas_call(select_kernel, out_shape=[jax.ShapeDtypeStruct((slots, wid...  1.19 us
  transfers between devices with their start and end apart: 13, of which 8 were waited for; matrix products, arithmetic and copies ran while one was open for 1% of the time, Pallas kernels for 28%

profile of v15, /device:TPU:0, one launch (start us, length us, event | category | flops | bytes accessed | tf_op | source)
XLA Modules:
  0.0 53.1 jit_solution(7453290772362785464)
XLA Ops:
  0.6 1.2 %shard_map.135 = (bf16[4,12416]{1,0:T(4,128)(2,1)S(1)}, f32[16,16]{1,0:T(8,128)S(1)}) custom-call(f32[8,16]{1,0:T(8,128)} %bitcast.6, s32[2,16]{1,0:T(2,128)} %bitcast.9, bf16[16,6144]{1,0:T(8,128)(2,1)} %tokens_in.1, bf16[4,6144]{1,0:T(4,128)(2,1)} %y_in.1), custom_call_target="tpu_custom_call" | custom-call | flops 1048576 | bytes 4194304 | tf_op jit(solution)/shard_map/pallas_call | solution.py:383
  1.8 4.1 %collective-permute-start = (bf16[4,12416]{1,0:T(4,128)(2,1)S(1)}, bf16[4,12416]{1,0:T(4,128)(2,1)S(1)}, u32[]{:S(2)}, u32[]{:S(2)}) collective-permute-start(bf16[4,12416]{1,0:T(4,128)(2,1)S(1)} %get-tuple-element.40.refs_2_), channel_id=1, source_target_pairs={{0,8},{1,9},{2,10},{3,11},{4,12},{5,13},{6,14},{7,15},{8,0},{9,1},... | collective-permute-start | bytes 297992 | tf_op jit(solution)/shard_map/ppermute | solution.py:369
  5.9 1.5 %collective-permute-start.2 = (bf16[4,12416]{1,0:T(4,128)(2,1)S(1)}, bf16[4,12416]{1,0:T(4,128)(2,1)S(1)}, u32[]{:S(2)}, u32[]{:S(2)}) collective-permute-start(bf16[4,12416]{1,0:T(4,128)(2,1)S(1)} %get-tuple-element.40.refs_2_), channel_id=1, source_target_pairs={{0,2},{1,5},{2,0},{3,7},{4,6},{5,1},{6,4},{7,3},{8,10},{9,13},{10,... | collective-permute-start | bytes 297992 | tf_op jit(solution)/shard_map/ppermute | solution.py:369
  7.4 1.6 %collective-permute-start.1 = (bf16[4,12416]{1,0:T(4,128)(2,1)S(1)}, bf16[4,12416]{1,0:T(4,128)(2,1)S(1)}, u32[]{:S(2)}, u32[]{:S(2)}) collective-permute-start(bf16[4,12416]{1,0:T(4,128)(2,1)S(1)} %get-tuple-element.40.refs_2_), channel_id=1, source_target_pairs={{0,4},{1,3},{2,6},{3,1},{4,0},{5,7},{6,2},{7,5},{8,12},{9,11},{10,... | collective-permute-start | bytes 297992 | tf_op jit(solution)/shard_map/ppermute | solution.py:369
  9.0 4.7 %shard_map.138 = (bf16[6144,512]{1,0:T(8,128)(2,1)S(1)}, bf16[6144,512]{1,0:T(8,128)(2,1)S(1)}) custom-call(bf16[6144,512]{1,0:T(8,128)(2,1)} %refs_0_.1, bf16[6144,512]{1,0:T(8,128)(2,1)} %refs_1_.1, bf16[4,12416]{1,0:T(4,128)(2,1)S(1)} %get-tuple-element.40.refs_2_), custom_call_target="tpu_custom_call" | custom-call | bytes 12582912 | tf_op jit(solution)/shard_map/pallas_call | solution.py:162
  13.7 0.0 collective-permute-done.block
  13.8 0.0 collective-permute-done.2.refs_2_
  13.8 0.0 collective-permute-done.1.refs_1_
  13.8 0.5 collective-permute-start.3
  14.3 0.6 %collective-permute-start.4 = (bf16[4,12416]{1,0:T(4,128)(2,1)S(1)}, bf16[4,12416]{1,0:T(4,128)(2,1)S(1)}, u32[]{:S(2)}, u32[]{:S(2)}) collective-permute-start(bf16[4,12416]{1,0:T(4,128)(2,1)S(1)} %shard_map.140), channel_id=1, source_target_pairs={{0,2},{1,5},{2,0},{3,7},{4,6},{5,1},{6,4},{7,3},{8,10},{9,13},{10,... | collective-permute-start | bytes 297992 | tf_op jit(solution)/shard_map/ppermute | solution.py:369
  14.9 1.6 %collective-permute-start.5 = (bf16[4,12416]{1,0:T(4,128)(2,1)S(1)}, bf16[4,12416]{1,0:T(4,128)(2,1)S(1)}, u32[]{:S(2)}, u32[]{:S(2)}) collective-permute-start(bf16[4,12416]{1,0:T(4,128)(2,1)S(1)} %collective-permute-done.2.refs_2_), channel_id=1, source_target_pairs={{0,4},{1,3},{2,6},{3,1},{4,0},{5,7},{6,2},{7,5},{8,12},{9,11},{10,... | collective-permute-start | bytes 297992 | tf_op jit(solution)/shard_map/ppermute | solution.py:369
  16.5 2.0 %collective-permute-done.3.block = bf16[4,12416]{1,0:T(4,128)(2,1)S(1)} collective-permute-done((bf16[4,12416]{1,0:T(4,128)(2,1)S(1)}, bf16[4,12416]{1,0:T(4,128)(2,1)S(1)}, u32[]{:S(2)}, u32[]{:S(2)}) %collective-permute-start.3) | collective-permute-done | bytes 99360 | tf_op jit(solution)/shard_map/ppermute | solution.py:369
  18.5 1.0 %collective-permute-start.6 = (bf16[4,12416]{1,0:T(4,128)(2,1)S(1)}, bf16[4,12416]{1,0:T(4,128)(2,1)S(1)}, u32[]{:S(2)}, u32[]{:S(2)}) collective-permute-start(bf16[4,12416]{1,0:T(4,128)(2,1)S(1)} %shard_map.141), channel_id=1, source_target_pairs={{0,2},{1,5},{2,0},{3,7},{4,6},{5,1},{6,4},{7,3},{8,10},{9,13},{10,... | collective-permute-start | bytes 297992 | tf_op jit(solution)/shard_map/ppermute | solution.py:369
  19.5 0.2 pad_maximum_fusion.refs_0_
  19.7 0.1 collective-permute-start.7
  19.8 0.2 collective-permute-done.5
  20.1 0.0 collective-permute-done.4
  20.1 3.2 %collective-permute-done.6 = bf16[4,12416]{1,0:T(4,128)(2,1)S(1)} collective-permute-done((bf16[4,12416]{1,0:T(4,128)(2,1)S(1)}, bf16[4,12416]{1,0:T(4,128)(2,1)S(1)}, u32[]{:S(2)}, u32[]{:S(2)}) %collective-permute-start.6) | collective-permute-done | bytes 99360 | tf_op jit(solution)/shard_map/ppermute | solution.py:369
  23.2 0.2 pad_maximum_fusion.1.refs_1_.after
  23.5 0.1 collective-permute-start.8
  23.5 0.0 collective-permute-done.7.refs_2_
  23.5 1.7 %collective-permute-done.8.refs_3_ = bf16[16,12416]{1,0:T(8,128)(2,1)S(1)} collective-permute-done((bf16[16,12416]{1,0:T(8,128)(2,1)S(1)}, bf16[16,12416]{1,0:T(8,128)(2,1)S(1)}, u32[]{:S(2)}, u32[]{:S(2)}) %collective-permute-start.8) | collective-permute-done | bytes 397344 | tf_op jit(solution)/shard_map/ppermute | solution.py:369
  25.2 8.8 %shard_map.142 = (bf16[32,6272]{1,0:T(8,128)(2,1)S(1)}, f32[32,6272]{1,0:T(8,128)S(1)}, bf16[512,64]{1,0:T(8,128)(2,1)S(1)}, bf16[64,1024]{1,0:T(8,128)(2,1)S(1)...) custom-call(bf16[16,12416]{1,0:T(8,128)(2,1)S(1)} %pad_maximum_fusion.refs_0_, ...), custom_call_target="tpu_custom_call" | custom-call | flops 6442450944 | bytes 12582912 | tf_op jit(solution)/shard_map/pallas_call | solution.py:446
  34.1 0.2 collective-permute-start.9
  34.3 1.3 %shard_map.149 = (f32[1,16]{1,0:T(1,128)}, f32[1,16]{1,0:T(1,128)}, f32[8,16]{1,0:T(8,128)S(1)}, f32[8,16]{1,0:T(8,128)S(1)}) custom-call(f32[8,16]{1,0:T(8,128)} %bitcast.7, f32[8,16]{1,0:T(8,128)} %bitcast.8, s32[2,16]{1,0:T(2,128)} %bitcast.10, bf16[16,12416]{1,0:T(8,128)(2,1)S(1)} %pad_maximum_fusion.1.refs_1_.after), custom_call_target="tpu_custom_call" | custom-call | flops 1048576 | bytes 4194304 | tf_op jit(solution)/shard_map/pallas_call | solution.py:422
  35.6 0.3 collective-permute-done.9.got
  35.9 0.2 shard_map.146
  36.0 1.0 %collective-permute-start.10 = (bf16[16,6272]{1,0:T(8,128)(2,1)S(1)}, bf16[16,6272]{1,0:T(8,128)(2,1)S(1)}, u32[]{:S(2)}, u32[]{:S(2)}) collective-permute-start(bf16[16,6272]{1,0:T(8,128)(2,1)S(1)} %get-tuple-element.61), channel_id=1, source_target_pairs={{0,2},{1,5},{2,0},{3,7},{4,6},{5,1},{6,4},{7,3},{8,10},{9,13},{10,... | collective-permute-start | bytes 602120 | tf_op jit(solution)/shard_map/ppermute | solution.py:369
  37.0 4.3 %shard_map.143 = (bf16[512,6144]{1,0:T(8,128)(2,1)}, bf16[6144,512]{1,0:T(8,128)(2,1)}, bf16[6144,512]{1,0:T(8,128)(2,1)}, bf16[256,512]{1,0:T(8,128)(2,1)S(1)}, bf16[256,512]{1,0:T(8,128)(2,1)S(1)}) custom-call(bf16[512,64]{1,0:T(8,128)(2,1)S(1)} %get-tuple-element.45.weighted_t, bf16[64,6144]{1,0:T(8,128)(2,1)S(1)} %get-tuple-element.46.y, ...), custom_call_target="tpu_custom_call" | custom-call | flops 2684354560 | bytes 10485760 | tf_op jit(solution)/shard_map/pallas_call | solution.py:346
  41.4 0.5 collective-permute-done.10.got
  41.8 0.1 shard_map.147
  42.0 0.5 collective-permute-start.11
  42.4 2.2 %shard_map.144 = (bf16[6144,512]{1,0:T(8,128)(2,1)}, bf16[6144,512]{1,0:T(8,128)(2,1)}, bf16[256,512]{1,0:T(8,128)(2,1)S(1)}, bf16[256,512]{1,0:T(8,128)(2,1)S(1)}) custom-call(bf16[6144,64]{1,0:T(8,128)(2,1)S(1)} %get-tuple-element.43.x_t, bf16[64,1024]{1,0:T(8,128)(2,1)S(1)} %get-tuple-element.44.d_both, ...), custom_call_target="tpu_custom_call", output_to_operand_aliasing={{0}: (4, {}), {1}: (5, {})} | custom-call | flops 1073741824 | bytes 4194304 | tf_op jit(solution)/shard_map/pallas_call | solution.py:346
  44.6 2.0 %collective-permute-done.11.got = bf16[8,6272]{1,0:T(8,128)(2,1)S(1)} collective-permute-done((bf16[8,6272]{1,0:T(8,128)(2,1)S(1)}, bf16[8,6272]{1,0:T(8,128)(2,1)S(1)}, u32[]{:S(2)}, u32[]{:S(2)}) %collective-permute-start.11) | collective-permute-done | bytes 100384 | tf_op jit(solution)/shard_map/ppermute | solution.py:369
  46.6 0.2 shard_map.148
  46.8 0.9 %collective-permute-start.12 = (bf16[4,6272]{1,0:T(4,128)(2,1)S(1)}, bf16[4,6272]{1,0:T(4,128)(2,1)S(1)}, u32[]{:S(2)}, u32[]{:S(2)}) collective-permute-start(bf16[4,6272]{1,0:T(4,128)(2,1)S(1)} %get-tuple-element.65), channel_id=1, source_target_pairs={{0,8},{1,9},{2,10},{3,11},{4,12},{5,13},{6,14},{7,15},{8,0},{9,1},... | collective-permute-start | bytes 150536 | tf_op jit(solution)/shard_map/ppermute | solution.py:369
  47.7 2.4 %shard_map.145 = (bf16[6144,512]{1,0:T(8,128)(2,1)}, bf16[6144,512]{1,0:T(8,128)(2,1)}) custom-call(bf16[6144,64]{1,0:T(8,128)(2,1)S(1)} %get-tuple-element.43.x_t, bf16[64,1024]{1,0:T(8,128)(2,1)S(1)} %get-tuple-element.44.d_both, bf16[256,512]{1,0:T(8,128)(2,1)S(1)} %get-tuple-element.51.refs_0_, ...), custom_call_target="tpu_custom_call", output_to_operand_aliasing={{0}: (4, {}), {1}: (5, {})} | custom-call | flops 1073741824 | bytes 4194304 | tf_op jit(solution)/shard_map/pallas_call | solution.py:346
  50.1 2.1 %collective-permute-done.12.got = bf16[4,6272]{1,0:T(4,128)(2,1)S(1)} collective-permute-done((bf16[4,6272]{1,0:T(4,128)(2,1)S(1)}, bf16[4,6272]{1,0:T(4,128)(2,1)S(1)}, u32[]{:S(2)}, u32[]{:S(2)}) %collective-permute-start.12) | collective-permute-done | bytes 50208 | tf_op jit(solution)/shard_map/ppermute | solution.py:369
  52.2 0.9 %shard_map.150 = (bf16[16,6144]{1,0:T(8,128)(2,1)}, f32[8,16]{1,0:T(8,128)}) custom-call(f32[4,6272]{1,0:T(4,128)S(1)} %get-tuple-element.64.have, bf16[4,6272]{1,0:T(4,128)(2,1)S(1)} %collective-permute-done.12.got, f32[16,16]{1,0:T(8,128)S(1)} %get-tuple-element.66.select, f32[8,16]{1,0:T(8,128)S(1)} %get-tuple-element.67.base, ...), custom_call_target="tpu_custom_call" | custom-call | flops 1048576 | bytes 262144 | tf_op jit(solution)/shard_map/pallas_call | solution.py:25
  (5 shorter events, 0.0 us)
Async XLA Ops:
  1.8 11.9 %collective-permute-start = (bf16[4,12416]{1,0:T(4,128)(2,1)S(1)}, bf16[4,12416]{1,0:T(4,128)(2,1)S(1)}, u32[]{:S(2)}, u32[]{:S(2)}) collective-permute-start(bf16[4,12416]{1,0:T(4,128)(2,1)S(1)} %get-tuple-element.40.refs_2_), channel_id=1, source_target_pairs={{0,8},{1,9},{2,10},{3,11},{4,12},{5,13},{6,14},{7,15},{8,0},{9,1},... | collective-permute-start | bytes 297992 | tf_op jit(solution)/shard_map/ppermute | solution.py:369
  5.9 7.8 %collective-permute-start.2 = (bf16[4,12416]{1,0:T(4,128)(2,1)S(1)}, bf16[4,12416]{1,0:T(4,128)(2,1)S(1)}, u32[]{:S(2)}, u32[]{:S(2)}) collective-permute-start(bf16[4,12416]{1,0:T(4,128)(2,1)S(1)} %get-tuple-element.40.refs_2_), channel_id=1, source_target_pairs={{0,2},{1,5},{2,0},{3,7},{4,6},{5,1},{6,4},{7,3},{8,10},{9,13},{10,... | collective-permute-start | bytes 297992 | tf_op jit(solution)/shard_map/ppermute | solution.py:369
  7.4 6.3 %collective-permute-start.1 = (bf16[4,12416]{1,0:T(4,128)(2,1)S(1)}, bf16[4,12416]{1,0:T(4,128)(2,1)S(1)}, u32[]{:S(2)}, u32[]{:S(2)}) collective-permute-start(bf16[4,12416]{1,0:T(4,128)(2,1)S(1)} %get-tuple-element.40.refs_2_), channel_id=1, source_target_pairs={{0,4},{1,3},{2,6},{3,1},{4,0},{5,7},{6,2},{7,5},{8,12},{9,11},{10,... | collective-permute-start | bytes 297992 | tf_op jit(solution)/shard_map/ppermute | solution.py:369
  13.8 4.7 %collective-permute-start.3 = (bf16[4,12416]{1,0:T(4,128)(2,1)S(1)}, bf16[4,12416]{1,0:T(4,128)(2,1)S(1)}, u32[]{:S(2)}, u32[]{:S(2)}) collective-permute-start(bf16[4,12416]{1,0:T(4,128)(2,1)S(1)} %shard_map.139.block), channel_id=1, source_target_pairs={{0,4},{1,3},{2,6},{3,1},{4,0},{5,7},{6,2},{7,5},{8,12},{9,11},{10,... | collective-permute-start | bytes 297992 | tf_op jit(solution)/shard_map/ppermute | solution.py:369
  14.3 5.7 %collective-permute-start.4 = (bf16[4,12416]{1,0:T(4,128)(2,1)S(1)}, bf16[4,12416]{1,0:T(4,128)(2,1)S(1)}, u32[]{:S(2)}, u32[]{:S(2)}) collective-permute-start(bf16[4,12416]{1,0:T(4,128)(2,1)S(1)} %shard_map.140), channel_id=1, source_target_pairs={{0,2},{1,5},{2,0},{3,7},{4,6},{5,1},{6,4},{7,3},{8,10},{9,13},{10,... | collective-permute-start | bytes 297992 | tf_op jit(solution)/shard_map/ppermute | solution.py:369
  14.9 5.1 %collective-permute-start.5 = (bf16[4,12416]{1,0:T(4,128)(2,1)S(1)}, bf16[4,12416]{1,0:T(4,128)(2,1)S(1)}, u32[]{:S(2)}, u32[]{:S(2)}) collective-permute-start(bf16[4,12416]{1,0:T(4,128)(2,1)S(1)} %collective-permute-done.2.refs_2_), channel_id=1, source_target_pairs={{0,4},{1,3},{2,6},{3,1},{4,0},{5,7},{6,2},{7,5},{8,12},{9,11},{10,... | collective-permute-start | bytes 297992 | tf_op jit(solution)/shard_map/ppermute | solution.py:369
  18.5 4.7 %collective-permute-start.6 = (bf16[4,12416]{1,0:T(4,128)(2,1)S(1)}, bf16[4,12416]{1,0:T(4,128)(2,1)S(1)}, u32[]{:S(2)}, u32[]{:S(2)}) collective-permute-start(bf16[4,12416]{1,0:T(4,128)(2,1)S(1)} %shard_map.141), channel_id=1, source_target_pairs={{0,2},{1,5},{2,0},{3,7},{4,6},{5,1},{6,4},{7,3},{8,10},{9,13},{10,... | collective-permute-start | bytes 297992 | tf_op jit(solution)/shard_map/ppermute | solution.py:369
  19.7 3.8 %collective-permute-start.7 = (bf16[16,12416]{1,0:T(8,128)(2,1)S(1)}, bf16[16,12416]{1,0:T(8,128)(2,1)S(1)}, u32[]{:S(2)}, u32[]{:S(2)}) collective-permute-start(bf16[16,12416]{1,0:T(8,128)(2,1)S(1)} %pad_maximum_fusion.refs_0_), channel_id=1, source_target_pairs={{0,1},{1,0},{2,3},{3,2},{4,5},{5,4},{6,7},{7,6},{8,9},{9,8},{10,11... | collective-permute-start | bytes 1191944 | tf_op jit(solution)/shard_map/ppermute | solution.py:369
  23.5 1.8 %collective-permute-start.8 = (bf16[16,12416]{1,0:T(8,128)(2,1)S(1)}, bf16[16,12416]{1,0:T(8,128)(2,1)S(1)}, u32[]{:S(2)}, u32[]{:S(2)}) collective-permute-start(bf16[16,12416]{1,0:T(8,128)(2,1)S(1)} %pad_maximum_fusion.1.refs_1_.after), channel_id=1, source_target_pairs={{0,1},{1,0},{2,3},{3,2},{4,5},{5,4},{6,7},{7,6},{8,9},{9,8},{10,11... | collective-permute-start | bytes 1191944 | tf_op jit(solution)/shard_map/ppermute | solution.py:369
  34.1 1.8 %collective-permute-start.9 = (bf16[32,6272]{1,0:T(8,128)(2,1)S(1)}, bf16[32,6272]{1,0:T(8,128)(2,1)S(1)}, u32[]{:S(2)}, u32[]{:S(2)}) collective-permute-start(bf16[32,6272]{1,0:T(8,128)(2,1)S(1)} %get-tuple-element.59), channel_id=1, source_target_pairs={{0,1},{1,0},{2,3},{3,2},{4,5},{5,4},{6,7},{7,6},{8,9},{9,8},{10,11... | collective-permute-start | bytes 1204232 | tf_op jit(solution)/shard_map/ppermute | solution.py:369
  36.0 5.8 %collective-permute-start.10 = (bf16[16,6272]{1,0:T(8,128)(2,1)S(1)}, bf16[16,6272]{1,0:T(8,128)(2,1)S(1)}, u32[]{:S(2)}, u32[]{:S(2)}) collective-permute-start(bf16[16,6272]{1,0:T(8,128)(2,1)S(1)} %get-tuple-element.61), channel_id=1, source_target_pairs={{0,2},{1,5},{2,0},{3,7},{4,6},{5,1},{6,4},{7,3},{8,10},{9,13},{10,... | collective-permute-start | bytes 602120 | tf_op jit(solution)/shard_map/ppermute | solution.py:369
  42.0 4.7 %collective-permute-start.11 = (bf16[8,6272]{1,0:T(8,128)(2,1)S(1)}, bf16[8,6272]{1,0:T(8,128)(2,1)S(1)}, u32[]{:S(2)}, u32[]{:S(2)}) collective-permute-start(bf16[8,6272]{1,0:T(8,128)(2,1)S(1)} %get-tuple-element.63), channel_id=1, source_target_pairs={{0,4},{1,3},{2,6},{3,1},{4,0},{5,7},{6,2},{7,5},{8,12},{9,11},{10,... | collective-permute-start | bytes 301064 | tf_op jit(solution)/shard_map/ppermute | solution.py:369
  46.8 5.4 %collective-permute-start.12 = (bf16[4,6272]{1,0:T(4,128)(2,1)S(1)}, bf16[4,6272]{1,0:T(4,128)(2,1)S(1)}, u32[]{:S(2)}, u32[]{:S(2)}) collective-permute-start(bf16[4,6272]{1,0:T(4,128)(2,1)S(1)} %get-tuple-element.65), channel_id=1, source_target_pairs={{0,8},{1,9},{2,10},{3,11},{4,12},{5,13},{6,14},{7,15},{8,0},{9,1},... | collective-permute-start | bytes 150536 | tf_op jit(solution)/shard_map/ppermute | solution.py:369

commit v16 on v15

--- a/solution.py
+++ b/solution.py
@@ -199,19 +199,15 @@
     copies = fetch_copies([(down_in, 0)], [down_w], sems)
     for copy in copies:
         copy.start()
-    for c in range(0, wide, LANES):
-        at = pl.ds(c, LANES)
-        block = jnp.concatenate([ref[:, at].astype(F32) for ref in pieces])
-        x[:, at] = block.astype(BF16)
-        if c < width:
-            x_t[at, :] = block.T.astype(BF16)
     quarter = rows // 4
     for i, ref in enumerate(pieces):
-        y[i * quarter : (i + 1) * quarter, :] = ref[:, wide:]
+        x[i * quarter : (i + 1) * quarter, :] = ref[:, :wide]
     pre_gate = dot(x[:, :width], gate_w[...], ((1,), (0,)))
     pre_up = dot(x[:, :width], up_w[...], ((1,), (0,)))
     for copy in copies:
         copy.wait()
+    for i, ref in enumerate(pieces):
+        y[i * quarter : (i + 1) * quarter, :] = ref[:, wide:]
     back = dot(y[...], down_w[...], ((1,), (1,)))
     g = x[:, width:][:, 0:1].astype(F32)
     sig = jax.nn.sigmoid(pre_gate)
@@ -233,6 +229,8 @@
         part += dot(d_both[:, hidden_dim:], up_w[at, :], ((1,), (1,)))
         keep[:, at] = part[:half]
         send[:, at] = part[half:].astype(BF16)
+        for c in range(i * wide, (i + 1) * wide, LANES):
+            x_t[c : c + LANES, :] = x[:, c : c + LANES].astype(F32).T.astype(BF16)
 
 
 def fold_kernel(have, got, keep, send):

time: 53.3 us -> 53.3 us (level)
  no operation moved by 1% of the time
where the time goes in v16:
time: 53.3 us; the launch traced here: 53.1 us
  Pallas kernels  26.3 us (49%)
  starting transfers between devices  13.6 us (26%)
  waiting for transfers between devices  12 us (23%)
  between operations  0.79 us (1%)
    ppermute x13, starting transfers between devices, swap(): return lax.ppermute(block, 'blk', [(i, i ^ bits[i % 2]) for i in range(n)])  13.6 us
    ppermute x13, waiting for transfers between devices, swap(): return lax.ppermute(block, 'blk', [(i, i ^ bits[i % 2]) for i in range(n)])  12 us
    pallas_call x3, Pallas kernels, grads_of(): pl.pallas_call(kernel, out_shape=outs, in_specs=whole(2 + len(down)) + (w...  8.86 us
    pallas_call x1, Pallas kernels, shards(): pl.pallas_call(expert_kernel, out_shape=[jax.ShapeDtypeStruct((half, wide...  8.8 us
    pallas_call x1, Pallas kernels, fetch(): pl.pallas_call(functools.partial(fetch_kernel, count), out_shape=[pltpu.V...  4.7 us
    pallas_call x4, Pallas kernels, call(): pl.pallas_call(kernel, out_shape=[jax.ShapeDtypeStruct(s, t) for s, t in...  1.38 us
    pallas_call x1, Pallas kernels, shards(): pl.pallas_call(router_kernel, out_shape=[jax.ShapeDtypeStruct((1, count),...  1.3 us
    pallas_call x1, Pallas kernels, shards(): pl.pallas_call(select_kernel, out_shape=[jax.ShapeDtypeStruct((slots, wid...  1.19 us
  transfers between devices with their start and end apart: 13, of which 8 were waited for; matrix products, arithmetic and copies ran while one was open for 1% of the time, Pallas kernels for 28%

profile of v16, /device:TPU:0, one launch (start us, length us, event | category | flops | bytes accessed | tf_op | source)
XLA Modules:
  0.0 53.1 jit_solution(13189152431761415648)
XLA Ops:
  0.6 1.2 %shard_map.135 = (bf16[4,12416]{1,0:T(4,128)(2,1)S(1)}, f32[16,16]{1,0:T(8,128)S(1)}) custom-call(f32[8,16]{1,0:T(8,128)} %bitcast.6, s32[2,16]{1,0:T(2,128)} %bitcast.9, bf16[16,6144]{1,0:T(8,128)(2,1)} %tokens_in.1, bf16[4,6144]{1,0:T(4,128)(2,1)} %y_in.1), custom_call_target="tpu_custom_call" | custom-call | flops 1048576 | bytes 4194304 | tf_op jit(solution)/shard_map/pallas_call | solution.py:381
  1.8 4.1 %collective-permute-start = (bf16[4,12416]{1,0:T(4,128)(2,1)S(1)}, bf16[4,12416]{1,0:T(4,128)(2,1)S(1)}, u32[]{:S(2)}, u32[]{:S(2)}) collective-permute-start(bf16[4,12416]{1,0:T(4,128)(2,1)S(1)} %get-tuple-element.40.refs_2_), channel_id=1, source_target_pairs={{0,8},{1,9},{2,10},{3,11},{4,12},{5,13},{6,14},{7,15},{8,0},{9,1},... | collective-permute-start | bytes 297992 | tf_op jit(solution)/shard_map/ppermute | solution.py:367
  5.9 1.5 %collective-permute-start.2 = (bf16[4,12416]{1,0:T(4,128)(2,1)S(1)}, bf16[4,12416]{1,0:T(4,128)(2,1)S(1)}, u32[]{:S(2)}, u32[]{:S(2)}) collective-permute-start(bf16[4,12416]{1,0:T(4,128)(2,1)S(1)} %get-tuple-element.40.refs_2_), channel_id=1, source_target_pairs={{0,2},{1,5},{2,0},{3,7},{4,6},{5,1},{6,4},{7,3},{8,10},{9,13},{10,... | collective-permute-start | bytes 297992 | tf_op jit(solution)/shard_map/ppermute | solution.py:367
  7.4 1.6 %collective-permute-start.1 = (bf16[4,12416]{1,0:T(4,128)(2,1)S(1)}, bf16[4,12416]{1,0:T(4,128)(2,1)S(1)}, u32[]{:S(2)}, u32[]{:S(2)}) collective-permute-start(bf16[4,12416]{1,0:T(4,128)(2,1)S(1)} %get-tuple-element.40.refs_2_), channel_id=1, source_target_pairs={{0,4},{1,3},{2,6},{3,1},{4,0},{5,7},{6,2},{7,5},{8,12},{9,11},{10,... | collective-permute-start | bytes 297992 | tf_op jit(solution)/shard_map/ppermute | solution.py:367
  9.0 4.7 %shard_map.138 = (bf16[6144,512]{1,0:T(8,128)(2,1)S(1)}, bf16[6144,512]{1,0:T(8,128)(2,1)S(1)}) custom-call(bf16[6144,512]{1,0:T(8,128)(2,1)} %refs_0_.1, bf16[6144,512]{1,0:T(8,128)(2,1)} %refs_1_.1, bf16[4,12416]{1,0:T(4,128)(2,1)S(1)} %get-tuple-element.40.refs_2_), custom_call_target="tpu_custom_call" | custom-call | bytes 12582912 | tf_op jit(solution)/shard_map/pallas_call | solution.py:162
  13.7 0.0 collective-permute-done.block
  13.8 0.0 collective-permute-done.2.refs_2_
  13.8 0.0 collective-permute-done.1.refs_1_
  13.8 0.5 collective-permute-start.3
  14.3 0.6 %collective-permute-start.4 = (bf16[4,12416]{1,0:T(4,128)(2,1)S(1)}, bf16[4,12416]{1,0:T(4,128)(2,1)S(1)}, u32[]{:S(2)}, u32[]{:S(2)}) collective-permute-start(bf16[4,12416]{1,0:T(4,128)(2,1)S(1)} %shard_map.140), channel_id=1, source_target_pairs={{0,2},{1,5},{2,0},{3,7},{4,6},{5,1},{6,4},{7,3},{8,10},{9,13},{10,... | collective-permute-start | bytes 297992 | tf_op jit(solution)/shard_map/ppermute | solution.py:367
  14.9 1.6 %collective-permute-start.5 = (bf16[4,12416]{1,0:T(4,128)(2,1)S(1)}, bf16[4,12416]{1,0:T(4,128)(2,1)S(1)}, u32[]{:S(2)}, u32[]{:S(2)}) collective-permute-start(bf16[4,12416]{1,0:T(4,128)(2,1)S(1)} %collective-permute-done.2.refs_2_), channel_id=1, source_target_pairs={{0,4},{1,3},{2,6},{3,1},{4,0},{5,7},{6,2},{7,5},{8,12},{9,11},{10,... | collective-permute-start | bytes 297992 | tf_op jit(solution)/shard_map/ppermute | solution.py:367
  16.5 2.0 %collective-permute-done.3.block = bf16[4,12416]{1,0:T(4,128)(2,1)S(1)} collective-permute-done((bf16[4,12416]{1,0:T(4,128)(2,1)S(1)}, bf16[4,12416]{1,0:T(4,128)(2,1)S(1)}, u32[]{:S(2)}, u32[]{:S(2)}) %collective-permute-start.3) | collective-permute-done | bytes 99360 | tf_op jit(solution)/shard_map/ppermute | solution.py:367
  18.5 1.0 %collective-permute-start.6 = (bf16[4,12416]{1,0:T(4,128)(2,1)S(1)}, bf16[4,12416]{1,0:T(4,128)(2,1)S(1)}, u32[]{:S(2)}, u32[]{:S(2)}) collective-permute-start(bf16[4,12416]{1,0:T(4,128)(2,1)S(1)} %shard_map.141), channel_id=1, source_target_pairs={{0,2},{1,5},{2,0},{3,7},{4,6},{5,1},{6,4},{7,3},{8,10},{9,13},{10,... | collective-permute-start | bytes 297992 | tf_op jit(solution)/shard_map/ppermute | solution.py:367
  19.5 0.2 pad_maximum_fusion.refs_0_
  19.7 0.1 collective-permute-start.7
  19.8 0.2 collective-permute-done.5
  20.1 0.0 collective-permute-done.4
  20.1 3.2 %collective-permute-done.6 = bf16[4,12416]{1,0:T(4,128)(2,1)S(1)} collective-permute-done((bf16[4,12416]{1,0:T(4,128)(2,1)S(1)}, bf16[4,12416]{1,0:T(4,128)(2,1)S(1)}, u32[]{:S(2)}, u32[]{:S(2)}) %collective-permute-start.6) | collective-permute-done | bytes 99360 | tf_op jit(solution)/shard_map/ppermute | solution.py:367
  23.2 0.2 pad_maximum_fusion.1.refs_1_.after
  23.5 0.1 collective-permute-start.8
  23.5 0.0 collective-permute-done.7.refs_2_
  23.5 1.7 %collective-permute-done.8.refs_3_ = bf16[16,12416]{1,0:T(8,128)(2,1)S(1)} collective-permute-done((bf16[16,12416]{1,0:T(8,128)(2,1)S(1)}, bf16[16,12416]{1,0:T(8,128)(2,1)S(1)}, u32[]{:S(2)}, u32[]{:S(2)}) %collective-permute-start.8) | collective-permute-done | bytes 397344 | tf_op jit(solution)/shard_map/ppermute | solution.py:367
  25.2 8.8 %shard_map.142 = (bf16[32,6272]{1,0:T(8,128)(2,1)S(1)}, f32[32,6272]{1,0:T(8,128)S(1)}, bf16[512,64]{1,0:T(8,128)(2,1)S(1)}, bf16[64,1024]{1,0:T(8,128)(2,1)S(1)...) custom-call(bf16[16,12416]{1,0:T(8,128)(2,1)S(1)} %pad_maximum_fusion.refs_0_, ...), custom_call_target="tpu_custom_call" | custom-call | flops 6442450944 | bytes 12582912 | tf_op jit(solution)/shard_map/pallas_call | solution.py:444
  34.0 0.2 collective-permute-start.9
  34.3 1.3 %shard_map.149 = (f32[1,16]{1,0:T(1,128)}, f32[1,16]{1,0:T(1,128)}, f32[8,16]{1,0:T(8,128)S(1)}, f32[8,16]{1,0:T(8,128)S(1)}) custom-call(f32[8,16]{1,0:T(8,128)} %bitcast.7, f32[8,16]{1,0:T(8,128)} %bitcast.8, s32[2,16]{1,0:T(2,128)} %bitcast.10, bf16[16,12416]{1,0:T(8,128)(2,1)S(1)} %pad_maximum_fusion.1.refs_1_.after), custom_call_target="tpu_custom_call" | custom-call | flops 1048576 | bytes 4194304 | tf_op jit(solution)/shard_map/pallas_call | solution.py:420
  35.6 0.3 collective-permute-done.9.got
  35.8 0.2 shard_map.146
  36.0 1.0 %collective-permute-start.10 = (bf16[16,6272]{1,0:T(8,128)(2,1)S(1)}, bf16[16,6272]{1,0:T(8,128)(2,1)S(1)}, u32[]{:S(2)}, u32[]{:S(2)}) collective-permute-start(bf16[16,6272]{1,0:T(8,128)(2,1)S(1)} %get-tuple-element.61), channel_id=1, source_target_pairs={{0,2},{1,5},{2,0},{3,7},{4,6},{5,1},{6,4},{7,3},{8,10},{9,13},{10,... | collective-permute-start | bytes 602120 | tf_op jit(solution)/shard_map/ppermute | solution.py:367
  37.0 4.3 %shard_map.143 = (bf16[512,6144]{1,0:T(8,128)(2,1)}, bf16[6144,512]{1,0:T(8,128)(2,1)}, bf16[6144,512]{1,0:T(8,128)(2,1)}, bf16[256,512]{1,0:T(8,128)(2,1)S(1)}, bf16[256,512]{1,0:T(8,128)(2,1)S(1)}) custom-call(bf16[512,64]{1,0:T(8,128)(2,1)S(1)} %get-tuple-element.45.weighted_t, bf16[64,6144]{1,0:T(8,128)(2,1)S(1)} %get-tuple-element.46.y, ...), custom_call_target="tpu_custom_call" | custom-call | flops 2684354560 | bytes 10485760 | tf_op jit(solution)/shard_map/pallas_call | solution.py:344
  41.4 0.4 collective-permute-done.10.got
  41.8 0.1 shard_map.147
  42.0 0.5 collective-permute-start.11
  42.4 2.2 %shard_map.144 = (bf16[6144,512]{1,0:T(8,128)(2,1)}, bf16[6144,512]{1,0:T(8,128)(2,1)}, bf16[256,512]{1,0:T(8,128)(2,1)S(1)}, bf16[256,512]{1,0:T(8,128)(2,1)S(1)}) custom-call(bf16[6144,64]{1,0:T(8,128)(2,1)S(1)} %get-tuple-element.43.x_t, bf16[64,1024]{1,0:T(8,128)(2,1)S(1)} %get-tuple-element.44.d_both, ...), custom_call_target="tpu_custom_call", output_to_operand_aliasing={{0}: (4, {}), {1}: (5, {})} | custom-call | flops 1073741824 | bytes 4194304 | tf_op jit(solution)/shard_map/pallas_call | solution.py:344
  44.6 2.0 %collective-permute-done.11.got = bf16[8,6272]{1,0:T(8,128)(2,1)S(1)} collective-permute-done((bf16[8,6272]{1,0:T(8,128)(2,1)S(1)}, bf16[8,6272]{1,0:T(8,128)(2,1)S(1)}, u32[]{:S(2)}, u32[]{:S(2)}) %collective-permute-start.11) | collective-permute-done | bytes 100384 | tf_op jit(solution)/shard_map/ppermute | solution.py:367
  46.6 0.2 shard_map.148
  46.8 0.9 %collective-permute-start.12 = (bf16[4,6272]{1,0:T(4,128)(2,1)S(1)}, bf16[4,6272]{1,0:T(4,128)(2,1)S(1)}, u32[]{:S(2)}, u32[]{:S(2)}) collective-permute-start(bf16[4,6272]{1,0:T(4,128)(2,1)S(1)} %get-tuple-element.65), channel_id=1, source_target_pairs={{0,8},{1,9},{2,10},{3,11},{4,12},{5,13},{6,14},{7,15},{8,0},{9,1},... | collective-permute-start | bytes 150536 | tf_op jit(solution)/shard_map/ppermute | solution.py:367
  47.7 2.4 %shard_map.145 = (bf16[6144,512]{1,0:T(8,128)(2,1)}, bf16[6144,512]{1,0:T(8,128)(2,1)}) custom-call(bf16[6144,64]{1,0:T(8,128)(2,1)S(1)} %get-tuple-element.43.x_t, bf16[64,1024]{1,0:T(8,128)(2,1)S(1)} %get-tuple-element.44.d_both, bf16[256,512]{1,0:T(8,128)(2,1)S(1)} %get-tuple-element.51.refs_0_, ...), custom_call_target="tpu_custom_call", output_to_operand_aliasing={{0}: (4, {}), {1}: (5, {})} | custom-call | flops 1073741824 | bytes 4194304 | tf_op jit(solution)/shard_map/pallas_call | solution.py:344
  50.1 2.1 %collective-permute-done.12.got = bf16[4,6272]{1,0:T(4,128)(2,1)S(1)} collective-permute-done((bf16[4,6272]{1,0:T(4,128)(2,1)S(1)}, bf16[4,6272]{1,0:T(4,128)(2,1)S(1)}, u32[]{:S(2)}, u32[]{:S(2)}) %collective-permute-start.12) | collective-permute-done | bytes 50208 | tf_op jit(solution)/shard_map/ppermute | solution.py:367
  52.2 0.9 %shard_map.150 = (bf16[16,6144]{1,0:T(8,128)(2,1)}, f32[8,16]{1,0:T(8,128)}) custom-call(f32[4,6272]{1,0:T(4,128)S(1)} %get-tuple-element.64.have, bf16[4,6272]{1,0:T(4,128)(2,1)S(1)} %collective-permute-done.12.got, f32[16,16]{1,0:T(8,128)S(1)} %get-tuple-element.66.select, f32[8,16]{1,0:T(8,128)S(1)} %get-tuple-element.67.base, ...), custom_call_target="tpu_custom_call" | custom-call | flops 1048576 | bytes 262144 | tf_op jit(solution)/shard_map/pallas_call | solution.py:25
  (5 shorter events, 0.0 us)
Async XLA Ops:
  1.8 11.9 %collective-permute-start = (bf16[4,12416]{1,0:T(4,128)(2,1)S(1)}, bf16[4,12416]{1,0:T(4,128)(2,1)S(1)}, u32[]{:S(2)}, u32[]{:S(2)}) collective-permute-start(bf16[4,12416]{1,0:T(4,128)(2,1)S(1)} %get-tuple-element.40.refs_2_), channel_id=1, source_target_pairs={{0,8},{1,9},{2,10},{3,11},{4,12},{5,13},{6,14},{7,15},{8,0},{9,1},... | collective-permute-start | bytes 297992 | tf_op jit(solution)/shard_map/ppermute | solution.py:367
  5.9 7.8 %collective-permute-start.2 = (bf16[4,12416]{1,0:T(4,128)(2,1)S(1)}, bf16[4,12416]{1,0:T(4,128)(2,1)S(1)}, u32[]{:S(2)}, u32[]{:S(2)}) collective-permute-start(bf16[4,12416]{1,0:T(4,128)(2,1)S(1)} %get-tuple-element.40.refs_2_), channel_id=1, source_target_pairs={{0,2},{1,5},{2,0},{3,7},{4,6},{5,1},{6,4},{7,3},{8,10},{9,13},{10,... | collective-permute-start | bytes 297992 | tf_op jit(solution)/shard_map/ppermute | solution.py:367
  7.4 6.3 %collective-permute-start.1 = (bf16[4,12416]{1,0:T(4,128)(2,1)S(1)}, bf16[4,12416]{1,0:T(4,128)(2,1)S(1)}, u32[]{:S(2)}, u32[]{:S(2)}) collective-permute-start(bf16[4,12416]{1,0:T(4,128)(2,1)S(1)} %get-tuple-element.40.refs_2_), channel_id=1, source_target_pairs={{0,4},{1,3},{2,6},{3,1},{4,0},{5,7},{6,2},{7,5},{8,12},{9,11},{10,... | collective-permute-start | bytes 297992 | tf_op jit(solution)/shard_map/ppermute | solution.py:367
  13.8 4.7 %collective-permute-start.3 = (bf16[4,12416]{1,0:T(4,128)(2,1)S(1)}, bf16[4,12416]{1,0:T(4,128)(2,1)S(1)}, u32[]{:S(2)}, u32[]{:S(2)}) collective-permute-start(bf16[4,12416]{1,0:T(4,128)(2,1)S(1)} %shard_map.139.block), channel_id=1, source_target_pairs={{0,4},{1,3},{2,6},{3,1},{4,0},{5,7},{6,2},{7,5},{8,12},{9,11},{10,... | collective-permute-start | bytes 297992 | tf_op jit(solution)/shard_map/ppermute | solution.py:367
  14.3 5.7 %collective-permute-start.4 = (bf16[4,12416]{1,0:T(4,128)(2,1)S(1)}, bf16[4,12416]{1,0:T(4,128)(2,1)S(1)}, u32[]{:S(2)}, u32[]{:S(2)}) collective-permute-start(bf16[4,12416]{1,0:T(4,128)(2,1)S(1)} %shard_map.140), channel_id=1, source_target_pairs={{0,2},{1,5},{2,0},{3,7},{4,6},{5,1},{6,4},{7,3},{8,10},{9,13},{10,... | collective-permute-start | bytes 297992 | tf_op jit(solution)/shard_map/ppermute | solution.py:367
  14.9 5.1 %collective-permute-start.5 = (bf16[4,12416]{1,0:T(4,128)(2,1)S(1)}, bf16[4,12416]{1,0:T(4,128)(2,1)S(1)}, u32[]{:S(2)}, u32[]{:S(2)}) collective-permute-start(bf16[4,12416]{1,0:T(4,128)(2,1)S(1)} %collective-permute-done.2.refs_2_), channel_id=1, source_target_pairs={{0,4},{1,3},{2,6},{3,1},{4,0},{5,7},{6,2},{7,5},{8,12},{9,11},{10,... | collective-permute-start | bytes 297992 | tf_op jit(solution)/shard_map/ppermute | solution.py:367
  18.5 4.7 %collective-permute-start.6 = (bf16[4,12416]{1,0:T(4,128)(2,1)S(1)}, bf16[4,12416]{1,0:T(4,128)(2,1)S(1)}, u32[]{:S(2)}, u32[]{:S(2)}) collective-permute-start(bf16[4,12416]{1,0:T(4,128)(2,1)S(1)} %shard_map.141), channel_id=1, source_target_pairs={{0,2},{1,5},{2,0},{3,7},{4,6},{5,1},{6,4},{7,3},{8,10},{9,13},{10,... | collective-permute-start | bytes 297992 | tf_op jit(solution)/shard_map/ppermute | solution.py:367
  19.7 3.8 %collective-permute-start.7 = (bf16[16,12416]{1,0:T(8,128)(2,1)S(1)}, bf16[16,12416]{1,0:T(8,128)(2,1)S(1)}, u32[]{:S(2)}, u32[]{:S(2)}) collective-permute-start(bf16[16,12416]{1,0:T(8,128)(2,1)S(1)} %pad_maximum_fusion.refs_0_), channel_id=1, source_target_pairs={{0,1},{1,0},{2,3},{3,2},{4,5},{5,4},{6,7},{7,6},{8,9},{9,8},{10,11... | collective-permute-start | bytes 1191944 | tf_op jit(solution)/shard_map/ppermute | solution.py:367
  23.5 1.8 %collective-permute-start.8 = (bf16[16,12416]{1,0:T(8,128)(2,1)S(1)}, bf16[16,12416]{1,0:T(8,128)(2,1)S(1)}, u32[]{:S(2)}, u32[]{:S(2)}) collective-permute-start(bf16[16,12416]{1,0:T(8,128)(2,1)S(1)} %pad_maximum_fusion.1.refs_1_.after), channel_id=1, source_target_pairs={{0,1},{1,0},{2,3},{3,2},{4,5},{5,4},{6,7},{7,6},{8,9},{9,8},{10,11... | collective-permute-start | bytes 1191944 | tf_op jit(solution)/shard_map/ppermute | solution.py:367
  34.0 1.8 %collective-permute-start.9 = (bf16[32,6272]{1,0:T(8,128)(2,1)S(1)}, bf16[32,6272]{1,0:T(8,128)(2,1)S(1)}, u32[]{:S(2)}, u32[]{:S(2)}) collective-permute-start(bf16[32,6272]{1,0:T(8,128)(2,1)S(1)} %get-tuple-element.59), channel_id=1, source_target_pairs={{0,1},{1,0},{2,3},{3,2},{4,5},{5,4},{6,7},{7,6},{8,9},{9,8},{10,11... | collective-permute-start | bytes 1204232 | tf_op jit(solution)/shard_map/ppermute | solution.py:367
  36.0 5.8 %collective-permute-start.10 = (bf16[16,6272]{1,0:T(8,128)(2,1)S(1)}, bf16[16,6272]{1,0:T(8,128)(2,1)S(1)}, u32[]{:S(2)}, u32[]{:S(2)}) collective-permute-start(bf16[16,6272]{1,0:T(8,128)(2,1)S(1)} %get-tuple-element.61), channel_id=1, source_target_pairs={{0,2},{1,5},{2,0},{3,7},{4,6},{5,1},{6,4},{7,3},{8,10},{9,13},{10,... | collective-permute-start | bytes 602120 | tf_op jit(solution)/shard_map/ppermute | solution.py:367
  42.0 4.7 %collective-permute-start.11 = (bf16[8,6272]{1,0:T(8,128)(2,1)S(1)}, bf16[8,6272]{1,0:T(8,128)(2,1)S(1)}, u32[]{:S(2)}, u32[]{:S(2)}) collective-permute-start(bf16[8,6272]{1,0:T(8,128)(2,1)S(1)} %get-tuple-element.63), channel_id=1, source_target_pairs={{0,4},{1,3},{2,6},{3,1},{4,0},{5,7},{6,2},{7,5},{8,12},{9,11},{10,... | collective-permute-start | bytes 301064 | tf_op jit(solution)/shard_map/ppermute | solution.py:367
  46.8 5.4 %collective-permute-start.12 = (bf16[4,6272]{1,0:T(4,128)(2,1)S(1)}, bf16[4,6272]{1,0:T(4,128)(2,1)S(1)}, u32[]{:S(2)}, u32[]{:S(2)}) collective-permute-start(bf16[4,6272]{1,0:T(4,128)(2,1)S(1)} %get-tuple-element.65), channel_id=1, source_target_pairs={{0,8},{1,9},{2,10},{3,11},{4,12},{5,13},{6,14},{7,15},{8,0},{9,1},... | collective-permute-start | bytes 150536 | tf_op jit(solution)/shard_map/ppermute | solution.py:367

commit v17 on v16

--- a/solution.py
+++ b/solution.py
@@ -167,7 +167,7 @@
         scratch_shapes=[pltpu.SemaphoreType.DMA((count, 4))],
         compiler_params=pltpu.CompilerParams(vmem_limit_bytes=8 * MIB),
         cost_estimate=pl.CostEstimate(
-            flops=0, bytes_accessed=2 * sum(w.size for w in weights), transcendentals=0
+            flops=0, bytes_accessed=2 * sum(w.shape[1] * r for w, r in zip(weights, rows)), transcendentals=0
         ),
     )(*[in_hbm(w) for w in weights], after)
     return [in_vmem(w) for w in out]
@@ -191,12 +191,12 @@
 
 
 def expert_kernel(*refs):
-    pieces, (down_in, gate_w, up_w), refs = refs[:4], refs[4:7], refs[7:]
-    send, keep, weighted_t, d_both, x_t, y, x, down_w, sems = refs
+    pieces, (down_in, gate_w, up_w, down_head), refs = refs[:4], refs[4:8], refs[8:]
+    send, keep, weighted_t, d_both, x_t, y, x, down_tail, sems = refs
     rows, width, hidden_dim = x.shape[0], gate_w.shape[0], gate_w.shape[1]
     wide = width + LANES
     half = rows // 2
-    copies = fetch_copies([(down_in, 0)], [down_w], sems)
+    copies = fetch_copies([(down_in, down_head.shape[0])], [down_tail], sems)
     for copy in copies:
         copy.start()
     quarter = rows // 4
@@ -204,11 +204,13 @@
         x[i * quarter : (i + 1) * quarter, :] = ref[:, :wide]
     pre_gate = dot(x[:, :width], gate_w[...], ((1,), (0,)))
     pre_up = dot(x[:, :width], up_w[...], ((1,), (0,)))
-    for copy in copies:
-        copy.wait()
     for i, ref in enumerate(pieces):
         y[i * quarter : (i + 1) * quarter, :] = ref[:, wide:]
-    back = dot(y[...], down_w[...], ((1,), (1,)))
+    back_head = dot(y[...], down_head[...], ((1,), (1,)))
+    for copy in copies:
+        copy.wait()
+    back_tail = dot(y[...], down_tail[...], ((1,), (1,)))
+    back = jnp.concatenate([back_head, back_tail], axis=1)
     g = x[:, width:][:, 0:1].astype(F32)
     sig = jax.nn.sigmoid(pre_gate)
     act = pre_gate * sig
@@ -361,7 +363,7 @@
     while bit > 4:
         levels.append((bit, bit))
         bit //= 2
-    levels += [(4, 2), (2, 4)]
+    levels += [(2, 4), (4, 2)]
 
     def swap(block, bits):
         return lax.ppermute(block, "blk", [(i, i ^ bits[i % 2]) for i in range(n)])
@@ -409,9 +411,11 @@
         gate_w, up_w = fetch([gate_weight, up_weight], [width, width], own)
         block_1 = relay(block_1, gate_w, block_2, block_3)
         block_12 = swap(block_1, second)
-        block_13 = swap(relay(block_1), third)
+        block_13_source = relay(block_1)
+        block_13 = swap(block_13_source, third)
         block_23 = swap(block_3, second)
-        block_123 = swap(relay(block_12), third)
+        (down_head,) = fetch([down_weight], [hidden // 2], relay(block_13_source))
+        block_123 = swap(relay(block_12, down_head), third)
         low_half = jnp.concatenate([own, block_1, block_2, block_12])
         high_half = jnp.concatenate([block_3, block_13, block_23, block_123])
         pieces = [low_half, high_half]
@@ -451,18 +455,18 @@
                 jax.ShapeDtypeStruct((width, rows), BF16),
                 jax.ShapeDtypeStruct((rows, width), BF16),
             ],
-            in_specs=whole(4) + [anywhere] + whole(2),
+            in_specs=whole(4) + [anywhere] + whole(3),
             out_specs=whole(6),
             scratch_shapes=[
                 pltpu.VMEM((rows, wide), BF16),
-                pltpu.VMEM((hidden, width), BF16),
+                pltpu.VMEM((hidden // 2, width), BF16),
                 pltpu.SemaphoreType.DMA((1, 4)),
             ],
             compiler_params=pltpu.CompilerParams(vmem_limit_bytes=24 * MIB),
             cost_estimate=pl.CostEstimate(
                 flops=16 * work, bytes_accessed=4 * width * hidden, transcendentals=0
             ),
-        )(*pieces, in_hbm(down_weight), gate_w, up_w)
+        )(*pieces, in_hbm(down_weight), gate_w, up_w, down_head)
 
         for bits in [(1, 1)] + levels[::-1]:
             got = swap(low, bits)

time: 53.3 us -> 55.1 us (1.034)
  Pallas kernels: 26.3 us -> 30.2 us
  waiting for transfers between devices: 12 us -> 8.42 us
  starting transfers between devices: 13.6 us -> 15 us
    ppermute x13, waiting for transfers between devices: 12 us -> 8.42 us  [swap(): return lax.ppermute(block, 'blk', [(i, i ^ bits[i % 2]) for i in range(n)])]
    pallas_call x1, Pallas kernels: 8.8 us -> 10.8 us  [shards(): pl.pallas_call(expert_kernel, out_shape=[jax.ShapeDtypeStruct((half, wide...]
    pallas_call x1 -> x2, Pallas kernels: 4.7 us -> 6.57 us  [fetch(): pl.pallas_call(functools.partial(fetch_kernel, count), out_shape=[pltpu.V...]
    ppermute x13, starting transfers between devices: 13.6 us -> 15 us  [swap(): return lax.ppermute(block, 'blk', [(i, i ^ bits[i % 2]) for i in range(n)])]
  transfers between devices with their start and end apart: 13 -> 13, of which waited for: 8 -> 7; matrix products, arithmetic and copies ran while one was open for 1% -> 1% of each run, Pallas kernels for 28% -> 31%
where the time goes in v17:
time: 55.1 us; the launch traced here: 54.9 us
  Pallas kernels  30.2 us (55%)
  starting transfers between devices  15 us (27%)
  waiting for transfers between devices  8.42 us (15%)
  between operations  0.81 us (1%)
    ppermute x13, starting transfers between devices, swap(): return lax.ppermute(block, 'blk', [(i, i ^ bits[i % 2]) for i in range(n)])  15 us
    pallas_call x1, Pallas kernels, shards(): pl.pallas_call(expert_kernel, out_shape=[jax.ShapeDtypeStruct((half, wide...  10.8 us
    pallas_call x3, Pallas kernels, grads_of(): pl.pallas_call(kernel, out_shape=outs, in_specs=whole(2 + len(down)) + (w...  8.86 us
    ppermute x13, waiting for transfers between devices, swap(): return lax.ppermute(block, 'blk', [(i, i ^ bits[i % 2]) for i in range(n)])  8.42 us
    pallas_call x2, Pallas kernels, fetch(): pl.pallas_call(functools.partial(fetch_kernel, count), out_shape=[pltpu.V...  6.57 us
    pallas_call x4, Pallas kernels, call(): pl.pallas_call(kernel, out_shape=[jax.ShapeDtypeStruct(s, t) for s, t in...  1.39 us
    pallas_call x1, Pallas kernels, shards(): pl.pallas_call(router_kernel, out_shape=[jax.ShapeDtypeStruct((1, count),...  1.3 us
    pallas_call x1, Pallas kernels, shards(): pl.pallas_call(select_kernel, out_shape=[jax.ShapeDtypeStruct((slots, wid...  1.19 us
  transfers between devices with their start and end apart: 13, of which 7 were waited for; matrix products, arithmetic and copies ran while one was open for 1% of the time, Pallas kernels for 31%

profile of v17, /device:TPU:0, one launch (start us, length us, event | category | flops | bytes accessed | tf_op | source)
XLA Modules:
  0.0 54.9 jit_solution(8381462179871458822)
XLA Ops:
  0.6 1.2 %shard_map.135 = (bf16[4,12416]{1,0:T(4,128)(2,1)S(1)}, f32[16,16]{1,0:T(8,128)S(1)}) custom-call(f32[8,16]{1,0:T(8,128)} %bitcast.6, s32[2,16]{1,0:T(2,128)} %bitcast.9, bf16[16,6144]{1,0:T(8,128)(2,1)} %tokens_in.1, bf16[4,6144]{1,0:T(4,128)(2,1)} %y_in.1), custom_call_target="tpu_custom_call" | custom-call | flops 1048576 | bytes 4194304 | tf_op jit(solution)/shard_map/pallas_call | solution.py:383
  1.8 4.1 %collective-permute-start = (bf16[4,12416]{1,0:T(4,128)(2,1)S(1)}, bf16[4,12416]{1,0:T(4,128)(2,1)S(1)}, u32[]{:S(2)}, u32[]{:S(2)}) collective-permute-start(bf16[4,12416]{1,0:T(4,128)(2,1)S(1)} %get-tuple-element.40.refs_2_), channel_id=1, source_target_pairs={{0,8},{1,9},{2,10},{3,11},{4,12},{5,13},{6,14},{7,15},{8,0},{9,1},... | collective-permute-start | bytes 297992 | tf_op jit(solution)/shard_map/ppermute | solution.py:369
  5.9 1.6 %collective-permute-start.2 = (bf16[4,12416]{1,0:T(4,128)(2,1)S(1)}, bf16[4,12416]{1,0:T(4,128)(2,1)S(1)}, u32[]{:S(2)}, u32[]{:S(2)}) collective-permute-start(bf16[4,12416]{1,0:T(4,128)(2,1)S(1)} %get-tuple-element.40.refs_2_), channel_id=1, source_target_pairs={{0,4},{1,3},{2,6},{3,1},{4,0},{5,7},{6,2},{7,5},{8,12},{9,11},{10,... | collective-permute-start | bytes 297992 | tf_op jit(solution)/shard_map/ppermute | solution.py:369
  7.5 1.5 %collective-permute-start.1 = (bf16[4,12416]{1,0:T(4,128)(2,1)S(1)}, bf16[4,12416]{1,0:T(4,128)(2,1)S(1)}, u32[]{:S(2)}, u32[]{:S(2)}) collective-permute-start(bf16[4,12416]{1,0:T(4,128)(2,1)S(1)} %get-tuple-element.40.refs_2_), channel_id=1, source_target_pairs={{0,2},{1,5},{2,0},{3,7},{4,6},{5,1},{6,4},{7,3},{8,10},{9,13},{10,... | collective-permute-start | bytes 297992 | tf_op jit(solution)/shard_map/ppermute | solution.py:369
  9.0 4.7 %shard_map.138 = (bf16[6144,512]{1,0:T(8,128)(2,1)S(1)}, bf16[6144,512]{1,0:T(8,128)(2,1)S(1)}) custom-call(bf16[6144,512]{1,0:T(8,128)(2,1)} %refs_0_.2, bf16[6144,512]{1,0:T(8,128)(2,1)} %refs_1_.1, bf16[4,12416]{1,0:T(4,128)(2,1)S(1)} %get-tuple-element.40.refs_2_), custom_call_target="tpu_custom_call" | custom-call | bytes 12582912 | tf_op jit(solution)/shard_map/pallas_call | solution.py:162
  13.7 0.0 collective-permute-done.block
  13.8 0.0 collective-permute-done.2.refs_2_
  13.8 0.0 collective-permute-done.1.refs_1_
  13.8 0.6 %collective-permute-start.3 = (bf16[4,12416]{1,0:T(4,128)(2,1)S(1)}, bf16[4,12416]{1,0:T(4,128)(2,1)S(1)}, u32[]{:S(2)}, u32[]{:S(2)}) collective-permute-start(bf16[4,12416]{1,0:T(4,128)(2,1)S(1)} %shard_map.139.block), channel_id=1, source_target_pairs={{0,2},{1,5},{2,0},{3,7},{4,6},{5,1},{6,4},{7,3},{8,10},{9,13},{10,... | collective-permute-start | bytes 297992 | tf_op jit(solution)/shard_map/ppermute | solution.py:369
  14.4 0.5 collective-permute-start.4
  15.0 1.9 %shard_map.142.refs_0_.refs_7_ = bf16[256,6144]{1,0:T(8,128)(2,1)S(1)} custom-call(bf16[512,6144]{1,0:T(8,128)(2,1)} %refs_4_.1, bf16[4,12416]{1,0:T(4,128)(2,1)S(1)} %shard_map.141.refs_1_), custom_call_target="tpu_custom_call" | custom-call | bytes 3145728 | tf_op jit(solution)/shard_map/pallas_call | solution.py:162
  16.8 1.6 %collective-permute-start.5 = (bf16[4,12416]{1,0:T(4,128)(2,1)S(1)}, bf16[4,12416]{1,0:T(4,128)(2,1)S(1)}, u32[]{:S(2)}, u32[]{:S(2)}) collective-permute-start(bf16[4,12416]{1,0:T(4,128)(2,1)S(1)} %collective-permute-done.2.refs_2_), channel_id=1, source_target_pairs={{0,2},{1,5},{2,0},{3,7},{4,6},{5,1},{6,4},{7,3},{8,10},{9,13},{10,... | collective-permute-start | bytes 297992 | tf_op jit(solution)/shard_map/ppermute | solution.py:369
  18.4 0.1 collective-permute-done.3.block
  18.5 1.5 %collective-permute-start.6 = (bf16[4,12416]{1,0:T(4,128)(2,1)S(1)}, bf16[4,12416]{1,0:T(4,128)(2,1)S(1)}, u32[]{:S(2)}, u32[]{:S(2)}) collective-permute-start(bf16[4,12416]{1,0:T(4,128)(2,1)S(1)} %shard_map.143), channel_id=1, source_target_pairs={{0,4},{1,3},{2,6},{3,1},{4,0},{5,7},{6,2},{7,5},{8,12},{9,11},{10,... | collective-permute-start | bytes 297992 | tf_op jit(solution)/shard_map/ppermute | solution.py:369
  20.1 0.2 pad_maximum_fusion.refs_0_
  20.3 0.1 collective-permute-start.7
  20.4 1.2 %collective-permute-done.5 = bf16[4,12416]{1,0:T(4,128)(2,1)S(1)} collective-permute-done((bf16[4,12416]{1,0:T(4,128)(2,1)S(1)}, bf16[4,12416]{1,0:T(4,128)(2,1)S(1)}, u32[]{:S(2)}, u32[]{:S(2)}) %collective-permute-start.5) | collective-permute-done | bytes 99360 | tf_op jit(solution)/shard_map/ppermute | solution.py:369
  21.5 0.0 collective-permute-done.4
  21.5 1.7 %collective-permute-done.6 = bf16[4,12416]{1,0:T(4,128)(2,1)S(1)} collective-permute-done((bf16[4,12416]{1,0:T(4,128)(2,1)S(1)}, bf16[4,12416]{1,0:T(4,128)(2,1)S(1)}, u32[]{:S(2)}, u32[]{:S(2)}) %collective-permute-start.6) | collective-permute-done | bytes 99360 | tf_op jit(solution)/shard_map/ppermute | solution.py:369
  23.2 0.2 pad_maximum_fusion.1.refs_1_.after
  23.5 0.1 collective-permute-start.8
  23.5 0.0 collective-permute-done.7.refs_2_
  23.5 1.7 %collective-permute-done.8.refs_3_ = bf16[16,12416]{1,0:T(8,128)(2,1)S(1)} collective-permute-done((bf16[16,12416]{1,0:T(8,128)(2,1)S(1)}, bf16[16,12416]{1,0:T(8,128)(2,1)S(1)}, u32[]{:S(2)}, u32[]{:S(2)}) %collective-permute-start.8) | collective-permute-done | bytes 397344 | tf_op jit(solution)/shard_map/ppermute | solution.py:369
  25.2 10.8 %shard_map.144 = (bf16[32,6272]{1,0:T(8,128)(2,1)S(1)}, f32[32,6272]{1,0:T(8,128)S(1)}, bf16[512,64]{1,0:T(8,128)(2,1)S(1)}, bf16[64,1024]{1,0:T(8,128)(2,1)S(1)...) custom-call(bf16[16,12416]{1,0:T(8,128)(2,1)S(1)} %pad_maximum_fusion.refs_0_, ...), custom_call_target="tpu_custom_call" | custom-call | flops 6442450944 | bytes 12582912 | tf_op jit(solution)/shard_map/pallas_call | solution.py:448
  36.1 0.2 collective-permute-start.9
  36.3 1.3 %shard_map.151 = (f32[1,16]{1,0:T(1,128)}, f32[1,16]{1,0:T(1,128)}, f32[8,16]{1,0:T(8,128)S(1)}, f32[8,16]{1,0:T(8,128)S(1)}) custom-call(f32[8,16]{1,0:T(8,128)} %bitcast.7, f32[8,16]{1,0:T(8,128)} %bitcast.8, s32[2,16]{1,0:T(2,128)} %bitcast.10, bf16[16,12416]{1,0:T(8,128)(2,1)S(1)} %pad_maximum_fusion.1.refs_1_.after), custom_call_target="tpu_custom_call" | custom-call | flops 1048576 | bytes 4194304 | tf_op jit(solution)/shard_map/pallas_call | solution.py:424
  37.6 0.3 collective-permute-done.9.got
  37.9 0.2 shard_map.148
  38.0 1.5 %collective-permute-start.10 = (bf16[16,6272]{1,0:T(8,128)(2,1)S(1)}, bf16[16,6272]{1,0:T(8,128)(2,1)S(1)}, u32[]{:S(2)}, u32[]{:S(2)}) collective-permute-start(bf16[16,6272]{1,0:T(8,128)(2,1)S(1)} %get-tuple-element.61), channel_id=1, source_target_pairs={{0,4},{1,3},{2,6},{3,1},{4,0},{5,7},{6,2},{7,5},{8,12},{9,11},{10,... | collective-permute-start | bytes 602120 | tf_op jit(solution)/shard_map/ppermute | solution.py:369
  39.6 4.4 %shard_map.145 = (bf16[512,6144]{1,0:T(8,128)(2,1)}, bf16[6144,512]{1,0:T(8,128)(2,1)}, bf16[6144,512]{1,0:T(8,128)(2,1)}, bf16[256,512]{1,0:T(8,128)(2,1)S(1)}, bf16[256,512]{1,0:T(8,128)(2,1)S(1)}) custom-call(bf16[512,64]{1,0:T(8,128)(2,1)S(1)} %get-tuple-element.45.weighted_t, bf16[64,6144]{1,0:T(8,128)(2,1)S(1)} %get-tuple-element.46.y, ...), custom_call_target="tpu_custom_call" | custom-call | flops 2684354560 | bytes 10485760 | tf_op jit(solution)/shard_map/pallas_call | solution.py:346
  43.9 0.0 collective-permute-done.10.got
  43.9 0.1 shard_map.149
  44.1 0.5 collective-permute-start.11
  44.6 2.2 %shard_map.146 = (bf16[6144,512]{1,0:T(8,128)(2,1)}, bf16[6144,512]{1,0:T(8,128)(2,1)}, bf16[256,512]{1,0:T(8,128)(2,1)S(1)}, bf16[256,512]{1,0:T(8,128)(2,1)S(1)}) custom-call(bf16[6144,64]{1,0:T(8,128)(2,1)S(1)} %get-tuple-element.43.x_t, bf16[64,1024]{1,0:T(8,128)(2,1)S(1)} %get-tuple-element.44.d_both, ...), custom_call_target="tpu_custom_call", output_to_operand_aliasing={{0}: (4, {}), {1}: (5, {})} | custom-call | flops 1073741824 | bytes 4194304 | tf_op jit(solution)/shard_map/pallas_call | solution.py:346
  46.8 2.0 %collective-permute-done.11.got = bf16[8,6272]{1,0:T(8,128)(2,1)S(1)} collective-permute-done((bf16[8,6272]{1,0:T(8,128)(2,1)S(1)}, bf16[8,6272]{1,0:T(8,128)(2,1)S(1)}, u32[]{:S(2)}, u32[]{:S(2)}) %collective-permute-start.11) | collective-permute-done | bytes 100384 | tf_op jit(solution)/shard_map/ppermute | solution.py:369
  48.8 0.2 shard_map.150
  48.9 1.1 %collective-permute-start.12 = (bf16[4,6272]{1,0:T(4,128)(2,1)S(1)}, bf16[4,6272]{1,0:T(4,128)(2,1)S(1)}, u32[]{:S(2)}, u32[]{:S(2)}) collective-permute-start(bf16[4,6272]{1,0:T(4,128)(2,1)S(1)} %get-tuple-element.65), channel_id=1, source_target_pairs={{0,8},{1,9},{2,10},{3,11},{4,12},{5,13},{6,14},{7,15},{8,0},{9,1},... | collective-permute-start | bytes 150536 | tf_op jit(solution)/shard_map/ppermute | solution.py:369
  50.1 2.3 %shard_map.147 = (bf16[6144,512]{1,0:T(8,128)(2,1)}, bf16[6144,512]{1,0:T(8,128)(2,1)}) custom-call(bf16[6144,64]{1,0:T(8,128)(2,1)S(1)} %get-tuple-element.43.x_t, bf16[64,1024]{1,0:T(8,128)(2,1)S(1)} %get-tuple-element.44.d_both, bf16[256,512]{1,0:T(8,128)(2,1)S(1)} %get-tuple-element.51.refs_0_, ...), custom_call_target="tpu_custom_call", output_to_operand_aliasing={{0}: (4, {}), {1}: (5, {})} | custom-call | flops 1073741824 | bytes 4194304 | tf_op jit(solution)/shard_map/pallas_call | solution.py:346
  52.4 1.5 %collective-permute-done.12.got = bf16[4,6272]{1,0:T(4,128)(2,1)S(1)} collective-permute-done((bf16[4,6272]{1,0:T(4,128)(2,1)S(1)}, bf16[4,6272]{1,0:T(4,128)(2,1)S(1)}, u32[]{:S(2)}, u32[]{:S(2)}) %collective-permute-start.12) | collective-permute-done | bytes 50208 | tf_op jit(solution)/shard_map/ppermute | solution.py:369
  53.9 0.9 %shard_map.152 = (bf16[16,6144]{1,0:T(8,128)(2,1)}, f32[8,16]{1,0:T(8,128)}) custom-call(f32[4,6272]{1,0:T(4,128)S(1)} %get-tuple-element.64.have, bf16[4,6272]{1,0:T(4,128)(2,1)S(1)} %collective-permute-done.12.got, f32[16,16]{1,0:T(8,128)S(1)} %get-tuple-element.66.select, f32[8,16]{1,0:T(8,128)S(1)} %get-tuple-element.67.base, ...), custom_call_target="tpu_custom_call" | custom-call | flops 1048576 | bytes 262144 | tf_op jit(solution)/shard_map/pallas_call | solution.py:25
  (6 shorter events, 0.1 us)
Async XLA Ops:
  1.8 11.9 %collective-permute-start = (bf16[4,12416]{1,0:T(4,128)(2,1)S(1)}, bf16[4,12416]{1,0:T(4,128)(2,1)S(1)}, u32[]{:S(2)}, u32[]{:S(2)}) collective-permute-start(bf16[4,12416]{1,0:T(4,128)(2,1)S(1)} %get-tuple-element.40.refs_2_), channel_id=1, source_target_pairs={{0,8},{1,9},{2,10},{3,11},{4,12},{5,13},{6,14},{7,15},{8,0},{9,1},... | collective-permute-start | bytes 297992 | tf_op jit(solution)/shard_map/ppermute | solution.py:369
  5.9 7.8 %collective-permute-start.2 = (bf16[4,12416]{1,0:T(4,128)(2,1)S(1)}, bf16[4,12416]{1,0:T(4,128)(2,1)S(1)}, u32[]{:S(2)}, u32[]{:S(2)}) collective-permute-start(bf16[4,12416]{1,0:T(4,128)(2,1)S(1)} %get-tuple-element.40.refs_2_), channel_id=1, source_target_pairs={{0,4},{1,3},{2,6},{3,1},{4,0},{5,7},{6,2},{7,5},{8,12},{9,11},{10,... | collective-permute-start | bytes 297992 | tf_op jit(solution)/shard_map/ppermute | solution.py:369
  7.5 6.3 %collective-permute-start.1 = (bf16[4,12416]{1,0:T(4,128)(2,1)S(1)}, bf16[4,12416]{1,0:T(4,128)(2,1)S(1)}, u32[]{:S(2)}, u32[]{:S(2)}) collective-permute-start(bf16[4,12416]{1,0:T(4,128)(2,1)S(1)} %get-tuple-element.40.refs_2_), channel_id=1, source_target_pairs={{0,2},{1,5},{2,0},{3,7},{4,6},{5,1},{6,4},{7,3},{8,10},{9,13},{10,... | collective-permute-start | bytes 297992 | tf_op jit(solution)/shard_map/ppermute | solution.py:369
  13.8 4.7 %collective-permute-start.3 = (bf16[4,12416]{1,0:T(4,128)(2,1)S(1)}, bf16[4,12416]{1,0:T(4,128)(2,1)S(1)}, u32[]{:S(2)}, u32[]{:S(2)}) collective-permute-start(bf16[4,12416]{1,0:T(4,128)(2,1)S(1)} %shard_map.139.block), channel_id=1, source_target_pairs={{0,2},{1,5},{2,0},{3,7},{4,6},{5,1},{6,4},{7,3},{8,10},{9,13},{10,... | collective-permute-start | bytes 297992 | tf_op jit(solution)/shard_map/ppermute | solution.py:369
  14.4 7.1 %collective-permute-start.4 = (bf16[4,12416]{1,0:T(4,128)(2,1)S(1)}, bf16[4,12416]{1,0:T(4,128)(2,1)S(1)}, u32[]{:S(2)}, u32[]{:S(2)}) collective-permute-start(bf16[4,12416]{1,0:T(4,128)(2,1)S(1)} %shard_map.140.block), channel_id=1, source_target_pairs={{0,4},{1,3},{2,6},{3,1},{4,0},{5,7},{6,2},{7,5},{8,12},{9,11},{10,... | collective-permute-start | bytes 297992 | tf_op jit(solution)/shard_map/ppermute | solution.py:369
  16.8 4.7 %collective-permute-start.5 = (bf16[4,12416]{1,0:T(4,128)(2,1)S(1)}, bf16[4,12416]{1,0:T(4,128)(2,1)S(1)}, u32[]{:S(2)}, u32[]{:S(2)}) collective-permute-start(bf16[4,12416]{1,0:T(4,128)(2,1)S(1)} %collective-permute-done.2.refs_2_), channel_id=1, source_target_pairs={{0,2},{1,5},{2,0},{3,7},{4,6},{5,1},{6,4},{7,3},{8,10},{9,13},{10,... | collective-permute-start | bytes 297992 | tf_op jit(solution)/shard_map/ppermute | solution.py:369
  18.5 4.7 %collective-permute-start.6 = (bf16[4,12416]{1,0:T(4,128)(2,1)S(1)}, bf16[4,12416]{1,0:T(4,128)(2,1)S(1)}, u32[]{:S(2)}, u32[]{:S(2)}) collective-permute-start(bf16[4,12416]{1,0:T(4,128)(2,1)S(1)} %shard_map.143), channel_id=1, source_target_pairs={{0,4},{1,3},{2,6},{3,1},{4,0},{5,7},{6,2},{7,5},{8,12},{9,11},{10,... | collective-permute-start | bytes 297992 | tf_op jit(solution)/shard_map/ppermute | solution.py:369
  20.3 3.2 %collective-permute-start.7 = (bf16[16,12416]{1,0:T(8,128)(2,1)S(1)}, bf16[16,12416]{1,0:T(8,128)(2,1)S(1)}, u32[]{:S(2)}, u32[]{:S(2)}) collective-permute-start(bf16[16,12416]{1,0:T(8,128)(2,1)S(1)} %pad_maximum_fusion.refs_0_), channel_id=1, source_target_pairs={{0,1},{1,0},{2,3},{3,2},{4,5},{5,4},{6,7},{7,6},{8,9},{9,8},{10,11... | collective-permute-start | bytes 1191944 | tf_op jit(solution)/shard_map/ppermute | solution.py:369
  23.5 1.8 %collective-permute-start.8 = (bf16[16,12416]{1,0:T(8,128)(2,1)S(1)}, bf16[16,12416]{1,0:T(8,128)(2,1)S(1)}, u32[]{:S(2)}, u32[]{:S(2)}) collective-permute-start(bf16[16,12416]{1,0:T(8,128)(2,1)S(1)} %pad_maximum_fusion.1.refs_1_.after), channel_id=1, source_target_pairs={{0,1},{1,0},{2,3},{3,2},{4,5},{5,4},{6,7},{7,6},{8,9},{9,8},{10,11... | collective-permute-start | bytes 1191944 | tf_op jit(solution)/shard_map/ppermute | solution.py:369
  36.1 1.8 %collective-permute-start.9 = (bf16[32,6272]{1,0:T(8,128)(2,1)S(1)}, bf16[32,6272]{1,0:T(8,128)(2,1)S(1)}, u32[]{:S(2)}, u32[]{:S(2)}) collective-permute-start(bf16[32,6272]{1,0:T(8,128)(2,1)S(1)} %get-tuple-element.59), channel_id=1, source_target_pairs={{0,1},{1,0},{2,3},{3,2},{4,5},{5,4},{6,7},{7,6},{8,9},{9,8},{10,11... | collective-permute-start | bytes 1204232 | tf_op jit(solution)/shard_map/ppermute | solution.py:369
  38.0 5.9 %collective-permute-start.10 = (bf16[16,6272]{1,0:T(8,128)(2,1)S(1)}, bf16[16,6272]{1,0:T(8,128)(2,1)S(1)}, u32[]{:S(2)}, u32[]{:S(2)}) collective-permute-start(bf16[16,6272]{1,0:T(8,128)(2,1)S(1)} %get-tuple-element.61), channel_id=1, source_target_pairs={{0,4},{1,3},{2,6},{3,1},{4,0},{5,7},{6,2},{7,5},{8,12},{9,11},{10,... | collective-permute-start | bytes 602120 | tf_op jit(solution)/shard_map/ppermute | solution.py:369
  44.1 4.7 %collective-permute-start.11 = (bf16[8,6272]{1,0:T(8,128)(2,1)S(1)}, bf16[8,6272]{1,0:T(8,128)(2,1)S(1)}, u32[]{:S(2)}, u32[]{:S(2)}) collective-permute-start(bf16[8,6272]{1,0:T(8,128)(2,1)S(1)} %get-tuple-element.63), channel_id=1, source_target_pairs={{0,2},{1,5},{2,0},{3,7},{4,6},{5,1},{6,4},{7,3},{8,10},{9,13},{10,... | collective-permute-start | bytes 301064 | tf_op jit(solution)/shard_map/ppermute | solution.py:369
  48.9 5.0 %collective-permute-start.12 = (bf16[4,6272]{1,0:T(4,128)(2,1)S(1)}, bf16[4,6272]{1,0:T(4,128)(2,1)S(1)}, u32[]{:S(2)}, u32[]{:S(2)}) collective-permute-start(bf16[4,6272]{1,0:T(4,128)(2,1)S(1)} %get-tuple-element.65), channel_id=1, source_target_pairs={{0,8},{1,9},{2,10},{3,11},{4,12},{5,13},{6,14},{7,15},{8,0},{9,1},... | collective-permute-start | bytes 150536 | tf_op jit(solution)/shard_map/ppermute | solution.py:369

commit v18 on v16

--- a/solution.py
+++ b/solution.py
@@ -233,27 +233,46 @@
             x_t[c : c + LANES, :] = x[:, c : c + LANES].astype(F32).T.astype(BF16)
 
 
-def fold_kernel(have, got, keep, send):
-    half = keep.shape[0]
-    width = keep.shape[1] - LANES
-    total = have[:, :width] + got[:, :width].astype(F32)
-    keep[:, :width] = total[:half]
-    send[:, :width] = total[half:].astype(BF16)
-    tail = have[:, width:] + got[:, width:].astype(F32)
-    value = tail[:, 0:1] + tail[:, 1:2]
-    keep[:, width:] = lane_pair(half, value[:half], 0.0)
-    send[:, width:] = split_pair(value[half:]).astype(BF16)
-
-
-def home_kernel(have, got, select, base, coef, grad_tokens, grad_logits):
+def folded(have, gots):
+    width = have.shape[1] - LANES
+    total, tail = have[:, :width], have[:, width:]
+    for got in gots:
+        total += got[:, :width].astype(F32)
+        tail += got[:, width:].astype(F32)
+    return total, tail[:, 0:1] + tail[:, 1:2]
+
+
+def put_keep(out, total, value):
+    width = total.shape[1]
+    out[:, :width] = total
+    out[:, width:] = lane_pair(total.shape[0], value, 0.0)
+
+
+def put_send(out, total, value):
+    width = total.shape[1]
+    out[:, :width] = total.astype(BF16)
+    out[:, width:] = split_pair(value).astype(BF16)
+
+
+def fold_kernel(have, *refs):
+    keep = next(i for i, ref in enumerate(refs) if ref.dtype == F32)
+    gots, keep, sends = refs[:keep], refs[keep], refs[keep + 1 :]
+    rows = keep.shape[0]
+    total, value = folded(have, gots)
+    put_keep(keep, total[:rows], value[:rows])
+    for i, send in enumerate(sends):
+        part = slice((i + 1) * rows, (i + 2) * rows)
+        put_send(send, total[part], value[part])
+
+
+def home_kernel(have, *refs):
+    gots, (select, base, coef, grad_tokens, grad_logits) = refs[:-5], refs[-5:]
     slots = have.shape[0]
-    width = have.shape[1] - LANES
     count = select.shape[0]
-    total = (have[:, :width] + got[:, :width].astype(F32)).astype(BF16)
-    padded = jnp.concatenate([total, jnp.zeros((count - slots, width), BF16)], axis=0)
+    total, value = folded(have, gots)
+    total = total.astype(BF16)
+    padded = jnp.concatenate([total, jnp.zeros((count - slots, total.shape[1]), BF16)], axis=0)
     grad_tokens[...] = dot(select[...].astype(BF16), padded, ((0,), (0,))).astype(BF16)
-    tail = have[:, width:] + got[:, width:].astype(F32)
-    value = tail[:, 0:1] + tail[:, 1:2]
     token_products = jnp.sum(select[0:slots, :] * value, axis=0, keepdims=True)
     grad_logits[...] = base[...] + coef[...] * token_products
 
@@ -464,20 +483,23 @@
             ),
         )(*pieces, in_hbm(down_weight), gate_w, up_w)
 
-        for bits in [(1, 1)] + levels[::-1]:
-            got = swap(low, bits)
-            if bits == levels[0]:
+        both = tuple(f ^ s for f, s in zip(first, second))
+        paths = [((1, 1),), (third,), (first, second, both)] + [(b,) for b in levels[:-3][::-1]]
+        sent = [low]
+        for path, following in zip(paths, paths[1:] + [()]):
+            gots = [swap(block, bits) for block, bits in zip(sent, path)]
+            if not following:
                 break
-            half //= 2
-            keep, low = call(
+            rows_kept = keep.shape[0] // (len(following) + 1)
+            keep, *sent = call(
                 fold_kernel,
-                [((half, wide), F32), ((half, wide), BF16)],
-                [keep, got],
-                4 * half * wide,
-                16 * half * wide,
+                [((rows_kept, wide), F32)] + [((rows_kept, wide), BF16)] * len(following),
+                [keep, *gots],
+                4 * keep.shape[0] * wide,
+                16 * keep.shape[0] * wide,
             )
 
-        cuts = [0, width // 3, 2 * width // 3, width]
+        cuts = [0, width // 3, width]
         grad_down, *pair = grads_of(x_t, d_both, 0, cuts[1], (), (weighted_t, y_all))
         for start, stop in zip(cuts[1:], cuts[2:]):
             pair = grads_of(x_t, d_both, start, stop - start, tuple(pair))
@@ -486,7 +508,7 @@
         grad_tokens, grad_logits = call(
             home_kernel,
             [((count, width), BF16), ((experts, count), F32)],
-            [keep, got, select, base, coef],
+            [keep, *gots, select, base, coef],
             1 << 20,
             1 << 18,
         )

time: 53.3 us -> 51.7 us (0.970)
  waiting for transfers between devices: 12 us -> 8.23 us
  starting transfers between devices: 13.6 us -> 16.6 us
  Pallas kernels: 26.3 us -> 25.4 us
    ppermute x13 -> x14, waiting for transfers between devices: 12 us -> 8.23 us  [swap(): return lax.ppermute(block, 'blk', [(i, i ^ bits[i % 2]) for i in range(n)])]
    ppermute x13 -> x14, starting transfers between devices: 13.6 us -> 16.6 us  [swap(): return lax.ppermute(block, 'blk', [(i, i ^ bits[i % 2]) for i in range(n)])]
    pallas_call x3 -> x2, Pallas kernels: 8.86 us -> 8.1 us  [grads_of(): pl.pallas_call(kernel, out_shape=outs, in_specs=whole(2 + len(down)) + (w...]
    pallas_call x4 -> x3, Pallas kernels: 1.38 us -> 1.24 us  [call(): pl.pallas_call(kernel, out_shape=[jax.ShapeDtypeStruct(s, t) for s, t in...]
  transfers between devices with their start and end apart: 13 -> 14, of which waited for: 8 -> 7; matrix products, arithmetic and copies ran while one was open for 1% -> 1% of each run, Pallas kernels for 28% -> 27%
where the time goes in v18:
time: 51.7 us; the launch traced here: 51.5 us
  Pallas kernels  25.4 us (49%)
  starting transfers between devices  16.6 us (32%)
  waiting for transfers between devices  8.23 us (16%)
  between operations  0.79 us (2%)
    ppermute x14, starting transfers between devices, swap(): return lax.ppermute(block, 'blk', [(i, i ^ bits[i % 2]) for i in range(n)])  16.6 us
    pallas_call x1, Pallas kernels, shards(): pl.pallas_call(expert_kernel, out_shape=[jax.ShapeDtypeStruct((half, wide...  8.8 us
    ppermute x14, waiting for transfers between devices, swap(): return lax.ppermute(block, 'blk', [(i, i ^ bits[i % 2]) for i in range(n)])  8.23 us
    pallas_call x2, Pallas kernels, grads_of(): pl.pallas_call(kernel, out_shape=outs, in_specs=whole(2 + len(down)) + (w...  8.1 us
    pallas_call x1, Pallas kernels, fetch(): pl.pallas_call(functools.partial(fetch_kernel, count), out_shape=[pltpu.V...  4.7 us
    pallas_call x1, Pallas kernels, shards(): pl.pallas_call(router_kernel, out_shape=[jax.ShapeDtypeStruct((1, count),...  1.3 us
    pallas_call x3, Pallas kernels, call(): pl.pallas_call(kernel, out_shape=[jax.ShapeDtypeStruct(s, t) for s, t in...  1.24 us
    pallas_call x1, Pallas kernels, shards(): pl.pallas_call(select_kernel, out_shape=[jax.ShapeDtypeStruct((slots, wid...  1.19 us
  transfers between devices with their start and end apart: 14, of which 7 were waited for; matrix products, arithmetic and copies ran while one was open for 1% of the time, Pallas kernels for 27%

profile of v18, /device:TPU:0, one launch (start us, length us, event | category | flops | bytes accessed | tf_op | source)
XLA Modules:
  0.0 51.5 jit_solution(18370105136752538094)
XLA Ops:
  0.6 1.2 %shard_map.135 = (bf16[4,12416]{1,0:T(4,128)(2,1)S(1)}, f32[16,16]{1,0:T(8,128)S(1)}) custom-call(f32[8,16]{1,0:T(8,128)} %bitcast.6, s32[2,16]{1,0:T(2,128)} %bitcast.9, bf16[16,6144]{1,0:T(8,128)(2,1)} %tokens_in.1, bf16[4,6144]{1,0:T(4,128)(2,1)} %y_in.1), custom_call_target="tpu_custom_call" | custom-call | flops 1048576 | bytes 4194304 | tf_op jit(solution)/shard_map/pallas_call | solution.py:400
  1.8 4.1 %collective-permute-start = (bf16[4,12416]{1,0:T(4,128)(2,1)S(1)}, bf16[4,12416]{1,0:T(4,128)(2,1)S(1)}, u32[]{:S(2)}, u32[]{:S(2)}) collective-permute-start(bf16[4,12416]{1,0:T(4,128)(2,1)S(1)} %get-tuple-element.36.refs_2_), channel_id=1, source_target_pairs={{0,8},{1,9},{2,10},{3,11},{4,12},{5,13},{6,14},{7,15},{8,0},{9,1},... | collective-permute-start | bytes 297992 | tf_op jit(solution)/shard_map/ppermute | solution.py:386
  5.9 1.5 %collective-permute-start.2 = (bf16[4,12416]{1,0:T(4,128)(2,1)S(1)}, bf16[4,12416]{1,0:T(4,128)(2,1)S(1)}, u32[]{:S(2)}, u32[]{:S(2)}) collective-permute-start(bf16[4,12416]{1,0:T(4,128)(2,1)S(1)} %get-tuple-element.36.refs_2_), channel_id=1, source_target_pairs={{0,2},{1,5},{2,0},{3,7},{4,6},{5,1},{6,4},{7,3},{8,10},{9,13},{10,... | collective-permute-start | bytes 297992 | tf_op jit(solution)/shard_map/ppermute | solution.py:386
  7.4 1.6 %collective-permute-start.1 = (bf16[4,12416]{1,0:T(4,128)(2,1)S(1)}, bf16[4,12416]{1,0:T(4,128)(2,1)S(1)}, u32[]{:S(2)}, u32[]{:S(2)}) collective-permute-start(bf16[4,12416]{1,0:T(4,128)(2,1)S(1)} %get-tuple-element.36.refs_2_), channel_id=1, source_target_pairs={{0,4},{1,3},{2,6},{3,1},{4,0},{5,7},{6,2},{7,5},{8,12},{9,11},{10,... | collective-permute-start | bytes 297992 | tf_op jit(solution)/shard_map/ppermute | solution.py:386
  9.0 4.7 %shard_map.138 = (bf16[6144,512]{1,0:T(8,128)(2,1)S(1)}, bf16[6144,512]{1,0:T(8,128)(2,1)S(1)}) custom-call(bf16[6144,512]{1,0:T(8,128)(2,1)} %refs_0_.1, bf16[6144,512]{1,0:T(8,128)(2,1)} %refs_1_.1, bf16[4,12416]{1,0:T(4,128)(2,1)S(1)} %get-tuple-element.36.refs_2_), custom_call_target="tpu_custom_call" | custom-call | bytes 12582912 | tf_op jit(solution)/shard_map/pallas_call | solution.py:162
  13.7 0.0 collective-permute-done.block
  13.8 0.0 collective-permute-done.2.refs_2_
  13.8 0.0 collective-permute-done.1.refs_1_
  13.8 0.5 %collective-permute-start.3 = (bf16[4,12416]{1,0:T(4,128)(2,1)S(1)}, bf16[4,12416]{1,0:T(4,128)(2,1)S(1)}, u32[]{:S(2)}, u32[]{:S(2)}) collective-permute-start(bf16[4,12416]{1,0:T(4,128)(2,1)S(1)} %shard_map.139.block), channel_id=1, source_target_pairs={{0,4},{1,3},{2,6},{3,1},{4,0},{5,7},{6,2},{7,5},{8,12},{9,11},{10,... | collective-permute-start | bytes 297992 | tf_op jit(solution)/shard_map/ppermute | solution.py:386
  14.3 0.6 %collective-permute-start.4 = (bf16[4,12416]{1,0:T(4,128)(2,1)S(1)}, bf16[4,12416]{1,0:T(4,128)(2,1)S(1)}, u32[]{:S(2)}, u32[]{:S(2)}) collective-permute-start(bf16[4,12416]{1,0:T(4,128)(2,1)S(1)} %shard_map.140), channel_id=1, source_target_pairs={{0,2},{1,5},{2,0},{3,7},{4,6},{5,1},{6,4},{7,3},{8,10},{9,13},{10,... | collective-permute-start | bytes 297992 | tf_op jit(solution)/shard_map/ppermute | solution.py:386
  14.9 1.6 %collective-permute-start.5 = (bf16[4,12416]{1,0:T(4,128)(2,1)S(1)}, bf16[4,12416]{1,0:T(4,128)(2,1)S(1)}, u32[]{:S(2)}, u32[]{:S(2)}) collective-permute-start(bf16[4,12416]{1,0:T(4,128)(2,1)S(1)} %collective-permute-done.2.refs_2_), channel_id=1, source_target_pairs={{0,4},{1,3},{2,6},{3,1},{4,0},{5,7},{6,2},{7,5},{8,12},{9,11},{10,... | collective-permute-start | bytes 297992 | tf_op jit(solution)/shard_map/ppermute | solution.py:386
  16.5 2.0 %collective-permute-done.3.block = bf16[4,12416]{1,0:T(4,128)(2,1)S(1)} collective-permute-done((bf16[4,12416]{1,0:T(4,128)(2,1)S(1)}, bf16[4,12416]{1,0:T(4,128)(2,1)S(1)}, u32[]{:S(2)}, u32[]{:S(2)}) %collective-permute-start.3) | collective-permute-done | bytes 99360 | tf_op jit(solution)/shard_map/ppermute | solution.py:386
  18.5 1.0 %collective-permute-start.6 = (bf16[4,12416]{1,0:T(4,128)(2,1)S(1)}, bf16[4,12416]{1,0:T(4,128)(2,1)S(1)}, u32[]{:S(2)}, u32[]{:S(2)}) collective-permute-start(bf16[4,12416]{1,0:T(4,128)(2,1)S(1)} %shard_map.141), channel_id=1, source_target_pairs={{0,2},{1,5},{2,0},{3,7},{4,6},{5,1},{6,4},{7,3},{8,10},{9,13},{10,... | collective-permute-start | bytes 297992 | tf_op jit(solution)/shard_map/ppermute | solution.py:386
  19.5 0.2 pad_maximum_fusion.refs_0_
  19.7 0.1 collective-permute-start.7
  19.8 0.2 collective-permute-done.5
  20.1 0.0 collective-permute-done.4
  20.1 3.2 %collective-permute-done.6 = bf16[4,12416]{1,0:T(4,128)(2,1)S(1)} collective-permute-done((bf16[4,12416]{1,0:T(4,128)(2,1)S(1)}, bf16[4,12416]{1,0:T(4,128)(2,1)S(1)}, u32[]{:S(2)}, u32[]{:S(2)}) %collective-permute-start.6) | collective-permute-done | bytes 99360 | tf_op jit(solution)/shard_map/ppermute | solution.py:386
  23.2 0.2 pad_maximum_fusion.1.refs_1_.after
  23.5 0.1 collective-permute-start.8
  23.5 0.0 collective-permute-done.7.refs_2_
  23.5 1.7 %collective-permute-done.8.refs_3_ = bf16[16,12416]{1,0:T(8,128)(2,1)S(1)} collective-permute-done((bf16[16,12416]{1,0:T(8,128)(2,1)S(1)}, bf16[16,12416]{1,0:T(8,128)(2,1)S(1)}, u32[]{:S(2)}, u32[]{:S(2)}) %collective-permute-start.8) | collective-permute-done | bytes 397344 | tf_op jit(solution)/shard_map/ppermute | solution.py:386
  25.2 8.8 %shard_map.142 = (bf16[32,6272]{1,0:T(8,128)(2,1)S(1)}, f32[32,6272]{1,0:T(8,128)S(1)}, bf16[512,64]{1,0:T(8,128)(2,1)S(1)}, bf16[64,1024]{1,0:T(8,128)(2,1)S(1)...) custom-call(bf16[16,12416]{1,0:T(8,128)(2,1)S(1)} %pad_maximum_fusion.refs_0_, ...), custom_call_target="tpu_custom_call" | custom-call | flops 6442450944 | bytes 12582912 | tf_op jit(solution)/shard_map/pallas_call | solution.py:463
  34.0 0.2 collective-permute-start.9
  34.3 1.3 %shard_map.147 = (f32[1,16]{1,0:T(1,128)}, f32[1,16]{1,0:T(1,128)}, f32[8,16]{1,0:T(8,128)S(1)}, f32[8,16]{1,0:T(8,128)S(1)}) custom-call(f32[8,16]{1,0:T(8,128)} %bitcast.7, f32[8,16]{1,0:T(8,128)} %bitcast.8, s32[2,16]{1,0:T(2,128)} %bitcast.10, bf16[16,12416]{1,0:T(8,128)(2,1)S(1)} %pad_maximum_fusion.1.refs_1_.after), custom_call_target="tpu_custom_call" | custom-call | flops 1048576 | bytes 4194304 | tf_op jit(solution)/shard_map/pallas_call | solution.py:439
  35.6 0.3 collective-permute-done.9.refs_0_
  35.8 0.2 shard_map.145
  36.0 1.0 %collective-permute-start.10 = (bf16[16,6272]{1,0:T(8,128)(2,1)S(1)}, bf16[16,6272]{1,0:T(8,128)(2,1)S(1)}, u32[]{:S(2)}, u32[]{:S(2)}) collective-permute-start(bf16[16,6272]{1,0:T(8,128)(2,1)S(1)} %get-tuple-element.53), channel_id=1, source_target_pairs={{0,2},{1,5},{2,0},{3,7},{4,6},{5,1},{6,4},{7,3},{8,10},{9,13},{10,... | collective-permute-start | bytes 602120 | tf_op jit(solution)/shard_map/ppermute | solution.py:386
  37.0 4.3 %shard_map.143 = (bf16[512,6144]{1,0:T(8,128)(2,1)}, bf16[6144,512]{1,0:T(8,128)(2,1)}, bf16[6144,512]{1,0:T(8,128)(2,1)}, bf16[256,512]{1,0:T(8,128)(2,1)S(1)}, bf16[256,512]{1,0:T(8,128)(2,1)S(1)}) custom-call(bf16[512,64]{1,0:T(8,128)(2,1)S(1)} %get-tuple-element.41.weighted_t, bf16[64,6144]{1,0:T(8,128)(2,1)S(1)} %get-tuple-element.42.y, ...), custom_call_target="tpu_custom_call" | custom-call | flops 2684354560 | bytes 10485760 | tf_op jit(solution)/shard_map/pallas_call | solution.py:363
  41.4 0.4 collective-permute-done.10.refs_0_
  41.8 0.2 shard_map.146
  42.0 1.0 %collective-permute-start.11 = (bf16[4,6272]{1,0:T(4,128)(2,1)S(1)}, bf16[4,6272]{1,0:T(4,128)(2,1)S(1)}, u32[]{:S(2)}, u32[]{:S(2)}) collective-permute-start(bf16[4,6272]{1,0:T(4,128)(2,1)S(1)} %get-tuple-element.55), channel_id=1, source_target_pairs={{0,8},{1,9},{2,10},{3,11},{4,12},{5,13},{6,14},{7,15},{8,0},{9,1},... | collective-permute-start | bytes 150536 | tf_op jit(solution)/shard_map/ppermute | solution.py:386
  42.9 1.7 %collective-permute-start.12 = (bf16[4,6272]{1,0:T(4,128)(2,1)S(1)}, bf16[4,6272]{1,0:T(4,128)(2,1)S(1)}, u32[]{:S(2)}, u32[]{:S(2)}) collective-permute-start(bf16[4,6272]{1,0:T(4,128)(2,1)S(1)} %get-tuple-element.56), channel_id=1, source_target_pairs={{0,4},{1,3},{2,6},{3,1},{4,0},{5,7},{6,2},{7,5},{8,12},{9,11},{10,... | collective-permute-start | bytes 150536 | tf_op jit(solution)/shard_map/ppermute | solution.py:386
  44.7 1.7 %collective-permute-start.13 = (bf16[4,6272]{1,0:T(4,128)(2,1)S(1)}, bf16[4,6272]{1,0:T(4,128)(2,1)S(1)}, u32[]{:S(2)}, u32[]{:S(2)}) collective-permute-start(bf16[4,6272]{1,0:T(4,128)(2,1)S(1)} %get-tuple-element.57), channel_id=1, source_target_pairs={{0,12},{1,11},{2,14},{3,9},{4,8},{5,15},{6,10},{7,13},{8,4},{9,3},... | collective-permute-start | bytes 150536 | tf_op jit(solution)/shard_map/ppermute | solution.py:386
  46.4 3.8 %shard_map.144 = (bf16[6144,512]{1,0:T(8,128)(2,1)}, bf16[6144,512]{1,0:T(8,128)(2,1)}) custom-call(bf16[6144,64]{1,0:T(8,128)(2,1)S(1)} %get-tuple-element.39.x_t, bf16[64,1024]{1,0:T(8,128)(2,1)S(1)} %get-tuple-element.40.d_both, bf16[256,512]{1,0:T(8,128)(2,1)S(1)} %get-tuple-element.43.refs_0_, ...), custom_call_target="tpu_custom_call", output_to_operand_aliasing={{0}: (4, {}), {1}: (5, {})} | custom-call | flops 2147483648 | bytes 8388608 | tf_op jit(solution)/shard_map/pallas_call | solution.py:363
  50.2 0.0 collective-permute-done.11.refs_0_
  50.2 0.0 collective-permute-done.12.refs_1_
  50.2 0.4 collective-permute-done.13.refs_2_
  50.6 0.9 %shard_map.148 = (bf16[16,6144]{1,0:T(8,128)(2,1)}, f32[8,16]{1,0:T(8,128)}) custom-call(f32[4,6272]{1,0:T(4,128)S(1)} %get-tuple-element.54.have, bf16[4,6272]{1,0:T(4,128)(2,1)S(1)} %collective-permute-done.11.refs_0_, bf16[4,6272]{1,0:T(4,128)(2,1)S(1)} %collective-permute-done.12.refs_1_, bf16[4,6272]{1,0:T(4,128)(2,1)S(1)} %collective-permute-done.13.refs_2_, ...), custom_call_target="tpu_custom_call" | custom-call | flops 1048576 | bytes 262144 | tf_op jit(solution)/shard_map/pallas_call | solution.py:25
  (5 shorter events, 0.0 us)
Async XLA Ops:
  1.8 11.9 %collective-permute-start = (bf16[4,12416]{1,0:T(4,128)(2,1)S(1)}, bf16[4,12416]{1,0:T(4,128)(2,1)S(1)}, u32[]{:S(2)}, u32[]{:S(2)}) collective-permute-start(bf16[4,12416]{1,0:T(4,128)(2,1)S(1)} %get-tuple-element.36.refs_2_), channel_id=1, source_target_pairs={{0,8},{1,9},{2,10},{3,11},{4,12},{5,13},{6,14},{7,15},{8,0},{9,1},... | collective-permute-start | bytes 297992 | tf_op jit(solution)/shard_map/ppermute | solution.py:386
  5.9 7.8 %collective-permute-start.2 = (bf16[4,12416]{1,0:T(4,128)(2,1)S(1)}, bf16[4,12416]{1,0:T(4,128)(2,1)S(1)}, u32[]{:S(2)}, u32[]{:S(2)}) collective-permute-start(bf16[4,12416]{1,0:T(4,128)(2,1)S(1)} %get-tuple-element.36.refs_2_), channel_id=1, source_target_pairs={{0,2},{1,5},{2,0},{3,7},{4,6},{5,1},{6,4},{7,3},{8,10},{9,13},{10,... | collective-permute-start | bytes 297992 | tf_op jit(solution)/shard_map/ppermute | solution.py:386
  7.4 6.3 %collective-permute-start.1 = (bf16[4,12416]{1,0:T(4,128)(2,1)S(1)}, bf16[4,12416]{1,0:T(4,128)(2,1)S(1)}, u32[]{:S(2)}, u32[]{:S(2)}) collective-permute-start(bf16[4,12416]{1,0:T(4,128)(2,1)S(1)} %get-tuple-element.36.refs_2_), channel_id=1, source_target_pairs={{0,4},{1,3},{2,6},{3,1},{4,0},{5,7},{6,2},{7,5},{8,12},{9,11},{10,... | collective-permute-start | bytes 297992 | tf_op jit(solution)/shard_map/ppermute | solution.py:386
  13.8 4.7 %collective-permute-start.3 = (bf16[4,12416]{1,0:T(4,128)(2,1)S(1)}, bf16[4,12416]{1,0:T(4,128)(2,1)S(1)}, u32[]{:S(2)}, u32[]{:S(2)}) collective-permute-start(bf16[4,12416]{1,0:T(4,128)(2,1)S(1)} %shard_map.139.block), channel_id=1, source_target_pairs={{0,4},{1,3},{2,6},{3,1},{4,0},{5,7},{6,2},{7,5},{8,12},{9,11},{10,... | collective-permute-start | bytes 297992 | tf_op jit(solution)/shard_map/ppermute | solution.py:386
  14.3 5.7 %collective-permute-start.4 = (bf16[4,12416]{1,0:T(4,128)(2,1)S(1)}, bf16[4,12416]{1,0:T(4,128)(2,1)S(1)}, u32[]{:S(2)}, u32[]{:S(2)}) collective-permute-start(bf16[4,12416]{1,0:T(4,128)(2,1)S(1)} %shard_map.140), channel_id=1, source_target_pairs={{0,2},{1,5},{2,0},{3,7},{4,6},{5,1},{6,4},{7,3},{8,10},{9,13},{10,... | collective-permute-start | bytes 297992 | tf_op jit(solution)/shard_map/ppermute | solution.py:386
  14.9 5.1 %collective-permute-start.5 = (bf16[4,12416]{1,0:T(4,128)(2,1)S(1)}, bf16[4,12416]{1,0:T(4,128)(2,1)S(1)}, u32[]{:S(2)}, u32[]{:S(2)}) collective-permute-start(bf16[4,12416]{1,0:T(4,128)(2,1)S(1)} %collective-permute-done.2.refs_2_), channel_id=1, source_target_pairs={{0,4},{1,3},{2,6},{3,1},{4,0},{5,7},{6,2},{7,5},{8,12},{9,11},{10,... | collective-permute-start | bytes 297992 | tf_op jit(solution)/shard_map/ppermute | solution.py:386
  18.5 4.7 %collective-permute-start.6 = (bf16[4,12416]{1,0:T(4,128)(2,1)S(1)}, bf16[4,12416]{1,0:T(4,128)(2,1)S(1)}, u32[]{:S(2)}, u32[]{:S(2)}) collective-permute-start(bf16[4,12416]{1,0:T(4,128)(2,1)S(1)} %shard_map.141), channel_id=1, source_target_pairs={{0,2},{1,5},{2,0},{3,7},{4,6},{5,1},{6,4},{7,3},{8,10},{9,13},{10,... | collective-permute-start | bytes 297992 | tf_op jit(solution)/shard_map/ppermute | solution.py:386
  19.7 3.8 %collective-permute-start.7 = (bf16[16,12416]{1,0:T(8,128)(2,1)S(1)}, bf16[16,12416]{1,0:T(8,128)(2,1)S(1)}, u32[]{:S(2)}, u32[]{:S(2)}) collective-permute-start(bf16[16,12416]{1,0:T(8,128)(2,1)S(1)} %pad_maximum_fusion.refs_0_), channel_id=1, source_target_pairs={{0,1},{1,0},{2,3},{3,2},{4,5},{5,4},{6,7},{7,6},{8,9},{9,8},{10,11... | collective-permute-start | bytes 1191944 | tf_op jit(solution)/shard_map/ppermute | solution.py:386
  23.5 1.8 %collective-permute-start.8 = (bf16[16,12416]{1,0:T(8,128)(2,1)S(1)}, bf16[16,12416]{1,0:T(8,128)(2,1)S(1)}, u32[]{:S(2)}, u32[]{:S(2)}) collective-permute-start(bf16[16,12416]{1,0:T(8,128)(2,1)S(1)} %pad_maximum_fusion.1.refs_1_.after), channel_id=1, source_target_pairs={{0,1},{1,0},{2,3},{3,2},{4,5},{5,4},{6,7},{7,6},{8,9},{9,8},{10,11... | collective-permute-start | bytes 1191944 | tf_op jit(solution)/shard_map/ppermute | solution.py:386
  34.0 1.8 %collective-permute-start.9 = (bf16[32,6272]{1,0:T(8,128)(2,1)S(1)}, bf16[32,6272]{1,0:T(8,128)(2,1)S(1)}, u32[]{:S(2)}, u32[]{:S(2)}) collective-permute-start(bf16[32,6272]{1,0:T(8,128)(2,1)S(1)} %get-tuple-element.51), channel_id=1, source_target_pairs={{0,1},{1,0},{2,3},{3,2},{4,5},{5,4},{6,7},{7,6},{8,9},{9,8},{10,11... | collective-permute-start | bytes 1204232 | tf_op jit(solution)/shard_map/ppermute | solution.py:386
  36.0 5.8 %collective-permute-start.10 = (bf16[16,6272]{1,0:T(8,128)(2,1)S(1)}, bf16[16,6272]{1,0:T(8,128)(2,1)S(1)}, u32[]{:S(2)}, u32[]{:S(2)}) collective-permute-start(bf16[16,6272]{1,0:T(8,128)(2,1)S(1)} %get-tuple-element.53), channel_id=1, source_target_pairs={{0,2},{1,5},{2,0},{3,7},{4,6},{5,1},{6,4},{7,3},{8,10},{9,13},{10,... | collective-permute-start | bytes 602120 | tf_op jit(solution)/shard_map/ppermute | solution.py:386
  42.0 8.2 %collective-permute-start.11 = (bf16[4,6272]{1,0:T(4,128)(2,1)S(1)}, bf16[4,6272]{1,0:T(4,128)(2,1)S(1)}, u32[]{:S(2)}, u32[]{:S(2)}) collective-permute-start(bf16[4,6272]{1,0:T(4,128)(2,1)S(1)} %get-tuple-element.55), channel_id=1, source_target_pairs={{0,8},{1,9},{2,10},{3,11},{4,12},{5,13},{6,14},{7,15},{8,0},{9,1},... | collective-permute-start | bytes 150536 | tf_op jit(solution)/shard_map/ppermute | solution.py:386
  42.9 7.2 %collective-permute-start.12 = (bf16[4,6272]{1,0:T(4,128)(2,1)S(1)}, bf16[4,6272]{1,0:T(4,128)(2,1)S(1)}, u32[]{:S(2)}, u32[]{:S(2)}) collective-permute-start(bf16[4,6272]{1,0:T(4,128)(2,1)S(1)} %get-tuple-element.56), channel_id=1, source_target_pairs={{0,4},{1,3},{2,6},{3,1},{4,0},{5,7},{6,2},{7,5},{8,12},{9,11},{10,... | collective-permute-start | bytes 150536 | tf_op jit(solution)/shard_map/ppermute | solution.py:386
  44.7 5.9 %collective-permute-start.13 = (bf16[4,6272]{1,0:T(4,128)(2,1)S(1)}, bf16[4,6272]{1,0:T(4,128)(2,1)S(1)}, u32[]{:S(2)}, u32[]{:S(2)}) collective-permute-start(bf16[4,6272]{1,0:T(4,128)(2,1)S(1)} %get-tuple-element.57), channel_id=1, source_target_pairs={{0,12},{1,11},{2,14},{3,9},{4,8},{5,15},{6,10},{7,13},{8,4},{9,3},... | collective-permute-start | bytes 150536 | tf_op jit(solution)/shard_map/ppermute | solution.py:386

commit v19 on v18

--- a/solution.py
+++ b/solution.py
@@ -422,15 +422,16 @@
         for bits in levels[:-3]:
             own = jnp.concatenate([own, swap(own, bits)])
         first, second, third = levels[-3:]
+        across = tuple(s ^ t for s, t in zip(second, third))
         block_1 = relay(relay(swap(own, first)))
         block_2 = swap(own, second)
         block_3 = swap(own, third)
         gate_w, up_w = fetch([gate_weight, up_weight], [width, width], own)
         block_1 = relay(block_1, gate_w, block_2, block_3)
-        block_12 = swap(block_1, second)
-        block_13 = swap(relay(block_1), third)
+        block_123 = relay(relay(swap(block_1, across)))
+        block_12 = relay(swap(block_1, second))
+        block_13 = swap(block_1, third)
         block_23 = swap(block_3, second)
-        block_123 = swap(relay(block_12), third)
         low_half = jnp.concatenate([own, block_1, block_2, block_12])
         high_half = jnp.concatenate([block_3, block_13, block_23, block_123])
         pieces = [low_half, high_half]
@@ -499,7 +500,7 @@
                 16 * keep.shape[0] * wide,
             )
 
-        cuts = [0, width // 3, width]
+        cuts = [0, width // 24 * 10, width]
         grad_down, *pair = grads_of(x_t, d_both, 0, cuts[1], (), (weighted_t, y_all))
         for start, stop in zip(cuts[1:], cuts[2:]):
             pair = grads_of(x_t, d_both, start, stop - start, tuple(pair))

time: 51.7 us -> 50.4 us (0.975)
  waiting for transfers between devices: 8.23 us -> 6.4 us
    ppermute x14, waiting for transfers between devices: 8.23 us -> 6.4 us  [swap(): return lax.ppermute(block, 'blk', [(i, i ^ bits[i % 2]) for i in range(n)])]
  transfers between devices with their start and end apart: 14 -> 14, of which waited for: 7 -> 7; matrix products, arithmetic and copies ran while one was open for 1% -> 1% of each run, Pallas kernels for 27% -> 28%
where the time goes in v19:
time: 50.4 us; the launch traced here: 50.2 us
  Pallas kernels  25.4 us (50%)
  starting transfers between devices  17.1 us (34%)
  waiting for transfers between devices  6.4 us (13%)
  between operations  0.81 us (2%)
    ppermute x14, starting transfers between devices, swap(): return lax.ppermute(block, 'blk', [(i, i ^ bits[i % 2]) for i in range(n)])  17.1 us
    pallas_call x1, Pallas kernels, shards(): pl.pallas_call(expert_kernel, out_shape=[jax.ShapeDtypeStruct((half, wide...  8.79 us
    pallas_call x2, Pallas kernels, grads_of(): pl.pallas_call(kernel, out_shape=outs, in_specs=whole(2 + len(down)) + (w...  8.1 us
    ppermute x14, waiting for transfers between devices, swap(): return lax.ppermute(block, 'blk', [(i, i ^ bits[i % 2]) for i in range(n)])  6.4 us
    pallas_call x1, Pallas kernels, fetch(): pl.pallas_call(functools.partial(fetch_kernel, count), out_shape=[pltpu.V...  4.7 us
    pallas_call x1, Pallas kernels, shards(): pl.pallas_call(router_kernel, out_shape=[jax.ShapeDtypeStruct((1, count),...  1.3 us
    pallas_call x3, Pallas kernels, call(): pl.pallas_call(kernel, out_shape=[jax.ShapeDtypeStruct(s, t) for s, t in...  1.24 us
    pallas_call x1, Pallas kernels, shards(): pl.pallas_call(select_kernel, out_shape=[jax.ShapeDtypeStruct((slots, wid...  1.19 us
  transfers between devices with their start and end apart: 14, of which 7 were waited for; matrix products, arithmetic and copies ran while one was open for 1% of the time, Pallas kernels for 28%

profile of v19, /device:TPU:0, one launch (start us, length us, event | category | flops | bytes accessed | tf_op | source)
XLA Modules:
  0.0 50.2 jit_solution(15794914332114119036)
XLA Ops:
  0.6 1.2 %shard_map.135 = (bf16[4,12416]{1,0:T(4,128)(2,1)S(1)}, f32[16,16]{1,0:T(8,128)S(1)}) custom-call(f32[8,16]{1,0:T(8,128)} %bitcast.6, s32[2,16]{1,0:T(2,128)} %bitcast.9, bf16[16,6144]{1,0:T(8,128)(2,1)} %tokens_in.1, bf16[4,6144]{1,0:T(4,128)(2,1)} %y_in.1), custom_call_target="tpu_custom_call" | custom-call | flops 1048576 | bytes 4194304 | tf_op jit(solution)/shard_map/pallas_call | solution.py:400
  1.8 4.1 %collective-permute-start = (bf16[4,12416]{1,0:T(4,128)(2,1)S(1)}, bf16[4,12416]{1,0:T(4,128)(2,1)S(1)}, u32[]{:S(2)}, u32[]{:S(2)}) collective-permute-start(bf16[4,12416]{1,0:T(4,128)(2,1)S(1)} %get-tuple-element.36.refs_2_), channel_id=1, source_target_pairs={{0,8},{1,9},{2,10},{3,11},{4,12},{5,13},{6,14},{7,15},{8,0},{9,1},... | collective-permute-start | bytes 297992 | tf_op jit(solution)/shard_map/ppermute | solution.py:386
  5.9 1.5 %collective-permute-start.2 = (bf16[4,12416]{1,0:T(4,128)(2,1)S(1)}, bf16[4,12416]{1,0:T(4,128)(2,1)S(1)}, u32[]{:S(2)}, u32[]{:S(2)}) collective-permute-start(bf16[4,12416]{1,0:T(4,128)(2,1)S(1)} %get-tuple-element.36.refs_2_), channel_id=1, source_target_pairs={{0,2},{1,5},{2,0},{3,7},{4,6},{5,1},{6,4},{7,3},{8,10},{9,13},{10,... | collective-permute-start | bytes 297992 | tf_op jit(solution)/shard_map/ppermute | solution.py:386
  7.4 1.6 %collective-permute-start.1 = (bf16[4,12416]{1,0:T(4,128)(2,1)S(1)}, bf16[4,12416]{1,0:T(4,128)(2,1)S(1)}, u32[]{:S(2)}, u32[]{:S(2)}) collective-permute-start(bf16[4,12416]{1,0:T(4,128)(2,1)S(1)} %get-tuple-element.36.refs_2_), channel_id=1, source_target_pairs={{0,4},{1,3},{2,6},{3,1},{4,0},{5,7},{6,2},{7,5},{8,12},{9,11},{10,... | collective-permute-start | bytes 297992 | tf_op jit(solution)/shard_map/ppermute | solution.py:386
  9.0 4.7 %shard_map.138 = (bf16[6144,512]{1,0:T(8,128)(2,1)S(1)}, bf16[6144,512]{1,0:T(8,128)(2,1)S(1)}) custom-call(bf16[6144,512]{1,0:T(8,128)(2,1)} %refs_0_.1, bf16[6144,512]{1,0:T(8,128)(2,1)} %refs_1_.1, bf16[4,12416]{1,0:T(4,128)(2,1)S(1)} %get-tuple-element.36.refs_2_), custom_call_target="tpu_custom_call" | custom-call | bytes 12582912 | tf_op jit(solution)/shard_map/pallas_call | solution.py:162
  13.7 0.0 collective-permute-done.block
  13.8 0.0 collective-permute-done.2.refs_2_
  13.8 0.0 collective-permute-done.1.refs_1_
  13.8 0.5 %collective-permute-start.3 = (bf16[4,12416]{1,0:T(4,128)(2,1)S(1)}, bf16[4,12416]{1,0:T(4,128)(2,1)S(1)}, u32[]{:S(2)}, u32[]{:S(2)}) collective-permute-start(bf16[4,12416]{1,0:T(4,128)(2,1)S(1)} %shard_map.139), channel_id=1, source_target_pairs={{0,4},{1,3},{2,6},{3,1},{4,0},{5,7},{6,2},{7,5},{8,12},{9,11},{10,... | collective-permute-start | bytes 297992 | tf_op jit(solution)/shard_map/ppermute | solution.py:386
  14.3 1.5 %collective-permute-start.6 = (bf16[4,12416]{1,0:T(4,128)(2,1)S(1)}, bf16[4,12416]{1,0:T(4,128)(2,1)S(1)}, u32[]{:S(2)}, u32[]{:S(2)}) collective-permute-start(bf16[4,12416]{1,0:T(4,128)(2,1)S(1)} %shard_map.139), channel_id=1, source_target_pairs={{0,6},{1,7},{2,4},{3,5},{4,2},{5,3},{6,0},{7,1},{8,14},{9,15},{10,... | collective-permute-start | bytes 297992 | tf_op jit(solution)/shard_map/ppermute | solution.py:386
  15.8 1.5 %collective-permute-start.4 = (bf16[4,12416]{1,0:T(4,128)(2,1)S(1)}, bf16[4,12416]{1,0:T(4,128)(2,1)S(1)}, u32[]{:S(2)}, u32[]{:S(2)}) collective-permute-start(bf16[4,12416]{1,0:T(4,128)(2,1)S(1)} %shard_map.139), channel_id=1, source_target_pairs={{0,2},{1,5},{2,0},{3,7},{4,6},{5,1},{6,4},{7,3},{8,10},{9,13},{10,... | collective-permute-start | bytes 297992 | tf_op jit(solution)/shard_map/ppermute | solution.py:386
  17.4 0.5 collective-permute-start.5
  17.8 1.7 %collective-permute-done.3.block = bf16[4,12416]{1,0:T(4,128)(2,1)S(1)} collective-permute-done((bf16[4,12416]{1,0:T(4,128)(2,1)S(1)}, bf16[4,12416]{1,0:T(4,128)(2,1)S(1)}, u32[]{:S(2)}, u32[]{:S(2)}) %collective-permute-start.3) | collective-permute-done | bytes 99360 | tf_op jit(solution)/shard_map/ppermute | solution.py:386
  19.5 0.2 pad_maximum_fusion.refs_0_
  19.8 1.2 %collective-permute-done.6.block = bf16[4,12416]{1,0:T(4,128)(2,1)S(1)} collective-permute-done((bf16[4,12416]{1,0:T(4,128)(2,1)S(1)}, bf16[4,12416]{1,0:T(4,128)(2,1)S(1)}, u32[]{:S(2)}, u32[]{:S(2)}) %collective-permute-start.6) | collective-permute-done | bytes 99360 | tf_op jit(solution)/shard_map/ppermute | solution.py:386
  21.0 0.1 collective-permute-start.7
  21.1 0.9 %collective-permute-done.5 = bf16[4,12416]{1,0:T(4,128)(2,1)S(1)} collective-permute-done((bf16[4,12416]{1,0:T(4,128)(2,1)S(1)}, bf16[4,12416]{1,0:T(4,128)(2,1)S(1)}, u32[]{:S(2)}, u32[]{:S(2)}) %collective-permute-start.5) | collective-permute-done | bytes 99360 | tf_op jit(solution)/shard_map/ppermute | solution.py:386
  22.0 0.0 collective-permute-done.4
  22.0 0.2 pad_maximum_fusion.1.refs_1_.after
  22.2 0.1 collective-permute-start.8
  22.3 0.5 collective-permute-done.7.refs_2_
  22.8 1.3 %collective-permute-done.8.refs_3_ = bf16[16,12416]{1,0:T(8,128)(2,1)S(1)} collective-permute-done((bf16[16,12416]{1,0:T(8,128)(2,1)S(1)}, bf16[16,12416]{1,0:T(8,128)(2,1)S(1)}, u32[]{:S(2)}, u32[]{:S(2)}) %collective-permute-start.8) | collective-permute-done | bytes 397344 | tf_op jit(solution)/shard_map/ppermute | solution.py:386
  24.0 8.8 %shard_map.143 = (bf16[32,6272]{1,0:T(8,128)(2,1)S(1)}, f32[32,6272]{1,0:T(8,128)S(1)}, bf16[512,64]{1,0:T(8,128)(2,1)S(1)}, bf16[64,1024]{1,0:T(8,128)(2,1)S(1)...) custom-call(bf16[16,12416]{1,0:T(8,128)(2,1)S(1)} %pad_maximum_fusion.refs_0_, ...), custom_call_target="tpu_custom_call" | custom-call | flops 6442450944 | bytes 12582912 | tf_op jit(solution)/shard_map/pallas_call | solution.py:464
  32.8 0.2 collective-permute-start.9
  33.0 1.3 %shard_map.148 = (f32[1,16]{1,0:T(1,128)}, f32[1,16]{1,0:T(1,128)}, f32[8,16]{1,0:T(8,128)S(1)}, f32[8,16]{1,0:T(8,128)S(1)}) custom-call(f32[8,16]{1,0:T(8,128)} %bitcast.7, f32[8,16]{1,0:T(8,128)} %bitcast.8, s32[2,16]{1,0:T(2,128)} %bitcast.10, bf16[16,12416]{1,0:T(8,128)(2,1)S(1)} %pad_maximum_fusion.1.refs_1_.after), custom_call_target="tpu_custom_call" | custom-call | flops 1048576 | bytes 4194304 | tf_op jit(solution)/shard_map/pallas_call | solution.py:440
  34.3 0.3 collective-permute-done.9.refs_0_
  34.6 0.2 shard_map.146
  34.8 1.1 %collective-permute-start.10 = (bf16[16,6272]{1,0:T(8,128)(2,1)S(1)}, bf16[16,6272]{1,0:T(8,128)(2,1)S(1)}, u32[]{:S(2)}, u32[]{:S(2)}) collective-permute-start(bf16[16,6272]{1,0:T(8,128)(2,1)S(1)} %get-tuple-element.53), channel_id=1, source_target_pairs={{0,2},{1,5},{2,0},{3,7},{4,6},{5,1},{6,4},{7,3},{8,10},{9,13},{10,... | collective-permute-start | bytes 602120 | tf_op jit(solution)/shard_map/ppermute | solution.py:386
  35.9 4.7 %shard_map.144 = (bf16[512,6144]{1,0:T(8,128)(2,1)}, bf16[6144,512]{1,0:T(8,128)(2,1)}, bf16[6144,512]{1,0:T(8,128)(2,1)}, bf16[256,512]{1,0:T(8,128)(2,1)S(1)}, bf16[256,512]{1,0:T(8,128)(2,1)S(1)}) custom-call(bf16[512,64]{1,0:T(8,128)(2,1)S(1)} %get-tuple-element.41.weighted_t, bf16[64,6144]{1,0:T(8,128)(2,1)S(1)} %get-tuple-element.42.y, ...), custom_call_target="tpu_custom_call" | custom-call | flops 2952790016 | bytes 11534336 | tf_op jit(solution)/shard_map/pallas_call | solution.py:363
  40.6 0.0 collective-permute-done.10.refs_0_
  40.7 0.2 shard_map.147
  40.8 0.5 %collective-permute-start.11 = (bf16[4,6272]{1,0:T(4,128)(2,1)S(1)}, bf16[4,6272]{1,0:T(4,128)(2,1)S(1)}, u32[]{:S(2)}, u32[]{:S(2)}) collective-permute-start(bf16[4,6272]{1,0:T(4,128)(2,1)S(1)} %get-tuple-element.55), channel_id=1, source_target_pairs={{0,8},{1,9},{2,10},{3,11},{4,12},{5,13},{6,14},{7,15},{8,0},{9,1},... | collective-permute-start | bytes 150536 | tf_op jit(solution)/shard_map/ppermute | solution.py:386
  41.3 2.0 %collective-permute-start.12 = (bf16[4,6272]{1,0:T(4,128)(2,1)S(1)}, bf16[4,6272]{1,0:T(4,128)(2,1)S(1)}, u32[]{:S(2)}, u32[]{:S(2)}) collective-permute-start(bf16[4,6272]{1,0:T(4,128)(2,1)S(1)} %get-tuple-element.56), channel_id=1, source_target_pairs={{0,4},{1,3},{2,6},{3,1},{4,0},{5,7},{6,2},{7,5},{8,12},{9,11},{10,... | collective-permute-start | bytes 150536 | tf_op jit(solution)/shard_map/ppermute | solution.py:386
  43.4 1.9 %collective-permute-start.13 = (bf16[4,6272]{1,0:T(4,128)(2,1)S(1)}, bf16[4,6272]{1,0:T(4,128)(2,1)S(1)}, u32[]{:S(2)}, u32[]{:S(2)}) collective-permute-start(bf16[4,6272]{1,0:T(4,128)(2,1)S(1)} %get-tuple-element.57), channel_id=1, source_target_pairs={{0,12},{1,11},{2,14},{3,9},{4,8},{5,15},{6,10},{7,13},{8,4},{9,3},... | collective-permute-start | bytes 150536 | tf_op jit(solution)/shard_map/ppermute | solution.py:386
  45.3 3.4 %shard_map.145 = (bf16[6144,512]{1,0:T(8,128)(2,1)}, bf16[6144,512]{1,0:T(8,128)(2,1)}) custom-call(bf16[6144,64]{1,0:T(8,128)(2,1)S(1)} %get-tuple-element.39.x_t, bf16[64,1024]{1,0:T(8,128)(2,1)S(1)} %get-tuple-element.40.d_both, bf16[256,512]{1,0:T(8,128)(2,1)S(1)} %get-tuple-element.43.refs_0_, ...), custom_call_target="tpu_custom_call", output_to_operand_aliasing={{0}: (4, {}), {1}: (5, {})} | custom-call | flops 1879048192 | bytes 7340032 | tf_op jit(solution)/shard_map/pallas_call | solution.py:363
  48.7 0.0 collective-permute-done.11.refs_0_
  48.7 0.0 collective-permute-done.12.refs_1_
  48.7 0.6 %collective-permute-done.13.refs_2_ = bf16[4,6272]{1,0:T(4,128)(2,1)S(1)} collective-permute-done((bf16[4,6272]{1,0:T(4,128)(2,1)S(1)}, bf16[4,6272]{1,0:T(4,128)(2,1)S(1)}, u32[]{:S(2)}, u32[]{:S(2)}) %collective-permute-start.13) | collective-permute-done | bytes 50208 | tf_op jit(solution)/shard_map/ppermute | solution.py:386
  49.3 0.9 %shard_map.149 = (bf16[16,6144]{1,0:T(8,128)(2,1)}, f32[8,16]{1,0:T(8,128)}) custom-call(f32[4,6272]{1,0:T(4,128)S(1)} %get-tuple-element.54.have, bf16[4,6272]{1,0:T(4,128)(2,1)S(1)} %collective-permute-done.11.refs_0_, bf16[4,6272]{1,0:T(4,128)(2,1)S(1)} %collective-permute-done.12.refs_1_, bf16[4,6272]{1,0:T(4,128)(2,1)S(1)} %collective-permute-done.13.refs_2_, ...), custom_call_target="tpu_custom_call" | custom-call | flops 1048576 | bytes 262144 | tf_op jit(solution)/shard_map/pallas_call | solution.py:25
  (6 shorter events, 0.1 us)
Async XLA Ops:
  1.8 11.9 %collective-permute-start = (bf16[4,12416]{1,0:T(4,128)(2,1)S(1)}, bf16[4,12416]{1,0:T(4,128)(2,1)S(1)}, u32[]{:S(2)}, u32[]{:S(2)}) collective-permute-start(bf16[4,12416]{1,0:T(4,128)(2,1)S(1)} %get-tuple-element.36.refs_2_), channel_id=1, source_target_pairs={{0,8},{1,9},{2,10},{3,11},{4,12},{5,13},{6,14},{7,15},{8,0},{9,1},... | collective-permute-start | bytes 297992 | tf_op jit(solution)/shard_map/ppermute | solution.py:386
  5.9 7.8 %collective-permute-start.2 = (bf16[4,12416]{1,0:T(4,128)(2,1)S(1)}, bf16[4,12416]{1,0:T(4,128)(2,1)S(1)}, u32[]{:S(2)}, u32[]{:S(2)}) collective-permute-start(bf16[4,12416]{1,0:T(4,128)(2,1)S(1)} %get-tuple-element.36.refs_2_), channel_id=1, source_target_pairs={{0,2},{1,5},{2,0},{3,7},{4,6},{5,1},{6,4},{7,3},{8,10},{9,13},{10,... | collective-permute-start | bytes 297992 | tf_op jit(solution)/shard_map/ppermute | solution.py:386
  7.4 6.3 %collective-permute-start.1 = (bf16[4,12416]{1,0:T(4,128)(2,1)S(1)}, bf16[4,12416]{1,0:T(4,128)(2,1)S(1)}, u32[]{:S(2)}, u32[]{:S(2)}) collective-permute-start(bf16[4,12416]{1,0:T(4,128)(2,1)S(1)} %get-tuple-element.36.refs_2_), channel_id=1, source_target_pairs={{0,4},{1,3},{2,6},{3,1},{4,0},{5,7},{6,2},{7,5},{8,12},{9,11},{10,... | collective-permute-start | bytes 297992 | tf_op jit(solution)/shard_map/ppermute | solution.py:386
  13.8 5.7 %collective-permute-start.3 = (bf16[4,12416]{1,0:T(4,128)(2,1)S(1)}, bf16[4,12416]{1,0:T(4,128)(2,1)S(1)}, u32[]{:S(2)}, u32[]{:S(2)}) collective-permute-start(bf16[4,12416]{1,0:T(4,128)(2,1)S(1)} %shard_map.139), channel_id=1, source_target_pairs={{0,4},{1,3},{2,6},{3,1},{4,0},{5,7},{6,2},{7,5},{8,12},{9,11},{10,... | collective-permute-start | bytes 297992 | tf_op jit(solution)/shard_map/ppermute | solution.py:386
  14.3 6.6 %collective-permute-start.6 = (bf16[4,12416]{1,0:T(4,128)(2,1)S(1)}, bf16[4,12416]{1,0:T(4,128)(2,1)S(1)}, u32[]{:S(2)}, u32[]{:S(2)}) collective-permute-start(bf16[4,12416]{1,0:T(4,128)(2,1)S(1)} %shard_map.139), channel_id=1, source_target_pairs={{0,6},{1,7},{2,4},{3,5},{4,2},{5,3},{6,0},{7,1},{8,14},{9,15},{10,... | collective-permute-start | bytes 297992 | tf_op jit(solution)/shard_map/ppermute | solution.py:386
  15.8 6.2 %collective-permute-start.4 = (bf16[4,12416]{1,0:T(4,128)(2,1)S(1)}, bf16[4,12416]{1,0:T(4,128)(2,1)S(1)}, u32[]{:S(2)}, u32[]{:S(2)}) collective-permute-start(bf16[4,12416]{1,0:T(4,128)(2,1)S(1)} %shard_map.139), channel_id=1, source_target_pairs={{0,2},{1,5},{2,0},{3,7},{4,6},{5,1},{6,4},{7,3},{8,10},{9,13},{10,... | collective-permute-start | bytes 297992 | tf_op jit(solution)/shard_map/ppermute | solution.py:386
  17.4 4.6 %collective-permute-start.5 = (bf16[4,12416]{1,0:T(4,128)(2,1)S(1)}, bf16[4,12416]{1,0:T(4,128)(2,1)S(1)}, u32[]{:S(2)}, u32[]{:S(2)}) collective-permute-start(bf16[4,12416]{1,0:T(4,128)(2,1)S(1)} %collective-permute-done.2.refs_2_), channel_id=1, source_target_pairs={{0,4},{1,3},{2,6},{3,1},{4,0},{5,7},{6,2},{7,5},{8,12},{9,11},{10,... | collective-permute-start | bytes 297992 | tf_op jit(solution)/shard_map/ppermute | solution.py:386
  21.0 1.8 %collective-permute-start.7 = (bf16[16,12416]{1,0:T(8,128)(2,1)S(1)}, bf16[16,12416]{1,0:T(8,128)(2,1)S(1)}, u32[]{:S(2)}, u32[]{:S(2)}) collective-permute-start(bf16[16,12416]{1,0:T(8,128)(2,1)S(1)} %pad_maximum_fusion.refs_0_), channel_id=1, source_target_pairs={{0,1},{1,0},{2,3},{3,2},{4,5},{5,4},{6,7},{7,6},{8,9},{9,8},{10,11... | collective-permute-start | bytes 1191944 | tf_op jit(solution)/shard_map/ppermute | solution.py:386
  22.2 1.8 %collective-permute-start.8 = (bf16[16,12416]{1,0:T(8,128)(2,1)S(1)}, bf16[16,12416]{1,0:T(8,128)(2,1)S(1)}, u32[]{:S(2)}, u32[]{:S(2)}) collective-permute-start(bf16[16,12416]{1,0:T(8,128)(2,1)S(1)} %pad_maximum_fusion.1.refs_1_.after), channel_id=1, source_target_pairs={{0,1},{1,0},{2,3},{3,2},{4,5},{5,4},{6,7},{7,6},{8,9},{9,8},{10,11... | collective-permute-start | bytes 1191944 | tf_op jit(solution)/shard_map/ppermute | solution.py:386
  32.8 1.8 %collective-permute-start.9 = (bf16[32,6272]{1,0:T(8,128)(2,1)S(1)}, bf16[32,6272]{1,0:T(8,128)(2,1)S(1)}, u32[]{:S(2)}, u32[]{:S(2)}) collective-permute-start(bf16[32,6272]{1,0:T(8,128)(2,1)S(1)} %get-tuple-element.51), channel_id=1, source_target_pairs={{0,1},{1,0},{2,3},{3,2},{4,5},{5,4},{6,7},{7,6},{8,9},{9,8},{10,11... | collective-permute-start | bytes 1204232 | tf_op jit(solution)/shard_map/ppermute | solution.py:386
  34.8 5.8 %collective-permute-start.10 = (bf16[16,6272]{1,0:T(8,128)(2,1)S(1)}, bf16[16,6272]{1,0:T(8,128)(2,1)S(1)}, u32[]{:S(2)}, u32[]{:S(2)}) collective-permute-start(bf16[16,6272]{1,0:T(8,128)(2,1)S(1)} %get-tuple-element.53), channel_id=1, source_target_pairs={{0,2},{1,5},{2,0},{3,7},{4,6},{5,1},{6,4},{7,3},{8,10},{9,13},{10,... | collective-permute-start | bytes 602120 | tf_op jit(solution)/shard_map/ppermute | solution.py:386
  40.8 7.9 %collective-permute-start.11 = (bf16[4,6272]{1,0:T(4,128)(2,1)S(1)}, bf16[4,6272]{1,0:T(4,128)(2,1)S(1)}, u32[]{:S(2)}, u32[]{:S(2)}) collective-permute-start(bf16[4,6272]{1,0:T(4,128)(2,1)S(1)} %get-tuple-element.55), channel_id=1, source_target_pairs={{0,8},{1,9},{2,10},{3,11},{4,12},{5,13},{6,14},{7,15},{8,0},{9,1},... | collective-permute-start | bytes 150536 | tf_op jit(solution)/shard_map/ppermute | solution.py:386
  41.3 7.3 %collective-permute-start.12 = (bf16[4,6272]{1,0:T(4,128)(2,1)S(1)}, bf16[4,6272]{1,0:T(4,128)(2,1)S(1)}, u32[]{:S(2)}, u32[]{:S(2)}) collective-permute-start(bf16[4,6272]{1,0:T(4,128)(2,1)S(1)} %get-tuple-element.56), channel_id=1, source_target_pairs={{0,4},{1,3},{2,6},{3,1},{4,0},{5,7},{6,2},{7,5},{8,12},{9,11},{10,... | collective-permute-start | bytes 150536 | tf_op jit(solution)/shard_map/ppermute | solution.py:386
  43.4 5.9 %collective-permute-start.13 = (bf16[4,6272]{1,0:T(4,128)(2,1)S(1)}, bf16[4,6272]{1,0:T(4,128)(2,1)S(1)}, u32[]{:S(2)}, u32[]{:S(2)}) collective-permute-start(bf16[4,6272]{1,0:T(4,128)(2,1)S(1)} %get-tuple-element.57), channel_id=1, source_target_pairs={{0,12},{1,11},{2,14},{3,9},{4,8},{5,15},{6,10},{7,13},{8,4},{9,3},... | collective-permute-start | bytes 150536 | tf_op jit(solution)/shard_map/ppermute | solution.py:386

commit v20 on v19

--- a/solution.py
+++ b/solution.py
@@ -21,15 +21,18 @@
     return [pl.BlockSpec(memory_space=pltpu.VMEM)] * count
 
 
-def call(kernel, outs, args, flops, moved, limit=8):
+def call(kernel, outs, args, flops, moved, limit=8, after=()):
+    def body(*refs):
+        kernel(*refs[: len(args)], *refs[len(args) + len(after) :])
+
     return pl.pallas_call(
-        kernel,
+        body,
         out_shape=[jax.ShapeDtypeStruct(s, t) for s, t in outs],
-        in_specs=whole(len(args)),
+        in_specs=whole(len(args)) + [pl.BlockSpec(memory_space=pl.ANY)] * len(after),
         out_specs=whole(len(outs)),
         compiler_params=pltpu.CompilerParams(vmem_limit_bytes=limit * MIB),
         cost_estimate=pl.CostEstimate(flops=flops, bytes_accessed=moved, transcendentals=0),
-    )(*args)
+    )(*args, *after)
 
 
 def in_hbm(array):
@@ -191,7 +194,7 @@
 
 
 def expert_kernel(*refs):
-    pieces, (down_in, gate_w, up_w), refs = refs[:4], refs[4:7], refs[7:]
+    pieces, (down_in, gate_w, up_w), refs = refs[:4], refs[4:7], refs[8:]
     send, keep, weighted_t, d_both, x_t, y, x, down_w, sems = refs
     rows, width, hidden_dim = x.shape[0], gate_w.shape[0], gate_w.shape[1]
     wide = width + LANES
@@ -320,7 +323,8 @@
         copy.wait()
 
 
-def first_kernel(weighted_t, y, x_t, d_both, down_out, *refs):
+def first_kernel(first_row, weighted_t, y, x_t, d_both, *refs):
+    left, down_out, refs = refs[:4], refs[4], refs[5:]
     down_buf, down_sems = refs[4:6]
     chunks, _, step = down_buf.shape
     copies = []
@@ -329,7 +333,7 @@
         tiles(down_buf.at[i], weighted_t, y.at[:, at])
         copies.append(pltpu.make_async_copy(down_buf.at[i], down_out.at[:, at], down_sems.at[i]))
         copies[i].start()
-    grads_kernel(0, False, x_t, d_both, *refs[:4], *refs[6:])
+    grads_kernel(first_row, False, x_t, d_both, *left, *refs[:4], *refs[6:])
     for copy in copies:
         copy.wait()
 
@@ -351,7 +355,7 @@
     ]
     kernel = functools.partial(grads_kernel, first_row, last)
     if down:
-        kernel = first_kernel
+        kernel = functools.partial(first_kernel, first_row)
         wide = 1024
         outs = [jax.ShapeDtypeStruct((cols, width), BF16)] + outs
         out_specs = [anywhere] + out_specs
@@ -366,7 +370,7 @@
         in_specs=whole(2 + len(down)) + (whole(2) + [anywhere] * 2 if before else []),
         out_specs=out_specs,
         scratch_shapes=scratch,
-        input_output_aliases={4: 0, 5: 1} if before else {},
+        input_output_aliases=({6: 1, 7: 2} if down else {4: 0, 5: 1}) if before else {},
         compiler_params=pltpu.CompilerParams(vmem_limit_bytes=20 * MIB),
         cost_estimate=pl.CostEstimate(
             flops=8 * slots * elements, bytes_accessed=2 * elements, transcendentals=0
@@ -471,7 +475,7 @@
                 jax.ShapeDtypeStruct((width, rows), BF16),
                 jax.ShapeDtypeStruct((rows, width), BF16),
             ],
-            in_specs=whole(4) + [anywhere] + whole(2),
+            in_specs=whole(4) + [anywhere] + whole(2) + [anywhere],
             out_specs=whole(6),
             scratch_shapes=[
                 pltpu.VMEM((rows, wide), BF16),
@@ -482,7 +486,15 @@
             cost_estimate=pl.CostEstimate(
                 flops=16 * work, bytes_accessed=4 * width * hidden, transcendentals=0
             ),
-        )(*pieces, in_hbm(down_weight), gate_w, up_w)
+        )(*pieces, in_hbm(down_weight), gate_w, up_w, base)
+
+        unit = width // 24
+        cuts = [0, 3 * unit, 12 * unit, width]
+        pair = first_pair = grads_of(x_t, d_both, 0, cuts[1], ())
+        grad_down, *pair = grads_of(
+            x_t, d_both, cuts[1], cuts[2] - cuts[1], tuple(pair), (weighted_t, y_all)
+        )
+        grad_gate, grad_up = grads_of(x_t, d_both, cuts[2], cuts[3] - cuts[2], tuple(pair))
 
         both = tuple(f ^ s for f, s in zip(first, second))
         paths = [((1, 1),), (third,), (first, second, both)] + [(b,) for b in levels[:-3][::-1]]
@@ -498,13 +510,9 @@
                 [keep, *gots],
                 4 * keep.shape[0] * wide,
                 16 * keep.shape[0] * wide,
+                after=[first_pair[2]] if path == paths[0] else [],
             )
 
-        cuts = [0, width // 24 * 10, width]
-        grad_down, *pair = grads_of(x_t, d_both, 0, cuts[1], (), (weighted_t, y_all))
-        for start, stop in zip(cuts[1:], cuts[2:]):
-            pair = grads_of(x_t, d_both, start, stop - start, tuple(pair))
-        grad_gate, grad_up = pair
 
         grad_tokens, grad_logits = call(
             home_kernel,

time: 50.4 us -> 50.4 us (level)
  waiting for transfers between devices: 6.4 us -> 5.52 us
  Pallas kernels: 25.4 us -> 26.2 us
    ppermute x14, waiting for transfers between devices: 6.4 us -> 5.52 us  [swap(): return lax.ppermute(block, 'blk', [(i, i ^ bits[i % 2]) for i in range(n)])]
    pallas_call x2 -> x3, Pallas kernels: 8.1 us -> 8.96 us  [grads_of(): pl.pallas_call(kernel, out_shape=outs, in_specs=whole(2 + len(down)) + (w...]
  transfers between devices with their start and end apart: 14 -> 14, of which waited for: 7 -> 6; matrix products, arithmetic and copies ran while one was open for 1% -> 1% of each run, Pallas kernels for 28% -> 30%
where the time goes in v20:
time: 50.4 us; the launch traced here: 50.1 us
  Pallas kernels  26.2 us (52%)
  starting transfers between devices  17.1 us (34%)
  waiting for transfers between devices  5.52 us (11%)
  between operations  0.82 us (2%)
    ppermute x14, starting transfers between devices, swap(): return lax.ppermute(block, 'blk', [(i, i ^ bits[i % 2]) for i in range(n)])  17.1 us
    pallas_call x3, Pallas kernels, grads_of(): pl.pallas_call(kernel, out_shape=outs, in_specs=whole(2 + len(down)) + (w...  8.96 us
    pallas_call x1, Pallas kernels, shards(): pl.pallas_call(expert_kernel, out_shape=[jax.ShapeDtypeStruct((half, wide...  8.78 us
    ppermute x14, waiting for transfers between devices, swap(): return lax.ppermute(block, 'blk', [(i, i ^ bits[i % 2]) for i in range(n)])  5.52 us
    pallas_call x1, Pallas kernels, fetch(): pl.pallas_call(functools.partial(fetch_kernel, count), out_shape=[pltpu.V...  4.7 us
    pallas_call x1, Pallas kernels, shards(): pl.pallas_call(router_kernel, out_shape=[jax.ShapeDtypeStruct((1, count),...  1.3 us
    pallas_call x3, Pallas kernels, call(): pl.pallas_call(body, out_shape=[jax.ShapeDtypeStruct(s, t) for s, t in ou...  1.24 us
    pallas_call x1, Pallas kernels, shards(): pl.pallas_call(select_kernel, out_shape=[jax.ShapeDtypeStruct((slots, wid...  1.19 us
  transfers between devices with their start and end apart: 14, of which 6 were waited for; matrix products, arithmetic and copies ran while one was open for 1% of the time, Pallas kernels for 30%

profile of v20, /device:TPU:0, one launch (start us, length us, event | category | flops | bytes accessed | tf_op | source)
XLA Modules:
  0.0 50.1 jit_solution(7953597729545608495)
XLA Ops:
  0.6 1.2 %shard_map.135 = (bf16[4,12416]{1,0:T(4,128)(2,1)S(1)}, f32[16,16]{1,0:T(8,128)S(1)}) custom-call(f32[8,16]{1,0:T(8,128)} %bitcast.6, s32[2,16]{1,0:T(2,128)} %bitcast.9, bf16[16,6144]{1,0:T(8,128)(2,1)} %tokens_in.1, bf16[4,6144]{1,0:T(4,128)(2,1)} %y_in.1), custom_call_target="tpu_custom_call" | custom-call | flops 1048576 | bytes 4194304 | tf_op jit(solution)/shard_map/pallas_call | solution.py:404
  1.8 4.1 %collective-permute-start = (bf16[4,12416]{1,0:T(4,128)(2,1)S(1)}, bf16[4,12416]{1,0:T(4,128)(2,1)S(1)}, u32[]{:S(2)}, u32[]{:S(2)}) collective-permute-start(bf16[4,12416]{1,0:T(4,128)(2,1)S(1)} %get-tuple-element.40.refs_2_), channel_id=1, source_target_pairs={{0,8},{1,9},{2,10},{3,11},{4,12},{5,13},{6,14},{7,15},{8,0},{9,1},... | collective-permute-start | bytes 297992 | tf_op jit(solution)/shard_map/ppermute | solution.py:390
  5.9 1.5 %collective-permute-start.2 = (bf16[4,12416]{1,0:T(4,128)(2,1)S(1)}, bf16[4,12416]{1,0:T(4,128)(2,1)S(1)}, u32[]{:S(2)}, u32[]{:S(2)}) collective-permute-start(bf16[4,12416]{1,0:T(4,128)(2,1)S(1)} %get-tuple-element.40.refs_2_), channel_id=1, source_target_pairs={{0,2},{1,5},{2,0},{3,7},{4,6},{5,1},{6,4},{7,3},{8,10},{9,13},{10,... | collective-permute-start | bytes 297992 | tf_op jit(solution)/shard_map/ppermute | solution.py:390
  7.5 1.6 %collective-permute-start.1 = (bf16[4,12416]{1,0:T(4,128)(2,1)S(1)}, bf16[4,12416]{1,0:T(4,128)(2,1)S(1)}, u32[]{:S(2)}, u32[]{:S(2)}) collective-permute-start(bf16[4,12416]{1,0:T(4,128)(2,1)S(1)} %get-tuple-element.40.refs_2_), channel_id=1, source_target_pairs={{0,4},{1,3},{2,6},{3,1},{4,0},{5,7},{6,2},{7,5},{8,12},{9,11},{10,... | collective-permute-start | bytes 297992 | tf_op jit(solution)/shard_map/ppermute | solution.py:390
  9.0 4.7 %shard_map.138 = (bf16[6144,512]{1,0:T(8,128)(2,1)S(1)}, bf16[6144,512]{1,0:T(8,128)(2,1)S(1)}) custom-call(bf16[6144,512]{1,0:T(8,128)(2,1)} %refs_0_.1, bf16[6144,512]{1,0:T(8,128)(2,1)} %refs_1_.1, bf16[4,12416]{1,0:T(4,128)(2,1)S(1)} %get-tuple-element.40.refs_2_), custom_call_target="tpu_custom_call" | custom-call | bytes 12582912 | tf_op jit(solution)/shard_map/pallas_call | solution.py:165
  13.7 0.0 collective-permute-done.block
  13.8 0.0 collective-permute-done.2.refs_2_
  13.8 0.0 collective-permute-done.1.refs_1_
  13.8 0.5 %collective-permute-start.3 = (bf16[4,12416]{1,0:T(4,128)(2,1)S(1)}, bf16[4,12416]{1,0:T(4,128)(2,1)S(1)}, u32[]{:S(2)}, u32[]{:S(2)}) collective-permute-start(bf16[4,12416]{1,0:T(4,128)(2,1)S(1)} %shard_map.139), channel_id=1, source_target_pairs={{0,4},{1,3},{2,6},{3,1},{4,0},{5,7},{6,2},{7,5},{8,12},{9,11},{10,... | collective-permute-start | bytes 297992 | tf_op jit(solution)/shard_map/ppermute | solution.py:390
  14.3 1.5 %collective-permute-start.6 = (bf16[4,12416]{1,0:T(4,128)(2,1)S(1)}, bf16[4,12416]{1,0:T(4,128)(2,1)S(1)}, u32[]{:S(2)}, u32[]{:S(2)}) collective-permute-start(bf16[4,12416]{1,0:T(4,128)(2,1)S(1)} %shard_map.139), channel_id=1, source_target_pairs={{0,6},{1,7},{2,4},{3,5},{4,2},{5,3},{6,0},{7,1},{8,14},{9,15},{10,... | collective-permute-start | bytes 297992 | tf_op jit(solution)/shard_map/ppermute | solution.py:390
  15.8 1.5 %collective-permute-start.4 = (bf16[4,12416]{1,0:T(4,128)(2,1)S(1)}, bf16[4,12416]{1,0:T(4,128)(2,1)S(1)}, u32[]{:S(2)}, u32[]{:S(2)}) collective-permute-start(bf16[4,12416]{1,0:T(4,128)(2,1)S(1)} %shard_map.139), channel_id=1, source_target_pairs={{0,2},{1,5},{2,0},{3,7},{4,6},{5,1},{6,4},{7,3},{8,10},{9,13},{10,... | collective-permute-start | bytes 297992 | tf_op jit(solution)/shard_map/ppermute | solution.py:390
  17.4 0.5 collective-permute-start.5
  17.8 1.7 %collective-permute-done.3.block = bf16[4,12416]{1,0:T(4,128)(2,1)S(1)} collective-permute-done((bf16[4,12416]{1,0:T(4,128)(2,1)S(1)}, bf16[4,12416]{1,0:T(4,128)(2,1)S(1)}, u32[]{:S(2)}, u32[]{:S(2)}) %collective-permute-start.3) | collective-permute-done | bytes 99360 | tf_op jit(solution)/shard_map/ppermute | solution.py:390
  19.5 0.2 pad_maximum_fusion.refs_0_
  19.8 1.2 %collective-permute-done.6.block = bf16[4,12416]{1,0:T(4,128)(2,1)S(1)} collective-permute-done((bf16[4,12416]{1,0:T(4,128)(2,1)S(1)}, bf16[4,12416]{1,0:T(4,128)(2,1)S(1)}, u32[]{:S(2)}, u32[]{:S(2)}) %collective-permute-start.6) | collective-permute-done | bytes 99360 | tf_op jit(solution)/shard_map/ppermute | solution.py:390
  21.0 0.1 collective-permute-start.7
  21.1 0.9 %collective-permute-done.5 = bf16[4,12416]{1,0:T(4,128)(2,1)S(1)} collective-permute-done((bf16[4,12416]{1,0:T(4,128)(2,1)S(1)}, bf16[4,12416]{1,0:T(4,128)(2,1)S(1)}, u32[]{:S(2)}, u32[]{:S(2)}) %collective-permute-start.5) | collective-permute-done | bytes 99360 | tf_op jit(solution)/shard_map/ppermute | solution.py:390
  22.0 0.0 collective-permute-done.4
  22.0 0.2 pad_maximum_fusion.1.after.refs_1_
  22.2 0.1 collective-permute-start.8
  22.3 1.3 %shard_map.143 = (f32[1,16]{1,0:T(1,128)}, f32[1,16]{1,0:T(1,128)}, f32[8,16]{1,0:T(8,128)S(1)}, f32[8,16]{1,0:T(8,128)S(1)}) custom-call(f32[8,16]{1,0:T(8,128)} %bitcast.7, f32[8,16]{1,0:T(8,128)} %bitcast.8, s32[2,16]{1,0:T(2,128)} %bitcast.10, bf16[16,12416]{1,0:T(8,128)(2,1)S(1)} %pad_maximum_fusion.1.after.refs_1_), custom_call_target="tpu_custom_call" | custom-call | flops 1048576 | bytes 4194304 | tf_op jit(solution)/shard_map/pallas_call | solution.py:444
  23.6 0.0 collective-permute-done.7.refs_2_
  23.6 0.4 collective-permute-done.8.refs_3_
  24.0 8.8 %shard_map.144 = (bf16[32,6272]{1,0:T(8,128)(2,1)S(1)}, f32[32,6272]{1,0:T(8,128)S(1)}, bf16[512,64]{1,0:T(8,128)(2,1)S(1)}, bf16[64,1024]{1,0:T(8,128)(2,1)S(1)...) custom-call(bf16[16,12416]{1,0:T(8,128)(2,1)S(1)} %pad_maximum_fusion.refs_0_, ...), custom_call_target="tpu_custom_call" | custom-call | flops 6442450944 | bytes 12582912 | tf_op jit(solution)/shard_map/pallas_call | solution.py:468
  32.8 0.2 collective-permute-start.9
  33.0 1.2 %shard_map.145 = (bf16[6144,512]{1,0:T(8,128)(2,1)}, bf16[6144,512]{1,0:T(8,128)(2,1)}, bf16[256,512]{1,0:T(8,128)(2,1)S(1)}, bf16[256,512]{1,0:T(8,128)(2,1)S(1)}) custom-call(bf16[6144,64]{1,0:T(8,128)(2,1)S(1)} %get-tuple-element.44.x_t, bf16[64,1024]{1,0:T(8,128)(2,1)S(1)} %get-tuple-element.45.d_both), custom_call_target="tpu_custom_call" | custom-call | flops 402653184 | bytes 1572864 | tf_op jit(solution)/shard_map/pallas_call | solution.py:367
  34.3 0.4 collective-permute-done.9.refs_1_
  34.6 0.2 shard_map.148
  34.8 1.1 %collective-permute-start.10 = (bf16[16,6272]{1,0:T(8,128)(2,1)S(1)}, bf16[16,6272]{1,0:T(8,128)(2,1)S(1)}, u32[]{:S(2)}, u32[]{:S(2)}) collective-permute-start(bf16[16,6272]{1,0:T(8,128)(2,1)S(1)} %get-tuple-element.62), channel_id=1, source_target_pairs={{0,2},{1,5},{2,0},{3,7},{4,6},{5,1},{6,4},{7,3},{8,10},{9,13},{10,... | collective-permute-start | bytes 602120 | tf_op jit(solution)/shard_map/ppermute | solution.py:390
  35.9 4.7 %shard_map.146 = (bf16[512,6144]{1,0:T(8,128)(2,1)}, bf16[6144,512]{1,0:T(8,128)(2,1)}, bf16[6144,512]{1,0:T(8,128)(2,1)}, bf16[256,512]{1,0:T(8,128)(2,1)S(1)}, bf16[256,512]{1,0:T(8,128)(2,1)S(1)}) custom-call(bf16[512,64]{1,0:T(8,128)(2,1)S(1)} %get-tuple-element.46.weighted_t, ...), custom_call_target="tpu_custom_call", output_to_operand_aliasing={{1}: (6, {}), {2}: (7, {})} | custom-call | flops 2818572288 | bytes 11010048 | tf_op jit(solution)/shard_map/pallas_call | solution.py:367
  40.6 0.0 collective-permute-done.10.refs_1_
  40.6 0.2 shard_map.149
  40.8 0.5 %collective-permute-start.11 = (bf16[4,6272]{1,0:T(4,128)(2,1)S(1)}, bf16[4,6272]{1,0:T(4,128)(2,1)S(1)}, u32[]{:S(2)}, u32[]{:S(2)}) collective-permute-start(bf16[4,6272]{1,0:T(4,128)(2,1)S(1)} %get-tuple-element.64), channel_id=1, source_target_pairs={{0,8},{1,9},{2,10},{3,11},{4,12},{5,13},{6,14},{7,15},{8,0},{9,1},... | collective-permute-start | bytes 150536 | tf_op jit(solution)/shard_map/ppermute | solution.py:390
  41.3 2.0 %collective-permute-start.12 = (bf16[4,6272]{1,0:T(4,128)(2,1)S(1)}, bf16[4,6272]{1,0:T(4,128)(2,1)S(1)}, u32[]{:S(2)}, u32[]{:S(2)}) collective-permute-start(bf16[4,6272]{1,0:T(4,128)(2,1)S(1)} %get-tuple-element.65), channel_id=1, source_target_pairs={{0,4},{1,3},{2,6},{3,1},{4,0},{5,7},{6,2},{7,5},{8,12},{9,11},{10,... | collective-permute-start | bytes 150536 | tf_op jit(solution)/shard_map/ppermute | solution.py:390
  43.3 1.9 %collective-permute-start.13 = (bf16[4,6272]{1,0:T(4,128)(2,1)S(1)}, bf16[4,6272]{1,0:T(4,128)(2,1)S(1)}, u32[]{:S(2)}, u32[]{:S(2)}) collective-permute-start(bf16[4,6272]{1,0:T(4,128)(2,1)S(1)} %get-tuple-element.66), channel_id=1, source_target_pairs={{0,12},{1,11},{2,14},{3,9},{4,8},{5,15},{6,10},{7,13},{8,4},{9,3},... | collective-permute-start | bytes 150536 | tf_op jit(solution)/shard_map/ppermute | solution.py:390
  45.2 3.1 %shard_map.147 = (bf16[6144,512]{1,0:T(8,128)(2,1)}, bf16[6144,512]{1,0:T(8,128)(2,1)}) custom-call(bf16[6144,64]{1,0:T(8,128)(2,1)S(1)} %get-tuple-element.44.x_t, bf16[64,1024]{1,0:T(8,128)(2,1)S(1)} %get-tuple-element.45.d_both, bf16[256,512]{1,0:T(8,128)(2,1)S(1)} %get-tuple-element.52.refs_0_, ...), custom_call_target="tpu_custom_call", output_to_operand_aliasing={{0}: (4, {}), {1}: (5, {})} | custom-call | flops 1610612736 | bytes 6291456 | tf_op jit(solution)/shard_map/pallas_call | solution.py:367
  48.3 0.0 collective-permute-done.11.refs_1_
  48.3 0.0 collective-permute-done.12.refs_2_
  48.3 0.9 %collective-permute-done.13.refs_3_ = bf16[4,6272]{1,0:T(4,128)(2,1)S(1)} collective-permute-done((bf16[4,6272]{1,0:T(4,128)(2,1)S(1)}, bf16[4,6272]{1,0:T(4,128)(2,1)S(1)}, u32[]{:S(2)}, u32[]{:S(2)}) %collective-permute-start.13) | collective-permute-done | bytes 50208 | tf_op jit(solution)/shard_map/ppermute | solution.py:390
  49.2 0.9 %shard_map.150 = (bf16[16,6144]{1,0:T(8,128)(2,1)}, f32[8,16]{1,0:T(8,128)}) custom-call(f32[4,6272]{1,0:T(4,128)S(1)} %get-tuple-element.63.refs_0_, bf16[4,6272]{1,0:T(4,128)(2,1)S(1)} %collective-permute-done.11.refs_1_, bf16[4,6272]{1,0:T(4,128)(2,1)S(1)} %collective-permute-done.12.refs_2_, bf16[4,6272]{1,0:T(4,128)(2,1)S(1)} %collective-permute-done.13.refs_3_, ...), custom_call_target="tpu_custom_call" | custom-call | flops 1048576 | bytes 262144 | tf_op jit(solution)/shard_map/pallas_call | solution.py:28
  (6 shorter events, 0.1 us)
Async XLA Ops:
  1.8 11.9 %collective-permute-start = (bf16[4,12416]{1,0:T(4,128)(2,1)S(1)}, bf16[4,12416]{1,0:T(4,128)(2,1)S(1)}, u32[]{:S(2)}, u32[]{:S(2)}) collective-permute-start(bf16[4,12416]{1,0:T(4,128)(2,1)S(1)} %get-tuple-element.40.refs_2_), channel_id=1, source_target_pairs={{0,8},{1,9},{2,10},{3,11},{4,12},{5,13},{6,14},{7,15},{8,0},{9,1},... | collective-permute-start | bytes 297992 | tf_op jit(solution)/shard_map/ppermute | solution.py:390
  5.9 7.8 %collective-permute-start.2 = (bf16[4,12416]{1,0:T(4,128)(2,1)S(1)}, bf16[4,12416]{1,0:T(4,128)(2,1)S(1)}, u32[]{:S(2)}, u32[]{:S(2)}) collective-permute-start(bf16[4,12416]{1,0:T(4,128)(2,1)S(1)} %get-tuple-element.40.refs_2_), channel_id=1, source_target_pairs={{0,2},{1,5},{2,0},{3,7},{4,6},{5,1},{6,4},{7,3},{8,10},{9,13},{10,... | collective-permute-start | bytes 297992 | tf_op jit(solution)/shard_map/ppermute | solution.py:390
  7.5 6.3 %collective-permute-start.1 = (bf16[4,12416]{1,0:T(4,128)(2,1)S(1)}, bf16[4,12416]{1,0:T(4,128)(2,1)S(1)}, u32[]{:S(2)}, u32[]{:S(2)}) collective-permute-start(bf16[4,12416]{1,0:T(4,128)(2,1)S(1)} %get-tuple-element.40.refs_2_), channel_id=1, source_target_pairs={{0,4},{1,3},{2,6},{3,1},{4,0},{5,7},{6,2},{7,5},{8,12},{9,11},{10,... | collective-permute-start | bytes 297992 | tf_op jit(solution)/shard_map/ppermute | solution.py:390
  13.8 5.7 %collective-permute-start.3 = (bf16[4,12416]{1,0:T(4,128)(2,1)S(1)}, bf16[4,12416]{1,0:T(4,128)(2,1)S(1)}, u32[]{:S(2)}, u32[]{:S(2)}) collective-permute-start(bf16[4,12416]{1,0:T(4,128)(2,1)S(1)} %shard_map.139), channel_id=1, source_target_pairs={{0,4},{1,3},{2,6},{3,1},{4,0},{5,7},{6,2},{7,5},{8,12},{9,11},{10,... | collective-permute-start | bytes 297992 | tf_op jit(solution)/shard_map/ppermute | solution.py:390
  14.3 6.6 %collective-permute-start.6 = (bf16[4,12416]{1,0:T(4,128)(2,1)S(1)}, bf16[4,12416]{1,0:T(4,128)(2,1)S(1)}, u32[]{:S(2)}, u32[]{:S(2)}) collective-permute-start(bf16[4,12416]{1,0:T(4,128)(2,1)S(1)} %shard_map.139), channel_id=1, source_target_pairs={{0,6},{1,7},{2,4},{3,5},{4,2},{5,3},{6,0},{7,1},{8,14},{9,15},{10,... | collective-permute-start | bytes 297992 | tf_op jit(solution)/shard_map/ppermute | solution.py:390
  15.8 6.2 %collective-permute-start.4 = (bf16[4,12416]{1,0:T(4,128)(2,1)S(1)}, bf16[4,12416]{1,0:T(4,128)(2,1)S(1)}, u32[]{:S(2)}, u32[]{:S(2)}) collective-permute-start(bf16[4,12416]{1,0:T(4,128)(2,1)S(1)} %shard_map.139), channel_id=1, source_target_pairs={{0,2},{1,5},{2,0},{3,7},{4,6},{5,1},{6,4},{7,3},{8,10},{9,13},{10,... | collective-permute-start | bytes 297992 | tf_op jit(solution)/shard_map/ppermute | solution.py:390
  17.4 4.6 %collective-permute-start.5 = (bf16[4,12416]{1,0:T(4,128)(2,1)S(1)}, bf16[4,12416]{1,0:T(4,128)(2,1)S(1)}, u32[]{:S(2)}, u32[]{:S(2)}) collective-permute-start(bf16[4,12416]{1,0:T(4,128)(2,1)S(1)} %collective-permute-done.2.refs_2_), channel_id=1, source_target_pairs={{0,4},{1,3},{2,6},{3,1},{4,0},{5,7},{6,2},{7,5},{8,12},{9,11},{10,... | collective-permute-start | bytes 297992 | tf_op jit(solution)/shard_map/ppermute | solution.py:390
  21.0 2.6 %collective-permute-start.7 = (bf16[16,12416]{1,0:T(8,128)(2,1)S(1)}, bf16[16,12416]{1,0:T(8,128)(2,1)S(1)}, u32[]{:S(2)}, u32[]{:S(2)}) collective-permute-start(bf16[16,12416]{1,0:T(8,128)(2,1)S(1)} %pad_maximum_fusion.refs_0_), channel_id=1, source_target_pairs={{0,1},{1,0},{2,3},{3,2},{4,5},{5,4},{6,7},{7,6},{8,9},{9,8},{10,11... | collective-permute-start | bytes 1191944 | tf_op jit(solution)/shard_map/ppermute | solution.py:390
  22.2 1.8 %collective-permute-start.8 = (bf16[16,12416]{1,0:T(8,128)(2,1)S(1)}, bf16[16,12416]{1,0:T(8,128)(2,1)S(1)}, u32[]{:S(2)}, u32[]{:S(2)}) collective-permute-start(bf16[16,12416]{1,0:T(8,128)(2,1)S(1)} %pad_maximum_fusion.1.after.refs_1_), channel_id=1, source_target_pairs={{0,1},{1,0},{2,3},{3,2},{4,5},{5,4},{6,7},{7,6},{8,9},{9,8},{10,11... | collective-permute-start | bytes 1191944 | tf_op jit(solution)/shard_map/ppermute | solution.py:390
  32.8 1.8 %collective-permute-start.9 = (bf16[32,6272]{1,0:T(8,128)(2,1)S(1)}, bf16[32,6272]{1,0:T(8,128)(2,1)S(1)}, u32[]{:S(2)}, u32[]{:S(2)}) collective-permute-start(bf16[32,6272]{1,0:T(8,128)(2,1)S(1)} %get-tuple-element.60), channel_id=1, source_target_pairs={{0,1},{1,0},{2,3},{3,2},{4,5},{5,4},{6,7},{7,6},{8,9},{9,8},{10,11... | collective-permute-start | bytes 1204232 | tf_op jit(solution)/shard_map/ppermute | solution.py:390
  34.8 5.8 %collective-permute-start.10 = (bf16[16,6272]{1,0:T(8,128)(2,1)S(1)}, bf16[16,6272]{1,0:T(8,128)(2,1)S(1)}, u32[]{:S(2)}, u32[]{:S(2)}) collective-permute-start(bf16[16,6272]{1,0:T(8,128)(2,1)S(1)} %get-tuple-element.62), channel_id=1, source_target_pairs={{0,2},{1,5},{2,0},{3,7},{4,6},{5,1},{6,4},{7,3},{8,10},{9,13},{10,... | collective-permute-start | bytes 602120 | tf_op jit(solution)/shard_map/ppermute | solution.py:390
  40.8 7.5 %collective-permute-start.11 = (bf16[4,6272]{1,0:T(4,128)(2,1)S(1)}, bf16[4,6272]{1,0:T(4,128)(2,1)S(1)}, u32[]{:S(2)}, u32[]{:S(2)}) collective-permute-start(bf16[4,6272]{1,0:T(4,128)(2,1)S(1)} %get-tuple-element.64), channel_id=1, source_target_pairs={{0,8},{1,9},{2,10},{3,11},{4,12},{5,13},{6,14},{7,15},{8,0},{9,1},... | collective-permute-start | bytes 150536 | tf_op jit(solution)/shard_map/ppermute | solution.py:390
  41.3 7.0 %collective-permute-start.12 = (bf16[4,6272]{1,0:T(4,128)(2,1)S(1)}, bf16[4,6272]{1,0:T(4,128)(2,1)S(1)}, u32[]{:S(2)}, u32[]{:S(2)}) collective-permute-start(bf16[4,6272]{1,0:T(4,128)(2,1)S(1)} %get-tuple-element.65), channel_id=1, source_target_pairs={{0,4},{1,3},{2,6},{3,1},{4,0},{5,7},{6,2},{7,5},{8,12},{9,11},{10,... | collective-permute-start | bytes 150536 | tf_op jit(solution)/shard_map/ppermute | solution.py:390
  43.3 5.9 %collective-permute-start.13 = (bf16[4,6272]{1,0:T(4,128)(2,1)S(1)}, bf16[4,6272]{1,0:T(4,128)(2,1)S(1)}, u32[]{:S(2)}, u32[]{:S(2)}) collective-permute-start(bf16[4,6272]{1,0:T(4,128)(2,1)S(1)} %get-tuple-element.66), channel_id=1, source_target_pairs={{0,12},{1,11},{2,14},{3,9},{4,8},{5,15},{6,10},{7,13},{8,4},{9,3},... | collective-permute-start | bytes 150536 | tf_op jit(solution)/shard_map/ppermute | solution.py:390

commit v21 on v20

--- a/solution.py
+++ b/solution.py
@@ -497,7 +497,7 @@
         grad_gate, grad_up = grads_of(x_t, d_both, cuts[2], cuts[3] - cuts[2], tuple(pair))
 
         both = tuple(f ^ s for f, s in zip(first, second))
-        paths = [((1, 1),), (third,), (first, second, both)] + [(b,) for b in levels[:-3][::-1]]
+        paths = [((1, 1),), (third,), (both, first, second)] + [(b,) for b in levels[:-3][::-1]]
         sent = [low]
         for path, following in zip(paths, paths[1:] + [()]):
             gots = [swap(block, bits) for block, bits in zip(sent, path)]
@@ -512,6 +512,8 @@
                 16 * keep.shape[0] * wide,
                 after=[first_pair[2]] if path == paths[0] else [],
             )
+            if len(sent) == 3:
+                sent = [sent[2], sent[0], sent[1]]
 
 
         grad_tokens, grad_logits = call(

time: 50.4 us -> 49.5 us (0.982)
  waiting for transfers between devices: 5.52 us -> 4.69 us
    ppermute x14, waiting for transfers between devices: 5.52 us -> 4.69 us  [swap(): return lax.ppermute(block, 'blk', [(i, i ^ bits[i % 2]) for i in range(n)])]
where the time goes in v21:
time: 49.5 us; the launch traced here: 49.3 us
  Pallas kernels  26.2 us (53%)
  starting transfers between devices  17.1 us (35%)
  waiting for transfers between devices  4.69 us (9%)
  between operations  0.82 us (2%)
    ppermute x14, starting transfers between devices, swap(): return lax.ppermute(block, 'blk', [(i, i ^ bits[i % 2]) for i in range(n)])  17.1 us
    pallas_call x3, Pallas kernels, grads_of(): pl.pallas_call(kernel, out_shape=outs, in_specs=whole(2 + len(down)) + (w...  8.96 us
    pallas_call x1, Pallas kernels, shards(): pl.pallas_call(expert_kernel, out_shape=[jax.ShapeDtypeStruct((half, wide...  8.78 us
    pallas_call x1, Pallas kernels, fetch(): pl.pallas_call(functools.partial(fetch_kernel, count), out_shape=[pltpu.V...  4.7 us
    ppermute x14, waiting for transfers between devices, swap(): return lax.ppermute(block, 'blk', [(i, i ^ bits[i % 2]) for i in range(n)])  4.69 us
    pallas_call x1, Pallas kernels, shards(): pl.pallas_call(router_kernel, out_shape=[jax.ShapeDtypeStruct((1, count),...  1.3 us
    pallas_call x3, Pallas kernels, call(): pl.pallas_call(body, out_shape=[jax.ShapeDtypeStruct(s, t) for s, t in ou...  1.24 us
    pallas_call x1, Pallas kernels, shards(): pl.pallas_call(select_kernel, out_shape=[jax.ShapeDtypeStruct((slots, wid...  1.19 us
  transfers between devices with their start and end apart: 14, of which 6 were waited for; matrix products, arithmetic and copies ran while one was open for 1% of the time, Pallas kernels for 30%

profile of v21, /device:TPU:0, one launch (start us, length us, event | category | flops | bytes accessed | tf_op | source)
XLA Modules:
  0.0 49.3 jit_solution(11967516702385347552)
XLA Ops:
  0.6 1.2 %shard_map.135 = (bf16[4,12416]{1,0:T(4,128)(2,1)S(1)}, f32[16,16]{1,0:T(8,128)S(1)}) custom-call(f32[8,16]{1,0:T(8,128)} %bitcast.6, s32[2,16]{1,0:T(2,128)} %bitcast.9, bf16[16,6144]{1,0:T(8,128)(2,1)} %tokens_in.1, bf16[4,6144]{1,0:T(4,128)(2,1)} %y_in.1), custom_call_target="tpu_custom_call" | custom-call | flops 1048576 | bytes 4194304 | tf_op jit(solution)/shard_map/pallas_call | solution.py:404
  1.8 4.1 %collective-permute-start = (bf16[4,12416]{1,0:T(4,128)(2,1)S(1)}, bf16[4,12416]{1,0:T(4,128)(2,1)S(1)}, u32[]{:S(2)}, u32[]{:S(2)}) collective-permute-start(bf16[4,12416]{1,0:T(4,128)(2,1)S(1)} %get-tuple-element.40.refs_2_), channel_id=1, source_target_pairs={{0,8},{1,9},{2,10},{3,11},{4,12},{5,13},{6,14},{7,15},{8,0},{9,1},... | collective-permute-start | bytes 297992 | tf_op jit(solution)/shard_map/ppermute | solution.py:390
  5.9 1.5 %collective-permute-start.2 = (bf16[4,12416]{1,0:T(4,128)(2,1)S(1)}, bf16[4,12416]{1,0:T(4,128)(2,1)S(1)}, u32[]{:S(2)}, u32[]{:S(2)}) collective-permute-start(bf16[4,12416]{1,0:T(4,128)(2,1)S(1)} %get-tuple-element.40.refs_2_), channel_id=1, source_target_pairs={{0,2},{1,5},{2,0},{3,7},{4,6},{5,1},{6,4},{7,3},{8,10},{9,13},{10,... | collective-permute-start | bytes 297992 | tf_op jit(solution)/shard_map/ppermute | solution.py:390
  7.5 1.6 %collective-permute-start.1 = (bf16[4,12416]{1,0:T(4,128)(2,1)S(1)}, bf16[4,12416]{1,0:T(4,128)(2,1)S(1)}, u32[]{:S(2)}, u32[]{:S(2)}) collective-permute-start(bf16[4,12416]{1,0:T(4,128)(2,1)S(1)} %get-tuple-element.40.refs_2_), channel_id=1, source_target_pairs={{0,4},{1,3},{2,6},{3,1},{4,0},{5,7},{6,2},{7,5},{8,12},{9,11},{10,... | collective-permute-start | bytes 297992 | tf_op jit(solution)/shard_map/ppermute | solution.py:390
  9.0 4.7 %shard_map.138 = (bf16[6144,512]{1,0:T(8,128)(2,1)S(1)}, bf16[6144,512]{1,0:T(8,128)(2,1)S(1)}) custom-call(bf16[6144,512]{1,0:T(8,128)(2,1)} %refs_0_.1, bf16[6144,512]{1,0:T(8,128)(2,1)} %refs_1_.1, bf16[4,12416]{1,0:T(4,128)(2,1)S(1)} %get-tuple-element.40.refs_2_), custom_call_target="tpu_custom_call" | custom-call | bytes 12582912 | tf_op jit(solution)/shard_map/pallas_call | solution.py:165
  13.7 0.0 collective-permute-done.block
  13.8 0.0 collective-permute-done.2.refs_2_
  13.8 0.0 collective-permute-done.1.refs_1_
  13.8 0.5 %collective-permute-start.3 = (bf16[4,12416]{1,0:T(4,128)(2,1)S(1)}, bf16[4,12416]{1,0:T(4,128)(2,1)S(1)}, u32[]{:S(2)}, u32[]{:S(2)}) collective-permute-start(bf16[4,12416]{1,0:T(4,128)(2,1)S(1)} %shard_map.139), channel_id=1, source_target_pairs={{0,4},{1,3},{2,6},{3,1},{4,0},{5,7},{6,2},{7,5},{8,12},{9,11},{10,... | collective-permute-start | bytes 297992 | tf_op jit(solution)/shard_map/ppermute | solution.py:390
  14.3 1.5 %collective-permute-start.6 = (bf16[4,12416]{1,0:T(4,128)(2,1)S(1)}, bf16[4,12416]{1,0:T(4,128)(2,1)S(1)}, u32[]{:S(2)}, u32[]{:S(2)}) collective-permute-start(bf16[4,12416]{1,0:T(4,128)(2,1)S(1)} %shard_map.139), channel_id=1, source_target_pairs={{0,6},{1,7},{2,4},{3,5},{4,2},{5,3},{6,0},{7,1},{8,14},{9,15},{10,... | collective-permute-start | bytes 297992 | tf_op jit(solution)/shard_map/ppermute | solution.py:390
  15.8 1.5 %collective-permute-start.4 = (bf16[4,12416]{1,0:T(4,128)(2,1)S(1)}, bf16[4,12416]{1,0:T(4,128)(2,1)S(1)}, u32[]{:S(2)}, u32[]{:S(2)}) collective-permute-start(bf16[4,12416]{1,0:T(4,128)(2,1)S(1)} %shard_map.139), channel_id=1, source_target_pairs={{0,2},{1,5},{2,0},{3,7},{4,6},{5,1},{6,4},{7,3},{8,10},{9,13},{10,... | collective-permute-start | bytes 297992 | tf_op jit(solution)/shard_map/ppermute | solution.py:390
  17.4 0.5 collective-permute-start.5
  17.8 1.7 %collective-permute-done.3.block = bf16[4,12416]{1,0:T(4,128)(2,1)S(1)} collective-permute-done((bf16[4,12416]{1,0:T(4,128)(2,1)S(1)}, bf16[4,12416]{1,0:T(4,128)(2,1)S(1)}, u32[]{:S(2)}, u32[]{:S(2)}) %collective-permute-start.3) | collective-permute-done | bytes 99360 | tf_op jit(solution)/shard_map/ppermute | solution.py:390
  19.5 0.2 pad_maximum_fusion.refs_0_
  19.8 1.2 %collective-permute-done.6.block = bf16[4,12416]{1,0:T(4,128)(2,1)S(1)} collective-permute-done((bf16[4,12416]{1,0:T(4,128)(2,1)S(1)}, bf16[4,12416]{1,0:T(4,128)(2,1)S(1)}, u32[]{:S(2)}, u32[]{:S(2)}) %collective-permute-start.6) | collective-permute-done | bytes 99360 | tf_op jit(solution)/shard_map/ppermute | solution.py:390
  21.0 0.1 collective-permute-start.7
  21.1 0.9 %collective-permute-done.5 = bf16[4,12416]{1,0:T(4,128)(2,1)S(1)} collective-permute-done((bf16[4,12416]{1,0:T(4,128)(2,1)S(1)}, bf16[4,12416]{1,0:T(4,128)(2,1)S(1)}, u32[]{:S(2)}, u32[]{:S(2)}) %collective-permute-start.5) | collective-permute-done | bytes 99360 | tf_op jit(solution)/shard_map/ppermute | solution.py:390
  22.0 0.0 collective-permute-done.4
  22.0 0.2 pad_maximum_fusion.1.after.refs_1_
  22.2 0.1 collective-permute-start.8
  22.3 1.3 %shard_map.143 = (f32[1,16]{1,0:T(1,128)}, f32[1,16]{1,0:T(1,128)}, f32[8,16]{1,0:T(8,128)S(1)}, f32[8,16]{1,0:T(8,128)S(1)}) custom-call(f32[8,16]{1,0:T(8,128)} %bitcast.7, f32[8,16]{1,0:T(8,128)} %bitcast.8, s32[2,16]{1,0:T(2,128)} %bitcast.10, bf16[16,12416]{1,0:T(8,128)(2,1)S(1)} %pad_maximum_fusion.1.after.refs_1_), custom_call_target="tpu_custom_call" | custom-call | flops 1048576 | bytes 4194304 | tf_op jit(solution)/shard_map/pallas_call | solution.py:444
  23.6 0.0 collective-permute-done.7.refs_2_
  23.6 0.4 collective-permute-done.8.refs_3_
  24.0 8.8 %shard_map.144 = (bf16[32,6272]{1,0:T(8,128)(2,1)S(1)}, f32[32,6272]{1,0:T(8,128)S(1)}, bf16[512,64]{1,0:T(8,128)(2,1)S(1)}, bf16[64,1024]{1,0:T(8,128)(2,1)S(1)...) custom-call(bf16[16,12416]{1,0:T(8,128)(2,1)S(1)} %pad_maximum_fusion.refs_0_, ...), custom_call_target="tpu_custom_call" | custom-call | flops 6442450944 | bytes 12582912 | tf_op jit(solution)/shard_map/pallas_call | solution.py:468
  32.8 0.2 collective-permute-start.9
  33.0 1.2 %shard_map.145 = (bf16[6144,512]{1,0:T(8,128)(2,1)}, bf16[6144,512]{1,0:T(8,128)(2,1)}, bf16[256,512]{1,0:T(8,128)(2,1)S(1)}, bf16[256,512]{1,0:T(8,128)(2,1)S(1)}) custom-call(bf16[6144,64]{1,0:T(8,128)(2,1)S(1)} %get-tuple-element.44.x_t, bf16[64,1024]{1,0:T(8,128)(2,1)S(1)} %get-tuple-element.45.d_both), custom_call_target="tpu_custom_call" | custom-call | flops 402653184 | bytes 1572864 | tf_op jit(solution)/shard_map/pallas_call | solution.py:367
  34.3 0.4 collective-permute-done.9.refs_1_
  34.6 0.2 shard_map.148
  34.8 1.1 %collective-permute-start.10 = (bf16[16,6272]{1,0:T(8,128)(2,1)S(1)}, bf16[16,6272]{1,0:T(8,128)(2,1)S(1)}, u32[]{:S(2)}, u32[]{:S(2)}) collective-permute-start(bf16[16,6272]{1,0:T(8,128)(2,1)S(1)} %get-tuple-element.62), channel_id=1, source_target_pairs={{0,2},{1,5},{2,0},{3,7},{4,6},{5,1},{6,4},{7,3},{8,10},{9,13},{10,... | collective-permute-start | bytes 602120 | tf_op jit(solution)/shard_map/ppermute | solution.py:390
  35.9 4.7 %shard_map.146 = (bf16[512,6144]{1,0:T(8,128)(2,1)}, bf16[6144,512]{1,0:T(8,128)(2,1)}, bf16[6144,512]{1,0:T(8,128)(2,1)}, bf16[256,512]{1,0:T(8,128)(2,1)S(1)}, bf16[256,512]{1,0:T(8,128)(2,1)S(1)}) custom-call(bf16[512,64]{1,0:T(8,128)(2,1)S(1)} %get-tuple-element.46.weighted_t, ...), custom_call_target="tpu_custom_call", output_to_operand_aliasing={{1}: (6, {}), {2}: (7, {})} | custom-call | flops 2818572288 | bytes 11010048 | tf_op jit(solution)/shard_map/pallas_call | solution.py:367
  40.6 0.0 collective-permute-done.10.refs_1_
  40.6 0.2 shard_map.149
  40.8 2.0 %collective-permute-start.11 = (bf16[4,6272]{1,0:T(4,128)(2,1)S(1)}, bf16[4,6272]{1,0:T(4,128)(2,1)S(1)}, u32[]{:S(2)}, u32[]{:S(2)}) collective-permute-start(bf16[4,6272]{1,0:T(4,128)(2,1)S(1)} %get-tuple-element.64), channel_id=1, source_target_pairs={{0,12},{1,11},{2,14},{3,9},{4,8},{5,15},{6,10},{7,13},{8,4},{9,3},... | collective-permute-start | bytes 150536 | tf_op jit(solution)/shard_map/ppermute | solution.py:390
  42.8 0.0 collective-permute-start.12
  42.8 2.5 %collective-permute-start.13 = (bf16[4,6272]{1,0:T(4,128)(2,1)S(1)}, bf16[4,6272]{1,0:T(4,128)(2,1)S(1)}, u32[]{:S(2)}, u32[]{:S(2)}) collective-permute-start(bf16[4,6272]{1,0:T(4,128)(2,1)S(1)} %get-tuple-element.66), channel_id=1, source_target_pairs={{0,4},{1,3},{2,6},{3,1},{4,0},{5,7},{6,2},{7,5},{8,12},{9,11},{10,... | collective-permute-start | bytes 150536 | tf_op jit(solution)/shard_map/ppermute | solution.py:390
  45.2 3.1 %shard_map.147 = (bf16[6144,512]{1,0:T(8,128)(2,1)}, bf16[6144,512]{1,0:T(8,128)(2,1)}) custom-call(bf16[6144,64]{1,0:T(8,128)(2,1)S(1)} %get-tuple-element.44.x_t, bf16[64,1024]{1,0:T(8,128)(2,1)S(1)} %get-tuple-element.45.d_both, bf16[256,512]{1,0:T(8,128)(2,1)S(1)} %get-tuple-element.52.refs_0_, ...), custom_call_target="tpu_custom_call", output_to_operand_aliasing={{0}: (4, {}), {1}: (5, {})} | custom-call | flops 1610612736 | bytes 6291456 | tf_op jit(solution)/shard_map/pallas_call | solution.py:367
  48.3 0.0 collective-permute-done.11.refs_1_
  48.3 0.1 collective-permute-done.12.refs_2_
  48.4 0.0 collective-permute-done.13.refs_3_
  48.4 0.9 %shard_map.150 = (bf16[16,6144]{1,0:T(8,128)(2,1)}, f32[8,16]{1,0:T(8,128)}) custom-call(f32[4,6272]{1,0:T(4,128)S(1)} %get-tuple-element.63.refs_0_, bf16[4,6272]{1,0:T(4,128)(2,1)S(1)} %collective-permute-done.11.refs_1_, bf16[4,6272]{1,0:T(4,128)(2,1)S(1)} %collective-permute-done.12.refs_2_, bf16[4,6272]{1,0:T(4,128)(2,1)S(1)} %collective-permute-done.13.refs_3_, ...), custom_call_target="tpu_custom_call" | custom-call | flops 1048576 | bytes 262144 | tf_op jit(solution)/shard_map/pallas_call | solution.py:28
  (6 shorter events, 0.1 us)
Async XLA Ops:
  1.8 11.9 %collective-permute-start = (bf16[4,12416]{1,0:T(4,128)(2,1)S(1)}, bf16[4,12416]{1,0:T(4,128)(2,1)S(1)}, u32[]{:S(2)}, u32[]{:S(2)}) collective-permute-start(bf16[4,12416]{1,0:T(4,128)(2,1)S(1)} %get-tuple-element.40.refs_2_), channel_id=1, source_target_pairs={{0,8},{1,9},{2,10},{3,11},{4,12},{5,13},{6,14},{7,15},{8,0},{9,1},... | collective-permute-start | bytes 297992 | tf_op jit(solution)/shard_map/ppermute | solution.py:390
  5.9 7.8 %collective-permute-start.2 = (bf16[4,12416]{1,0:T(4,128)(2,1)S(1)}, bf16[4,12416]{1,0:T(4,128)(2,1)S(1)}, u32[]{:S(2)}, u32[]{:S(2)}) collective-permute-start(bf16[4,12416]{1,0:T(4,128)(2,1)S(1)} %get-tuple-element.40.refs_2_), channel_id=1, source_target_pairs={{0,2},{1,5},{2,0},{3,7},{4,6},{5,1},{6,4},{7,3},{8,10},{9,13},{10,... | collective-permute-start | bytes 297992 | tf_op jit(solution)/shard_map/ppermute | solution.py:390
  7.5 6.3 %collective-permute-start.1 = (bf16[4,12416]{1,0:T(4,128)(2,1)S(1)}, bf16[4,12416]{1,0:T(4,128)(2,1)S(1)}, u32[]{:S(2)}, u32[]{:S(2)}) collective-permute-start(bf16[4,12416]{1,0:T(4,128)(2,1)S(1)} %get-tuple-element.40.refs_2_), channel_id=1, source_target_pairs={{0,4},{1,3},{2,6},{3,1},{4,0},{5,7},{6,2},{7,5},{8,12},{9,11},{10,... | collective-permute-start | bytes 297992 | tf_op jit(solution)/shard_map/ppermute | solution.py:390
  13.8 5.7 %collective-permute-start.3 = (bf16[4,12416]{1,0:T(4,128)(2,1)S(1)}, bf16[4,12416]{1,0:T(4,128)(2,1)S(1)}, u32[]{:S(2)}, u32[]{:S(2)}) collective-permute-start(bf16[4,12416]{1,0:T(4,128)(2,1)S(1)} %shard_map.139), channel_id=1, source_target_pairs={{0,4},{1,3},{2,6},{3,1},{4,0},{5,7},{6,2},{7,5},{8,12},{9,11},{10,... | collective-permute-start | bytes 297992 | tf_op jit(solution)/shard_map/ppermute | solution.py:390
  14.3 6.6 %collective-permute-start.6 = (bf16[4,12416]{1,0:T(4,128)(2,1)S(1)}, bf16[4,12416]{1,0:T(4,128)(2,1)S(1)}, u32[]{:S(2)}, u32[]{:S(2)}) collective-permute-start(bf16[4,12416]{1,0:T(4,128)(2,1)S(1)} %shard_map.139), channel_id=1, source_target_pairs={{0,6},{1,7},{2,4},{3,5},{4,2},{5,3},{6,0},{7,1},{8,14},{9,15},{10,... | collective-permute-start | bytes 297992 | tf_op jit(solution)/shard_map/ppermute | solution.py:390
  15.8 6.2 %collective-permute-start.4 = (bf16[4,12416]{1,0:T(4,128)(2,1)S(1)}, bf16[4,12416]{1,0:T(4,128)(2,1)S(1)}, u32[]{:S(2)}, u32[]{:S(2)}) collective-permute-start(bf16[4,12416]{1,0:T(4,128)(2,1)S(1)} %shard_map.139), channel_id=1, source_target_pairs={{0,2},{1,5},{2,0},{3,7},{4,6},{5,1},{6,4},{7,3},{8,10},{9,13},{10,... | collective-permute-start | bytes 297992 | tf_op jit(solution)/shard_map/ppermute | solution.py:390
  17.4 4.6 %collective-permute-start.5 = (bf16[4,12416]{1,0:T(4,128)(2,1)S(1)}, bf16[4,12416]{1,0:T(4,128)(2,1)S(1)}, u32[]{:S(2)}, u32[]{:S(2)}) collective-permute-start(bf16[4,12416]{1,0:T(4,128)(2,1)S(1)} %collective-permute-done.2.refs_2_), channel_id=1, source_target_pairs={{0,4},{1,3},{2,6},{3,1},{4,0},{5,7},{6,2},{7,5},{8,12},{9,11},{10,... | collective-permute-start | bytes 297992 | tf_op jit(solution)/shard_map/ppermute | solution.py:390
  21.0 2.6 %collective-permute-start.7 = (bf16[16,12416]{1,0:T(8,128)(2,1)S(1)}, bf16[16,12416]{1,0:T(8,128)(2,1)S(1)}, u32[]{:S(2)}, u32[]{:S(2)}) collective-permute-start(bf16[16,12416]{1,0:T(8,128)(2,1)S(1)} %pad_maximum_fusion.refs_0_), channel_id=1, source_target_pairs={{0,1},{1,0},{2,3},{3,2},{4,5},{5,4},{6,7},{7,6},{8,9},{9,8},{10,11... | collective-permute-start | bytes 1191944 | tf_op jit(solution)/shard_map/ppermute | solution.py:390
  22.2 1.8 %collective-permute-start.8 = (bf16[16,12416]{1,0:T(8,128)(2,1)S(1)}, bf16[16,12416]{1,0:T(8,128)(2,1)S(1)}, u32[]{:S(2)}, u32[]{:S(2)}) collective-permute-start(bf16[16,12416]{1,0:T(8,128)(2,1)S(1)} %pad_maximum_fusion.1.after.refs_1_), channel_id=1, source_target_pairs={{0,1},{1,0},{2,3},{3,2},{4,5},{5,4},{6,7},{7,6},{8,9},{9,8},{10,11... | collective-permute-start | bytes 1191944 | tf_op jit(solution)/shard_map/ppermute | solution.py:390
  32.8 1.8 %collective-permute-start.9 = (bf16[32,6272]{1,0:T(8,128)(2,1)S(1)}, bf16[32,6272]{1,0:T(8,128)(2,1)S(1)}, u32[]{:S(2)}, u32[]{:S(2)}) collective-permute-start(bf16[32,6272]{1,0:T(8,128)(2,1)S(1)} %get-tuple-element.60), channel_id=1, source_target_pairs={{0,1},{1,0},{2,3},{3,2},{4,5},{5,4},{6,7},{7,6},{8,9},{9,8},{10,11... | collective-permute-start | bytes 1204232 | tf_op jit(solution)/shard_map/ppermute | solution.py:390
  34.8 5.8 %collective-permute-start.10 = (bf16[16,6272]{1,0:T(8,128)(2,1)S(1)}, bf16[16,6272]{1,0:T(8,128)(2,1)S(1)}, u32[]{:S(2)}, u32[]{:S(2)}) collective-permute-start(bf16[16,6272]{1,0:T(8,128)(2,1)S(1)} %get-tuple-element.62), channel_id=1, source_target_pairs={{0,2},{1,5},{2,0},{3,7},{4,6},{5,1},{6,4},{7,3},{8,10},{9,13},{10,... | collective-permute-start | bytes 602120 | tf_op jit(solution)/shard_map/ppermute | solution.py:390
  40.8 7.5 %collective-permute-start.11 = (bf16[4,6272]{1,0:T(4,128)(2,1)S(1)}, bf16[4,6272]{1,0:T(4,128)(2,1)S(1)}, u32[]{:S(2)}, u32[]{:S(2)}) collective-permute-start(bf16[4,6272]{1,0:T(4,128)(2,1)S(1)} %get-tuple-element.64), channel_id=1, source_target_pairs={{0,12},{1,11},{2,14},{3,9},{4,8},{5,15},{6,10},{7,13},{8,4},{9,3},... | collective-permute-start | bytes 150536 | tf_op jit(solution)/shard_map/ppermute | solution.py:390
  42.8 5.6 %collective-permute-start.12 = (bf16[4,6272]{1,0:T(4,128)(2,1)S(1)}, bf16[4,6272]{1,0:T(4,128)(2,1)S(1)}, u32[]{:S(2)}, u32[]{:S(2)}) collective-permute-start(bf16[4,6272]{1,0:T(4,128)(2,1)S(1)} %get-tuple-element.65), channel_id=1, source_target_pairs={{0,8},{1,9},{2,10},{3,11},{4,12},{5,13},{6,14},{7,15},{8,0},{9,1},... | collective-permute-start | bytes 150536 | tf_op jit(solution)/shard_map/ppermute | solution.py:390
  42.8 5.6 %collective-permute-start.13 = (bf16[4,6272]{1,0:T(4,128)(2,1)S(1)}, bf16[4,6272]{1,0:T(4,128)(2,1)S(1)}, u32[]{:S(2)}, u32[]{:S(2)}) collective-permute-start(bf16[4,6272]{1,0:T(4,128)(2,1)S(1)} %get-tuple-element.66), channel_id=1, source_target_pairs={{0,4},{1,3},{2,6},{3,1},{4,0},{5,7},{6,2},{7,5},{8,12},{9,11},{10,... | collective-permute-start | bytes 150536 | tf_op jit(solution)/shard_map/ppermute | solution.py:390
